TPU v7x, 32 devices: a whole 2x2x4 slice. The times are simulated.
32 devices in a mesh: seq: 8 (over z, core), mp: 2 (over y), dp: 2 (over x).
Axes of the slice: x: 2, y: 2, z: 4, core: 2. Of those that a mesh axis runs over, the one named last changes fastest.
Arguments:
- latents: bfloat16 [2, 1536, 1792], P('dp', 'seq', 'mp'), may hold values from -6 to 6
- grad_out: bfloat16 [2, 1536, 1792], P('dp', 'seq', 'mp'), may hold values from -6 to 6
- sync_mod: bfloat16 [2, 1200, 3584], P('dp', 'seq'), may hold values from -3 to 3
- w_qkv: bfloat16 [1792, 3, 1024], P(None, None, 'mp'), may hold values from -0.125 to 0.125
- w_out: bfloat16 [1024, 1792], P('mp'), may hold values from -0.1875 to 0.1875
- q_gain: float32 [8, 128], P('mp'), may hold values from 0.5 to 2.5
- k_gain: float32 [8, 128], P('mp'), may hold values from 0.5 to 2.5
- frame_of: int32 [2, 1536], P('dp', 'seq'), may hold values from 0 to 1199, as said below
- group_id: int32 [2, 1536], P('dp'), may hold values from 0 to 31, never falling along the last dimension, each value on 1 to 96 neighbouring positions
- clip_len: int32 [2], P('dp'), may hold values from 768 to 1536
Outputs:
- mixed: bfloat16 [2, 1536, 1792], P('dp', 'seq', 'mp')
- grad_latents: bfloat16 [2, 1536, 1792], P('dp', 'seq', 'mp')
- grad_wqkv: float32 [1792, 3, 1024], P(('seq', 'dp'), None, 'mp')
- grad_wout: float32 [1024, 1792], P('mp', ('seq', 'dp'))
Inputs may be any that keep to these rules, and one draw needn't show every extreme that they name: frame_of[c, l] = floor((96 l + s) / 125) with a phase s of 0 to 124 drawn for each clip, so the latents on seq index j read frames held by seq indices j - 1 and j only.
All inputs are finite; a program needn't handle non-finite values.
Results may differ from a plain program's by a relative error of at most 0.012.
The roundings to bfloat16 on the way count: a program that leaves them out, or rounds other values in their place, can miss the bound.
Values may be sent and summed in bfloat16 or wider, within the bound.
No kernel may reach another device: no remote copies, remote signals or barrier semaphores. Data moves between devices by JAX's collectives and lax.ppermute only.
A program may use at most 128 MiB of HBM per device.

v0:
```python
import jax
import jax.numpy as jnp
from jax import lax
from jax.sharding import PartitionSpec as P

EPSILON = 1e-06
NEG_FILL = -1e30


def from_behind(value, axis, steps):
    count = lax.axis_size(axis)
    leading, last = (max(0, -steps), min(count, count - steps))
    return lax.ppermute(value, axis, [(source, source + steps) for source in range(leading, last)])


def inv_rms(values):
    return lax.rsqrt(jnp.mean(values * values, axis=-1, keepdims=True) + EPSILON)


def norm_back(raw, inv_norm, gains, upstream):
    inner_dot = jnp.mean(upstream * gains * raw, axis=-1, keepdims=True)
    return inv_norm * (gains * upstream - raw * inv_norm * inv_norm * inner_dot)


def group_mask(group_ids, clip_length, query_first, query_span, key_span):
    query_group = lax.dynamic_slice_in_dim(group_ids, query_first, query_span, 1)
    key_place = lax.iota(jnp.int32, key_span)
    allowed = (group_ids[:, None, :] <= query_group[:, :, None]) & (
        key_place[None, None, :] < clip_length[:, None, None]
    )
    return allowed[:, None, :, :]


def head_logits(queries, keys, factor):
    return jnp.einsum("cqhd,ckhd->chqk", queries, keys, preferred_element_type=jnp.float32) * factor


def on_device(
    latents, grad_out, sync_mod, w_qkv, w_out, q_gain, k_gain, frame_of, group_id, clip_len
):
    clip_count, row_count, width_part = latents.shape
    frame_count = sync_mod.shape[1]
    model_width = sync_mod.shape[2] // 2
    heads_here, head_dim = q_gain.shape
    inner_width = heads_here * head_dim
    factor = head_dim ** (-0.5)
    seq_place = lax.axis_index("seq")
    model_place = lax.axis_index("mp")
    query_first = seq_place * row_count
    inputs_full, upstream_full = (
        lax.all_gather(latents, "mp", axis=2, tiled=True),
        lax.all_gather(grad_out, "mp", axis=2, tiled=True),
    )
    earlier = from_behind(sync_mod, "seq", 1)
    window = jnp.concatenate([earlier, sync_mod], axis=1)
    local_frame = frame_of - (seq_place * frame_count - frame_count)
    selector = (
        local_frame[:, :, None] == lax.iota(jnp.int32, 2 * frame_count)[None, None, :]
    ).astype(jnp.bfloat16)
    modulation = jnp.einsum("clf,cfe->cle", selector, window, preferred_element_type=jnp.float32)
    mod_scale = modulation[:, :, :model_width]
    mod_gate = modulation[:, :, model_width:]
    inputs_f = inputs_full.astype(jnp.float32)
    inv_norm = inv_rms(inputs_f)
    normed = inputs_f * inv_norm
    hidden = (normed * (1.0 + mod_scale)).astype(jnp.bfloat16)
    flat_hidden = hidden.reshape(clip_count * row_count, model_width)
    flat_weight = w_qkv.reshape(model_width, 3 * inner_width)
    projected = jnp.dot(flat_hidden, flat_weight, preferred_element_type=jnp.float32)
    projected = projected.reshape(clip_count, row_count, 3, heads_here, head_dim)
    query_raw = projected[:, :, 0]
    key_raw = projected[:, :, 1]
    query_inv = inv_rms(query_raw)
    key_inv = inv_rms(key_raw)
    query_norm = (query_raw * query_inv * q_gain).astype(jnp.bfloat16)
    key_norm = (key_raw * key_inv * k_gain).astype(jnp.bfloat16)
    values = projected[:, :, 2].astype(jnp.bfloat16)
    row_max = jnp.full((clip_count, heads_here, row_count), NEG_FILL, jnp.float32)
    key_piece = lax.all_gather(key_norm, "seq", axis=1, tiled=True)
    value_piece = lax.all_gather(values, "seq", axis=1, tiled=True)
    span_len = key_piece.shape[1]
    allowed = group_mask(group_id, clip_len, query_first, row_count, span_len)
    logits = jnp.where(allowed, head_logits(query_norm, key_piece, factor), NEG_FILL)
    new_max = jnp.maximum(row_max, jnp.max(logits, axis=-1))
    unnorm = jnp.where(allowed, jnp.exp(logits - new_max[..., None]), 0.0)
    row_sum = jnp.sum(unnorm, axis=-1)
    row_acc = jnp.einsum(
        "chqk,ckhd->chqd",
        unnorm.astype(jnp.bfloat16),
        value_piece,
        preferred_element_type=jnp.float32,
    )
    row_max, row_sum, row_acc = (new_max, row_sum, row_acc)
    key_all, value_all = (
        lax.all_gather(key_norm, "seq", axis=1, tiled=True),
        lax.all_gather(values, "seq", axis=1, tiled=True),
    )
    heads_out = jnp.transpose(row_acc / row_sum[..., None], (0, 2, 1, 3)).astype(jnp.bfloat16)
    out_rows = heads_out.reshape(clip_count * row_count, inner_width)
    attn_part = jnp.dot(out_rows, w_out, preferred_element_type=jnp.float32).reshape(
        clip_count, row_count, model_width
    )
    attn_mine = lax.psum_scatter(attn_part, "mp", scatter_dimension=2, tiled=True)
    gate_mine = lax.dynamic_slice_in_dim(mod_gate, model_place * width_part, width_part, 2)
    mixed = (latents.astype(jnp.float32) + gate_mine * attn_mine).astype(jnp.bfloat16)
    grad_attn = (upstream_full.astype(jnp.float32) * mod_gate).astype(jnp.bfloat16)
    flat_grad = grad_attn.reshape(clip_count * row_count, model_width)
    grad_wout = jnp.einsum("ti,td->id", out_rows, flat_grad, preferred_element_type=jnp.float32)
    grad_heads = jnp.einsum(
        "td,id->ti", flat_grad, w_out, preferred_element_type=jnp.float32
    ).astype(jnp.bfloat16)
    grad_heads = grad_heads.reshape(clip_count, row_count, heads_here, head_dim)
    out_dot = jnp.transpose(
        jnp.sum(grad_heads.astype(jnp.float32) * heads_out.astype(jnp.float32), axis=-1), (0, 2, 1)
    )
    allowed_all = group_mask(group_id, clip_len, query_first, row_count, key_all.shape[1])
    logits_all = head_logits(query_norm, key_all, factor)
    probs = jnp.where(
        allowed_all, jnp.exp(logits_all - row_max[..., None]) / row_sum[..., None], 0.0
    )
    grad_probs = jnp.einsum(
        "cqhd,ckhd->chqk", grad_heads, value_all, preferred_element_type=jnp.float32
    )
    grad_logits = (probs * (grad_probs - out_dot[..., None])).astype(jnp.bfloat16)
    grad_qnorm = (
        jnp.einsum("chqk,ckhd->cqhd", grad_logits, key_all, preferred_element_type=jnp.float32)
        * factor
    )
    grad_key_all = (
        jnp.einsum("chqk,cqhd->ckhd", grad_logits, query_norm, preferred_element_type=jnp.float32)
        * factor
    )
    grad_value_all = jnp.einsum(
        "chqk,cqhd->ckhd",
        probs.astype(jnp.bfloat16),
        grad_heads,
        preferred_element_type=jnp.float32,
    )
    key_terms = jnp.stack([grad_key_all, grad_value_all], axis=2)
    key_share = lax.psum_scatter(key_terms, "seq", scatter_dimension=1, tiled=True)
    grad_knorm = key_share[:, :, 0]
    grad_values = key_share[:, :, 1]
    grad_query = norm_back(query_raw, query_inv, q_gain, grad_qnorm)
    grad_key = norm_back(key_raw, key_inv, k_gain, grad_knorm)
    grad_proj = jnp.stack([grad_query, grad_key, grad_values], axis=2).astype(jnp.bfloat16)
    grad_proj = grad_proj.reshape(clip_count * row_count, 3 * inner_width)
    grad_wqkv = jnp.einsum(
        "te,tf->ef", flat_hidden, grad_proj, preferred_element_type=jnp.float32
    ).reshape(model_width, 3, inner_width)
    grad_wqkv, grad_wout = (
        lax.psum_scatter(grad_wqkv, ("seq", "dp"), scatter_dimension=0, tiled=True),
        lax.psum_scatter(grad_wout, ("seq", "dp"), scatter_dimension=1, tiled=True),
    )
    grad_hidden = jnp.einsum(
        "tf,ef->te", grad_proj, flat_weight, preferred_element_type=jnp.float32
    )
    grad_hidden = grad_hidden.reshape(clip_count, row_count, model_width)
    grad_mine = lax.psum_scatter(grad_hidden, "mp", scatter_dimension=2, tiled=True)
    scale_mine = lax.dynamic_slice_in_dim(mod_scale, model_place * width_part, width_part, 2)
    normed_mine = lax.dynamic_slice_in_dim(normed, model_place * width_part, width_part, 2)
    grad_normed = grad_mine * (1.0 + scale_mine)
    partial_dot = jnp.sum(grad_normed * normed_mine, axis=-1, keepdims=True)
    full_dot = lax.psum(partial_dot, "mp")
    grad_inputs = inv_norm * (grad_normed - normed_mine * (full_dot / model_width))
    grad_latents = (grad_out.astype(jnp.float32) + grad_inputs).astype(jnp.bfloat16)
    return (mixed, grad_latents, grad_wqkv, grad_wout)


def solution(mesh):
    in_specs = (
        P("dp", "seq", "mp"),
        P("dp", "seq", "mp"),
        P("dp", "seq", None),
        P(None, None, "mp"),
        P("mp", None),
        P("mp", None),
        P("mp", None),
        P("dp", "seq"),
        P("dp", None),
        P("dp"),
    )
    out_specs = (
        P("dp", "seq", "mp"),
        P("dp", "seq", "mp"),
        P(("seq", "dp"), None, "mp"),
        P("mp", ("seq", "dp")),
    )
    return jax.shard_map(
        on_device, mesh=mesh, in_specs=in_specs, out_specs=out_specs, check_vma=False
    )
```

profile of v0, /device:TPU:0, one launch (start us, length us, event | category | flops | bytes accessed | tf_op | source)
XLA Modules:
  0.0 431.1 jit_solution(11951408667808481590)
XLA Ops:
  7.2 0.0 all-gather.4.cloned.1.call-start
  7.2 3.5 collective-permute-start
  10.7 8.3 %copy.18 = bf16[1792,3,512]{0,2,1:T(8,128)(2,1)} copy(bf16[1792,3,512]{2,0,1:T(8,128)(2,1)} %param.13) | data formatting | bytes 11010048 | tf_op args[3]
  19.0 11.6 %all_gather.14 = bf16[1,192,1792]{2,1,0:T(8,128)(2,1)S(1)} all-gather(bf16[1,192,896]{2,1,0:T(8,128)(2,1)S(1)} %copy-done.12), channel_id=1, replica_groups=mesh['seq'=8,'mp'=2,'dp'=2] {'mp'}, dimensions={2}, use_global_device_ids=true | all-gather | bytes 1032192 | tf_op jit(solution)/shard_map/all_gather | solution.py:51
  30.6 0.2 fusion.15
  30.9 2.3 convolution_bitcast_fusion
  33.2 2.3 fusion.85
  35.6 0.5 copy-done.1
  36.1 1.9 convolution_bitcast_fusion.4
  38.0 0.4 fusion.51
  38.4 0.8 fusion.50
  39.3 0.0 all-gather.4.cloned.1.call-update
  39.3 0.0 all-gather.6.cloned.1.call-start
  40.0 0.1 constant_dynamic-slice_fusion
  40.1 0.7 slice.58
  40.8 0.0 all-gather.6.cloned.1.call-update
  40.8 0.0 reduce-scatter.8.cloned.1.call-start
  40.9 0.3 compare_and_fusion
  41.2 11.7 %all_gather.17 = bf16[1,192,1792]{2,1,0:T(8,128)(2,1)S(1)} all-gather(bf16[1,192,896]{2,1,0:T(8,128)(2,1)} %param.11), channel_id=1, replica_groups=mesh['seq'=8,'mp'=2,'dp'=2] {'mp'}, dimensions={2}, use_global_device_ids=true | all-gather | bytes 1032192 | tf_op jit(solution)/shard_map/all_gather | solution.py:52
  52.9 0.9 copy-done.5
  53.7 2.1 convolution_convert_fusion
  55.9 0.9 reshape.498
  56.8 7.5 %all-gather.4.cloned.1.call-done = bf16[1,1536,4,128]{3,1,2,0:T(8,128)(2,1)} async-done(((bf16[1,192,4,128]{3,1,2,0:T(8,128)(2,1)}), bf16[1,1536,4,128]{3,1,2,0:T(8,128)(2,1)}) %all-gather.4.cloned.1.call-update) | async-done | bytes 1572880 | tf_op jit(solution)/shard_map/all_gather | solution.py:79
  64.3 2.6 select_reduce_fusion
  66.9 1.5 fusion
  68.4 0.6 copy-done.2
  69.0 3.5 convolution_bitcast_fusion.1
  72.5 18.6 %all-gather.6.cloned.1.call-done = bf16[1,1536,1,4,128]{4,1,3,2,0:T(8,128)(2,1)} async-done(((bf16[1,192,1,4,128]{4,1,3,2,0:T(8,128)(2,1)}), bf16[1,1536,1,4,128]{4,1,3,2,0:T(8,128)(2,1)}) %all-gather.6.cloned.1.call-update) | async-done | bytes 1572880 | tf_op jit(solution)/shard_map/all_gather | solution.py:80
  91.1 5.2 %fusion.60 = (f32[192,4]{0,1:T(4,128)S(1)}, bf16[1,192,4,128]{3,1,2,0:T(8,128)(2,1)}) fusion(f32[1,192,4,128]{3,2,1,0:T(4,128)} %reshape.498, f32[4,192]{1,0:T(4,128)S(1)} %fusion, bf16[1,1536,1,4,128]{4,1,3,2,0:T(8,128)(2,1)} %all-gather.6.cloned.1.call-done, f32[4,192,1536]{2,1,0:T(8,128)} %copy-done.2, f32[4,192]{1,0:T(4,128)S(1)} %broadcast_maximum_fusion, ...), kind=kOutput, calls=%fused_computation.73 | convolution fusion | flops 308378880 | bytes 7185408 | tf_op jit(solution)/shard_map/chqk,ckhd->chqd/dot_general | solution.py:87
  96.3 2.2 multiply_convert_fusion
  98.5 1.5 fusion.2
  100.0 1.3 copy-done.8
  101.3 3.1 pad_maximum_fusion
  104.4 0.0 reduce-scatter.8.cloned.1.call-update
  104.4 0.0 reduce-scatter.6.cloned.1.call-start
  104.5 0.9 copy-done.16
  105.3 0.2 copy.19
  105.5 1.6 convolution_bitcast_fusion.3
  107.1 0.3 reduce-scatter.10.cloned.1.call-start
  107.4 66.5 %reduce-scatter.8.cloned.1.call-done = f32[1,192,2,4,128]{4,1,3,2,0:T(8,128)} async-done(((f32[1,1536,2,4,128]{4,1,3,2,0:T(8,128)}), f32[1,192,2,4,128]{4,1,3,2,0:T(8,128)}) %reduce-scatter.8.cloned.1.call-update) | async-done | bytes 786448 | tf_op jit(solution)/shard_map/reduce_scatter | solution.py:140
  173.9 3.2 fusion.57
  177.1 0.3 fusion.56
  177.4 0.3 subtract_multiply_fusion
  177.6 0.1 maximum_convert_fusion
  177.7 0.5 copy.25
  178.2 1.0 convert_element_type.139
  179.2 5.6 %convolution_bitcast_fusion.2 = f32[1,192,1792]{2,1,0:T(8,128)} fusion(bf16[192,1536]{1,0:T(8,128)(2,1)} %convert_element_type.139, bf16[1792,1536]{0,1:T(8,128)(2,1)} %bitcast.173), kind=kOutput, calls=%fused_computation.11 | convolution fusion | flops 1056964608 | bytes 7471104 | tf_op jit(solution)/shard_map/tf,ef->te/dot_general | solution.py:154
  184.8 0.0 reduce-scatter.10.cloned.1.call-update
  184.9 0.0 reduce-scatter.14.cloned.1.call-start
  184.9 4.0 fusion.63
  188.9 0.0 reduce-scatter.14.cloned.1.call-update
  188.9 0.0 reduce-scatter.12.cloned.1.call-start
  189.0 1.0 copy-done.10
  190.0 0.2 copy-done.11
  190.2 5.8 %fusion.42 = f32[1792,3,512]{2,0,1:T(8,128)} fusion(bf16[1,192,1792]{2,1,0:T(8,128)(2,1)S(1)} %copy-done.10, bf16[24,3,8,512]{3,2,1,0:T(8,128)(2,1)S(1)} %bitcast.179), kind=kOutput, calls=%fused_computation.42 | convolution fusion | flops 1056964608 | bytes 12288000 | tf_op jit(solution)/shard_map/te,tf->ef/dot_general | solution.py:147
  196.0 0.0 reduce-scatter.12.cloned.1.call-update
  196.0 2.3 reduce-scatter.6.cloned.1.call-done
  198.3 2.1 add_convert_fusion.1
  200.5 24.0 %reduce-scatter.10.cloned.1.call-done = f32[1,192,896]{2,1,0:T(8,128)} async-done(((f32[1,192,1792]{2,1,0:T(8,128)}), f32[1,192,896]{2,1,0:T(8,128)}) %reduce-scatter.10.cloned.1.call-update) | async-done | bytes 688144 | tf_op jit(solution)/shard_map/reduce_scatter | solution.py:158
  224.5 1.5 multiply_reduce_fusion
  226.0 4.9 %psum.7 = f32[1,192,1]{1,2,0:T(1,128)S(1)} all-reduce(f32[1,192,1]{1,2,0:T(1,128)S(1)} %bitcast.182), channel_id=1, replica_groups=mesh['seq'=8,'mp'=2,'dp'=2] {'mp'}, use_global_device_ids=true, to_apply=%region_12.13 | all-reduce | flops 192 | bytes 1536 | tf_op jit(solution)/shard_map/psum | solution.py:163
  230.9 2.4 add_convert_fusion
  233.3 64.2 %reduce-scatter.14.cloned.1.call-done = f32[512,112]{0,1:T(8,128)} async-done(((f32[512,1792]{0,1:T(8,128)}), f32[512,112]{0,1:T(8,128)}) %reduce-scatter.14.cloned.1.call-update) | async-done | bytes 229392 | tf_op jit(solution)/shard_map/reduce_scatter | solution.py:152
  297.5 126.8 %reduce-scatter.12.cloned.1.call-done = f32[112,3,512]{2,0,1:T(8,128)} async-done(((f32[1792,3,512]{2,0,1:T(8,128)}), f32[112,3,512]{2,0,1:T(8,128)}) %reduce-scatter.12.cloned.1.call-update) | async-done | bytes 688144 | tf_op jit(solution)/shard_map/reduce_scatter | solution.py:151
  (56 shorter events, 0.2 us)
Async XLA Ops:
  7.2 46.6 %copy-start = (bf16[512,1792]{1,0:T(8,128)(2,1)S(1)}, bf16[512,1792]{1,0:T(8,128)(2,1)}, u32[]{:S(2)}) copy-start(bf16[512,1792]{1,0:T(8,128)(2,1)} %param.14) | copy-start | bytes 5505028
  7.2 57.1 %all-gather.4.cloned.1.call-start = ((), (), s32[]{:S(2)}) async-start(), calls=%async_computation.5 | async-start | bytes 1769472 | tf_op jit(solution)/shard_map/all_gather | solution.py:79
  7.2 23.6 %collective-permute-start = (bf16[1,150,3584]{2,1,0:T(8,128)(2,1)}, bf16[1,150,3584]{2,1,0:T(8,128)(2,1)}, u32[]{:S(2)}, u32[]{:S(2)}) collective-permute-start(bf16[1,150,3584]{2,1,0:T(8,128)(2,1)} %param.12), channel_id=1, source_target_pairs={{0,4},{4,8},{8,12},{12,16},{16,20},{20,24},{24,28},{1,5},{5,9},{9,... | collective-permute-start | bytes 3225608 | tf_op jit(solution)/shard_map/ppermute | solution.py:13
  10.7 8.3 %copy-start.12 = (bf16[1,192,896]{2,1,0:T(8,128)(2,1)S(1)}, bf16[1,192,896]{2,1,0:T(8,128)(2,1)}, u32[]{:S(2)}) copy-start(bf16[1,192,896]{2,1,0:T(8,128)(2,1)} %param.10) | copy-start | bytes 1032196
  10.7 20.1 %copy-start.21 = (s32[1,192]{1,0:T(1,128)S(1)}, s32[1,192]{1,0:T(1,128)}, u32[]{:S(2)}) copy-start(s32[1,192]{1,0:T(1,128)} %param.17) | copy-start | bytes 2308
  10.7 20.2 %copy-start.15 = (bf16[1,150,3584]{2,1,0:T(8,128)(2,1)S(1)}, bf16[1,150,3584]{2,1,0:T(8,128)(2,1)}, u32[]{:S(2)}) copy-start(bf16[1,150,3584]{2,1,0:T(8,128)(2,1)} %param.12) | copy-start | bytes 3225604
  30.8 2.4 copy-start.19
  30.9 5.2 %slice-start = ((s8[5505024]{0:T(1024)(128)(4,1)}), s8[4194304]{0:T(1024)(128)(4,1)S(1)}, s32[]{:S(2)}) async-start(s8[5505024]{0:T(1024)(128)(4,1)} %bitcast.174), calls=%async_computation.12 | async-start | bytes 8388608
  33.2 2.8 copy-start.1
  33.2 2.8 slice-start.1
  36.1 2.0 copy-start.9
  36.1 2.3 copy-start.18
  36.1 3.9 copy-start.20
  39.3 51.8 %all-gather.6.cloned.1.call-start = ((), (), s32[]{:S(2)}) async-start(), calls=%async_computation.11 | async-start | bytes 1769472 | tf_op jit(solution)/shard_map/all_gather | solution.py:80
  40.8 133.1 %reduce-scatter.8.cloned.1.call-start = ((), (), s32[]{:S(2)}) async-start(), calls=%async_computation.7 | async-start | bytes 7077888 | tf_op jit(solution)/shard_map/reduce_scatter | solution.py:140
  52.9 0.9 copy-start.5
  53.7 10.6 %copy-start.17 = (f32[4,128]{1,0:T(4,128)S(1)}, f32[4,128]{1,0:T(4,128)}, u32[]{:S(2)}) copy-start(f32[4,128]{1,0:T(4,128)} %param.15) | copy-start | bytes 6148
  66.9 2.1 copy-start.2
  91.1 5.2 %copy-start.3 = (f32[4,192,1536]{2,1,0:T(8,128)S(1)}, f32[4,192,1536]{2,1,0:T(8,128)}, u32[]{:S(2)}) copy-start(f32[4,192,1536]{2,1,0:T(8,128)} %copy-done.2) | copy-start | bytes 14155780
  91.1 5.2 %copy-start.22 = (bf16[1,1536,1,4,128]{4,1,3,2,0:T(8,128)(2,1)S(1)}, bf16[1,1536,1,4,128]{4,1,3,2,0:T(8,128)(2,1)}, u32[]{:S(2)}) copy-start(bf16[1,1536,1,4,128]{4,1,3,2,0:T(8,128)(2,1)} %all-gather.6.cloned.1.call-done) | copy-start | bytes 4718596
  98.5 1.5 copy-start.4
  98.5 2.7 copy-start.8
  104.4 0.9 copy-start.16
  104.4 93.9 %reduce-scatter.6.cloned.1.call-start = ((), (), s32[]{:S(2)}) async-start(), calls=%async_computation.6 | async-start | bytes 2064384 | tf_op jit(solution)/shard_map/reduce_scatter | solution.py:103
  107.1 117.4 %reduce-scatter.10.cloned.1.call-start = ((), (), s32[]{:S(2)}) async-start(), calls=%async_computation.8 | async-start | bytes 2064384 | tf_op jit(solution)/shard_map/reduce_scatter | solution.py:158
  173.9 3.5 copy-start.14
  179.2 5.7 %copy-start.6 = (bf16[1,192,1792]{2,1,0:T(8,128)(2,1)S(1)}, bf16[1,192,1792]{2,1,0:T(8,128)(2,1)}, u32[]{:S(2)}) copy-start(bf16[1,192,1792]{2,1,0:T(8,128)(2,1)} %copy-done.5) | copy-start | bytes 2064388
  184.9 112.6 %reduce-scatter.14.cloned.1.call-start = ((), (), s32[]{:S(2)}) async-start(), calls=%async_computation.10 | async-start | bytes 3899392 | tf_op jit(solution)/shard_map/reduce_scatter | solution.py:152
  188.9 1.1 copy-start.10
  188.9 1.3 copy-start.11
  188.9 235.3 %reduce-scatter.12.cloned.1.call-start = ((), (), s32[]{:S(2)}) async-start(), calls=%async_computation.9 | async-start | bytes 11698176 | tf_op jit(solution)/shard_map/reduce_scatter | solution.py:151
  196.0 2.4 copy-start.13
  196.0 28.5 %copy-start.7 = (f32[1,192,1792]{2,1,0:T(8,128)S(1)}, f32[1,192,1792]{2,1,0:T(8,128)}, u32[]{:S(2)}) copy-start(f32[1,192,1792]{2,1,0:T(8,128)} %get-tuple-element.8) | copy-start | bytes 4128772
Sparse Core Ops, SparseCore 0:
  39.4 24.8 all-gather.3
  66.5 24.5 all-gather.5
  104.5 69.3 reduce-scatter.7
  176.0 22.2 reduce-scatter.5
  200.5 23.8 reduce-scatter.9
  228.8 68.6 reduce-scatter.13
  302.7 121.4 reduce-scatter.11
where the time goes:
time: 432 us; the launch traced here: 431 us
  waiting for transfers between devices  310 us (72%)
  matrix products  41.5 us (10%)
  blocking collectives  28.2 us (7%)
  local copies, waits for them, and re-layouts  17 us (4%)
  other arithmetic  15.3 us (4%)
  between operations  15.1 us (3%)
    reduce_scatter x1, waiting for transfers between devices, on_device(): lax.psum_scatter(grad_wqkv, ('seq', 'dp'), scatter_dimension=0, tiled=True)  127 us
    reduce_scatter x1, waiting for transfers between devices, on_device(): lax.psum_scatter(key_terms, 'seq', scatter_dimension=1, tiled=True)  66.5 us
    reduce_scatter x1, waiting for transfers between devices, on_device(): lax.psum_scatter(grad_wout, ('seq', 'dp'), scatter_dimension=1, tiled=True)  64.2 us
    reduce_scatter x1, waiting for transfers between devices, on_device(): lax.psum_scatter(grad_hidden, 'mp', scatter_dimension=2, tiled=True)  24 us
    all_gather x1, waiting for transfers between devices, on_device(): value_piece = lax.all_gather(values, 'seq', axis=1, tiled=True)  18.6 us
    unnamed x51, local copies, waits for them, and re-layouts  13.7 us
    all_gather x1, blocking collectives, on_device(): lax.all_gather(grad_out, 'mp', axis=2, tiled=True)  11.7 us
    all_gather x1, blocking collectives, on_device(): lax.all_gather(latents, 'mp', axis=2, tiled=True)  11.6 us
  transfers between devices with their start and end apart: 8, of which 7 were waited for; matrix products, arithmetic and copies ran while one was open for 11% of the time, Pallas kernels for 0%

commit v1 on v0

v1 whole, which is shorter than its diff:
```python
import functools
import math

import jax
import jax.numpy as jnp
from jax import lax
from jax.experimental import pallas as pl
from jax.experimental.pallas import tpu as pltpu
from jax.sharding import PartitionSpec as P

EPSILON = 1e-06
NEG_FILL = -1e30
GROUP_MOST = 96
FRAME_UP, FRAME_DOWN = 96, 125
NO_GROUP = 1 << 30
BF = jnp.bfloat16
F32 = jnp.float32


def swap(value, axis, distance):
    count = lax.axis_size(axis)
    return lax.ppermute(value, axis, [(i, i ^ distance) for i in range(count)])


def unxor(pieces, place):
    pieces = list(pieces)
    for bit in range((len(pieces) - 1).bit_length()):
        odd = ((place >> bit) & 1) == 1
        pieces = [jnp.where(odd, pieces[j ^ (1 << bit)], pieces[j]) for j in range(len(pieces))]
    return pieces


def full_width(value):
    count = lax.axis_size("mp")
    pieces = [value] + [swap(value, "mp", t) for t in range(1, count)]
    return jnp.concatenate(unxor(pieces, lax.axis_index("mp")), axis=-1)


def width_sum(partial, width_part):
    place = lax.axis_index("mp")
    total = lax.dynamic_slice_in_dim(partial, place * width_part, width_part, 1)
    for t in range(1, lax.axis_size("mp")):
        other = lax.dynamic_slice_in_dim(partial, (place ^ t) * width_part, width_part, 1)
        total = total + swap(other.astype(BF), "mp", t).astype(F32)
    return total


def inv_rms(values):
    return lax.rsqrt(jnp.mean(values * values, axis=-1, keepdims=True) + EPSILON)


def norm_back(raw, inv_norm, gains, upstream):
    inner_dot = jnp.mean(upstream * gains * raw, axis=-1, keepdims=True)
    return inv_norm * (gains * upstream - raw * inv_norm * inv_norm * inner_dot)


def round_up(value, step):
    return -(-value // step) * step


def attention_kernel(heads, sharers, rows, block, factor, *refs):
    place_ref, key_group_ref, query_group_ref = refs[:3]
    at = 3
    own = refs[at : at + heads]
    at += heads
    shared = refs[at : at + heads * (sharers - 1)]
    at += heads * (sharers - 1)
    ups = refs[at : at + heads]
    at += heads
    outs = refs[at : at + heads]
    at += heads
    key_grads = refs[at : at + heads * sharers]
    at += heads * sharers
    key_s, value_s, query_s, up_s, out_s, dq_s, dk_s, dv_s = refs[at:]
    head = place_ref[0]
    part = place_ref[1]
    span = heads * sharers * rows
    total = heads * rows
    for t in range(heads):
        m = head ^ t
        query_s[m] = own[t][0]
        up_s[m] = ups[t][...]
        key_s[m * sharers + part] = own[t][1]
        value_s[m * sharers + part] = own[t][2]
        for u in range(1, sharers):
            piece = shared[t * (sharers - 1) + u - 1]
            key_s[m * sharers + (part ^ u)] = piece[0]
            value_s[m * sharers + (part ^ u)] = piece[1]
    dk_s[...] = jnp.zeros_like(dk_s)
    dv_s[...] = jnp.zeros_like(dv_s)
    keys = key_s[...].reshape(span, key_s.shape[-1])
    values = value_s[...].reshape(span, key_s.shape[-1])
    queries = query_s[...].reshape(total, key_s.shape[-1])
    upstream = up_s[...].reshape(total, key_s.shape[-1])
    group_col = jnp.transpose(jnp.broadcast_to(key_group_ref[...], (128, span)))
    group_col = jnp.concatenate([group_col] * (-(-block // 128)), axis=1)[:, :block]
    scale = factor * math.log2(math.e)
    over_last = (((1,), (1,)), ((), ()))
    over_first = (((0,), (0,)), ((), ()))
    for j in range(total // block):
        last = ((j + 1) * block - 1) // rows
        reach = min(span, round_up((last + 1) * sharers * rows + GROUP_MOST - 1, 128))
        lanes = slice(j * block, (j + 1) * block)
        query = queries[lanes]
        up = upstream[lanes]
        key = keys[:reach]
        value = values[:reach]
        logits = lax.dot_general(key, query, over_last, preferred_element_type=F32)
        logits = jnp.where(group_col[:reach] <= query_group_ref[:, lanes], logits, NEG_FILL)
        row_max = jnp.max(logits, axis=0, keepdims=True)
        unnorm = jnp.exp2((logits - row_max) * scale)
        inverse = 1.0 / jnp.sum(unnorm, axis=0, keepdims=True)
        out = lax.dot_general(value, unnorm.astype(BF), over_first, preferred_element_type=F32)
        out = (out * inverse).astype(BF)
        up_t = jnp.transpose(up.astype(F32))
        out_dot = jnp.sum(up_t * out.astype(F32), axis=0, keepdims=True)
        probs = unnorm * inverse
        grad_probs = lax.dot_general(value, up, over_last, preferred_element_type=F32)
        grad_logits = (probs * (grad_probs - out_dot)).astype(BF)
        grad_query = lax.dot_general(key, grad_logits, over_first, preferred_element_type=F32)
        out_s[lanes, :] = jnp.transpose(out.astype(F32)).astype(BF)
        dq_s[lanes, :] = jnp.transpose(grad_query * factor).astype(BF)
        dk_s[:reach, :] += jnp.dot(grad_logits, query, preferred_element_type=F32)
        dv_s[:reach, :] += jnp.dot(probs.astype(BF), up, preferred_element_type=F32)
    for t in range(heads):
        m = head ^ t
        here = pl.ds(pl.multiple_of(m * rows, 64), rows)
        outs[t][0] = out_s[here, :]
        outs[t][1] = dq_s[here, :]
        for u in range(sharers):
            there = pl.ds(pl.multiple_of((m * sharers + (part ^ u)) * rows, 64), rows)
            ref = key_grads[t * sharers + u]
            ref[0] = (dk_s[there, :] * factor).astype(ref.dtype)
            ref[1] = dv_s[there, :].astype(ref.dtype)


def attention(head, part, group_ids, clip_length, own, shared, ups):
    heads = len(own)
    sharers = len(shared) // heads + 1
    rows, width = ups[0].shape
    span = heads * sharers * rows
    total = heads * rows
    block = 256 if total % 256 == 0 else total
    positions = lax.iota(jnp.int32, span)
    key_group = jnp.where(positions < clip_length, group_ids, NO_GROUP)[None, :]
    query_group = lax.dynamic_index_in_dim(
        group_ids.reshape(heads, sharers, rows), part, 1, keepdims=False
    ).reshape(1, total)
    place = jnp.stack([head, part]).astype(jnp.int32)
    vmem = pl.BlockSpec(memory_space=pltpu.VMEM)
    pair = (2, rows, width)
    out_shape = [jax.ShapeDtypeStruct(pair, BF)] * heads
    for _ in range(heads):
        out_shape.append(jax.ShapeDtypeStruct(pair, F32))
        out_shape.extend([jax.ShapeDtypeStruct(pair, BF)] * (sharers - 1))
    got = pl.pallas_call(
        functools.partial(attention_kernel, heads, sharers, rows, block, width ** (-0.5)),
        out_shape=out_shape,
        in_specs=[pl.BlockSpec(memory_space=pltpu.SMEM)]
        + [vmem] * (2 + 2 * heads + heads * (sharers - 1)),
        out_specs=[vmem] * len(out_shape),
        scratch_shapes=[
            pltpu.VMEM((heads * sharers, rows, width), BF),
            pltpu.VMEM((heads * sharers, rows, width), BF),
            pltpu.VMEM((heads, rows, width), BF),
            pltpu.VMEM((heads, rows, width), BF),
            pltpu.VMEM((total, width), BF),
            pltpu.VMEM((total, width), BF),
            pltpu.VMEM((span, width), F32),
            pltpu.VMEM((span, width), F32),
        ],
        compiler_params=pltpu.CompilerParams(vmem_limit_bytes=48 * 1024 * 1024),
        cost_estimate=pl.CostEstimate(
            flops=12 * total * span * width, bytes_accessed=4 << 20, transcendentals=total * span
        ),
        name="attention",
    )(place, key_group, query_group, *own, *shared, *ups)
    outs = got[:heads]
    key_grads = [got[heads + t * sharers : heads + (t + 1) * sharers] for t in range(heads)]
    return outs, key_grads


def weight_grad(left_t, right):
    count, clips = lax.axis_size("seq"), lax.axis_size("dp")
    seq, clip = lax.axis_index("seq"), lax.axis_index("dp")
    core = seq % 2
    span = left_t.shape[0] // (count * clips)
    rows = left_t.shape[1]
    blocks = left_t.reshape(count // 2, 2 * clips, span, rows)
    lefts, rights = [], []
    for w in range(clips):
        for u in range(2):
            mine = lax.dynamic_index_in_dim(
                blocks, (core ^ u) * clips + (clip ^ w), 1, keepdims=False
            )
            if u or w:
                pairs = [
                    (s * clips + x, (s ^ u) * clips + (x ^ w))
                    for s in range(count)
                    for x in range(clips)
                ]
                mine = lax.ppermute(mine, ("seq", "dp"), pairs)
            lefts.append(mine.reshape(count // 2 * span, rows))
        far = right if w == 0 else swap(right, "dp", w)
        rights.extend([far, swap(far, "seq", 1)])
    total = 0.0
    for a in range(0, len(lefts), 2):
        left = jnp.concatenate(lefts[a : a + 2], axis=1)
        total = total + jnp.dot(
            left, jnp.concatenate(rights[a : a + 2], axis=0), preferred_element_type=F32
        )
    total = total.reshape(count // 2, span, right.shape[1])
    step = 2
    while total.shape[0] > 1:
        halves = total.reshape(total.shape[0] // 2, 2, span, right.shape[1])
        odd = (seq // step) % 2
        keep = lax.dynamic_index_in_dim(halves, odd, 1, keepdims=False)
        send = lax.dynamic_index_in_dim(halves, 1 - odd, 1, keepdims=False).astype(BF)
        total = keep + swap(send, "seq", step).astype(F32)
        step *= 2
    return total[0]


def on_device(
    latents, grad_out, sync_mod, w_qkv, w_out, q_gain, k_gain, frame_of, group_id, clip_len
):
    latents, grad_out, sync_mod = latents[0], grad_out[0], sync_mod[0]
    frame_of, group_id, clip_len = frame_of[0], group_id[0], clip_len[0]
    row_count, width_part = latents.shape
    frame_count = sync_mod.shape[0]
    model_width = sync_mod.shape[1] // 2
    heads, head_dim = q_gain.shape
    inner_width = heads * head_dim
    count = lax.axis_size("seq")
    sharers = count // heads
    seq = lax.axis_index("seq")
    head, part = seq // sharers, seq % sharers
    model_place = lax.axis_index("mp")

    inputs = full_width(latents)
    upstream = full_width(grad_out)

    back = max(
        frame_count * j - (FRAME_UP * row_count * j) // FRAME_DOWN for j in range(count)
    )
    back = min(frame_count, round_up(max(back, 1), 16))
    earlier = lax.ppermute(
        sync_mod[frame_count - back :], "seq", [(i, i + 1) for i in range(count - 1)]
    )
    window = jnp.concatenate([earlier, sync_mod], axis=0)
    local_frame = frame_of - (seq * frame_count - back)
    selector = (
        local_frame[:, None] == lax.iota(jnp.int32, frame_count + back)[None, :]
    ).astype(BF)
    modulation = jnp.dot(selector, window, preferred_element_type=F32)
    mod_scale = modulation[:, :model_width]
    mod_gate = modulation[:, model_width:]

    inputs_f = inputs.astype(F32)
    inv_norm = inv_rms(inputs_f)
    normed = inputs_f * inv_norm
    hidden = (normed * (1.0 + mod_scale)).astype(BF)
    flat_weight = w_qkv.reshape(model_width, 3 * inner_width)
    projected = jnp.dot(hidden, flat_weight, preferred_element_type=F32)
    projected = projected.reshape(row_count, 3, heads, head_dim)
    query_raw, key_raw = projected[:, 0], projected[:, 1]
    query_inv, key_inv = inv_rms(query_raw), inv_rms(key_raw)
    query_norm = (query_raw * query_inv * q_gain).astype(BF)
    key_norm = (key_raw * key_inv * k_gain).astype(BF)
    values = projected[:, 2].astype(BF)

    qkv = [
        jnp.stack([query_norm[:, j], key_norm[:, j], values[:, j]], axis=0) for j in range(heads)
    ]
    qkv = unxor(qkv, head)
    own = [qkv[0]] + [swap(qkv[t], "seq", t * sharers) for t in range(1, heads)]
    shared = [swap(own[t][1:], "seq", u) for t in range(heads) for u in range(1, sharers)]

    grad_attn = (upstream.astype(F32) * mod_gate).astype(BF)
    grad_heads = jnp.einsum("td,id->ti", grad_attn, w_out, preferred_element_type=F32)
    grad_heads = grad_heads.astype(BF)
    ups = unxor([grad_heads[:, j * head_dim : (j + 1) * head_dim] for j in range(heads)], head)
    ups = [ups[0]] + [swap(ups[t], "seq", t * sharers) for t in range(1, heads)]

    outs, key_grads = attention(head, part, group_id, clip_len, own, shared, ups)
    back_out, back_key = [], []
    for t in range(heads):
        total = key_grads[t][0]
        for u in range(1, sharers):
            total = total + swap(key_grads[t][u], "seq", u).astype(F32)
        if t:
            back_out.append(swap(outs[t], "seq", t * sharers))
            back_key.append(swap(total.astype(BF), "seq", t * sharers))
        else:
            back_out.append(outs[t])
            back_key.append(total.astype(BF))
    back_out, back_key = unxor(back_out, head), unxor(back_key, head)
    out_rows = jnp.concatenate([b[0] for b in back_out], axis=1)
    grad_qnorm = jnp.stack([b[1] for b in back_out], axis=1).astype(F32)
    grad_knorm = jnp.stack([b[0] for b in back_key], axis=1).astype(F32)
    grad_values = jnp.stack([b[1] for b in back_key], axis=1)

    attn_part = jnp.dot(out_rows, w_out, preferred_element_type=F32)
    attn_mine = width_sum(attn_part, width_part)
    gate_mine = lax.dynamic_slice_in_dim(mod_gate, model_place * width_part, width_part, 1)
    mixed = (latents.astype(F32) + gate_mine * attn_mine).astype(BF)

    grad_query = norm_back(query_raw, query_inv, q_gain, grad_qnorm).astype(BF)
    grad_key = norm_back(key_raw, key_inv, k_gain, grad_knorm).astype(BF)
    grad_proj = jnp.concatenate(
        [g.reshape(row_count, inner_width) for g in (grad_query, grad_key, grad_values)], axis=1
    )

    grad_wout = weight_grad(jnp.transpose(grad_attn), out_rows)
    grad_wqkv = weight_grad(jnp.transpose(hidden), grad_proj)

    grad_hidden = jnp.einsum("tf,ef->te", grad_proj, flat_weight, preferred_element_type=F32)
    full_dot = jnp.sum(grad_hidden * (1.0 + mod_scale) * normed, axis=-1, keepdims=True)
    part_dot = full_dot
    full_dot = sum(
        [swap(part_dot, "mp", t) for t in range(1, lax.axis_size("mp"))], part_dot
    )
    grad_mine = width_sum(grad_hidden, width_part)
    scale_mine = lax.dynamic_slice_in_dim(mod_scale, model_place * width_part, width_part, 1)
    normed_mine = latents.astype(F32) * inv_norm
    grad_normed = grad_mine * (1.0 + scale_mine)
    grad_inputs = inv_norm * (grad_normed - normed_mine * (full_dot / model_width))
    grad_latents = (grad_out.astype(F32) + grad_inputs).astype(BF)
    return (
        mixed[None],
        grad_latents[None],
        grad_wqkv.reshape(-1, 3, inner_width),
        jnp.transpose(grad_wout),
    )


def solution(mesh):
    in_specs = (
        P("dp", "seq", "mp"),
        P("dp", "seq", "mp"),
        P("dp", "seq", None),
        P(None, None, "mp"),
        P("mp", None),
        P("mp", None),
        P("mp", None),
        P("dp", "seq"),
        P("dp", None),
        P("dp"),
    )
    out_specs = (
        P("dp", "seq", "mp"),
        P("dp", "seq", "mp"),
        P(("seq", "dp"), None, "mp"),
        P("mp", ("seq", "dp")),
    )
    return jax.shard_map(
        on_device, mesh=mesh, in_specs=in_specs, out_specs=out_specs, check_vma=False
    )
```

time: 432 us -> 198 us (0.46)
  waiting for transfers between devices: 310 us -> 45.3 us
  local copies, waits for them, and re-layouts: 17 us -> 70.7 us
  starting transfers between devices: 3.99 us -> 43.9 us
  blocking collectives: 28.2 us -> 0 us
  matrix products: 41.5 us -> 13.5 us
  between operations: 15.1 us -> 2.37 us
  Pallas kernels: 0 us -> 6.27 us
    reduce_scatter x5 -> x0, waiting for transfers between devices: 284 us -> none  [the longest x1 127 us: on_device(): lax.psum_scatter(grad_wqkv, ('seq', 'dp'), scatter_dimension=0, tiled=True)]
    ppermute x1 -> x42, waiting for transfers between devices: 0.01 us -> 45.3 us  [the longest x35 45.3 us: swap(): return lax.ppermute(value, axis, [(i, i ^ distance) for i in range(count)])]
    ppermute x1 -> x42, starting transfers between devices: 3.48 us -> 43.9 us  [the longest x35 37.4 us: swap(): return lax.ppermute(value, axis, [(i, i ^ distance) for i in range(count)])]
    dot_general x13 -> x9, matrix products: 41.5 us -> 13.5 us  [the longest x4 4.59 us: weight_grad(): jnp.dot(left, jnp.concatenate(rights[a:a + 2], axis=0), preferred_element...]
    all_gather x2 -> x0, waiting for transfers between devices: 26.1 us -> none  [the longest x1 18.6 us: on_device(): value_piece = lax.all_gather(values, 'seq', axis=1, tiled=True)]
    all_gather x2 -> x0, blocking collectives: 23.3 us -> none  [the longest x1 11.7 us: on_device(): lax.all_gather(grad_out, 'mp', axis=2, tiled=True)]
    unnamed x51 -> x162, local copies, waits for them, and re-layouts: 13.7 us -> 30.4 us
    reshape x0 -> x11, local copies, waits for them, and re-layouts: none -> 14 us  [the longest x8 7.74 us: weight_grad(): lefts.append(mine.reshape(count // 2 * span, rows))]
  transfers between devices with their start and end apart: 8 -> 42, of which waited for: 7 -> 7; matrix products, arithmetic and copies ran while one was open for 11% -> 39% of each run, Pallas kernels for 0% -> 3%
where the time goes in v1:
time: 198 us; the launch traced here: 197 us
  local copies, waits for them, and re-layouts  70.7 us (36%)
  waiting for transfers between devices  45.3 us (23%)
  starting transfers between devices  43.9 us (22%)
  other arithmetic  14.7 us (7%)
  matrix products  13.5 us (7%)
  Pallas kernels  6.27 us (3%)
  between operations  2.37 us (1%)
    ppermute x35, waiting for transfers between devices, swap(): return lax.ppermute(value, axis, [(i, i ^ distance) for i in range(count)])  45.3 us
    ppermute x35, starting transfers between devices, swap(): return lax.ppermute(value, axis, [(i, i ^ distance) for i in range(count)])  37.4 us
    unnamed x162, local copies, waits for them, and re-layouts  30.4 us
    dynamic_slice x1, local copies, waits for them, and re-layouts, weight_grad(): lax.dynamic_index_in_dim(blocks, (core ^ u) * clips + (clip ^ w), 1, keep...  9.02 us
    reshape x8, local copies, waits for them, and re-layouts, weight_grad(): lefts.append(mine.reshape(count // 2 * span, rows))  7.74 us
    ppermute x6, local copies, waits for them, and re-layouts, weight_grad(): mine = lax.ppermute(mine, ('seq', 'dp'), pairs)  6.52 us
    pallas_call x1, Pallas kernels, attention(): pl.pallas_call(functools.partial(attention_kernel, heads, sharers, rows,...  6.27 us
    reshape x2, local copies, waits for them, and re-layouts, weight_grad(): blocks = left_t.reshape(count // 2, 2 * clips, span, rows)  6.17 us
  transfers between devices with their start and end apart: 42, of which 7 were waited for; matrix products, arithmetic and copies ran while one was open for 39% of the time, Pallas kernels for 3%

profile of v1, /device:TPU:0, one launch (start us, length us, event | category | flops | bytes accessed | tf_op | source)
XLA Modules:
  0.0 196.6 jit_solution(1170574514556943673)
XLA Ops:
  0.6 3.0 %collective-permute-start.1 = (bf16[192,896]{1,0:T(8,128)(2,1)}, bf16[192,896]{1,0:T(8,128)(2,1)}, u32[]{:S(2)}, u32[]{:S(2)}) collective-permute-start(bf16[192,896]{1,0:T(8,128)(2,1)} %bitcast.239), channel_id=1, source_target_pairs={{0,2},{2,0},{1,3},{3,1},{4,6},{6,4},{5,7},{7,5},{8,10},{10,8},{9,1... | collective-permute-start | bytes 1032200 | tf_op jit(solution)/shard_map/ppermute | solution.py:22
  3.7 1.0 slice_bitcast_fusion
  4.7 2.2 %collective-permute-start = (bf16[32,3584]{1,0:T(8,128)(2,1)S(1)}, bf16[32,3584]{1,0:T(8,128)(2,1)}, u32[]{:S(2)}, u32[]{:S(2)}) collective-permute-start(bf16[32,3584]{1,0:T(8,128)(2,1)S(1)} %slice_bitcast_fusion), channel_id=1, source_target_pairs={{0,4},{4,8},{8,12},{12,16},{16,20},{20,24},{24,28},{1,5},{5,9},{9,... | collective-permute-start | bytes 688136 | tf_op jit(solution)/shard_map/ppermute | solution.py:247
  9.5 8.4 %copy.73 = bf16[1792,3,512]{0,2,1:T(8,128)(2,1)} copy(bf16[1792,3,512]{2,0,1:T(8,128)(2,1)} %param.13) | data formatting | bytes 11010048 | tf_op args[3]
  17.9 1.6 fusion.5
  19.5 1.5 broadcast_select_fusion.3
  21.3 2.0 %fusion.85 = (bf16[1792,192]{0,1:T(8,128)(2,1)}, bf16[192,1792]{1,0:T(8,128)(2,1)S(1)}, f32[192,1792]{1,0:T(8,128)}, f32[192,1792]{1,0:T(8,128)}) fusion(f32[192,3584]{1,0:T(8,128)S(1)} %fusion.5, bf16[192,896]{1,0:T(8,128)(2,1)S(1)} %get-tuple-element.63, bf16[192,896]{1,0:T(8,128)(2,1)S(1)} %get-tuple-element.62, f32[192]{0:T(256)S(1)} %add_rsqrt_fusion.2, ...), kind=kLoop, calls=%fused_computation.221 | loop fusion | flops 4816896 | bytes 8258304 | tf_op jit(solution)/shard_map/transpose | solution.py:314
  23.3 1.3 slice-done
  25.0 1.9 fusion.27
  30.2 1.5 collective-permute-start.2
  31.7 2.6 %collective-permute-start.3 = (bf16[3,192,128]{2,1,0:T(8,128)(2,1)}, bf16[3,192,128]{2,1,0:T(8,128)(2,1)S(1)}, u32[]{:S(2)}, u32[]{:S(2)}) collective-permute-start(bf16[3,192,128]{2,1,0:T(8,128)(2,1)} %broadcast_select_fusion.9), channel_id=1, source_target_pairs={{0,16},{4,20},{8,24},{12,28},{16,0},{20,4},{24,8},{28,12},{1,17},{... | collective-permute-start | bytes 442376 | tf_op jit(solution)/shard_map/ppermute | solution.py:22
  36.7 3.5 %collective-permute-start.11 = (bf16[192,128]{1,0:T(8,128)(2,1)}, bf16[192,128]{1,0:T(8,128)(2,1)S(1)}, u32[]{:S(2)}, u32[]{:S(2)}) collective-permute-start(bf16[192,128]{1,0:T(8,128)(2,1)} %get-tuple-element.77), channel_id=1, source_target_pairs={{0,16},{4,20},{8,24},{12,28},{16,0},{20,4},{24,8},{28,12},{1,17},{... | collective-permute-start | bytes 147464 | tf_op jit(solution)/shard_map/ppermute | solution.py:22
  40.9 3.9 %reshape.146 = bf16[4,4,112,192]{2,1,0,3:T(4,128)(2,1)} reshape(bf16[1792,192]{0,1:T(8,128)(2,1)} %get-tuple-element.46) | data formatting | bytes 1376256 | tf_op jit(solution)/shard_map/reshape | solution.py:189
  44.8 2.3 %reshape.141 = bf16[4,4,112,192]{2,1,0,3:T(4,128)(2,1)} reshape(bf16[1792,192]{0,1:T(8,128)(2,1)S(1)} %bitcast.231) | data formatting | bytes 1376256 | tf_op jit(solution)/shard_map/reshape | solution.py:189
  47.1 2.2 %collective-permute-start.12 = (bf16[192,128]{1,0:T(8,128)(2,1)}, bf16[192,128]{1,0:T(8,128)(2,1)S(1)}, u32[]{:S(2)}, u32[]{:S(2)}) collective-permute-start(bf16[192,128]{1,0:T(8,128)(2,1)} %get-tuple-element.75), channel_id=1, source_target_pairs={{0,24},{4,28},{8,16},{12,20},{16,8},{20,12},{24,0},{28,4},{1,25},{... | collective-permute-start | bytes 147464 | tf_op jit(solution)/shard_map/ppermute | solution.py:22
  51.2 9.0 %constant_dynamic-slice_fusion.1 = (bf16[4,1,112,192]{2,1,0,3:T(2,128)(2,1)S(1)}, bf16[4,1,112,192]{2,1,0,3:T(2,128)(2,1)}, bf16[4,112,192]{1,0,2:T(4,128)(2,1)}...) fusion(bf16[4,4,112,192]{2,1,0,3:T(4,128)(2,1)} %reshape.146, ...), kind=kLoop, calls=%fused_computation.199 | loop fusion | bytes 2752528 | tf_op jit(solution)/shard_map/jit(dynamic_index_in_dim)/dynamic_slice | solution.py:193
  62.1 1.2 collective-permute-start.29
  63.5 1.8 copy.143
  65.3 1.7 copy.141
  71.0 1.4 collective-permute-start.37
  72.5 0.9 copy-done.3
  73.4 0.9 copy-done.7
  74.3 0.9 copy-done.11
  75.2 0.9 copy-done.15
  77.7 6.3 %attention.1 = (bf16[2,192,128]{2,1,0:T(8,128)(2,1)S(1)}, bf16[2,192,128]{2,1,0:T(8,128)(2,1)S(1)}, bf16[2,192,128]{2,1,0:T(8,128)(2,1)S(1)}, bf16[2,192,128]{2,...) custom-call(s32[2]{0:T(128)S(1)} %pad_add_fusion.refs_0_, ...), custom_call_target="tpu_custom_call" | custom-call | flops 1811939328 | bytes 4194304 | tf_op jit(solution)/shard_map/attention/pallas_call | solution.py:156
  90.0 2.0 %copy.80 = f32[192,1,4,128]{3,2,0,1:T(4,128)} copy(f32[192,1,4,128]{3,0,2,1:T(8,128)} %get-tuple-element.51) | data formatting | bytes 786432 | tf_op jit(solution)/shard_map/slice | solution.py:266
  92.0 1.0 copy.76
  93.0 1.8 reshape.142
  95.7 1.1 copy.85
  96.7 0.8 reshape.143
  97.6 1.1 copy.89
  99.5 1.1 copy.87
  100.6 0.9 reshape.144
  101.5 1.1 copy.94
  103.5 1.1 copy.98
  104.6 0.8 reshape.150
  105.4 1.1 copy.96
  106.5 0.8 reshape.149
  108.4 2.5 %collective-permute-start.13 = (bf16[2,192,128]{2,1,0:T(8,128)(2,1)S(1)}, bf16[2,192,128]{2,1,0:T(8,128)(2,1)S(1)}, u32[]{:S(2)}, u32[]{:S(2)}) collective-permute-start(bf16[2,192,128]{2,1,0:T(8,128)(2,1)S(1)} %copy-done.13), channel_id=1, source_target_pairs={{0,24},{4,28},{8,16},{12,20},{16,8},{20,12},{24,0},{28,4},{1,25},{... | collective-permute-start | bytes 294920 | tf_op jit(solution)/shard_map/ppermute | solution.py:22
  110.9 0.9 add_convert_fusion.2
  111.8 2.0 collective-permute-start.15
  113.8 1.1 collective-permute-start.20
  115.0 1.0 collective-permute-done.13
  115.9 2.5 %collective-permute-start.18 = (bf16[2,192,128]{2,1,0:T(8,128)(2,1)S(1)}, bf16[2,192,128]{2,1,0:T(8,128)(2,1)S(1)}, u32[]{:S(2)}, u32[]{:S(2)}) collective-permute-start(bf16[2,192,128]{2,1,0:T(8,128)(2,1)S(1)} %add_convert_fusion.3), channel_id=1, source_target_pairs={{0,24},{4,28},{8,16},{12,20},{16,8},{20,12},{24,0},{28,4},{1,25},{... | collective-permute-start | bytes 294920 | tf_op jit(solution)/shard_map/ppermute | solution.py:22
  118.4 5.6 %collective-permute-done.14 = bf16[2,192,128]{2,1,0:T(8,128)(2,1)S(1)} collective-permute-done((bf16[2,192,128]{2,1,0:T(8,128)(2,1)S(1)}, bf16[2,192,128]{2,1,0:T(8,128)(2,1)S(1)}, u32[]{:S(2)}, u32[]{:S(2)}) %collective-permute-start.14) | collective-permute-done | bytes 98336 | tf_op jit(solution)/shard_map/ppermute | solution.py:22
  125.5 1.4 collective-permute-start.38
  126.9 1.7 collective-permute-done.22
  134.3 1.5 collective-permute-start.30
  135.8 1.6 collective-permute-start.16
  138.0 4.1 %fusion.3 = (f32[192]{0:T(256)S(1)}, f32[192,1792]{1,0:T(8,128)S(1)}) fusion(f32[192]{0:T(256)S(1)} %add_rsqrt_fusion.2, bf16[192,896]{1,0:T(8,128)(2,1)S(1)} %copy-done.32, bf16[192,896]{1,0:T(8,128)(2,1)S(1)} %copy-done.30, f32[192,3584]{1,0:T(8,128)S(1)} %copy-done.25, bf16[1792,1536]{0,1:T(8,128)(2,1)} %bitcast.224, ...), kind=kOutput, calls=%fused_computation.6 | convolution fusion | flops 1061830464 | bytes 9537024 | tf_op jit(solution)/shard_map/tf,ef->te/dot_general | solution.py:317
  142.7 5.5 %collective-permute-done.30 = bf16[192,1536]{1,0:T(8,128)(2,1)S(1)} collective-permute-done((bf16[192,1536]{1,0:T(8,128)(2,1)S(1)}, bf16[192,1536]{1,0:T(8,128)(2,1)S(1)}, u32[]{:S(2)}, u32[]{:S(2)}) %collective-permute-start.30) | collective-permute-done | bytes 589856 | tf_op jit(solution)/shard_map/ppermute | solution.py:22
  148.2 1.3 fusion.47
  149.6 1.4 convolution_add_fusion.1
  151.1 2.1 %collective-permute-start.40 = (bf16[2,112,512]{2,1,0:T(8,128)(2,1)S(1)}, bf16[2,112,512]{2,1,0:T(8,128)(2,1)S(1)}, u32[]{:S(2)}, u32[]{:S(2)}) collective-permute-start(bf16[2,112,512]{2,1,0:T(8,128)(2,1)S(1)} %fusion.74), channel_id=1, source_target_pairs={{0,8},{4,12},{8,0},{12,4},{16,24},{20,28},{24,16},{28,20},{1,9},{5... | collective-permute-start | bytes 688136 | tf_op jit(solution)/shard_map/ppermute | solution.py:22
  153.2 0.9 fusion.9
  154.2 0.9 convolution_add_fusion
  155.3 1.6 collective-permute-start.24
  156.9 2.7 %collective-permute-done.40 = bf16[2,112,512]{2,1,0:T(8,128)(2,1)S(1)} collective-permute-done((bf16[2,112,512]{2,1,0:T(8,128)(2,1)S(1)}, bf16[2,112,512]{2,1,0:T(8,128)(2,1)S(1)}, u32[]{:S(2)}, u32[]{:S(2)}) %collective-permute-start.40) | collective-permute-done | bytes 229408 | tf_op jit(solution)/shard_map/ppermute | solution.py:22
  159.8 3.2 %collective-permute-start.41 = (bf16[1,112,512]{2,1,0:T(8,128)(2,1)S(1)}, bf16[1,112,512]{2,1,0:T(8,128)(2,1)S(1)}, u32[]{:S(2)}, u32[]{:S(2)}) collective-permute-start(bf16[1,112,512]{2,1,0:T(8,128)(2,1)S(1)} %dynamic-slice_convert_fusion.3), channel_id=1, source_target_pairs={{0,16},{4,20},{8,24},{12,28},{16,0},{20,4},{24,8},{28,12},{1,17},{... | collective-permute-start | bytes 344072 | tf_op jit(solution)/shard_map/ppermute | solution.py:22
  163.0 13.6 %collective-permute-done.32 = bf16[2,112,1536]{2,1,0:T(8,128)(2,1)S(1)} collective-permute-done((bf16[2,112,1536]{2,1,0:T(8,128)(2,1)S(1)}, bf16[2,112,1536]{2,1,0:T(8,128)(2,1)S(1)}, u32[]{:S(2)}, u32[]{:S(2)}) %collective-permute-start.32) | collective-permute-done | bytes 688160 | tf_op jit(solution)/shard_map/ppermute | solution.py:22
  176.9 1.0 collective-permute-start.33
  177.9 1.3 fusion.73
  179.9 15.2 %collective-permute-done.33 = bf16[1,112,1536]{2,1,0:T(8,128)(2,1)S(1)} collective-permute-done((bf16[1,112,1536]{2,1,0:T(8,128)(2,1)S(1)}, bf16[1,112,1536]{2,1,0:T(8,128)(2,1)S(1)}, u32[]{:S(2)}, u32[]{:S(2)}) %collective-permute-start.33) | collective-permute-done | bytes 344096 | tf_op jit(solution)/shard_map/ppermute | solution.py:22
  195.5 1.1 copy.100
  (282 shorter events, 38.0 us)
Async XLA Ops:
  0.6 34.0 %copy-start = (bf16[512,1792]{1,0:T(8,128)(2,1)S(1)}, bf16[512,1792]{1,0:T(8,128)(2,1)}, u32[]{:S(2)}) copy-start(bf16[512,1792]{1,0:T(8,128)(2,1)} %param.14) | copy-start | bytes 5505028
  0.6 18.8 %collective-permute-start.1 = (bf16[192,896]{1,0:T(8,128)(2,1)}, bf16[192,896]{1,0:T(8,128)(2,1)}, u32[]{:S(2)}, u32[]{:S(2)}) collective-permute-start(bf16[192,896]{1,0:T(8,128)(2,1)} %bitcast.239), channel_id=1, source_target_pairs={{0,2},{2,0},{1,3},{3,1},{4,6},{6,4},{5,7},{7,5},{8,10},{10,8},{9,1... | collective-permute-start | bytes 1032200 | tf_op jit(solution)/shard_map/ppermute | solution.py:22
  4.7 13.2 %collective-permute-start = (bf16[32,3584]{1,0:T(8,128)(2,1)S(1)}, bf16[32,3584]{1,0:T(8,128)(2,1)}, u32[]{:S(2)}, u32[]{:S(2)}) collective-permute-start(bf16[32,3584]{1,0:T(8,128)(2,1)S(1)} %slice_bitcast_fusion), channel_id=1, source_target_pairs={{0,4},{4,8},{8,12},{12,16},{16,20},{20,24},{24,28},{1,5},{5,9},{9,... | collective-permute-start | bytes 688136 | tf_op jit(solution)/shard_map/ppermute | solution.py:247
  6.9 14.4 %collective-permute-start.9 = (bf16[192,896]{1,0:T(8,128)(2,1)}, bf16[192,896]{1,0:T(8,128)(2,1)S(1)}, u32[]{:S(2)}, u32[]{:S(2)}) collective-permute-start(bf16[192,896]{1,0:T(8,128)(2,1)} %bitcast.240), channel_id=1, source_target_pairs={{0,2},{2,0},{1,3},{3,1},{4,6},{6,4},{5,7},{7,5},{8,10},{10,8},{9,1... | collective-permute-start | bytes 1032200 | tf_op jit(solution)/shard_map/ppermute | solution.py:22
  9.4 8.4 %copy-start.35 = (bf16[1,150,3584]{2,1,0:T(8,128)(2,1)S(1)}, bf16[1,150,3584]{2,1,0:T(8,128)(2,1)}, u32[]{:S(2)}) copy-start(bf16[1,150,3584]{2,1,0:T(8,128)(2,1)} %param.12) | copy-start | bytes 3225604
  19.5 15.2 %copy-start.24 = (f32[192,3584]{1,0:T(8,128)}, f32[192,3584]{1,0:T(8,128)S(1)}, u32[]{:S(2)}) copy-start(f32[192,3584]{1,0:T(8,128)S(1)} %fusion.5) | copy-start | bytes 8257540
  30.2 16.8 %collective-permute-start.2 = (bf16[3,192,128]{2,1,0:T(8,128)(2,1)}, bf16[3,192,128]{2,1,0:T(8,128)(2,1)S(1)}, u32[]{:S(2)}, u32[]{:S(2)}) collective-permute-start(bf16[3,192,128]{2,1,0:T(8,128)(2,1)} %broadcast_select_fusion.10), channel_id=1, source_target_pairs={{0,8},{4,12},{8,0},{12,4},{16,24},{20,28},{24,16},{28,20},{1,9},{5... | collective-permute-start | bytes 442376 | tf_op jit(solution)/shard_map/ppermute | solution.py:22
  31.7 15.4 %collective-permute-start.3 = (bf16[3,192,128]{2,1,0:T(8,128)(2,1)}, bf16[3,192,128]{2,1,0:T(8,128)(2,1)S(1)}, u32[]{:S(2)}, u32[]{:S(2)}) collective-permute-start(bf16[3,192,128]{2,1,0:T(8,128)(2,1)} %broadcast_select_fusion.9), channel_id=1, source_target_pairs={{0,16},{4,20},{8,24},{12,28},{16,0},{20,4},{24,8},{28,12},{1,17},{... | collective-permute-start | bytes 442376 | tf_op jit(solution)/shard_map/ppermute | solution.py:22
  34.3 15.7 %collective-permute-start.4 = (bf16[3,192,128]{2,1,0:T(8,128)(2,1)}, bf16[3,192,128]{2,1,0:T(8,128)(2,1)S(1)}, u32[]{:S(2)}, u32[]{:S(2)}) collective-permute-start(bf16[3,192,128]{2,1,0:T(8,128)(2,1)} %broadcast_select_fusion.8), channel_id=1, source_target_pairs={{0,24},{4,28},{8,16},{12,20},{16,8},{20,12},{24,0},{28,4},{1,25},{... | collective-permute-start | bytes 442376 | tf_op jit(solution)/shard_map/ppermute | solution.py:22
  36.1 14.5 %collective-permute-start.10 = (bf16[192,128]{1,0:T(8,128)(2,1)}, bf16[192,128]{1,0:T(8,128)(2,1)S(1)}, u32[]{:S(2)}, u32[]{:S(2)}) collective-permute-start(bf16[192,128]{1,0:T(8,128)(2,1)} %get-tuple-element.76), channel_id=1, source_target_pairs={{0,8},{4,12},{8,0},{12,4},{16,24},{20,28},{24,16},{28,20},{1,9},{5... | collective-permute-start | bytes 147464 | tf_op jit(solution)/shard_map/ppermute | solution.py:22
  36.7 14.5 %collective-permute-start.11 = (bf16[192,128]{1,0:T(8,128)(2,1)}, bf16[192,128]{1,0:T(8,128)(2,1)S(1)}, u32[]{:S(2)}, u32[]{:S(2)}) collective-permute-start(bf16[192,128]{1,0:T(8,128)(2,1)} %get-tuple-element.77), channel_id=1, source_target_pairs={{0,16},{4,20},{8,24},{12,28},{16,0},{20,4},{24,8},{28,12},{1,17},{... | collective-permute-start | bytes 147464 | tf_op jit(solution)/shard_map/ppermute | solution.py:22
  47.1 15.0 %collective-permute-start.5 = (bf16[2,192,128]{2,1,0:T(8,128)(2,1)}, bf16[2,192,128]{2,1,0:T(8,128)(2,1)S(1)}, u32[]{:S(2)}, u32[]{:S(2)}) collective-permute-start(bf16[2,192,128]{2,1,0:T(8,128)(2,1)} %slice.190), channel_id=1, source_target_pairs={{0,4},{4,0},{8,12},{12,8},{16,20},{20,16},{24,28},{28,24},{1,5},{5... | collective-permute-start | bytes 294920 | tf_op jit(solution)/shard_map/ppermute | solution.py:22
  47.1 14.6 %collective-permute-start.12 = (bf16[192,128]{1,0:T(8,128)(2,1)}, bf16[192,128]{1,0:T(8,128)(2,1)S(1)}, u32[]{:S(2)}, u32[]{:S(2)}) collective-permute-start(bf16[192,128]{1,0:T(8,128)(2,1)} %get-tuple-element.75), channel_id=1, source_target_pairs={{0,24},{4,28},{8,16},{12,20},{16,8},{20,12},{24,0},{28,4},{1,25},{... | collective-permute-start | bytes 147464 | tf_op jit(solution)/shard_map/ppermute | solution.py:22
  50.0 18.4 %collective-permute-start.6 = (bf16[2,192,128]{2,1,0:T(8,128)(2,1)S(1)}, bf16[2,192,128]{2,1,0:T(8,128)(2,1)S(1)}, u32[]{:S(2)}, u32[]{:S(2)}) collective-permute-start(bf16[2,192,128]{2,1,0:T(8,128)(2,1)S(1)} %slice.191), channel_id=1, source_target_pairs={{0,4},{4,0},{8,12},{12,8},{16,20},{20,16},{24,28},{28,24},{1,5},{5... | collective-permute-start | bytes 294920 | tf_op jit(solution)/shard_map/ppermute | solution.py:22
  50.6 19.0 %collective-permute-start.7 = (bf16[2,192,128]{2,1,0:T(8,128)(2,1)}, bf16[2,192,128]{2,1,0:T(8,128)(2,1)S(1)}, u32[]{:S(2)}, u32[]{:S(2)}) collective-permute-start(bf16[2,192,128]{2,1,0:T(8,128)(2,1)} %slice.192), channel_id=1, source_target_pairs={{0,4},{4,0},{8,12},{12,8},{16,20},{20,16},{24,28},{28,24},{1,5},{5... | collective-permute-start | bytes 294920 | tf_op jit(solution)/shard_map/ppermute | solution.py:22
  51.2 9.1 %copy-start.20 = (bf16[192,128]{1,0:T(8,128)(2,1)}, bf16[192,128]{1,0:T(8,128)(2,1)S(1)}, u32[]{:S(2)}) copy-start(bf16[192,128]{1,0:T(8,128)(2,1)S(1)} %collective-permute-done.11.refs_13_) | copy-start | bytes 147460
  51.2 19.2 %collective-permute-start.8 = (bf16[2,192,128]{2,1,0:T(8,128)(2,1)}, bf16[2,192,128]{2,1,0:T(8,128)(2,1)S(1)}, u32[]{:S(2)}, u32[]{:S(2)}) collective-permute-start(bf16[2,192,128]{2,1,0:T(8,128)(2,1)} %slice.193), channel_id=1, source_target_pairs={{0,4},{4,0},{8,12},{12,8},{16,20},{20,16},{24,28},{28,24},{1,5},{5... | collective-permute-start | bytes 294920 | tf_op jit(solution)/shard_map/ppermute | solution.py:22
  61.7 10.8 %copy-start.22 = (bf16[192,128]{1,0:T(8,128)(2,1)}, bf16[192,128]{1,0:T(8,128)(2,1)S(1)}, u32[]{:S(2)}) copy-start(bf16[192,128]{1,0:T(8,128)(2,1)S(1)} %collective-permute-done.12.refs_14_) | copy-start | bytes 147460
  61.7 25.5 %collective-permute-start.26 = (bf16[4,112,192]{1,2,0:T(8,128)(2,1)}, bf16[4,112,192]{1,2,0:T(8,128)(2,1)}, u32[]{:S(2)}, u32[]{:S(2)}) collective-permute-start(bf16[4,112,192]{1,2,0:T(8,128)(2,1)} %bitcast.220), channel_id=1, source_target_pairs={{0,4},{1,5},{4,0},{5,1},{8,12},{9,13},{12,8},{13,9},{16,20},{17,21... | collective-permute-start | bytes 516104 | tf_op jit(solution)/shard_map/ppermute | solution.py:202
  62.1 10.4 %copy-start.2 = (bf16[2,192,128]{2,1,0:T(8,128)(2,1)}, bf16[2,192,128]{2,1,0:T(8,128)(2,1)S(1)}, u32[]{:S(2)}) copy-start(bf16[2,192,128]{2,1,0:T(8,128)(2,1)S(1)} %collective-permute-done.5.refs_7_) | copy-start | bytes 294916
  62.1 25.6 %collective-permute-start.29 = (bf16[4,112,192]{1,2,0:T(8,128)(2,1)}, bf16[4,112,192]{1,2,0:T(8,128)(2,1)}, u32[]{:S(2)}, u32[]{:S(2)}) collective-permute-start(bf16[4,112,192]{1,2,0:T(8,128)(2,1)} %bitcast.218), channel_id=1, source_target_pairs={{0,5},{1,4},{4,1},{5,0},{8,13},{9,12},{12,9},{13,8},{16,21},{17,20... | collective-permute-start | bytes 516104 | tf_op jit(solution)/shard_map/ppermute | solution.py:202
  69.1 30.5 %collective-permute-start.28 = (bf16[4,112,192]{1,2,0:T(8,128)(2,1)}, bf16[4,112,192]{1,2,0:T(8,128)(2,1)}, u32[]{:S(2)}, u32[]{:S(2)}) collective-permute-start(bf16[4,112,192]{1,2,0:T(8,128)(2,1)} %bitcast.219), channel_id=1, source_target_pairs={{0,1},{1,0},{4,5},{5,4},{8,9},{9,8},{12,13},{13,12},{16,17},{17,16... | collective-permute-start | bytes 516104 | tf_op jit(solution)/shard_map/ppermute | solution.py:202
  70.2 31.3 %collective-permute-start.34 = (bf16[4,112,192]{1,2,0:T(8,128)(2,1)}, bf16[4,112,192]{1,2,0:T(8,128)(2,1)}, u32[]{:S(2)}, u32[]{:S(2)}) collective-permute-start(bf16[4,112,192]{1,2,0:T(8,128)(2,1)} %bitcast.217), channel_id=1, source_target_pairs={{0,4},{1,5},{4,0},{5,1},{8,12},{9,13},{12,8},{13,9},{16,20},{17,21... | collective-permute-start | bytes 516104 | tf_op jit(solution)/shard_map/ppermute | solution.py:202
  71.0 32.4 %collective-permute-start.37 = (bf16[4,112,192]{1,2,0:T(8,128)(2,1)}, bf16[4,112,192]{1,2,0:T(8,128)(2,1)}, u32[]{:S(2)}, u32[]{:S(2)}) collective-permute-start(bf16[4,112,192]{1,2,0:T(8,128)(2,1)} %bitcast.215), channel_id=1, source_target_pairs={{0,5},{1,4},{4,1},{5,0},{8,13},{9,12},{12,9},{13,8},{16,21},{17,20... | collective-permute-start | bytes 516104 | tf_op jit(solution)/shard_map/ppermute | solution.py:202
  77.7 10.0 %copy-start.27 = (f32[192,3,4,128]{3,0,2,1:T(8,128)S(1)}, f32[192,3,4,128]{3,0,2,1:T(8,128)}, u32[]{:S(2)}) copy-start(f32[192,3,4,128]{3,0,2,1:T(8,128)} %copy-done.26) | copy-start | bytes 3538948
  87.2 18.3 %collective-permute-start.36 = (bf16[4,112,192]{1,2,0:T(8,128)(2,1)}, bf16[4,112,192]{1,2,0:T(8,128)(2,1)}, u32[]{:S(2)}, u32[]{:S(2)}) collective-permute-start(bf16[4,112,192]{1,2,0:T(8,128)(2,1)} %bitcast.216), channel_id=1, source_target_pairs={{0,1},{1,0},{4,5},{5,4},{8,9},{9,8},{12,13},{13,12},{16,17},{17,16... | collective-permute-start | bytes 516104 | tf_op jit(solution)/shard_map/ppermute | solution.py:202
  87.7 23.2 %collective-permute-start.19 = (bf16[2,192,128]{2,1,0:T(8,128)(2,1)}, bf16[2,192,128]{2,1,0:T(8,128)(2,1)}, u32[]{:S(2)}, u32[]{:S(2)}) collective-permute-start(bf16[2,192,128]{2,1,0:T(8,128)(2,1)} %get-tuple-element.23), channel_id=1, source_target_pairs={{0,4},{4,0},{8,12},{12,8},{16,20},{20,16},{24,28},{28,24},{1,5},{5... | collective-permute-start | bytes 294920 | tf_op jit(solution)/shard_map/ppermute | solution.py:22
  100.6 7.8 %copy-start.13 = (bf16[2,192,128]{2,1,0:T(8,128)(2,1)S(1)}, bf16[2,192,128]{2,1,0:T(8,128)(2,1)}, u32[]{:S(2)}) copy-start(bf16[2,192,128]{2,1,0:T(8,128)(2,1)} %copy-done.12) | copy-start | bytes 294916
  100.6 10.2 %copy-start.9 = (bf16[2,192,128]{2,1,0:T(8,128)(2,1)S(1)}, bf16[2,192,128]{2,1,0:T(8,128)(2,1)}, u32[]{:S(2)}) copy-start(bf16[2,192,128]{2,1,0:T(8,128)(2,1)} %copy-done.8) | copy-start | bytes 294916
  101.5 10.3 %copy-start.5 = (bf16[2,192,128]{2,1,0:T(8,128)(2,1)S(1)}, bf16[2,192,128]{2,1,0:T(8,128)(2,1)}, u32[]{:S(2)}) copy-start(bf16[2,192,128]{2,1,0:T(8,128)(2,1)} %copy-done.4) | copy-start | bytes 294916
  107.4 4.4 %collective-permute-start.17 = (bf16[2,192,128]{2,1,0:T(8,128)(2,1)S(1)}, bf16[2,192,128]{2,1,0:T(8,128)(2,1)S(1)}, u32[]{:S(2)}, u32[]{:S(2)}) collective-permute-start(bf16[2,192,128]{2,1,0:T(8,128)(2,1)S(1)} %copy-done.19), channel_id=1, source_target_pairs={{0,4},{4,0},{8,12},{12,8},{16,20},{20,16},{24,28},{28,24},{1,5},{5... | collective-permute-start | bytes 294920 | tf_op jit(solution)/shard_map/ppermute | solution.py:22
  107.9 6.0 %collective-permute-start.21 = (bf16[2,192,128]{2,1,0:T(8,128)(2,1)S(1)}, bf16[2,192,128]{2,1,0:T(8,128)(2,1)S(1)}, u32[]{:S(2)}, u32[]{:S(2)}) collective-permute-start(bf16[2,192,128]{2,1,0:T(8,128)(2,1)S(1)} %copy-done.17), channel_id=1, source_target_pairs={{0,4},{4,0},{8,12},{12,8},{16,20},{20,16},{24,28},{28,24},{1,5},{5... | collective-permute-start | bytes 294920 | tf_op jit(solution)/shard_map/ppermute | solution.py:22
  107.9 17.6 %collective-permute-start.23 = (bf16[2,192,128]{2,1,0:T(8,128)(2,1)S(1)}, bf16[2,192,128]{2,1,0:T(8,128)(2,1)S(1)}, u32[]{:S(2)}, u32[]{:S(2)}) collective-permute-start(bf16[2,192,128]{2,1,0:T(8,128)(2,1)S(1)} %get-tuple-element.27), channel_id=1, source_target_pairs={{0,4},{4,0},{8,12},{12,8},{16,20},{20,16},{24,28},{28,24},{1,5},{5... | collective-permute-start | bytes 294920 | tf_op jit(solution)/shard_map/ppermute | solution.py:22
  108.4 7.5 %collective-permute-start.13 = (bf16[2,192,128]{2,1,0:T(8,128)(2,1)S(1)}, bf16[2,192,128]{2,1,0:T(8,128)(2,1)S(1)}, u32[]{:S(2)}, u32[]{:S(2)}) collective-permute-start(bf16[2,192,128]{2,1,0:T(8,128)(2,1)S(1)} %copy-done.13), channel_id=1, source_target_pairs={{0,24},{4,28},{8,16},{12,20},{16,8},{20,12},{24,0},{28,4},{1,25},{... | collective-permute-start | bytes 294920 | tf_op jit(solution)/shard_map/ppermute | solution.py:22
  110.9 13.1 %collective-permute-start.14 = (bf16[2,192,128]{2,1,0:T(8,128)(2,1)S(1)}, bf16[2,192,128]{2,1,0:T(8,128)(2,1)S(1)}, u32[]{:S(2)}, u32[]{:S(2)}) collective-permute-start(bf16[2,192,128]{2,1,0:T(8,128)(2,1)S(1)} %copy-done.9), channel_id=1, source_target_pairs={{0,16},{4,20},{8,24},{12,28},{16,0},{20,4},{24,8},{28,12},{1,17},{... | collective-permute-start | bytes 294920 | tf_op jit(solution)/shard_map/ppermute | solution.py:22
  111.8 12.2 %collective-permute-start.15 = (bf16[2,192,128]{2,1,0:T(8,128)(2,1)S(1)}, bf16[2,192,128]{2,1,0:T(8,128)(2,1)S(1)}, u32[]{:S(2)}, u32[]{:S(2)}) collective-permute-start(bf16[2,192,128]{2,1,0:T(8,128)(2,1)S(1)} %copy-done.5), channel_id=1, source_target_pairs={{0,8},{4,12},{8,0},{12,4},{16,24},{20,28},{24,16},{28,20},{1,9},{5... | collective-permute-start | bytes 294920 | tf_op jit(solution)/shard_map/ppermute | solution.py:22
  113.8 13.1 %collective-permute-start.20 = (bf16[2,192,128]{2,1,0:T(8,128)(2,1)S(1)}, bf16[2,192,128]{2,1,0:T(8,128)(2,1)S(1)}, u32[]{:S(2)}, u32[]{:S(2)}) collective-permute-start(bf16[2,192,128]{2,1,0:T(8,128)(2,1)S(1)} %add_convert_fusion.2), channel_id=1, source_target_pairs={{0,16},{4,20},{8,24},{12,28},{16,0},{20,4},{24,8},{28,12},{1,17},{... | collective-permute-start | bytes 294920 | tf_op jit(solution)/shard_map/ppermute | solution.py:22
  115.9 11.0 %collective-permute-start.18 = (bf16[2,192,128]{2,1,0:T(8,128)(2,1)S(1)}, bf16[2,192,128]{2,1,0:T(8,128)(2,1)S(1)}, u32[]{:S(2)}, u32[]{:S(2)}) collective-permute-start(bf16[2,192,128]{2,1,0:T(8,128)(2,1)S(1)} %add_convert_fusion.3), channel_id=1, source_target_pairs={{0,24},{4,28},{8,16},{12,20},{16,8},{20,12},{24,0},{28,4},{1,25},{... | collective-permute-start | bytes 294920 | tf_op jit(solution)/shard_map/ppermute | solution.py:22
  124.0 4.6 %collective-permute-start.22 = (bf16[2,192,128]{2,1,0:T(8,128)(2,1)S(1)}, bf16[2,192,128]{2,1,0:T(8,128)(2,1)S(1)}, u32[]{:S(2)}, u32[]{:S(2)}) collective-permute-start(bf16[2,192,128]{2,1,0:T(8,128)(2,1)S(1)} %add_convert_fusion.1), channel_id=1, source_target_pairs={{0,8},{4,12},{8,0},{12,4},{16,24},{20,28},{24,16},{28,20},{1,9},{5... | collective-permute-start | bytes 294920 | tf_op jit(solution)/shard_map/ppermute | solution.py:22
  125.5 16.6 %collective-permute-start.35 = (bf16[192,512]{1,0:T(8,128)(2,1)}, bf16[192,512]{1,0:T(8,128)(2,1)}, u32[]{:S(2)}, u32[]{:S(2)}) collective-permute-start(bf16[192,512]{1,0:T(8,128)(2,1)} %pad_maximum_fusion.2), channel_id=1, source_target_pairs={{0,4},{4,0},{8,12},{12,8},{16,20},{20,16},{24,28},{28,24},{1,5},{5... | collective-permute-start | bytes 589832 | tf_op jit(solution)/shard_map/ppermute | solution.py:22
  125.5 11.9 %collective-permute-start.38 = (bf16[192,512]{1,0:T(8,128)(2,1)}, bf16[192,512]{1,0:T(8,128)(2,1)}, u32[]{:S(2)}, u32[]{:S(2)}) collective-permute-start(bf16[192,512]{1,0:T(8,128)(2,1)} %pad_maximum_fusion.2), channel_id=1, source_target_pairs={{0,1},{1,0},{2,3},{3,2},{4,5},{5,4},{6,7},{7,6},{8,9},{9,8},{10,11... | collective-permute-start | bytes 589832 | tf_op jit(solution)/shard_map/ppermute | solution.py:22
  134.3 13.9 %collective-permute-start.30 = (bf16[192,1536]{1,0:T(8,128)(2,1)S(1)}, bf16[192,1536]{1,0:T(8,128)(2,1)S(1)}, u32[]{:S(2)}, u32[]{:S(2)}) collective-permute-start(bf16[192,1536]{1,0:T(8,128)(2,1)S(1)} %pad_maximum_fusion.1), channel_id=1, source_target_pairs={{0,1},{1,0},{2,3},{3,2},{4,5},{5,4},{6,7},{7,6},{8,9},{9,8},{10,11... | collective-permute-start | bytes 1769480 | tf_op jit(solution)/shard_map/ppermute | solution.py:22
  135.8 42.0 %collective-permute-start.16 = (bf16[192,896]{1,0:T(8,128)(2,1)S(1)}, bf16[192,896]{1,0:T(8,128)(2,1)S(1)}, u32[]{:S(2)}, u32[]{:S(2)}) collective-permute-start(bf16[192,896]{1,0:T(8,128)(2,1)S(1)} %dynamic-slice_convert_fusion.2), channel_id=1, source_target_pairs={{0,2},{2,0},{1,3},{3,1},{4,6},{6,4},{5,7},{7,5},{8,10},{10,8},{9,1... | collective-permute-start | bytes 1032200 | tf_op jit(solution)/shard_map/ppermute | solution.py:22
  137.5 15.7 %collective-permute-start.27 = (bf16[192,1536]{1,0:T(8,128)(2,1)S(1)}, bf16[192,1536]{1,0:T(8,128)(2,1)S(1)}, u32[]{:S(2)}, u32[]{:S(2)}) collective-permute-start(bf16[192,1536]{1,0:T(8,128)(2,1)S(1)} %pad_maximum_fusion.1), channel_id=1, source_target_pairs={{0,4},{4,0},{8,12},{12,8},{16,20},{20,16},{24,28},{28,24},{1,5},{5... | collective-permute-start | bytes 1769480 | tf_op jit(solution)/shard_map/ppermute | solution.py:22
  137.5 12.1 %collective-permute-start.39 = (bf16[192,512]{1,0:T(8,128)(2,1)}, bf16[192,512]{1,0:T(8,128)(2,1)S(1)}, u32[]{:S(2)}, u32[]{:S(2)}) collective-permute-start(bf16[192,512]{1,0:T(8,128)(2,1)} %collective-permute-done.38), channel_id=1, source_target_pairs={{0,4},{4,0},{8,12},{12,8},{16,20},{20,16},{24,28},{28,24},{1,5},{5... | collective-permute-start | bytes 589832 | tf_op jit(solution)/shard_map/ppermute | solution.py:22
  138.0 10.2 %copy-start.57 = (bf16[192,128]{1,0:T(8,128)(2,1)S(1)}, bf16[192,128]{1,0:T(8,128)(2,1)}, u32[]{:S(2)}) copy-start(bf16[192,128]{1,0:T(8,128)(2,1)} %copy-done.56) | copy-start | bytes 147460
  138.0 10.2 %copy-start.59 = (bf16[192,128]{1,0:T(8,128)(2,1)S(1)}, bf16[192,128]{1,0:T(8,128)(2,1)}, u32[]{:S(2)}) copy-start(bf16[192,128]{1,0:T(8,128)(2,1)} %copy-done.58) | copy-start | bytes 147460
  138.0 10.2 %copy-start.61 = (bf16[192,128]{1,0:T(8,128)(2,1)S(1)}, bf16[192,128]{1,0:T(8,128)(2,1)}, u32[]{:S(2)}) copy-start(bf16[192,128]{1,0:T(8,128)(2,1)} %copy-done.60) | copy-start | bytes 147460
  138.0 10.2 %copy-start.63 = (bf16[192,128]{1,0:T(8,128)(2,1)S(1)}, bf16[192,128]{1,0:T(8,128)(2,1)}, u32[]{:S(2)}) copy-start(bf16[192,128]{1,0:T(8,128)(2,1)} %copy-done.62) | copy-start | bytes 147460
  138.0 10.2 %copy-start.68 = (bf16[448,192]{0,1:T(8,128)(2,1)S(1)}, bf16[448,192]{0,1:T(8,128)(2,1)}, u32[]{:S(2)}) copy-start(bf16[448,192]{0,1:T(8,128)(2,1)} %reshape.147) | copy-start | bytes 516100
  138.0 10.2 %copy-start.69 = (bf16[448,192]{0,1:T(8,128)(2,1)S(1)}, bf16[448,192]{0,1:T(8,128)(2,1)}, u32[]{:S(2)}) copy-start(bf16[448,192]{0,1:T(8,128)(2,1)} %reshape.148) | copy-start | bytes 516100
  142.1 7.5 %copy-start.44 = (bf16[448,192]{0,1:T(8,128)(2,1)S(1)}, bf16[448,192]{0,1:T(8,128)(2,1)}, u32[]{:S(2)}) copy-start(bf16[448,192]{0,1:T(8,128)(2,1)} %reshape.150) | copy-start | bytes 516100
  142.2 7.5 %copy-start.45 = (bf16[448,192]{0,1:T(8,128)(2,1)S(1)}, bf16[448,192]{0,1:T(8,128)(2,1)}, u32[]{:S(2)}) copy-start(bf16[448,192]{0,1:T(8,128)(2,1)} %reshape.149) | copy-start | bytes 516100
  142.2 14.8 %collective-permute-start.25 = (f32[192,1]{0,1:T(1,128)S(1)}, f32[192,1]{0,1:T(1,128)S(1)}, u32[]{:S(2)}, u32[]{:S(2)}) collective-permute-start(f32[192,1]{0,1:T(1,128)S(1)} %bitcast.245), channel_id=1, source_target_pairs={{0,2},{2,0},{1,3},{3,1},{4,6},{6,4},{5,7},{7,5},{8,10},{10,8},{9,1... | collective-permute-start | bytes 2312 | tf_op jit(solution)/shard_map/ppermute | solution.py:22
  148.2 6.0 %collective-permute-start.31 = (bf16[192,1536]{1,0:T(8,128)(2,1)S(1)}, bf16[192,1536]{1,0:T(8,128)(2,1)S(1)}, u32[]{:S(2)}, u32[]{:S(2)}) collective-permute-start(bf16[192,1536]{1,0:T(8,128)(2,1)S(1)} %collective-permute-done.30), channel_id=1, source_target_pairs={{0,4},{4,0},{8,12},{12,8},{16,20},{20,16},{24,28},{28,24},{1,5},{5... | collective-permute-start | bytes 1769480 | tf_op jit(solution)/shard_map/ppermute | solution.py:22
  151.1 8.5 %collective-permute-start.40 = (bf16[2,112,512]{2,1,0:T(8,128)(2,1)S(1)}, bf16[2,112,512]{2,1,0:T(8,128)(2,1)S(1)}, u32[]{:S(2)}, u32[]{:S(2)}) collective-permute-start(bf16[2,112,512]{2,1,0:T(8,128)(2,1)S(1)} %fusion.74), channel_id=1, source_target_pairs={{0,8},{4,12},{8,0},{12,4},{16,24},{20,28},{24,16},{28,20},{1,9},{5... | collective-permute-start | bytes 688136 | tf_op jit(solution)/shard_map/ppermute | solution.py:22
  155.2 21.5 %collective-permute-start.32 = (bf16[2,112,1536]{2,1,0:T(8,128)(2,1)S(1)}, bf16[2,112,1536]{2,1,0:T(8,128)(2,1)S(1)}, u32[]{:S(2)}, u32[]{:S(2)}) collective-permute-start(bf16[2,112,1536]{2,1,0:T(8,128)(2,1)S(1)} %fusion.26), channel_id=1, source_target_pairs={{0,8},{4,12},{8,0},{12,4},{16,24},{20,28},{24,16},{28,20},{1,9},{5... | collective-permute-start | bytes 2064392 | tf_op jit(solution)/shard_map/ppermute | solution.py:22
  155.3 22.6 %collective-permute-start.24 = (bf16[192,896]{1,0:T(8,128)(2,1)S(1)}, bf16[192,896]{1,0:T(8,128)(2,1)S(1)}, u32[]{:S(2)}, u32[]{:S(2)}) collective-permute-start(bf16[192,896]{1,0:T(8,128)(2,1)S(1)} %dynamic-slice_convert_fusion.1), channel_id=1, source_target_pairs={{0,2},{2,0},{1,3},{3,1},{4,6},{6,4},{5,7},{7,5},{8,10},{10,8},{9,1... | collective-permute-start | bytes 1032200 | tf_op jit(solution)/shard_map/ppermute | solution.py:22
  159.7 18.1 %copy-start.33 = (f32[192,1792]{1,0:T(8,128)S(1)}, f32[192,1792]{1,0:T(8,128)}, u32[]{:S(2)}) copy-start(f32[192,1792]{1,0:T(8,128)} %get-tuple-element.48) | copy-start | bytes 4128772
  159.8 18.1 %copy-start.34 = (f32[192,1792]{1,0:T(8,128)S(1)}, f32[192,1792]{1,0:T(8,128)}, u32[]{:S(2)}) copy-start(f32[192,1792]{1,0:T(8,128)} %get-tuple-element.49) | copy-start | bytes 4128772
  159.8 18.1 %copy-start.40 = (bf16[1,192,896]{2,1,0:T(8,128)(2,1)S(1)}, bf16[1,192,896]{2,1,0:T(8,128)(2,1)}, u32[]{:S(2)}) copy-start(bf16[1,192,896]{2,1,0:T(8,128)(2,1)} %param.10) | copy-start | bytes 1032196
  159.8 18.1 %copy-start.42 = (bf16[1,192,896]{2,1,0:T(8,128)(2,1)S(1)}, bf16[1,192,896]{2,1,0:T(8,128)(2,1)}, u32[]{:S(2)}) copy-start(bf16[1,192,896]{2,1,0:T(8,128)(2,1)} %param.11) | copy-start | bytes 1032196
  159.8 19.4 %collective-permute-start.41 = (bf16[1,112,512]{2,1,0:T(8,128)(2,1)S(1)}, bf16[1,112,512]{2,1,0:T(8,128)(2,1)S(1)}, u32[]{:S(2)}, u32[]{:S(2)}) collective-permute-start(bf16[1,112,512]{2,1,0:T(8,128)(2,1)S(1)} %dynamic-slice_convert_fusion.3), channel_id=1, source_target_pairs={{0,16},{4,20},{8,24},{12,28},{16,0},{20,4},{24,8},{28,12},{1,17},{... | collective-permute-start | bytes 344072 | tf_op jit(solution)/shard_map/ppermute | solution.py:22
  176.9 18.2 %collective-permute-start.33 = (bf16[1,112,1536]{2,1,0:T(8,128)(2,1)S(1)}, bf16[1,112,1536]{2,1,0:T(8,128)(2,1)S(1)}, u32[]{:S(2)}, u32[]{:S(2)}) collective-permute-start(bf16[1,112,1536]{2,1,0:T(8,128)(2,1)S(1)} %dynamic-slice_convert_fusion), channel_id=1, source_target_pairs={{0,16},{4,20},{8,24},{12,28},{16,0},{20,4},{24,8},{28,12},{1,17},{... | collective-permute-start | bytes 1032200 | tf_op jit(solution)/shard_map/ppermute | solution.py:22
  (54 other events, 126.6 us)

commit v2 on v1

v2 whole, which is shorter than its diff:
```python
import functools
import math

import jax
import jax.numpy as jnp
from jax import lax
from jax.experimental import pallas as pl
from jax.experimental.pallas import tpu as pltpu
from jax.sharding import PartitionSpec as P

EPSILON = 1e-06
NEG_FILL = -1e30
GROUP_MOST = 96
FRAME_UP, FRAME_DOWN = 96, 125
NO_GROUP = 1 << 30
LANES = 128
BF = jnp.bfloat16
F32 = jnp.float32
ANY = pl.BlockSpec(memory_space=pl.ANY)
VMEM = pl.BlockSpec(memory_space=pltpu.VMEM)
SMEM = pl.BlockSpec(memory_space=pltpu.SMEM)
OVER_LAST = (((1,), (1,)), ((), ()))
OVER_FIRST = (((0,), (0,)), ((), ()))


def swap(value, axis, distance):
    count = lax.axis_size(axis)
    return lax.ppermute(value, axis, [(i, i ^ distance) for i in range(count)])


def unxor(pieces, place):
    pieces = list(pieces)
    for bit in range((len(pieces) - 1).bit_length()):
        odd = ((place >> bit) & 1) == 1
        pieces = [jnp.where(odd, pieces[j ^ (1 << bit)], pieces[j]) for j in range(len(pieces))]
    return pieces


def inv_rms(values):
    return lax.rsqrt(jnp.mean(values * values, axis=-1, keepdims=True) + EPSILON)


def norm_back(raw, gains, upstream):
    inv_norm = inv_rms(raw)
    inner_dot = jnp.mean(upstream * gains * raw, axis=-1, keepdims=True)
    return inv_norm * (gains * upstream - raw * inv_norm * inv_norm * inner_dot)


def round_up(value, step):
    return -(-value // step) * step


class Copies:
    def __init__(self, sems):
        self.sems, self.made = sems, []

    def start(self, source, target):
        copy = pltpu.make_async_copy(source, target, self.sems.at[len(self.made)])
        copy.start()
        self.made.append(copy)
        return copy

    def wait(self):
        for copy in self.made:
            copy.wait()


def call(kernel, name, out, specs, args, scratch, copies, mib, flops, out_specs=None):
    results = pl.pallas_call(
        kernel,
        out_shape=[jax.ShapeDtypeStruct(*o) for o in out],
        in_specs=specs,
        out_specs=out_specs or [ANY] * len(out),
        scratch_shapes=scratch + [pltpu.SemaphoreType.DMA((copies,))],
        compiler_params=pltpu.CompilerParams(vmem_limit_bytes=mib << 20),
        cost_estimate=pl.CostEstimate(flops=flops, bytes_accessed=2 << 20, transcendentals=0),
        name=name,
    )(*args)
    return list(results)


def spread(place, pieces, target, copies):
    width = pieces[0].shape[-1]
    for t, piece in enumerate(pieces):
        if len(pieces) == 1:
            columns = slice(None)
        else:
            columns = pl.ds(pl.multiple_of((place ^ t) * width, LANES), width)
        copies.start(piece, target.at[:, columns])


def width_pieces(value):
    pieces = [value] + [swap(value, "mp", t) for t in range(1, lax.axis_size("mp"))]
    if value.shape[-1] % LANES:
        return [jnp.concatenate(unxor(pieces, lax.axis_index("mp")), axis=-1)]
    return pieces


def width_outs(rows, width, width_part):
    if width_part % LANES:
        return [((rows, width), F32)]
    others = width // width_part - 1
    return [((rows, width_part), F32)] + [((rows, width_part), BF)] * others


def write_width(place, source, refs):
    if len(refs) == 1:
        refs[0][...] = source[...]
        return
    width = refs[0].shape[-1]
    for t, ref in enumerate(refs):
        columns = pl.ds(pl.multiple_of((place ^ t) * width, LANES), width)
        ref[...] = source[:, columns].astype(ref.dtype)


def width_sum(parts, width_part):
    place = lax.axis_index("mp")
    count = lax.axis_size("mp")
    if width_part % LANES:
        whole = parts[0]
        parts = [
            lax.dynamic_slice_in_dim(whole, (place ^ t) * width_part, width_part, 1)
            for t in range(count)
        ]
    total = parts[0]
    for t in range(1, count):
        total = total + swap(parts[t].astype(BF), "mp", t).astype(F32)
    return total


def project_kernel(heads, width_count, *refs):
    place_ref, q_gain_ref, k_gain_ref, weight_ref, mod_ref = refs[:5]
    inputs = refs[5 : 5 + width_count]
    refs = refs[5 + width_count :]
    pieces = refs[:heads]
    hidden_ref, raw_ref, inv_ref, inputs_s, pieces_s, sems = refs[heads:]
    copies = Copies(sems)
    spread(place_ref[2], inputs, inputs_s, copies)
    copies.wait()
    model_width = inputs_s.shape[1]
    values = inputs_s[...].astype(F32)
    inv_norm = inv_rms(values)
    inv_ref[...] = inv_norm
    scale = 1.0 + mod_ref[:, :model_width].astype(F32)
    hidden = (values * inv_norm * scale).astype(BF)
    hidden_ref[...] = hidden
    raw_ref[...] = jnp.dot(hidden, weight_ref[...], preferred_element_type=F32)
    inner = raw_ref.shape[1] // 3
    dim = inner // heads
    head = place_ref[0]
    for t in range(heads):
        own = head ^ t
        at = pl.multiple_of(own * dim, LANES)
        query = raw_ref[:, pl.ds(at, dim)]
        key = raw_ref[:, pl.ds(at + inner, dim)]
        q_gain = q_gain_ref[pl.ds(own, 1), :]
        k_gain = k_gain_ref[pl.ds(own, 1), :]
        pieces_s[t, 0] = (query * inv_rms(query) * q_gain).astype(BF)
        pieces_s[t, 1] = (key * inv_rms(key) * k_gain).astype(BF)
        pieces_s[t, 2] = raw_ref[:, pl.ds(at + 2 * inner, dim)].astype(BF)
        copies.start(pieces_s.at[t], pieces[t])
    for copy in copies.made[width_count:]:
        copy.wait()


def upstream_kernel(heads, width_count, *refs):
    place_ref, weight_ref, mod_ref = refs[:3]
    upstream = refs[3 : 3 + width_count]
    refs = refs[3 + width_count :]
    pieces = refs[:heads]
    grad_ref, upstream_s, heads_s, sems = refs[heads:]
    copies = Copies(sems)
    spread(place_ref[2], upstream, upstream_s, copies)
    copies.wait()
    model_width = upstream_s.shape[1]
    grad = (upstream_s[...].astype(F32) * mod_ref[:, model_width:].astype(F32)).astype(BF)
    grad_ref[...] = grad
    heads_s[...] = lax.dot_general(
        grad, weight_ref[...], OVER_LAST, preferred_element_type=F32
    ).astype(BF)
    dim = heads_s.shape[1] // heads
    for t in range(heads):
        columns = pl.ds(pl.multiple_of((place_ref[0] ^ t) * dim, LANES), dim)
        copies.start(heads_s.at[:, columns], pieces[t])
    for copy in copies.made[width_count:]:
        copy.wait()


def turn_kernel(blocks, clips, *refs):
    place_ref, hidden_ref, grad_ref = refs[:3]
    pieces = refs[3 : 3 + 2 * clips]
    turned_s, sems = refs[3 + 2 * clips :]
    span = turned_s.shape[-2]
    for at, ref in enumerate((hidden_ref, grad_ref)):
        turned = jnp.transpose(ref[...].astype(F32))
        for b in range(blocks * 2 * clips):
            turned_s[at, b // (2 * clips), b % (2 * clips)] = turned[
                b * span : (b + 1) * span
            ].astype(BF)
    copies = Copies(sems)
    for u in range(2):
        for w in range(clips):
            own = (place_ref[3] ^ u) * clips + (place_ref[4] ^ w)
            copies.start(turned_s.at[:, :, own], pieces[u * clips + w])
    copies.wait()


def attention_kernel(heads, sharers, rows, block, factor, *refs):
    place_ref, key_group_ref, query_group_ref = refs[:3]
    at = 3
    own = refs[at : at + heads]
    at += heads
    shared = refs[at : at + heads * (sharers - 1)]
    at += heads * (sharers - 1)
    ups = refs[at : at + heads]
    at += heads
    outs = refs[at : at + heads]
    at += heads
    key_grads = refs[at : at + heads * sharers]
    at += heads * sharers
    key_s, value_s, query_s, up_s, out_s, dk_s, dv_s, half_s, sems = refs[at:]
    head = place_ref[0]
    part = place_ref[1]
    dim = key_s.shape[-1]
    span = heads * sharers * rows
    total = heads * rows
    copies = Copies(sems)
    for t in range(heads):
        m = head ^ t
        copies.start(own[t].at[0], query_s.at[m])
        copies.start(own[t].at[1], key_s.at[m * sharers + part])
        copies.start(own[t].at[2], value_s.at[m * sharers + part])
        for u in range(1, sharers):
            piece = shared[t * (sharers - 1) + u - 1]
            copies.start(piece.at[0], key_s.at[m * sharers + (part ^ u)])
            copies.start(piece.at[1], value_s.at[m * sharers + (part ^ u)])
        copies.start(ups[t], up_s.at[m])
    dk_s[...] = jnp.zeros_like(dk_s)
    dv_s[...] = jnp.zeros_like(dv_s)
    group_col = jnp.transpose(jnp.broadcast_to(key_group_ref[...], (128, span)))
    group_col = jnp.concatenate([group_col] * (-(-block // 128)), axis=1)[:, :block]
    copies.wait()
    loaded = len(copies.made)
    keys = key_s[...].reshape(span, dim)
    values = value_s[...].reshape(span, dim)
    queries = query_s[...].reshape(total, dim)
    upstream = up_s[...].reshape(total, dim)
    scale = factor * math.log2(math.e)
    for j in range(total // block):
        last = ((j + 1) * block - 1) // rows
        reach = min(span, round_up((last + 1) * sharers * rows + GROUP_MOST - 1, 128))
        lanes = slice(j * block, (j + 1) * block)
        query = queries[lanes]
        up = upstream[lanes]
        key = keys[:reach]
        value = values[:reach]
        logits = lax.dot_general(key, query, OVER_LAST, preferred_element_type=F32)
        logits = jnp.where(group_col[:reach] <= query_group_ref[:, lanes], logits, NEG_FILL)
        row_max = jnp.max(logits, axis=0, keepdims=True)
        unnorm = jnp.exp2((logits - row_max) * scale)
        inverse = 1.0 / jnp.sum(unnorm, axis=0, keepdims=True)
        out = lax.dot_general(value, unnorm.astype(BF), OVER_FIRST, preferred_element_type=F32)
        out = (out * inverse).astype(BF)
        up_t = jnp.transpose(up.astype(F32))
        out_dot = jnp.sum(up_t * out.astype(F32), axis=0, keepdims=True)
        probs = unnorm * inverse
        grad_probs = lax.dot_general(value, up, OVER_LAST, preferred_element_type=F32)
        grad_logits = (probs * (grad_probs - out_dot)).astype(BF)
        grad_query = lax.dot_general(key, grad_logits, OVER_FIRST, preferred_element_type=F32)
        out_s[0, lanes, :] = jnp.transpose(out.astype(F32)).astype(BF)
        out_s[1, lanes, :] = jnp.transpose(grad_query * factor).astype(BF)
        dk_s[:reach, :] += jnp.dot(grad_logits, query, preferred_element_type=F32)
        dv_s[:reach, :] += jnp.dot(probs.astype(BF), up, preferred_element_type=F32)
    for t in range(heads):
        m = head ^ t
        for u in range(sharers):
            there = pl.ds(pl.multiple_of((m * sharers + (part ^ u)) * rows, 64), rows)
            ref = key_grads[t * sharers + u]
            if u == 0:
                copies.start(dk_s.at[there, :], ref.at[0])
                copies.start(dv_s.at[there, :], ref.at[1])
            else:
                slot = half_s.at[t * (sharers - 1) + u - 1]
                slot[0] = dk_s[there, :].astype(BF)
                slot[1] = dv_s[there, :].astype(BF)
                copies.start(slot, ref)
        here = pl.ds(pl.multiple_of(m * rows, 64), rows)
        copies.start(out_s.at[:, here, :], outs[t])
    for copy in copies.made[loaded:]:
        copy.wait()


def attention(place, part, group_ids, clip_length, own, shared, ups):
    heads = len(own)
    sharers = len(shared) // heads + 1
    rows, width = ups[0].shape
    span = heads * sharers * rows
    total = heads * rows
    block = 256 if total % 256 == 0 else total
    positions = lax.iota(jnp.int32, span)
    key_group = jnp.where(positions < clip_length, group_ids, NO_GROUP)[None, :]
    query_group = lax.dynamic_index_in_dim(
        group_ids.reshape(heads, sharers, rows), part, 1, keepdims=False
    ).reshape(1, total)
    pair = (2, rows, width)
    out = [(pair, BF)] * heads
    for _ in range(heads):
        out.append((pair, F32))
        out.extend([(pair, BF)] * (sharers - 1))
    loads = heads * (4 + 2 * (sharers - 1))
    stores = heads * (3 + sharers - 1)
    got = call(
        functools.partial(attention_kernel, heads, sharers, rows, block, width ** (-0.5)),
        "attention",
        out,
        [SMEM, VMEM, VMEM] + [ANY] * (2 * heads + heads * (sharers - 1)),
        [place, key_group, query_group, *own, *shared, *ups],
        [
            pltpu.VMEM((heads * sharers, rows, width), BF),
            pltpu.VMEM((heads * sharers, rows, width), BF),
            pltpu.VMEM((heads, rows, width), BF),
            pltpu.VMEM((heads, rows, width), BF),
            pltpu.VMEM((2, total, width), BF),
            pltpu.VMEM((span, width), F32),
            pltpu.VMEM((span, width), F32),
            pltpu.VMEM((max(1, heads * (sharers - 1)),) + pair, BF),
        ],
        loads + stores,
        40,
        12 * total * span * width,
    )
    outs = got[:heads]
    key_grads = [got[heads + t * sharers : heads + (t + 1) * sharers] for t in range(heads)]
    return outs, key_grads


def share_kernel(heads, sharers, factor, *refs):
    terms = refs[: heads * sharers]
    sums = refs[heads * sharers : heads * sharers + heads]
    own_s, others_s, sums_s, sems = refs[heads * sharers + heads :]
    copies = Copies(sems)
    for t in range(heads):
        copies.start(terms[t * sharers], own_s.at[t])
        for u in range(1, sharers):
            copies.start(terms[t * sharers + u], others_s.at[t * (sharers - 1) + u - 1])
    copies.wait()
    loaded = len(copies.made)
    for t in range(heads):
        total = own_s[t]
        for u in range(1, sharers):
            total = total + others_s[t * (sharers - 1) + u - 1].astype(F32)
        sums_s[t, 0] = (total[0] * factor).astype(BF)
        sums_s[t, 1] = total[1].astype(BF)
        copies.start(sums_s.at[t], sums[t])
    for copy in copies.made[loaded:]:
        copy.wait()


def query_kernel(heads, *refs):
    place_ref, gain_ref, raw_ref = refs[:3]
    pieces = refs[3 : 3 + heads]
    rows_ref, grad_ref, pieces_s, sems = refs[3 + heads :]
    copies = Copies(sems)
    for t in range(heads):
        copies.start(pieces[t], pieces_s.at[t])
    copies.wait()
    dim = pieces_s.shape[-1]
    for t in range(heads):
        own = place_ref[0] ^ t
        columns = pl.ds(pl.multiple_of(own * dim, LANES), dim)
        rows_ref[:, columns] = pieces_s[t, 0]
        grad_ref[:, columns] = norm_back(
            raw_ref[:, columns], gain_ref[pl.ds(own, 1), :], pieces_s[t, 1].astype(F32)
        ).astype(BF)


def key_kernel(heads, *refs):
    place_ref, gain_ref, raw_ref = refs[:3]
    pieces = refs[3 : 3 + heads]
    key_ref, value_ref, pieces_s, sems = refs[3 + heads :]
    copies = Copies(sems)
    for t in range(heads):
        copies.start(pieces[t], pieces_s.at[t])
    copies.wait()
    dim = pieces_s.shape[-1]
    inner = heads * dim
    for t in range(heads):
        own = place_ref[0] ^ t
        at = pl.multiple_of(own * dim, LANES)
        columns = pl.ds(at, dim)
        key_ref[:, columns] = norm_back(
            raw_ref[:, pl.ds(at + inner, dim)],
            gain_ref[pl.ds(own, 1), :],
            pieces_s[t, 0].astype(F32),
        ).astype(BF)
        value_ref[:, columns] = pieces_s[t, 1]


def mix_kernel(place_ref, rows_ref, weight_ref, *refs):
    whole_s = refs[-2]
    whole_s[...] = jnp.dot(rows_ref[...], weight_ref[...], preferred_element_type=F32)
    write_width(place_ref[2], whole_s, refs[:-2])


def hidden_kernel(width_count, *refs):
    place_ref, grads, weight_ref, mod_ref, inv_ref = refs[0], refs[1:4], *refs[4:7]
    inputs = refs[7 : 7 + width_count]
    dot_ref = refs[7 + width_count]
    outs = refs[8 + width_count : -3]
    whole_s, inputs_s, sems = refs[-3:]
    copies = Copies(sems)
    spread(place_ref[2], inputs, inputs_s, copies)
    inner = grads[0].shape[1]
    total = 0.0
    for at, grad in enumerate(grads):
        total = total + lax.dot_general(
            grad[...],
            weight_ref[:, at * inner : (at + 1) * inner],
            OVER_LAST,
            preferred_element_type=F32,
        )
    whole_s[...] = total
    copies.wait()
    write_width(place_ref[2], whole_s, outs)
    model_width = inputs_s.shape[1]
    scale = 1.0 + mod_ref[:, :model_width].astype(F32)
    normed = inputs_s[...].astype(F32) * inv_ref[...]
    dot = jnp.sum(whole_s[...] * scale * normed, axis=1, keepdims=True)
    turned = jnp.transpose(jnp.broadcast_to(dot, (dot.shape[0], LANES)))
    dot_ref[...] = turned[:8]


def outer_kernel(step, *refs):
    place_ref = refs[0]
    count = (len(refs) - 4) // 2
    lefts, rights = refs[1 : 1 + count], refs[1 + count : 1 + 2 * count]
    send_ref, keep_ref, _ = refs[1 + 2 * count :]
    blocks, span, rows = lefts[0].shape
    total = 0.0
    for left, right in zip(lefts, rights):
        total = total + jnp.dot(
            left[...].reshape(blocks * span, rows), right[...], preferred_element_type=F32
        )
    total = total.reshape(blocks, span, total.shape[1])
    odd = (place_ref[5] // step) % 2
    for b in range(blocks // 2):
        first, second = total[2 * b], total[2 * b + 1]
        keep_ref[b] = jnp.where(odd == 1, second, first)
        send_ref[b] = jnp.where(odd == 1, first, second).astype(BF)


def gathered(right):
    rights = []
    for w in range(lax.axis_size("dp")):
        far = right if w == 0 else swap(right, "dp", w)
        rights.append(far)
    return rights + [swap(far, "seq", 1) for far in rights]


def weight_grad(place, lefts, right, seq):
    rights = gathered(right)
    blocks, span, rows = lefts[0].shape
    width = right.shape[1]
    half = (blocks // 2, span, width)
    send, keep = call(
        functools.partial(outer_kernel, 2),
        "weight_sum",
        [(half, BF), (half, F32)],
        [SMEM] + [VMEM] * (2 * len(lefts)),
        [place, *lefts, *rights],
        [],
        1,
        24,
        2 * blocks * span * rows * width * len(lefts),
        [VMEM, VMEM],
    )
    step = 2
    while True:
        total = keep + swap(send, "seq", step).astype(F32)
        step *= 2
        if total.shape[0] == 1:
            return total[0]
        halves = total.reshape(total.shape[0] // 2, 2, span, width)
        odd = (seq // step) % 2
        keep = lax.dynamic_index_in_dim(halves, odd, 1, keepdims=False)
        send = lax.dynamic_index_in_dim(halves, 1 - odd, 1, keepdims=False).astype(BF)


def on_device(
    latents, grad_out, sync_mod, w_qkv, w_out, q_gain, k_gain, frame_of, group_id, clip_len
):
    latents, grad_out, sync_mod = latents[0], grad_out[0], sync_mod[0]
    frame_of, group_id, clip_len = frame_of[0], group_id[0], clip_len[0]
    rows, width_part = latents.shape
    frame_count = sync_mod.shape[0]
    model_width = sync_mod.shape[1] // 2
    heads, head_dim = q_gain.shape
    inner = heads * head_dim
    count, clips = lax.axis_size("seq"), lax.axis_size("dp")
    sharers = count // heads
    seq, clip = lax.axis_index("seq"), lax.axis_index("dp")
    head, part = seq // sharers, seq % sharers
    model_place = lax.axis_index("mp")
    place = jnp.stack([head, part, model_place, seq % 2, clip, seq]).astype(jnp.int32)

    inputs = width_pieces(latents)
    upstream = width_pieces(grad_out)
    width_count = len(inputs)

    back = max(frame_count * j - (FRAME_UP * rows * j) // FRAME_DOWN for j in range(count))
    back = min(frame_count, round_up(max(back, 1), 16))
    earlier = lax.ppermute(
        sync_mod[frame_count - back :], "seq", [(i, i + 1) for i in range(count - 1)]
    )
    window = jnp.concatenate([earlier, sync_mod], axis=0)
    local_frame = frame_of - (seq * frame_count - back)
    selector = (
        local_frame[:, None] == lax.iota(jnp.int32, frame_count + back)[None, :]
    ).astype(BF)
    mod = jnp.dot(selector, window, preferred_element_type=F32).astype(BF)

    weight = w_qkv.reshape(model_width, 3 * inner)
    got = call(
        functools.partial(project_kernel, heads, width_count),
        "project",
        [((3, rows, head_dim), BF)] * heads
        + [((rows, model_width), BF), ((rows, 3 * inner), F32), ((rows, 1), F32)],
        [SMEM] + [VMEM] * 4 + [ANY] * width_count,
        [place, q_gain, k_gain, weight, mod, *inputs],
        [pltpu.VMEM((rows, model_width), BF), pltpu.VMEM((heads, 3, rows, head_dim), BF)],
        width_count + heads,
        32,
        6 * rows * model_width * inner,
        [ANY] * heads + [VMEM] * 3,
    )
    own, (hidden, raw, inv_norm) = got[:heads], got[heads:]
    own = [own[0]] + [swap(own[t], "seq", t * sharers) for t in range(1, heads)]
    shared = [swap(own[t][1:], "seq", u) for t in range(heads) for u in range(1, sharers)]

    got = call(
        functools.partial(upstream_kernel, heads, width_count),
        "upstream",
        [((rows, head_dim), BF)] * heads + [((rows, model_width), BF)],
        [SMEM] + [VMEM] * 2 + [ANY] * width_count,
        [place, w_out, mod, *upstream],
        [pltpu.VMEM((rows, model_width), BF), pltpu.VMEM((rows, inner), BF)],
        width_count + heads,
        24,
        2 * rows * model_width * inner,
        [ANY] * heads + [VMEM],
    )
    ups, grad_attn = got[:heads], got[heads]
    ups = [ups[0]] + [swap(ups[t], "seq", t * sharers) for t in range(1, heads)]

    blocks = count // 2
    span = model_width // (count * clips)
    lefts = call(
        functools.partial(turn_kernel, blocks, clips),
        "turn",
        [((2, blocks, span, rows), BF)] * (2 * clips),
        [SMEM, VMEM, VMEM],
        [place, hidden, grad_attn],
        [pltpu.VMEM((2, blocks, 2 * clips, span, rows), BF)],
        2 * clips,
        24,
        1 << 28,
    )
    for u in range(2):
        for w in range(clips):
            if u or w:
                pairs = [
                    (s * clips + x, (s ^ u) * clips + (x ^ w))
                    for s in range(count)
                    for x in range(clips)
                ]
                lefts[u * clips + w] = lax.ppermute(lefts[u * clips + w], ("seq", "dp"), pairs)

    outs, key_grads = attention(place, part, group_id, clip_len, own, shared, ups)
    terms = []
    for t in range(heads):
        terms.append(key_grads[t][0])
        terms.extend(swap(key_grads[t][u], "seq", u) for u in range(1, sharers))
    pair = (2, rows, head_dim)
    sums = call(
        functools.partial(share_kernel, heads, sharers, head_dim ** (-0.5)),
        "share",
        [(pair, BF)] * heads,
        [ANY] * len(terms),
        terms,
        [
            pltpu.VMEM((heads,) + pair, F32),
            pltpu.VMEM((max(1, heads * (sharers - 1)),) + pair, BF),
            pltpu.VMEM((heads,) + pair, BF),
        ],
        heads * sharers + heads,
        16,
        1 << 24,
    )
    back_out = [outs[0]] + [swap(outs[t], "seq", t * sharers) for t in range(1, heads)]
    back_key = [sums[0]] + [swap(sums[t], "seq", t * sharers) for t in range(1, heads)]
    out_rows, grad_query = call(
        functools.partial(query_kernel, heads),
        "query_back",
        [((rows, inner), BF)] * 2,
        [SMEM, VMEM, VMEM] + [ANY] * heads,
        [place, q_gain, raw, *back_out],
        [pltpu.VMEM((heads,) + pair, BF)],
        heads,
        16,
        1 << 24,
        [VMEM] * 2,
    )
    grad_key, grad_value = call(
        functools.partial(key_kernel, heads),
        "key_back",
        [((rows, inner), BF)] * 2,
        [SMEM, VMEM, VMEM] + [ANY] * heads,
        [place, k_gain, raw, *back_key],
        [pltpu.VMEM((heads,) + pair, BF)],
        heads,
        16,
        1 << 24,
        [VMEM] * 2,
    )

    parts = call(
        mix_kernel,
        "mix",
        width_outs(rows, model_width, width_part),
        [SMEM, VMEM, VMEM],
        [place, out_rows, w_out],
        [pltpu.VMEM((rows, model_width), F32)],
        1,
        24,
        2 * rows * model_width * inner,
        [VMEM] * len(width_outs(rows, model_width, width_part)),
    )
    attn_mine = width_sum(parts, width_part)
    gate_mine = lax.dynamic_slice_in_dim(
        mod, model_width + model_place * width_part, width_part, 1
    )
    mixed = (latents.astype(F32) + gate_mine.astype(F32) * attn_mine).astype(BF)

    got = call(
        functools.partial(hidden_kernel, width_count),
        "hidden_back",
        [((8, rows), F32)] + width_outs(rows, model_width, width_part),
        [SMEM] + [VMEM] * 6 + [ANY] * width_count,
        [place, grad_query, grad_key, grad_value, weight, mod, inv_norm, *inputs],
        [pltpu.VMEM((rows, model_width), F32), pltpu.VMEM((rows, model_width), BF)],
        width_count,
        40,
        6 * rows * model_width * inner,
        [VMEM] * (1 + len(width_outs(rows, model_width, width_part))),
    )
    part_dot, parts = got[0], got[1:]
    full_dot = part_dot
    for t in range(1, lax.axis_size("mp")):
        full_dot = full_dot + swap(part_dot, "mp", t)
    grad_mine = width_sum(parts, width_part)
    scale_mine = lax.dynamic_slice_in_dim(mod, model_place * width_part, width_part, 1)
    normed_mine = latents.astype(F32) * inv_norm
    grad_normed = grad_mine * (1.0 + scale_mine.astype(F32))
    inner_mean = full_dot[0][:, None] / model_width
    grad_inputs = inv_norm * (grad_normed - normed_mine * inner_mean)
    grad_latents = (grad_out.astype(F32) + grad_inputs).astype(BF)

    left_hidden = [left[0] for left in lefts]
    left_grad = [left[1] for left in lefts]
    grad_wout = weight_grad(place, left_grad, out_rows, seq)
    grad_wqkv = jnp.stack(
        [weight_grad(place, left_hidden, g, seq) for g in (grad_query, grad_key, grad_value)],
        axis=1,
    )
    return mixed[None], grad_latents[None], grad_wqkv, jnp.transpose(grad_wout)


def solution(mesh):
    in_specs = (
        P("dp", "seq", "mp"),
        P("dp", "seq", "mp"),
        P("dp", "seq", None),
        P(None, None, "mp"),
        P("mp", None),
        P("mp", None),
        P("mp", None),
        P("dp", "seq"),
        P("dp", None),
        P("dp"),
    )
    out_specs = (
        P("dp", "seq", "mp"),
        P("dp", "seq", "mp"),
        P(("seq", "dp"), None, "mp"),
        P("mp", ("seq", "dp")),
    )
    return jax.shard_map(
        on_device, mesh=mesh, in_specs=in_specs, out_specs=out_specs, check_vma=False
    )
```

time: 198 us -> 182 us (0.919)
  Pallas kernels: 6.27 us -> 34.2 us
  local copies, waits for them, and re-layouts: 70.7 us -> 43.5 us
  matrix products: 13.5 us -> 0.57 us
  other arithmetic: 14.7 us -> 4.05 us
  waiting for transfers between devices: 45.3 us -> 49.7 us
  starting transfers between devices: 43.9 us -> 47 us
    pallas_call x1 -> x13, Pallas kernels: 6.27 us -> 34.2 us  [call(): pl.pallas_call(kernel, out_shape=[jax.ShapeDtypeStruct(*o) for o in out],...]
    dot_general x9 -> x1, matrix products: 13.5 us -> 0.57 us  [on_device(): mod = jnp.dot(selector, window, preferred_element_type=F32).astype(BF)]
    dynamic_slice x1 -> x0, local copies, waits for them, and re-layouts: 9.02 us -> none  [weight_grad(): lax.dynamic_index_in_dim(blocks, (core ^ u) * clips + (clip ^ w), 1, keep...]
    ppermute x6 -> x0, local copies, waits for them, and re-layouts: 6.52 us -> none  [weight_grad(): mine = lax.ppermute(mine, ('seq', 'dp'), pairs)]
    reshape x10 -> x1, local copies, waits for them, and re-layouts: 13.9 us -> 8.39 us  [on_device(): weight = w_qkv.reshape(model_width, 3 * inner)]
    select_n x10 -> x0, other arithmetic: 4.59 us -> none  [unxor(): jnp.where(odd, pieces[j ^ 1 << bit], pieces[j])]
    ppermute x35 -> x45, waiting for transfers between devices: 45.3 us -> 49.7 us  [swap(): return lax.ppermute(value, axis, [(i, i ^ distance) for i in range(count)])]
    squeeze x0 -> x4, local copies, waits for them, and re-layouts: none -> 3.95 us  [on_device(): left_grad = [left[1] for left in lefts]]
  transfers between devices with their start and end apart: 42 -> 49, of which waited for: 7 -> 17; matrix products, arithmetic and copies ran while one was open for 39% -> 15% of each run, Pallas kernels for 3% -> 13%
where the time goes in v2:
time: 182 us; the launch traced here: 181 us
  waiting for transfers between devices  49.7 us (27%)
  starting transfers between devices  47 us (26%)
  local copies, waits for them, and re-layouts  43.5 us (24%)
  Pallas kernels  34.2 us (19%)
  other arithmetic  4.05 us (2%)
  between operations  2.1 us (1%)
    ppermute x45, waiting for transfers between devices, swap(): return lax.ppermute(value, axis, [(i, i ^ distance) for i in range(count)])  49.7 us
    ppermute x45, starting transfers between devices, swap(): return lax.ppermute(value, axis, [(i, i ^ distance) for i in range(count)])  41.1 us
    pallas_call x13, Pallas kernels, call(): pl.pallas_call(kernel, out_shape=[jax.ShapeDtypeStruct(*o) for o in out],...  34.2 us
    unnamed x117, local copies, waits for them, and re-layouts  26.6 us
    reshape x1, local copies, waits for them, and re-layouts, on_device(): weight = w_qkv.reshape(model_width, 3 * inner)  8.39 us
    squeeze x4, local copies, waits for them, and re-layouts, on_device(): left_grad = [left[1] for left in lefts]  3.95 us
  transfers between devices with their start and end apart: 49, of which 17 were waited for; matrix products, arithmetic and copies ran while one was open for 15% of the time, Pallas kernels for 13%

profile of v2, /device:TPU:0, one launch (start us, length us, event | category | flops | bytes accessed | tf_op | source)
XLA Modules:
  0.0 181.1 jit_solution(18282972014423115670)
XLA Ops:
  0.6 1.0 slice_bitcast_fusion.8
  1.7 2.4 %collective-permute-start = (bf16[32,3584]{1,0:T(8,128)(2,1)S(1)}, bf16[32,3584]{1,0:T(8,128)(2,1)S(1)}, u32[]{:S(2)}, u32[]{:S(2)}) collective-permute-start(bf16[32,3584]{1,0:T(8,128)(2,1)S(1)} %slice_bitcast_fusion.8), channel_id=1, source_target_pairs={{0,4},{4,8},{8,12},{12,16},{16,20},{20,24},{24,28},{1,5},{5,9},{9,... | collective-permute-start | bytes 688136 | tf_op jit(solution)/shard_map/ppermute | solution.py:512
  4.0 2.4 %collective-permute-start.1 = (bf16[192,896]{1,0:T(8,128)(2,1)}, bf16[192,896]{1,0:T(8,128)(2,1)S(1)}, u32[]{:S(2)}, u32[]{:S(2)}) collective-permute-start(bf16[192,896]{1,0:T(8,128)(2,1)} %bitcast.48), channel_id=1, source_target_pairs={{0,2},{2,0},{1,3},{3,1},{4,6},{6,4},{5,7},{7,5},{8,10},{10,8},{9,1... | collective-permute-start | bytes 1032200 | tf_op jit(solution)/shard_map/ppermute | solution.py:28
  7.2 8.1 %copy.16 = bf16[1792,3,512]{0,2,1:T(8,128)(2,1)} copy(bf16[1792,3,512]{2,0,1:T(8,128)(2,1)} %param.13) | data formatting | bytes 11010048 | tf_op args[3]
  15.3 8.4 %copy.17.refs_3_.refs_4_ = bf16[1792,1536]{1,0:T(8,128)(2,1)} copy(bf16[1792,1536]{0,1:T(8,128)(2,1)} %bitcast.53) | data formatting | bytes 11010048 | tf_op jit(solution)/shard_map/reshape | solution.py:522
  25.3 2.6 %copy-done = bf16[1792,1536]{1,0:T(8,128)(2,1)S(1)} copy-done((bf16[1792,1536]{1,0:T(8,128)(2,1)S(1)}, bf16[1792,1536]{1,0:T(8,128)(2,1)}, u32[]{:S(2)}) %copy-start) | copy-done | bytes 5505048
  27.9 3.5 %project.1 = (bf16[3,192,128]{2,1,0:T(8,128)(2,1)S(1)}, bf16[3,192,128]{2,1,0:T(8,128)(2,1)S(1)}, bf16[3,192,128]{2,1,0:T(8,128)(2,1)S(1)}, bf16[3,192,128]{2,1,...) custom-call(s32[6]{0:T(128)S(1)} %copy-done.34, ...), custom_call_target="tpu_custom_call" | custom-call | flops 1056964608 | bytes 2097152 | tf_op jit(solution)/shard_map/project/pallas_call | solution.py:69
  31.4 2.2 %collective-permute-start.2 = (bf16[3,192,128]{2,1,0:T(8,128)(2,1)S(1)}, bf16[3,192,128]{2,1,0:T(8,128)(2,1)S(1)}, u32[]{:S(2)}, u32[]{:S(2)}) collective-permute-start(bf16[3,192,128]{2,1,0:T(8,128)(2,1)S(1)} %get-tuple-element.55), channel_id=1, source_target_pairs={{0,8},{4,12},{8,0},{12,4},{16,24},{20,28},{24,16},{28,20},{1,9},{5... | collective-permute-start | bytes 442376 | tf_op jit(solution)/shard_map/ppermute | solution.py:28
  33.6 2.6 %collective-permute-start.3 = (bf16[3,192,128]{2,1,0:T(8,128)(2,1)S(1)}, bf16[3,192,128]{2,1,0:T(8,128)(2,1)S(1)}, u32[]{:S(2)}, u32[]{:S(2)}) collective-permute-start(bf16[3,192,128]{2,1,0:T(8,128)(2,1)S(1)} %get-tuple-element.56), channel_id=1, source_target_pairs={{0,16},{4,20},{8,24},{12,28},{16,0},{20,4},{24,8},{28,12},{1,17},{... | collective-permute-start | bytes 442376 | tf_op jit(solution)/shard_map/ppermute | solution.py:28
  36.3 3.0 %upstream.1 = (bf16[192,128]{1,0:T(8,128)(2,1)S(1)}, bf16[192,128]{1,0:T(8,128)(2,1)S(1)}, bf16[192,128]{1,0:T(8,128)(2,1)S(1)}, bf16[192,128]{1,0:T(8,128)(2,1)}, bf16[192,1792]{1,0:T(8,128)(2,1)S(1)}) custom-call(s32[6]{0:T(128)S(1)} %copy-done.34, bf16[512,1792]{1,0:T(8,128)(2,1)S(1)} %copy-done.2, ...), custom_call_target="tpu_custom_call" | custom-call | flops 352321536 | bytes 2097152 | tf_op jit(solution)/shard_map/upstream/pallas_call | solution.py:69
  39.3 0.9 copy-done.15
  40.2 0.9 collective-permute-start.10
  41.1 3.5 %collective-permute-start.11 = (bf16[192,128]{1,0:T(8,128)(2,1)S(1)}, bf16[192,128]{1,0:T(8,128)(2,1)S(1)}, u32[]{:S(2)}, u32[]{:S(2)}) collective-permute-start(bf16[192,128]{1,0:T(8,128)(2,1)S(1)} %get-tuple-element.60), channel_id=1, source_target_pairs={{0,16},{4,20},{8,24},{12,28},{16,0},{20,4},{24,8},{28,12},{1,17},{... | collective-permute-start | bytes 147464 | tf_op jit(solution)/shard_map/ppermute | solution.py:28
  46.6 1.1 collective-permute-done.3.refs_5_
  47.7 3.5 %collective-permute-start.12 = (bf16[192,128]{1,0:T(8,128)(2,1)}, bf16[192,128]{1,0:T(8,128)(2,1)}, u32[]{:S(2)}, u32[]{:S(2)}) collective-permute-start(bf16[192,128]{1,0:T(8,128)(2,1)} %get-tuple-element.61), channel_id=1, source_target_pairs={{0,24},{4,28},{8,16},{12,20},{16,8},{20,12},{24,0},{28,4},{1,25},{... | collective-permute-start | bytes 147464 | tf_op jit(solution)/shard_map/ppermute | solution.py:28
  55.6 1.0 collective-permute-done.8.refs_10_
  56.6 0.9 copy-done.37
  57.5 0.9 copy-done.39
  60.8 10.4 %attention.1 = (bf16[2,192,128]{2,1,0:T(8,128)(2,1)S(1)}, bf16[2,192,128]{2,1,0:T(8,128)(2,1)}, bf16[2,192,128]{2,1,0:T(8,128)(2,1)}, bf16[2,192,128]{2,1,0:T(8,...) custom-call(s32[6]{0:T(128)S(1)} %copy-done.35, ...), custom_call_target="tpu_custom_call" | custom-call | flops 1811939328 | bytes 2097152 | tf_op jit(solution)/shard_map/attention/pallas_call | solution.py:69
  71.9 1.9 %turn.1 = (bf16[2,4,112,192]{3,2,1,0:T(8,128)(2,1)S(1)}, bf16[2,4,112,192]{3,2,1,0:T(8,128)(2,1)}, bf16[2,4,112,192]{3,2,1,0:T(8,128)(2,1)S(1)}, bf16[2,4,112,192]{3,2,1,0:T(8,128)(2,1)S(1)}) custom-call(s32[6]{0:T(128)S(1)} %copy-done.35, bf16[192,1792]{1,0:T(8,128)(2,1)S(1)} %copy-done.14, bf16[192,1792]{1,0:T(8,128)(2,1)S(1)} %copy-done.16), custom_call_target="tpu_custom_call" | custom-call | flops 268435456 | bytes 2097152 | tf_op jit(solution)/shard_map/turn/pallas_call | solution.py:69
  75.5 1.1 collective-permute-start.14
  76.6 2.7 %collective-permute-start.15 = (bf16[2,192,128]{2,1,0:T(8,128)(2,1)}, bf16[2,192,128]{2,1,0:T(8,128)(2,1)}, u32[]{:S(2)}, u32[]{:S(2)}) collective-permute-start(bf16[2,192,128]{2,1,0:T(8,128)(2,1)} %get-tuple-element.65), channel_id=1, source_target_pairs={{0,24},{4,28},{8,16},{12,20},{16,8},{20,12},{24,0},{28,4},{1,25},{... | collective-permute-start | bytes 294920 | tf_op jit(solution)/shard_map/ppermute | solution.py:28
  79.3 1.5 collective-permute-start.26
  82.0 4.5 %collective-permute-done.14.refs_5_ = bf16[2,192,128]{2,1,0:T(8,128)(2,1)} collective-permute-done((bf16[2,192,128]{2,1,0:T(8,128)(2,1)}, bf16[2,192,128]{2,1,0:T(8,128)(2,1)}, u32[]{:S(2)}, u32[]{:S(2)}) %collective-permute-start.14) | collective-permute-done | bytes 98336 | tf_op jit(solution)/shard_map/ppermute | solution.py:28
  87.6 1.8 slice_bitcast_fusion.6
  89.5 1.3 copy-done.4
  90.8 0.9 copy-done.29
  91.7 0.9 copy-done.33
  92.6 2.1 %query_back.1 = (bf16[192,512]{1,0:T(8,128)(2,1)S(1)}, bf16[192,512]{1,0:T(8,128)(2,1)S(1)}) custom-call(s32[6]{0:T(128)S(1)} %copy-done.35, f32[4,128]{1,0:T(4,128)S(1)} %copy-done.41, f32[192,1536]{1,0:T(8,128)S(1)} %copy-done.4, bf16[2,192,128]{2,1,0:T(8,128)(2,1)S(1)} %copy-done.29, bf16[2,192,128]{2,1,0:T(8,128)(2,1)S(1)} %copy-done.33, ...), custom_call_target="tpu_custom_call" | custom-call | flops 16777216 | bytes 2097152 | tf_op jit(solution)/shard_map/query_back/pallas_call | solution.py:69
  94.7 1.7 collective-permute-start.28
  97.0 2.9 %share.1 = (bf16[2,192,128]{2,1,0:T(8,128)(2,1)S(1)}, bf16[2,192,128]{2,1,0:T(8,128)(2,1)S(1)}, bf16[2,192,128]{2,1,0:T(8,128)(2,1)S(1)}, bf16[2,192,128]{2,1,0:T(8,128)(2,1)S(1)}) custom-call(f32[2,192,128]{2,1,0:T(8,128)S(1)} %copy-done.21, bf16[2,192,128]{2,1,0:T(8,128)(2,1)S(1)} %copy-done.31, f32[2,192,128]{2,1,0:T(8,128)S(1)} %copy-done.23, ...), custom_call_target="tpu_custom_call" | custom-call | flops 16777216 | bytes 2097152 | tf_op jit(solution)/shard_map/share/pallas_call | solution.py:69
  99.9 1.5 collective-permute-start.21
  101.4 1.1 slice_bitcast_fusion.2
  103.3 1.8 %collective-permute-done.21.refs_4_ = bf16[2,192,128]{2,1,0:T(8,128)(2,1)S(1)} collective-permute-done((bf16[2,192,128]{2,1,0:T(8,128)(2,1)S(1)}, bf16[2,192,128]{2,1,0:T(8,128)(2,1)S(1)}, u32[]{:S(2)}, u32[]{:S(2)}) %collective-permute-start.21) | collective-permute-done | bytes 98336 | tf_op jit(solution)/shard_map/ppermute | solution.py:28
  105.2 1.7 collective-permute-start.23
  106.9 1.1 slice_bitcast_fusion.1
  107.9 5.0 %collective-permute-done.22.refs_5_ = bf16[2,192,128]{2,1,0:T(8,128)(2,1)S(1)} collective-permute-done((bf16[2,192,128]{2,1,0:T(8,128)(2,1)S(1)}, bf16[2,192,128]{2,1,0:T(8,128)(2,1)S(1)}, u32[]{:S(2)}, u32[]{:S(2)}) %collective-permute-start.22) | collective-permute-done | bytes 98336 | tf_op jit(solution)/shard_map/ppermute | solution.py:28
  113.0 1.4 key_back.1
  114.4 2.6 %copy-done.1 = bf16[1792,1536]{1,0:T(8,128)(2,1)S(1)} copy-done((bf16[1792,1536]{1,0:T(8,128)(2,1)S(1)}, bf16[1792,1536]{1,0:T(8,128)(2,1)}, u32[]{:S(2)}) %copy-start.1) | copy-done | bytes 5505048
  117.0 3.1 %hidden_back.1 = (f32[8,192]{1,0:T(8,128)S(1)}, f32[192,896]{1,0:T(8,128)S(1)}, bf16[192,896]{1,0:T(8,128)(2,1)S(1)}) custom-call(s32[6]{0:T(128)S(1)} %copy-done.35, bf16[192,512]{1,0:T(8,128)(2,1)S(1)} %get-tuple-element.70.refs_1_.refs_5_, bf16[192,512]{1,0:T(8,128)(2,1)S(1)} %get-tuple-element.83.refs_2_.refs_5_, ...), custom_call_target="tpu_custom_call" | custom-call | flops 1056964608 | bytes 2097152 | tf_op jit(solution)/shard_map/hidden_back/pallas_call | solution.py:69
  120.1 1.6 collective-permute-start.25
  121.7 1.2 mix.1
  122.8 1.6 collective-permute-start.44
  124.4 0.9 collective-permute-start.16
  125.3 1.2 collective-permute-start.24
  126.5 2.0 %collective-permute-done.44.refs_6_ = bf16[192,512]{1,0:T(8,128)(2,1)S(1)} collective-permute-done((bf16[192,512]{1,0:T(8,128)(2,1)S(1)}, bf16[192,512]{1,0:T(8,128)(2,1)S(1)}, u32[]{:S(2)}, u32[]{:S(2)}) %collective-permute-start.44) | collective-permute-done | bytes 196640 | tf_op jit(solution)/shard_map/ppermute | solution.py:28
  128.6 1.5 collective-permute-start.39
  130.6 1.2 weight_sum.4
  132.4 1.2 weight_sum.7
  133.6 2.5 %collective-permute-done.39.refs_6_ = bf16[192,512]{1,0:T(8,128)(2,1)S(1)} collective-permute-done((bf16[192,512]{1,0:T(8,128)(2,1)S(1)}, bf16[192,512]{1,0:T(8,128)(2,1)S(1)}, u32[]{:S(2)}, u32[]{:S(2)}) %collective-permute-start.39) | collective-permute-done | bytes 196640 | tf_op jit(solution)/shard_map/ppermute | solution.py:28
  136.0 2.1 %collective-permute-done.34.refs_6_ = bf16[192,512]{1,0:T(8,128)(2,1)S(1)} collective-permute-done((bf16[192,512]{1,0:T(8,128)(2,1)S(1)}, bf16[192,512]{1,0:T(8,128)(2,1)S(1)}, u32[]{:S(2)}, u32[]{:S(2)}) %collective-permute-start.34) | collective-permute-done | bytes 196640 | tf_op jit(solution)/shard_map/ppermute | solution.py:28
  138.7 3.6 %collective-permute-done.24 = bf16[192,896]{1,0:T(8,128)(2,1)S(1)} collective-permute-done((bf16[192,896]{1,0:T(8,128)(2,1)S(1)}, bf16[192,896]{1,0:T(8,128)(2,1)S(1)}, u32[]{:S(2)}, u32[]{:S(2)}) %collective-permute-start.24) | collective-permute-done | bytes 344096 | tf_op jit(solution)/shard_map/ppermute | solution.py:28
  142.3 2.1 %collective-permute-start.32 = (bf16[2,112,512]{2,1,0:T(8,128)(2,1)S(1)}, bf16[2,112,512]{2,1,0:T(8,128)(2,1)S(1)}, u32[]{:S(2)}, u32[]{:S(2)}) collective-permute-start(bf16[2,112,512]{2,1,0:T(8,128)(2,1)S(1)} %get-tuple-element.95), channel_id=1, source_target_pairs={{0,8},{4,12},{8,0},{12,4},{16,24},{20,28},{24,16},{28,20},{1,9},{5... | collective-permute-start | bytes 688136 | tf_op jit(solution)/shard_map/ppermute | solution.py:28
  144.3 1.3 fusion.9
  145.6 1.2 weight_sum.6
  146.8 2.1 %collective-permute-start.42 = (bf16[2,112,512]{2,1,0:T(8,128)(2,1)S(1)}, bf16[2,112,512]{2,1,0:T(8,128)(2,1)S(1)}, u32[]{:S(2)}, u32[]{:S(2)}) collective-permute-start(bf16[2,112,512]{2,1,0:T(8,128)(2,1)S(1)} %get-tuple-element.99), channel_id=1, source_target_pairs={{0,8},{4,12},{8,0},{12,4},{16,24},{20,28},{24,16},{28,20},{1,9},{5... | collective-permute-start | bytes 688136 | tf_op jit(solution)/shard_map/ppermute | solution.py:28
  148.9 1.2 weight_sum.5
  150.9 2.8 %collective-permute-start.33 = (bf16[1,112,512]{2,1,0:T(8,128)(2,1)S(1)}, bf16[1,112,512]{2,1,0:T(8,128)(2,1)S(1)}, u32[]{:S(2)}, u32[]{:S(2)}) collective-permute-start(bf16[1,112,512]{2,1,0:T(8,128)(2,1)S(1)} %dynamic-slice_convert_fusion.3), channel_id=1, source_target_pairs={{0,16},{4,20},{8,24},{12,28},{16,0},{20,4},{24,8},{28,12},{1,17},{... | collective-permute-start | bytes 344072 | tf_op jit(solution)/shard_map/ppermute | solution.py:28
  153.7 4.5 %collective-permute-done.47 = bf16[2,112,512]{2,1,0:T(8,128)(2,1)S(1)} collective-permute-done((bf16[2,112,512]{2,1,0:T(8,128)(2,1)S(1)}, bf16[2,112,512]{2,1,0:T(8,128)(2,1)S(1)}, u32[]{:S(2)}, u32[]{:S(2)}) %collective-permute-start.47) | collective-permute-done | bytes 229408 | tf_op jit(solution)/shard_map/ppermute | solution.py:28
  158.6 7.0 %collective-permute-done.42 = bf16[2,112,512]{2,1,0:T(8,128)(2,1)S(1)} collective-permute-done((bf16[2,112,512]{2,1,0:T(8,128)(2,1)S(1)}, bf16[2,112,512]{2,1,0:T(8,128)(2,1)S(1)}, u32[]{:S(2)}, u32[]{:S(2)}) %collective-permute-start.42) | collective-permute-done | bytes 229408 | tf_op jit(solution)/shard_map/ppermute | solution.py:28
  165.9 4.5 %collective-permute-done.37 = bf16[2,112,512]{2,1,0:T(8,128)(2,1)S(1)} collective-permute-done((bf16[2,112,512]{2,1,0:T(8,128)(2,1)S(1)}, bf16[2,112,512]{2,1,0:T(8,128)(2,1)S(1)}, u32[]{:S(2)}, u32[]{:S(2)}) %collective-permute-start.37) | collective-permute-done | bytes 229408 | tf_op jit(solution)/shard_map/ppermute | solution.py:28
  171.3 7.4 %collective-permute-done.43 = bf16[1,112,512]{2,1,0:T(8,128)(2,1)S(1)} collective-permute-done((bf16[1,112,512]{2,1,0:T(8,128)(2,1)S(1)}, bf16[1,112,512]{2,1,0:T(8,128)(2,1)S(1)}, u32[]{:S(2)}, u32[]{:S(2)}) %collective-permute-start.43) | collective-permute-done | bytes 114720 | tf_op jit(solution)/shard_map/ppermute | solution.py:28
  178.8 1.4 collective-permute-done.38
  180.2 0.9 pad_maximum_fusion
  (197 shorter events, 20.7 us)
Async XLA Ops:
  1.7 22.7 %collective-permute-start = (bf16[32,3584]{1,0:T(8,128)(2,1)S(1)}, bf16[32,3584]{1,0:T(8,128)(2,1)S(1)}, u32[]{:S(2)}, u32[]{:S(2)}) collective-permute-start(bf16[32,3584]{1,0:T(8,128)(2,1)S(1)} %slice_bitcast_fusion.8), channel_id=1, source_target_pairs={{0,4},{4,8},{8,12},{12,16},{16,20},{20,24},{24,28},{1,5},{5,9},{9,... | collective-permute-start | bytes 688136 | tf_op jit(solution)/shard_map/ppermute | solution.py:512
  4.0 20.9 %collective-permute-start.1 = (bf16[192,896]{1,0:T(8,128)(2,1)}, bf16[192,896]{1,0:T(8,128)(2,1)S(1)}, u32[]{:S(2)}, u32[]{:S(2)}) collective-permute-start(bf16[192,896]{1,0:T(8,128)(2,1)} %bitcast.48), channel_id=1, source_target_pairs={{0,2},{2,0},{1,3},{3,1},{4,6},{6,4},{5,7},{7,5},{8,10},{10,8},{9,1... | collective-permute-start | bytes 1032200 | tf_op jit(solution)/shard_map/ppermute | solution.py:28
  6.4 29.8 %collective-permute-start.9 = (bf16[192,896]{1,0:T(8,128)(2,1)}, bf16[192,896]{1,0:T(8,128)(2,1)}, u32[]{:S(2)}, u32[]{:S(2)}) collective-permute-start(bf16[192,896]{1,0:T(8,128)(2,1)} %bitcast.51), channel_id=1, source_target_pairs={{0,2},{2,0},{1,3},{3,1},{4,6},{6,4},{5,7},{7,5},{8,10},{10,8},{9,1... | collective-permute-start | bytes 1032200 | tf_op jit(solution)/shard_map/ppermute | solution.py:28
  31.4 13.9 %copy-start.36 = (bf16[3,192,128]{2,1,0:T(8,128)(2,1)}, bf16[3,192,128]{2,1,0:T(8,128)(2,1)S(1)}, u32[]{:S(2)}) copy-start(bf16[3,192,128]{2,1,0:T(8,128)(2,1)S(1)} %get-tuple-element.54.refs_3_) | copy-start | bytes 442372
  31.4 14.5 %collective-permute-start.2 = (bf16[3,192,128]{2,1,0:T(8,128)(2,1)S(1)}, bf16[3,192,128]{2,1,0:T(8,128)(2,1)S(1)}, u32[]{:S(2)}, u32[]{:S(2)}) collective-permute-start(bf16[3,192,128]{2,1,0:T(8,128)(2,1)S(1)} %get-tuple-element.55), channel_id=1, source_target_pairs={{0,8},{4,12},{8,0},{12,4},{16,24},{20,28},{24,16},{28,20},{1,9},{5... | collective-permute-start | bytes 442376 | tf_op jit(solution)/shard_map/ppermute | solution.py:28
  33.6 14.0 %collective-permute-start.3 = (bf16[3,192,128]{2,1,0:T(8,128)(2,1)S(1)}, bf16[3,192,128]{2,1,0:T(8,128)(2,1)S(1)}, u32[]{:S(2)}, u32[]{:S(2)}) collective-permute-start(bf16[3,192,128]{2,1,0:T(8,128)(2,1)S(1)} %get-tuple-element.56), channel_id=1, source_target_pairs={{0,16},{4,20},{8,24},{12,28},{16,0},{20,4},{24,8},{28,12},{1,17},{... | collective-permute-start | bytes 442376 | tf_op jit(solution)/shard_map/ppermute | solution.py:28
  36.2 18.7 %copy-start.57 = (s32[1,1536]{1,0:T(1,128)S(1)}, s32[1,1536]{1,0:T(1,128)}, u32[]{:S(2)}) copy-start(s32[1,1536]{1,0:T(1,128)} %param.18) | copy-start | bytes 18436
  36.2 20.3 %copy-start.35 = (s32[6]{0:T(128)S(1)}, s32[6]{0:T(128)}, u32[]{:S(2)}) copy-start(s32[6]{0:T(128)} %stack.27.refs_0_.place_ref) | copy-start | bytes 76
  36.2 15.6 %collective-permute-start.4 = (bf16[3,192,128]{2,1,0:T(8,128)(2,1)S(1)}, bf16[3,192,128]{2,1,0:T(8,128)(2,1)S(1)}, u32[]{:S(2)}, u32[]{:S(2)}) collective-permute-start(bf16[3,192,128]{2,1,0:T(8,128)(2,1)S(1)} %get-tuple-element.57), channel_id=1, source_target_pairs={{0,24},{4,28},{8,16},{12,20},{16,8},{20,12},{24,0},{28,4},{1,25},{... | collective-permute-start | bytes 442376 | tf_op jit(solution)/shard_map/ppermute | solution.py:28
  40.2 14.7 %copy-start.50 = (bf16[192,128]{1,0:T(8,128)(2,1)}, bf16[192,128]{1,0:T(8,128)(2,1)S(1)}, u32[]{:S(2)}) copy-start(bf16[192,128]{1,0:T(8,128)(2,1)S(1)} %get-tuple-element.58.refs_11_) | copy-start | bytes 147460
  40.2 12.9 %collective-permute-start.10 = (bf16[192,128]{1,0:T(8,128)(2,1)S(1)}, bf16[192,128]{1,0:T(8,128)(2,1)S(1)}, u32[]{:S(2)}, u32[]{:S(2)}) collective-permute-start(bf16[192,128]{1,0:T(8,128)(2,1)S(1)} %get-tuple-element.59), channel_id=1, source_target_pairs={{0,8},{4,12},{8,0},{12,4},{16,24},{20,28},{24,16},{28,20},{1,9},{5... | collective-permute-start | bytes 147464 | tf_op jit(solution)/shard_map/ppermute | solution.py:28
  41.1 13.2 %collective-permute-start.11 = (bf16[192,128]{1,0:T(8,128)(2,1)S(1)}, bf16[192,128]{1,0:T(8,128)(2,1)S(1)}, u32[]{:S(2)}, u32[]{:S(2)}) collective-permute-start(bf16[192,128]{1,0:T(8,128)(2,1)S(1)} %get-tuple-element.60), channel_id=1, source_target_pairs={{0,16},{4,20},{8,24},{12,28},{16,0},{20,4},{24,8},{28,12},{1,17},{... | collective-permute-start | bytes 147464 | tf_op jit(solution)/shard_map/ppermute | solution.py:28
  45.9 9.2 %collective-permute-start.5 = (bf16[2,192,128]{2,1,0:T(8,128)(2,1)}, bf16[2,192,128]{2,1,0:T(8,128)(2,1)}, u32[]{:S(2)}, u32[]{:S(2)}) collective-permute-start(bf16[2,192,128]{2,1,0:T(8,128)(2,1)} %slice.47), channel_id=1, source_target_pairs={{0,4},{4,0},{8,12},{12,8},{16,20},{20,16},{24,28},{28,24},{1,5},{5... | collective-permute-start | bytes 294920 | tf_op jit(solution)/shard_map/ppermute | solution.py:28
  47.7 7.5 %collective-permute-start.12 = (bf16[192,128]{1,0:T(8,128)(2,1)}, bf16[192,128]{1,0:T(8,128)(2,1)}, u32[]{:S(2)}, u32[]{:S(2)}) collective-permute-start(bf16[192,128]{1,0:T(8,128)(2,1)} %get-tuple-element.61), channel_id=1, source_target_pairs={{0,24},{4,28},{8,16},{12,20},{16,8},{20,12},{24,0},{28,4},{1,25},{... | collective-permute-start | bytes 147464 | tf_op jit(solution)/shard_map/ppermute | solution.py:28
  51.8 3.3 %collective-permute-start.6 = (bf16[2,192,128]{2,1,0:T(8,128)(2,1)}, bf16[2,192,128]{2,1,0:T(8,128)(2,1)}, u32[]{:S(2)}, u32[]{:S(2)}) collective-permute-start(bf16[2,192,128]{2,1,0:T(8,128)(2,1)} %slice.60), channel_id=1, source_target_pairs={{0,4},{4,0},{8,12},{12,8},{16,20},{20,16},{24,28},{28,24},{1,5},{5... | collective-permute-start | bytes 294920 | tf_op jit(solution)/shard_map/ppermute | solution.py:28
  53.8 1.8 collective-permute-start.7
  54.9 1.6 collective-permute-start.8
  60.8 11.2 %copy-start.14 = (bf16[192,1792]{1,0:T(8,128)(2,1)S(1)}, bf16[192,1792]{1,0:T(8,128)(2,1)}, u32[]{:S(2)}) copy-start(bf16[192,1792]{1,0:T(8,128)(2,1)} %copy-done.13) | copy-start | bytes 2064388
  60.8 11.2 %copy-start.16 = (bf16[192,1792]{1,0:T(8,128)(2,1)S(1)}, bf16[192,1792]{1,0:T(8,128)(2,1)}, u32[]{:S(2)}) copy-start(bf16[192,1792]{1,0:T(8,128)(2,1)} %copy-done.15) | copy-start | bytes 2064388
  71.2 9.5 %copy-start.47 = (bf16[2,192,128]{2,1,0:T(8,128)(2,1)}, bf16[2,192,128]{2,1,0:T(8,128)(2,1)S(1)}, u32[]{:S(2)}) copy-start(bf16[2,192,128]{2,1,0:T(8,128)(2,1)S(1)} %get-tuple-element.78) | copy-start | bytes 294916
  71.3 18.1 %copy-start.19 = (f32[192,1]{1,0:T(8,128)S(1)}, f32[192,1]{1,0:T(8,128)}, u32[]{:S(2)}) copy-start(f32[192,1]{1,0:T(8,128)} %copy-done.18) | copy-start | bytes 2308
  71.3 18.2 %copy-start.41 = (f32[4,128]{1,0:T(4,128)S(1)}, f32[4,128]{1,0:T(4,128)}, u32[]{:S(2)}) copy-start(f32[4,128]{1,0:T(4,128)} %refs_1_.6) | copy-start | bytes 6148
  71.3 9.6 %collective-permute-start.13 = (bf16[2,192,128]{2,1,0:T(8,128)(2,1)}, bf16[2,192,128]{2,1,0:T(8,128)(2,1)S(1)}, u32[]{:S(2)}, u32[]{:S(2)}) collective-permute-start(bf16[2,192,128]{2,1,0:T(8,128)(2,1)} %get-tuple-element.63), channel_id=1, source_target_pairs={{0,8},{4,12},{8,0},{12,4},{16,24},{20,28},{24,16},{28,20},{1,9},{5... | collective-permute-start | bytes 294920 | tf_op jit(solution)/shard_map/ppermute | solution.py:28
  75.5 11.0 %collective-permute-start.14 = (bf16[2,192,128]{2,1,0:T(8,128)(2,1)}, bf16[2,192,128]{2,1,0:T(8,128)(2,1)}, u32[]{:S(2)}, u32[]{:S(2)}) collective-permute-start(bf16[2,192,128]{2,1,0:T(8,128)(2,1)} %get-tuple-element.64), channel_id=1, source_target_pairs={{0,16},{4,20},{8,24},{12,28},{16,0},{20,4},{24,8},{28,12},{1,17},{... | collective-permute-start | bytes 294920 | tf_op jit(solution)/shard_map/ppermute | solution.py:28
  76.6 9.9 %collective-permute-start.15 = (bf16[2,192,128]{2,1,0:T(8,128)(2,1)}, bf16[2,192,128]{2,1,0:T(8,128)(2,1)}, u32[]{:S(2)}, u32[]{:S(2)}) collective-permute-start(bf16[2,192,128]{2,1,0:T(8,128)(2,1)} %get-tuple-element.65), channel_id=1, source_target_pairs={{0,24},{4,28},{8,16},{12,20},{16,8},{20,12},{24,0},{28,4},{1,25},{... | collective-permute-start | bytes 294920 | tf_op jit(solution)/shard_map/ppermute | solution.py:28
  79.3 20.7 %collective-permute-start.26 = (bf16[2,4,112,192]{3,2,1,0:T(8,128)(2,1)}, bf16[2,4,112,192]{3,2,1,0:T(8,128)(2,1)}, u32[]{:S(2)}, u32[]{:S(2)}) collective-permute-start(bf16[2,4,112,192]{3,2,1,0:T(8,128)(2,1)} %get-tuple-element.91), channel_id=1, source_target_pairs={{0,1},{1,0},{4,5},{5,4},{8,9},{9,8},{12,13},{13,12},{16,17},{17,16... | collective-permute-start | bytes 1032200 | tf_op jit(solution)/shard_map/ppermute | solution.py:576
  80.8 6.2 %collective-permute-start.17 = (bf16[2,192,128]{2,1,0:T(8,128)(2,1)}, bf16[2,192,128]{2,1,0:T(8,128)(2,1)S(1)}, u32[]{:S(2)}, u32[]{:S(2)}) collective-permute-start(bf16[2,192,128]{2,1,0:T(8,128)(2,1)} %get-tuple-element.72), channel_id=1, source_target_pairs={{0,4},{4,0},{8,12},{12,8},{16,20},{20,16},{24,28},{28,24},{1,5},{5... | collective-permute-start | bytes 294920 | tf_op jit(solution)/shard_map/ppermute | solution.py:28
  81.5 21.0 %collective-permute-start.27 = (bf16[2,4,112,192]{3,2,1,0:T(8,128)(2,1)}, bf16[2,4,112,192]{3,2,1,0:T(8,128)(2,1)}, u32[]{:S(2)}, u32[]{:S(2)}) collective-permute-start(bf16[2,4,112,192]{3,2,1,0:T(8,128)(2,1)} %copy-done.46), channel_id=1, source_target_pairs={{0,4},{1,5},{4,0},{5,1},{8,12},{9,13},{12,8},{13,9},{16,20},{17,21... | collective-permute-start | bytes 1032200 | tf_op jit(solution)/shard_map/ppermute | solution.py:576
  86.4 8.2 %collective-permute-start.18 = (bf16[2,192,128]{2,1,0:T(8,128)(2,1)}, bf16[2,192,128]{2,1,0:T(8,128)(2,1)}, u32[]{:S(2)}, u32[]{:S(2)}) collective-permute-start(bf16[2,192,128]{2,1,0:T(8,128)(2,1)} %copy-done.49), channel_id=1, source_target_pairs={{0,4},{4,0},{8,12},{12,8},{16,20},{20,16},{24,28},{28,24},{1,5},{5... | collective-permute-start | bytes 294920 | tf_op jit(solution)/shard_map/ppermute | solution.py:28
  86.4 9.9 %collective-permute-start.19 = (bf16[2,192,128]{2,1,0:T(8,128)(2,1)}, bf16[2,192,128]{2,1,0:T(8,128)(2,1)}, u32[]{:S(2)}, u32[]{:S(2)}) collective-permute-start(bf16[2,192,128]{2,1,0:T(8,128)(2,1)} %copy-done.48), channel_id=1, source_target_pairs={{0,4},{4,0},{8,12},{12,8},{16,20},{20,16},{24,28},{28,24},{1,5},{5... | collective-permute-start | bytes 294920 | tf_op jit(solution)/shard_map/ppermute | solution.py:28
  87.6 9.3 %collective-permute-start.20 = (bf16[2,192,128]{2,1,0:T(8,128)(2,1)}, bf16[2,192,128]{2,1,0:T(8,128)(2,1)}, u32[]{:S(2)}, u32[]{:S(2)}) collective-permute-start(bf16[2,192,128]{2,1,0:T(8,128)(2,1)} %copy-done.47), channel_id=1, source_target_pairs={{0,4},{4,0},{8,12},{12,8},{16,20},{20,16},{24,28},{28,24},{1,5},{5... | collective-permute-start | bytes 294920 | tf_op jit(solution)/shard_map/ppermute | solution.py:28
  94.7 29.7 %collective-permute-start.28 = (bf16[2,4,112,192]{3,2,1,0:T(8,128)(2,1)S(1)}, bf16[2,4,112,192]{3,2,1,0:T(8,128)(2,1)S(1)}, u32[]{:S(2)}, u32[]{:S(2)}) collective-permute-start(bf16[2,4,112,192]{3,2,1,0:T(8,128)(2,1)S(1)} %copy-done.45), channel_id=1, source_target_pairs={{0,5},{1,4},{4,1},{5,0},{8,13},{9,12},{12,9},{13,8},{16,21},{17,20... | collective-permute-start | bytes 1032200 | tf_op jit(solution)/shard_map/ppermute | solution.py:576
  96.4 29.0 %collective-permute-start.29 = (bf16[192,512]{1,0:T(8,128)(2,1)S(1)}, bf16[192,512]{1,0:T(8,128)(2,1)S(1)}, u32[]{:S(2)}, u32[]{:S(2)}) collective-permute-start(bf16[192,512]{1,0:T(8,128)(2,1)S(1)} %get-tuple-element.70.refs_1_.refs_5_), channel_id=1, source_target_pairs={{0,1},{1,0},{2,3},{3,2},{4,5},{5,4},{6,7},{7,6},{8,9},{9,8},{10,11... | collective-permute-start | bytes 589832 | tf_op jit(solution)/shard_map/ppermute | solution.py:28
  96.9 29.6 %collective-permute-start.30 = (bf16[192,512]{1,0:T(8,128)(2,1)S(1)}, bf16[192,512]{1,0:T(8,128)(2,1)S(1)}, u32[]{:S(2)}, u32[]{:S(2)}) collective-permute-start(bf16[192,512]{1,0:T(8,128)(2,1)S(1)} %get-tuple-element.70.refs_1_.refs_5_), channel_id=1, source_target_pairs={{0,4},{4,0},{8,12},{12,8},{16,20},{20,16},{24,28},{28,24},{1,5},{5... | collective-permute-start | bytes 589832 | tf_op jit(solution)/shard_map/ppermute | solution.py:28
  96.9 16.0 %copy-start.5 = (f32[192,1536]{1,0:T(8,128)S(1)}, f32[192,1536]{1,0:T(8,128)}, u32[]{:S(2)}) copy-start(f32[192,1536]{1,0:T(8,128)} %copy-done.3) | copy-start | bytes 3538948
  97.0 16.0 %copy-start.43 = (f32[4,128]{1,0:T(4,128)S(1)}, f32[4,128]{1,0:T(4,128)}, u32[]{:S(2)}) copy-start(f32[4,128]{1,0:T(4,128)} %refs_1_.7) | copy-start | bytes 6148
  99.9 5.3 %collective-permute-start.21 = (bf16[2,192,128]{2,1,0:T(8,128)(2,1)S(1)}, bf16[2,192,128]{2,1,0:T(8,128)(2,1)S(1)}, u32[]{:S(2)}, u32[]{:S(2)}) collective-permute-start(bf16[2,192,128]{2,1,0:T(8,128)(2,1)S(1)} %get-tuple-element.80), channel_id=1, source_target_pairs={{0,8},{4,12},{8,0},{12,4},{16,24},{20,28},{24,16},{28,20},{1,9},{5... | collective-permute-start | bytes 294920 | tf_op jit(solution)/shard_map/ppermute | solution.py:28
  102.5 11.9 %copy-start.7 = (bf16[1,192,896]{2,1,0:T(8,128)(2,1)S(1)}, bf16[1,192,896]{2,1,0:T(8,128)(2,1)}, u32[]{:S(2)}) copy-start(bf16[1,192,896]{2,1,0:T(8,128)(2,1)} %param.10) | copy-start | bytes 1032196
  102.5 11.9 %copy-start.9 = (bf16[192,896]{1,0:T(8,128)(2,1)S(1)}, bf16[192,896]{1,0:T(8,128)(2,1)}, u32[]{:S(2)}) copy-start(bf16[192,896]{1,0:T(8,128)(2,1)} %copy-done.8) | copy-start | bytes 1032196
  102.5 10.5 %collective-permute-start.22 = (bf16[2,192,128]{2,1,0:T(8,128)(2,1)S(1)}, bf16[2,192,128]{2,1,0:T(8,128)(2,1)S(1)}, u32[]{:S(2)}, u32[]{:S(2)}) collective-permute-start(bf16[2,192,128]{2,1,0:T(8,128)(2,1)S(1)} %get-tuple-element.81), channel_id=1, source_target_pairs={{0,16},{4,20},{8,24},{12,28},{16,0},{20,4},{24,8},{28,12},{1,17},{... | collective-permute-start | bytes 294920 | tf_op jit(solution)/shard_map/ppermute | solution.py:28
  105.2 7.8 %collective-permute-start.23 = (bf16[2,192,128]{2,1,0:T(8,128)(2,1)S(1)}, bf16[2,192,128]{2,1,0:T(8,128)(2,1)S(1)}, u32[]{:S(2)}, u32[]{:S(2)}) collective-permute-start(bf16[2,192,128]{2,1,0:T(8,128)(2,1)S(1)} %get-tuple-element.82), channel_id=1, source_target_pairs={{0,24},{4,28},{8,16},{12,20},{16,8},{20,12},{24,0},{28,4},{1,25},{... | collective-permute-start | bytes 294920 | tf_op jit(solution)/shard_map/ppermute | solution.py:28
  120.1 4.3 %collective-permute-start.25 = (f32[8,192]{1,0:T(8,128)S(1)}, f32[8,192]{1,0:T(8,128)S(1)}, u32[]{:S(2)}, u32[]{:S(2)}) collective-permute-start(f32[8,192]{1,0:T(8,128)S(1)} %get-tuple-element.87), channel_id=1, source_target_pairs={{0,2},{2,0},{1,3},{3,1},{4,6},{6,4},{5,7},{7,5},{8,10},{10,8},{9,1... | collective-permute-start | bytes 18440 | tf_op jit(solution)/shard_map/ppermute | solution.py:28
  122.8 9.6 %copy-start.12 = (bf16[4,112,192]{2,1,0:T(8,128)(2,1)S(1)}, bf16[4,112,192]{2,1,0:T(8,128)(2,1)}, u32[]{:S(2)}) copy-start(bf16[4,112,192]{2,1,0:T(8,128)(2,1)} %get-tuple-element.110.refs_1_) | copy-start | bytes 516100
  122.8 5.7 %collective-permute-start.44 = (bf16[192,512]{1,0:T(8,128)(2,1)S(1)}, bf16[192,512]{1,0:T(8,128)(2,1)S(1)}, u32[]{:S(2)}, u32[]{:S(2)}) collective-permute-start(bf16[192,512]{1,0:T(8,128)(2,1)S(1)} %get-tuple-element.66.rows_ref.refs_5_), channel_id=1, source_target_pairs={{0,1},{1,0},{2,3},{3,2},{4,5},{5,4},{6,7},{7,6},{8,9},{9,8},{10,11... | collective-permute-start | bytes 589832 | tf_op jit(solution)/shard_map/ppermute | solution.py:28
  124.4 5.7 %collective-permute-start.45 = (bf16[192,512]{1,0:T(8,128)(2,1)S(1)}, bf16[192,512]{1,0:T(8,128)(2,1)S(1)}, u32[]{:S(2)}, u32[]{:S(2)}) collective-permute-start(bf16[192,512]{1,0:T(8,128)(2,1)S(1)} %get-tuple-element.66.rows_ref.refs_5_), channel_id=1, source_target_pairs={{0,4},{4,0},{8,12},{12,8},{16,20},{20,16},{24,28},{28,24},{1,5},{5... | collective-permute-start | bytes 589832 | tf_op jit(solution)/shard_map/ppermute | solution.py:28
  124.4 13.7 %collective-permute-start.16 = (bf16[192,896]{1,0:T(8,128)(2,1)S(1)}, bf16[192,896]{1,0:T(8,128)(2,1)S(1)}, u32[]{:S(2)}, u32[]{:S(2)}) collective-permute-start(bf16[192,896]{1,0:T(8,128)(2,1)S(1)} %get-tuple-element.68), channel_id=1, source_target_pairs={{0,2},{2,0},{1,3},{3,1},{4,6},{6,4},{5,7},{7,5},{8,10},{10,8},{9,1... | collective-permute-start | bytes 1032200 | tf_op jit(solution)/shard_map/ppermute | solution.py:28
  125.3 16.9 %collective-permute-start.24 = (bf16[192,896]{1,0:T(8,128)(2,1)S(1)}, bf16[192,896]{1,0:T(8,128)(2,1)S(1)}, u32[]{:S(2)}, u32[]{:S(2)}) collective-permute-start(bf16[192,896]{1,0:T(8,128)(2,1)S(1)} %get-tuple-element.86), channel_id=1, source_target_pairs={{0,2},{2,0},{1,3},{3,1},{4,6},{6,4},{5,7},{7,5},{8,10},{10,8},{9,1... | collective-permute-start | bytes 1032200 | tf_op jit(solution)/shard_map/ppermute | solution.py:28
  126.5 4.1 %collective-permute-start.31 = (bf16[192,512]{1,0:T(8,128)(2,1)S(1)}, bf16[192,512]{1,0:T(8,128)(2,1)S(1)}, u32[]{:S(2)}, u32[]{:S(2)}) collective-permute-start(bf16[192,512]{1,0:T(8,128)(2,1)S(1)} %collective-permute-done.29.refs_6_), channel_id=1, source_target_pairs={{0,4},{4,0},{8,12},{12,8},{16,20},{20,16},{24,28},{28,24},{1,5},{5... | collective-permute-start | bytes 589832 | tf_op jit(solution)/shard_map/ppermute | solution.py:28
  128.6 7.5 %collective-permute-start.39 = (bf16[192,512]{1,0:T(8,128)(2,1)S(1)}, bf16[192,512]{1,0:T(8,128)(2,1)S(1)}, u32[]{:S(2)}, u32[]{:S(2)}) collective-permute-start(bf16[192,512]{1,0:T(8,128)(2,1)S(1)} %get-tuple-element.84.refs_3_.refs_5_), channel_id=1, source_target_pairs={{0,1},{1,0},{2,3},{3,2},{4,5},{5,4},{6,7},{7,6},{8,9},{9,8},{10,11... | collective-permute-start | bytes 589832 | tf_op jit(solution)/shard_map/ppermute | solution.py:28
  130.1 8.1 %collective-permute-start.34 = (bf16[192,512]{1,0:T(8,128)(2,1)S(1)}, bf16[192,512]{1,0:T(8,128)(2,1)S(1)}, u32[]{:S(2)}, u32[]{:S(2)}) collective-permute-start(bf16[192,512]{1,0:T(8,128)(2,1)S(1)} %get-tuple-element.83.refs_2_.refs_5_), channel_id=1, source_target_pairs={{0,1},{1,0},{2,3},{3,2},{4,5},{5,4},{6,7},{7,6},{8,9},{9,8},{10,11... | collective-permute-start | bytes 589832 | tf_op jit(solution)/shard_map/ppermute | solution.py:28
  130.6 1.4 collective-permute-start.46
  130.6 13.7 %copy-start.11 = (bf16[1,192,896]{2,1,0:T(8,128)(2,1)S(1)}, bf16[1,192,896]{2,1,0:T(8,128)(2,1)}, u32[]{:S(2)}) copy-start(bf16[1,192,896]{2,1,0:T(8,128)(2,1)} %param.11) | copy-start | bytes 1032196
  132.1 13.6 %collective-permute-start.40 = (bf16[192,512]{1,0:T(8,128)(2,1)S(1)}, bf16[192,512]{1,0:T(8,128)(2,1)S(1)}, u32[]{:S(2)}, u32[]{:S(2)}) collective-permute-start(bf16[192,512]{1,0:T(8,128)(2,1)S(1)} %get-tuple-element.84.refs_3_.refs_5_), channel_id=1, source_target_pairs={{0,4},{4,0},{8,12},{12,8},{16,20},{20,16},{24,28},{28,24},{1,5},{5... | collective-permute-start | bytes 589832 | tf_op jit(solution)/shard_map/ppermute | solution.py:28
  136.0 12.9 %collective-permute-start.35 = (bf16[192,512]{1,0:T(8,128)(2,1)S(1)}, bf16[192,512]{1,0:T(8,128)(2,1)S(1)}, u32[]{:S(2)}, u32[]{:S(2)}) collective-permute-start(bf16[192,512]{1,0:T(8,128)(2,1)S(1)} %get-tuple-element.83.refs_2_.refs_5_), channel_id=1, source_target_pairs={{0,4},{4,0},{8,12},{12,8},{16,20},{20,16},{24,28},{28,24},{1,5},{5... | collective-permute-start | bytes 589832 | tf_op jit(solution)/shard_map/ppermute | solution.py:28
  138.1 7.5 %collective-permute-start.41 = (bf16[192,512]{1,0:T(8,128)(2,1)S(1)}, bf16[192,512]{1,0:T(8,128)(2,1)S(1)}, u32[]{:S(2)}, u32[]{:S(2)}) collective-permute-start(bf16[192,512]{1,0:T(8,128)(2,1)S(1)} %collective-permute-done.39.refs_6_), channel_id=1, source_target_pairs={{0,4},{4,0},{8,12},{12,8},{16,20},{20,16},{24,28},{28,24},{1,5},{5... | collective-permute-start | bytes 589832 | tf_op jit(solution)/shard_map/ppermute | solution.py:28
  138.2 10.8 %collective-permute-start.36 = (bf16[192,512]{1,0:T(8,128)(2,1)S(1)}, bf16[192,512]{1,0:T(8,128)(2,1)S(1)}, u32[]{:S(2)}, u32[]{:S(2)}) collective-permute-start(bf16[192,512]{1,0:T(8,128)(2,1)S(1)} %collective-permute-done.34.refs_6_), channel_id=1, source_target_pairs={{0,4},{4,0},{8,12},{12,8},{16,20},{20,16},{24,28},{28,24},{1,5},{5... | collective-permute-start | bytes 589832 | tf_op jit(solution)/shard_map/ppermute | solution.py:28
  142.3 8.5 %collective-permute-start.32 = (bf16[2,112,512]{2,1,0:T(8,128)(2,1)S(1)}, bf16[2,112,512]{2,1,0:T(8,128)(2,1)S(1)}, u32[]{:S(2)}, u32[]{:S(2)}) collective-permute-start(bf16[2,112,512]{2,1,0:T(8,128)(2,1)S(1)} %get-tuple-element.95), channel_id=1, source_target_pairs={{0,8},{4,12},{8,0},{12,4},{16,24},{20,28},{24,16},{28,20},{1,9},{5... | collective-permute-start | bytes 688136 | tf_op jit(solution)/shard_map/ppermute | solution.py:28
  145.6 12.5 %collective-permute-start.47 = (bf16[2,112,512]{2,1,0:T(8,128)(2,1)S(1)}, bf16[2,112,512]{2,1,0:T(8,128)(2,1)S(1)}, u32[]{:S(2)}, u32[]{:S(2)}) collective-permute-start(bf16[2,112,512]{2,1,0:T(8,128)(2,1)S(1)} %get-tuple-element.101), channel_id=1, source_target_pairs={{0,8},{4,12},{8,0},{12,4},{16,24},{20,28},{24,16},{28,20},{1,9},{5... | collective-permute-start | bytes 688136 | tf_op jit(solution)/shard_map/ppermute | solution.py:28
  146.8 18.7 %collective-permute-start.42 = (bf16[2,112,512]{2,1,0:T(8,128)(2,1)S(1)}, bf16[2,112,512]{2,1,0:T(8,128)(2,1)S(1)}, u32[]{:S(2)}, u32[]{:S(2)}) collective-permute-start(bf16[2,112,512]{2,1,0:T(8,128)(2,1)S(1)} %get-tuple-element.99), channel_id=1, source_target_pairs={{0,8},{4,12},{8,0},{12,4},{16,24},{20,28},{24,16},{28,20},{1,9},{5... | collective-permute-start | bytes 688136 | tf_op jit(solution)/shard_map/ppermute | solution.py:28
  150.1 20.2 %collective-permute-start.37 = (bf16[2,112,512]{2,1,0:T(8,128)(2,1)S(1)}, bf16[2,112,512]{2,1,0:T(8,128)(2,1)S(1)}, u32[]{:S(2)}, u32[]{:S(2)}) collective-permute-start(bf16[2,112,512]{2,1,0:T(8,128)(2,1)S(1)} %get-tuple-element.97), channel_id=1, source_target_pairs={{0,8},{4,12},{8,0},{12,4},{16,24},{20,28},{24,16},{28,20},{1,9},{5... | collective-permute-start | bytes 688136 | tf_op jit(solution)/shard_map/ppermute | solution.py:28
  150.9 19.6 %collective-permute-start.33 = (bf16[1,112,512]{2,1,0:T(8,128)(2,1)S(1)}, bf16[1,112,512]{2,1,0:T(8,128)(2,1)S(1)}, u32[]{:S(2)}, u32[]{:S(2)}) collective-permute-start(bf16[1,112,512]{2,1,0:T(8,128)(2,1)S(1)} %dynamic-slice_convert_fusion.3), channel_id=1, source_target_pairs={{0,16},{4,20},{8,24},{12,28},{16,0},{20,4},{24,8},{28,12},{1,17},{... | collective-permute-start | bytes 344072 | tf_op jit(solution)/shard_map/ppermute | solution.py:28
  158.3 12.3 %collective-permute-start.48 = (bf16[1,112,512]{2,1,0:T(8,128)(2,1)S(1)}, bf16[1,112,512]{2,1,0:T(8,128)(2,1)S(1)}, u32[]{:S(2)}, u32[]{:S(2)}) collective-permute-start(bf16[1,112,512]{2,1,0:T(8,128)(2,1)S(1)} %dynamic-slice_convert_fusion), channel_id=1, source_target_pairs={{0,16},{4,20},{8,24},{12,28},{16,0},{20,4},{24,8},{28,12},{1,17},{... | collective-permute-start | bytes 344072 | tf_op jit(solution)/shard_map/ppermute | solution.py:28
  165.6 13.1 %collective-permute-start.43 = (bf16[1,112,512]{2,1,0:T(8,128)(2,1)S(1)}, bf16[1,112,512]{2,1,0:T(8,128)(2,1)S(1)}, u32[]{:S(2)}, u32[]{:S(2)}) collective-permute-start(bf16[1,112,512]{2,1,0:T(8,128)(2,1)S(1)} %dynamic-slice_convert_fusion.1), channel_id=1, source_target_pairs={{0,16},{4,20},{8,24},{12,28},{16,0},{20,4},{24,8},{28,12},{1,17},{... | collective-permute-start | bytes 344072 | tf_op jit(solution)/shard_map/ppermute | solution.py:28
  170.4 9.8 %collective-permute-start.38 = (bf16[1,112,512]{2,1,0:T(8,128)(2,1)S(1)}, bf16[1,112,512]{2,1,0:T(8,128)(2,1)S(1)}, u32[]{:S(2)}, u32[]{:S(2)}) collective-permute-start(bf16[1,112,512]{2,1,0:T(8,128)(2,1)S(1)} %dynamic-slice_convert_fusion.2), channel_id=1, source_target_pairs={{0,16},{4,20},{8,24},{12,28},{16,0},{20,4},{24,8},{28,12},{1,17},{... | collective-permute-start | bytes 344072 | tf_op jit(solution)/shard_map/ppermute | solution.py:28
  (43 other events, 149.0 us)

commit v3 on v2

v3 whole, which is shorter than its diff:
```python
import functools
import math

import jax
import jax.numpy as jnp
from jax import lax
from jax.experimental import pallas as pl
from jax.experimental.pallas import tpu as pltpu
from jax.sharding import PartitionSpec as P

EPSILON = 1e-06
NEG_FILL = -1e30
GROUP_MOST = 96
FRAME_UP, FRAME_DOWN = 96, 125
NO_GROUP = 1 << 30
ATTENTION_MIB = 24
LANES = 128
BF = jnp.bfloat16
F32 = jnp.float32
ANY = pl.BlockSpec(memory_space=pl.ANY)
HBM = pl.BlockSpec(memory_space=pltpu.HBM)
VMEM = pl.BlockSpec(memory_space=pltpu.VMEM)
OVER_LAST = (((1,), (1,)), ((), ()))
OVER_FIRST = (((0,), (0,)), ((), ()))


def swap(value, axis, distance):
    count = lax.axis_size(axis)
    return lax.ppermute(value, axis, [(i, i ^ distance) for i in range(count)])


def unxor(pieces, place):
    pieces = list(pieces)
    for bit in range((len(pieces) - 1).bit_length()):
        odd = ((place >> bit) & 1) == 1
        pieces = [jnp.where(odd, pieces[j ^ (1 << bit)], pieces[j]) for j in range(len(pieces))]
    return pieces


def inv_rms(values):
    return lax.rsqrt(jnp.mean(values * values, axis=-1, keepdims=True) + EPSILON)


def norm_back(raw, gains, upstream):
    inv_norm = inv_rms(raw)
    inner_dot = jnp.mean(upstream * gains * raw, axis=-1, keepdims=True)
    return inv_norm * (gains * upstream - raw * inv_norm * inv_norm * inner_dot)


def round_up(value, step):
    return -(-value // step) * step


def head_place(heads):
    sharers = lax.axis_size("seq") // heads
    seq = lax.axis_index("seq")
    return seq // sharers, seq % sharers


def call(kernel, name, out, args, scratch, mib, flops, after=(), specs=None, copies=0):
    given, late = len(args), len(after)

    def body(*refs):
        kernel(*refs[:given], *refs[given + late :])

    scratch = [pltpu.VMEM(*s) for s in scratch]
    if copies:
        scratch.append(pltpu.SemaphoreType.DMA((copies,)))
    return list(
        pl.pallas_call(
            body,
            out_shape=[jax.ShapeDtypeStruct(*o) for o in out],
            in_specs=(specs or [VMEM] * given) + [ANY] * late,
            out_specs=[VMEM] * len(out),
            scratch_shapes=scratch,
            compiler_params=pltpu.CompilerParams(vmem_limit_bytes=mib << 20),
            cost_estimate=pl.CostEstimate(flops=flops, bytes_accessed=1 << 20, transcendentals=0),
            name=name,
        )(*args, *after)
    )


class Copies:
    def __init__(self, sems):
        self.sems, self.made = sems, []

    def start(self, source, target):
        copy = pltpu.make_async_copy(source, target, self.sems.at[len(self.made)])
        copy.start()
        self.made.append(copy)

    def wait(self):
        for copy in self.made:
            copy.wait()


def stage_kernel(count, *refs):
    copies = Copies(refs[-1])
    for source, target in zip(refs[:count], refs[count : 2 * count]):
        copies.start(source, target)
    copies.wait()


def columns_of(place, width):
    return pl.ds(pl.multiple_of(place * width, LANES), width)


def spread(pieces, target):
    place = lax.axis_index("mp")
    width = pieces[0].shape[-1]
    for t, piece in enumerate(pieces):
        if len(pieces) == 1:
            target[...] = piece[...]
        else:
            target[:, columns_of(place ^ t, width)] = piece[...]


def width_pieces(value):
    pieces = [value] + [swap(value, "mp", t) for t in range(1, lax.axis_size("mp"))]
    if value.shape[-1] % LANES:
        return [jnp.concatenate(unxor(pieces, lax.axis_index("mp")), axis=-1)]
    return pieces


def width_outs(rows, width, width_part):
    if width_part % LANES:
        return [((rows, width), F32)]
    others = width // width_part - 1
    return [((rows, width_part), F32)] + [((rows, width_part), BF)] * others


def write_width(source, refs):
    if len(refs) == 1:
        refs[0][...] = source[...]
        return
    place = lax.axis_index("mp")
    for t, ref in enumerate(refs):
        ref[...] = source[:, columns_of(place ^ t, ref.shape[-1])].astype(ref.dtype)


def width_sum(parts, width_part):
    place = lax.axis_index("mp")
    count = lax.axis_size("mp")
    if width_part % LANES:
        whole = parts[0]
        parts = [
            lax.dynamic_slice_in_dim(whole, (place ^ t) * width_part, width_part, 1)
            for t in range(count)
        ]
    total = parts[0]
    for t in range(1, count):
        total = total + swap(parts[t].astype(BF), "mp", t).astype(F32)
    return total


def project_kernel(heads, width_count, *refs):
    q_gain_ref, k_gain_ref, weight_ref, mod_ref = refs[:4]
    inputs = refs[4 : 4 + width_count]
    refs = refs[4 + width_count :]
    pieces = refs[:heads]
    hidden_ref, raw_ref, inv_ref, inputs_s, values_s = refs[heads:]
    spread(inputs, inputs_s)
    model_width = inputs_s.shape[1]
    values = inputs_s[...].astype(F32)
    inv_norm = inv_rms(values)
    inv_ref[...] = inv_norm
    scale = 1.0 + mod_ref[:, :model_width].astype(F32)
    hidden = (values * inv_norm * scale).astype(BF)
    hidden_ref[...] = hidden
    for at in range(2):
        raw_ref[at] = jnp.dot(hidden, weight_ref[at], preferred_element_type=F32)
    values_s[...] = jnp.dot(hidden, weight_ref[2], preferred_element_type=F32).astype(BF)
    dim = values_s.shape[1] // heads
    head, _ = head_place(heads)
    for t in range(heads):
        own = head ^ t
        columns = columns_of(own, dim)
        for at, gain_ref in enumerate((q_gain_ref, k_gain_ref)):
            raw = raw_ref[at, :, columns]
            pieces[t][at] = (raw * inv_rms(raw) * gain_ref[pl.ds(own, 1), :]).astype(BF)
        pieces[t][2] = values_s[:, columns]


def upstream_kernel(heads, width_count, *refs):
    weight_ref, mod_ref = refs[:2]
    upstream = refs[2 : 2 + width_count]
    refs = refs[2 + width_count :]
    pieces = refs[:heads]
    grad_ref, upstream_s, heads_s = refs[heads:]
    spread(upstream, upstream_s)
    model_width = upstream_s.shape[1]
    grad = (upstream_s[...].astype(F32) * mod_ref[:, model_width:].astype(F32)).astype(BF)
    grad_ref[...] = grad
    heads_s[...] = lax.dot_general(
        grad, weight_ref[...], OVER_LAST, preferred_element_type=F32
    ).astype(BF)
    dim = heads_s.shape[1] // heads
    head, _ = head_place(heads)
    for t in range(heads):
        pieces[t][...] = heads_s[:, columns_of(head ^ t, dim)]


def turn_kernel(blocks, clips, *refs):
    sources = refs[:2]
    pieces = refs[2 : 2 + 2 * clips]
    turned_s = refs[-1]
    span = turned_s.shape[-2]
    core, clip = lax.axis_index("seq") % 2, lax.axis_index("dp")
    for at, ref in enumerate(sources):
        turned = jnp.transpose(ref[...].astype(F32))
        for b in range(blocks * 2 * clips):
            rows = turned[b * span : (b + 1) * span]
            turned_s[at, b // (2 * clips), b % (2 * clips)] = rows.astype(BF)
        for u in range(2):
            for w in range(clips):
                own = (core ^ u) * clips + (clip ^ w)
                for b in range(blocks):
                    pieces[u * clips + w][at, b] = turned_s[at, b, own]


def attention_kernel(heads, sharers, rows, block, factor, *refs):
    key_group_ref, query_group_ref = refs[:2]
    at = 2
    own = refs[at : at + heads]
    at += heads
    shared = refs[at : at + heads * (sharers - 1)]
    at += heads * (sharers - 1)
    ups = refs[at : at + heads]
    at += heads
    outs = refs[at : at + heads]
    at += heads
    key_grads = refs[at : at + sharers]
    at += sharers
    key_s, value_s, query_s, up_s, out_s, dk_s, dv_s, sems = refs[at:]
    head, part = head_place(heads)
    dim = key_s.shape[-1]
    span = heads * sharers * rows
    total = heads * rows
    copies = Copies(sems)
    for t in range(heads):
        m = head ^ t
        for u in range(1, sharers):
            piece = shared[t * (sharers - 1) + u - 1]
            copies.start(piece.at[1], key_s.at[m * sharers + (part ^ u)])
            copies.start(piece.at[2], value_s.at[m * sharers + (part ^ u)])
        if t:
            copies.start(own[t].at[0], query_s.at[m])
            copies.start(own[t].at[1], key_s.at[m * sharers + part])
            copies.start(own[t].at[2], value_s.at[m * sharers + part])
            copies.start(ups[t], up_s.at[m])
    query_s[head] = own[0][0]
    key_s[head * sharers + part] = own[0][1]
    value_s[head * sharers + part] = own[0][2]
    up_s[head] = ups[0][...]
    dk_s[...] = jnp.zeros_like(dk_s)
    dv_s[...] = jnp.zeros_like(dv_s)
    group_col = jnp.transpose(jnp.broadcast_to(key_group_ref[...], (128, span)))
    group_col = jnp.concatenate([group_col] * (-(-block // 128)), axis=1)[:, :block]
    copies.wait()
    keys = key_s[...].reshape(span, dim)
    values = value_s[...].reshape(span, dim)
    queries = query_s[...].reshape(total, dim)
    upstream = up_s[...].reshape(total, dim)
    scale = factor * math.log2(math.e)
    for j in range(total // block):
        last = ((j + 1) * block - 1) // rows
        reach = min(span, round_up((last + 1) * sharers * rows + GROUP_MOST - 1, 128))
        lanes = slice(j * block, (j + 1) * block)
        query = queries[lanes]
        up = upstream[lanes]
        key = keys[:reach]
        value = values[:reach]
        logits = lax.dot_general(key, query, OVER_LAST, preferred_element_type=F32)
        logits = jnp.where(group_col[:reach] <= query_group_ref[:, lanes], logits, NEG_FILL)
        row_max = jnp.max(logits, axis=0, keepdims=True)
        unnorm = jnp.exp2((logits - row_max) * scale)
        inverse = 1.0 / jnp.sum(unnorm, axis=0, keepdims=True)
        out = lax.dot_general(value, unnorm.astype(BF), OVER_FIRST, preferred_element_type=F32)
        out = (out * inverse).astype(BF)
        up_t = jnp.transpose(up.astype(F32))
        out_dot = jnp.sum(up_t * out.astype(F32), axis=0, keepdims=True)
        probs = unnorm * inverse
        grad_probs = lax.dot_general(value, up, OVER_LAST, preferred_element_type=F32)
        grad_logits = (probs * (grad_probs - out_dot)).astype(BF)
        grad_query = lax.dot_general(key, grad_logits, OVER_FIRST, preferred_element_type=F32)
        out_s[0, lanes, :] = jnp.transpose(out.astype(F32)).astype(BF)
        out_s[1, lanes, :] = jnp.transpose(grad_query * factor).astype(BF)
        dk_s[:reach, :] += jnp.dot(grad_logits, query, preferred_element_type=F32)
        dv_s[:reach, :] += jnp.dot(probs.astype(BF), up, preferred_element_type=F32)
    for t in range(heads):
        m = head ^ t
        for u in range(sharers):
            there = pl.ds(pl.multiple_of((m * sharers + (part ^ u)) * rows, 64), rows)
            ref = key_grads[u]
            ref[t, 0] = (dk_s[there, :] * factor).astype(ref.dtype)
            ref[t, 1] = dv_s[there, :].astype(ref.dtype)
        here = pl.ds(pl.multiple_of(m * rows, 64), rows)
        outs[t][...] = out_s[:, here, :]


def attention_groups(part, group_ids, clip_length, heads, sharers):
    span = group_ids.shape[0]
    positions = lax.iota(jnp.int32, span)
    key_group = jnp.where(positions < clip_length, group_ids, NO_GROUP)[None, :]
    query_group = lax.dynamic_index_in_dim(
        group_ids.reshape(heads, sharers, span // (heads * sharers)), part, 1, keepdims=False
    ).reshape(1, span // sharers)
    return key_group, query_group


def attention(key_group, query_group, own, shared, ups, after):
    heads = len(own)
    sharers = len(shared) // heads + 1
    rows, width = ups[0].shape
    span = heads * sharers * rows
    total = heads * rows
    block = 256 if total % 256 == 0 else total
    pair = (2, rows, width)
    got = call(
        functools.partial(attention_kernel, heads, sharers, rows, block, width ** (-0.5)),
        "attention",
        [(pair, BF)] * heads + [((heads,) + pair, F32)] + [((heads,) + pair, BF)] * (sharers - 1),
        [key_group, query_group, *own, *shared, *ups],
        [
            ((heads * sharers, rows, width), BF),
            ((heads * sharers, rows, width), BF),
            ((heads, rows, width), BF),
            ((heads, rows, width), BF),
            ((2, total, width), BF),
            ((span, width), F32),
            ((span, width), F32),
        ],
        ATTENTION_MIB,
        12 * total * span * width,
        after,
        [VMEM] * 3
        + [HBM] * (heads - 1 + heads * (sharers - 1))
        + [VMEM]
        + [HBM] * (heads - 1),
        2 * heads * (sharers - 1) + 4 * (heads - 1),
    )
    return got[:heads], got[heads:]


def share_kernel(sharers, *refs):
    terms, sums = refs[:sharers], refs[sharers:]
    for t, ref in enumerate(sums):
        total = terms[0][t]
        for u in range(1, sharers):
            total = total + terms[u][t].astype(F32)
        ref[...] = total.astype(BF)


def query_kernel(heads, *refs):
    gain_ref, raw_ref = refs[:2]
    pieces, (rows_ref, grad_ref) = refs[2 : 2 + heads], refs[2 + heads :]
    inner = raw_ref.shape[-1]
    dim = inner // heads
    head, _ = head_place(heads)
    for t in range(heads):
        own = head ^ t
        rows_ref[:, columns_of(own, dim)] = pieces[t][0]
        grad = norm_back(
            raw_ref[0, :, columns_of(own, dim)],
            gain_ref[pl.ds(own, 1), :],
            pieces[t][1].astype(F32),
        )
        grad_ref[:, columns_of(own, dim)] = grad.astype(BF)


def key_kernel(heads, *refs):
    gain_ref, raw_ref = refs[:2]
    pieces, (key_ref, value_ref) = refs[2 : 2 + heads], refs[2 + heads :]
    inner = raw_ref.shape[-1]
    dim = inner // heads
    head, _ = head_place(heads)
    for t in range(heads):
        own = head ^ t
        grad = norm_back(
            raw_ref[1, :, columns_of(own, dim)],
            gain_ref[pl.ds(own, 1), :],
            pieces[t][0].astype(F32),
        )
        key_ref[:, columns_of(own, dim)] = grad.astype(BF)
        value_ref[:, columns_of(own, dim)] = pieces[t][1]


def mix_kernel(rows_ref, weight_ref, *refs):
    whole_s = refs[-1]
    whole_s[...] = jnp.dot(rows_ref[...], weight_ref[...], preferred_element_type=F32)
    write_width(whole_s, refs[:-1])


def hidden_kernel(width_count, *refs):
    grads, (weight_ref, mod_ref, inv_ref) = refs[:3], refs[3:6]
    inputs = refs[6 : 6 + width_count]
    dot_ref = refs[6 + width_count]
    outs = refs[7 + width_count : -2]
    whole_s, inputs_s = refs[-2:]
    spread(inputs, inputs_s)
    total = 0.0
    for at, grad in enumerate(grads):
        total = total + lax.dot_general(
            grad[...], weight_ref[at], OVER_LAST, preferred_element_type=F32
        )
    whole_s[...] = total
    write_width(whole_s, outs)
    model_width = inputs_s.shape[1]
    scale = 1.0 + mod_ref[:, :model_width].astype(F32)
    normed = inputs_s[...].astype(F32) * inv_ref[...]
    dot = jnp.sum(whole_s[...] * scale * normed, axis=1, keepdims=True)
    turned = jnp.transpose(jnp.broadcast_to(dot, (dot.shape[0], LANES)))
    dot_ref[...] = turned[:8]


def halve(total, step, send_ref, keep_ref):
    odd = (lax.axis_index("seq") // step) % 2 == 1
    for b in range(total.shape[0] // 2):
        first, second = total[2 * b], total[2 * b + 1]
        keep_ref[b] = jnp.where(odd, second, first)
        send_ref[b] = jnp.where(odd, first, second).astype(BF)


def outer_kernel(which, *refs):
    count = (len(refs) - 2) // 2
    lefts, rights = refs[:count], refs[count : 2 * count]
    _, blocks, span, rows = lefts[0].shape
    total = 0.0
    for left, right in zip(lefts, rights):
        total = total + jnp.dot(
            left[which].reshape(blocks * span, rows), right[...], preferred_element_type=F32
        )
    halve(total.reshape(blocks, span, total.shape[1]), 2, *refs[2 * count :])


def step_kernel(step, got_ref, kept_ref, send_ref, keep_ref):
    halve(kept_ref[...] + got_ref[...].astype(F32), step, send_ref, keep_ref)


def halves(blocks, span, width):
    return [((blocks // 2, span, width), BF), ((blocks // 2, span, width), F32)]


class WeightSum:
    def __init__(self, lefts, which, right):
        rights = [right] + [swap(right, "dp", w) for w in range(1, lax.axis_size("dp"))]
        self.rights = rights + [swap(far, "seq", 1) for far in rights]
        self.lefts, self.which, self.step = lefts, which, 2

    def outer(self, after):
        _, blocks, span, rows = self.lefts[0].shape
        width = self.rights[0].shape[1]
        self.send, self.keep = call(
            functools.partial(outer_kernel, self.which),
            "weight_sum",
            halves(blocks, span, width),
            [*self.lefts, *self.rights],
            [],
            8,
            2 * blocks * span * rows * width * len(self.lefts),
            after,
        )
        return [self.send]

    def exchange(self):
        self.got = swap(self.send, "seq", self.step)
        self.step *= 2

    def halve(self, after):
        self.send, self.keep = call(
            functools.partial(step_kernel, self.step),
            "weight_step",
            halves(*self.keep.shape),
            [self.got, self.keep],
            [],
            4,
            1 << 22,
            after,
        )
        return [self.send]


def total_kernel(*refs):
    out_ref, in_ref = refs[-1], refs[-2]
    targets = (out_ref, in_ref.at[0], in_ref.at[1], in_ref.at[2])
    for at, target in enumerate(targets):
        target[...] = refs[2 * at][0].astype(F32) + refs[2 * at + 1][0]


def on_device(
    latents, grad_out, sync_mod, w_qkv, w_out, q_gain, k_gain, frame_of, group_id, clip_len
):
    latents, grad_out, sync_mod = latents[0], grad_out[0], sync_mod[0]
    frame_of, group_id, clip_len = frame_of[0], group_id[0], clip_len[0]
    rows, width_part = latents.shape
    frame_count = sync_mod.shape[0]
    model_width = sync_mod.shape[1] // 2
    heads, head_dim = q_gain.shape
    inner = heads * head_dim
    count, clips = lax.axis_size("seq"), lax.axis_size("dp")
    sharers = count // heads
    seq = lax.axis_index("seq")
    _, part = head_place(heads)
    model_place = lax.axis_index("mp")

    inputs = width_pieces(latents)
    upstream = width_pieces(grad_out)
    width_count = len(inputs)

    back = max(frame_count * j - (FRAME_UP * rows * j) // FRAME_DOWN for j in range(count))
    back = min(frame_count, round_up(max(back, 1), 16))
    earlier = lax.ppermute(
        sync_mod[frame_count - back :], "seq", [(i, i + 1) for i in range(count - 1)]
    )
    window = jnp.concatenate([earlier, sync_mod], axis=0)
    local_frame = frame_of - (seq * frame_count - back)
    selector = (
        local_frame[:, None] == lax.iota(jnp.int32, frame_count + back)[None, :]
    ).astype(BF)
    mod = jnp.dot(selector, window, preferred_element_type=F32).astype(BF)

    key_group, query_group = attention_groups(part, group_id, clip_len, heads, sharers)
    weight = jnp.transpose(w_qkv, (1, 0, 2))
    staged = [weight, w_out, key_group, query_group]
    weight, w_out, key_group, query_group = call(
        functools.partial(stage_kernel, len(staged)),
        "stage",
        [(array.shape, array.dtype) for array in staged],
        staged,
        [],
        2,
        1 << 22,
        [mod],
        [HBM, HBM, VMEM, VMEM],
        len(staged),
    )
    got = call(
        functools.partial(project_kernel, heads, width_count),
        "project",
        [((3, rows, head_dim), BF)] * heads
        + [((rows, model_width), BF), ((2, rows, inner), F32), ((rows, 1), F32)],
        [q_gain, k_gain, weight, mod, *inputs],
        [((rows, model_width), BF), ((rows, inner), BF)],
        8,
        6 * rows * model_width * inner,
    )
    own, (hidden, raw, inv_norm) = got[:heads], got[heads:]
    own = [own[0]] + [swap(own[t], "seq", t * sharers) for t in range(1, heads)]
    shared = [swap(own[t], "seq", u) for t in range(heads) for u in range(1, sharers)]

    got = call(
        functools.partial(upstream_kernel, heads, width_count),
        "upstream",
        [((rows, head_dim), BF)] * heads + [((rows, model_width), BF)],
        [w_out, mod, *upstream],
        [((rows, model_width), BF), ((rows, inner), BF)],
        8,
        2 * rows * model_width * inner,
    )
    ups, grad_attn = got[:heads], got[heads]
    ups = [ups[0]] + [swap(ups[t], "seq", t * sharers) for t in range(1, heads)]

    blocks = count // 2
    span = model_width // (count * clips)
    lefts = call(
        functools.partial(turn_kernel, blocks, clips),
        "turn",
        [((2, blocks, span, rows), BF)] * (2 * clips),
        [hidden, grad_attn],
        [((2, blocks, 2 * clips, span, rows), BF)],
        8,
        1 << 28,
    )
    for u in range(2):
        for w in range(clips):
            if u or w:
                pairs = [
                    (s * clips + x, (s ^ u) * clips + (x ^ w))
                    for s in range(count)
                    for x in range(clips)
                ]
                lefts[u * clips + w] = lax.ppermute(lefts[u * clips + w], ("seq", "dp"), pairs)

    outs, key_grads = attention(key_group, query_group, own, shared, ups, lefts[:1])
    back_out = [outs[0]] + [swap(outs[t], "seq", t * sharers) for t in range(1, heads)]
    terms = key_grads[:1] + [swap(key_grads[u], "seq", u) for u in range(1, sharers)]
    pair = (2, rows, head_dim)
    sums = call(
        functools.partial(share_kernel, sharers),
        "share",
        [(pair, BF)] * heads,
        terms,
        [],
        4,
        1 << 24,
    )
    back_key = [sums[0]] + [swap(sums[t], "seq", t * sharers) for t in range(1, heads)]
    out_rows, grad_query = call(
        functools.partial(query_kernel, heads),
        "query_back",
        [((rows, inner), BF)] * 2,
        [q_gain, raw, *back_out],
        [],
        4,
        1 << 24,
        sums[:1],
    )
    sum_out = WeightSum(lefts, 1, out_rows)
    sum_query = WeightSum(lefts, 0, grad_query)
    parts = call(
        mix_kernel,
        "mix",
        width_outs(rows, model_width, width_part),
        [out_rows, w_out],
        [((rows, model_width), F32)],
        8,
        2 * rows * model_width * inner,
    )
    grad_key, grad_value = call(
        functools.partial(key_kernel, heads),
        "key_back",
        [((rows, inner), BF)] * 2,
        [k_gain, raw, *back_key],
        [],
        4,
        1 << 24,
        parts[:1],
    )
    sum_key = WeightSum(lefts, 0, grad_key)
    sum_value = WeightSum(lefts, 0, grad_value)
    token = sum_out.outer([grad_key])
    got = call(
        functools.partial(hidden_kernel, width_count),
        "hidden_back",
        [((8, rows), F32)] + width_outs(rows, model_width, width_part),
        [grad_query, grad_key, grad_value, weight, mod, inv_norm, *inputs],
        [((rows, model_width), F32), ((rows, model_width), BF)],
        8,
        6 * rows * model_width * inner,
        token,
    )
    part_dot, hidden_parts = got[0], got[1:]
    sum_out.exchange()
    token = sum_query.outer([part_dot])
    sum_query.exchange()
    token = sum_key.outer(token)
    sum_key.exchange()
    sums = [sum_out, sum_query, sum_key, sum_value]
    while sum_out.keep.shape[0] > 1:
        for at, total in enumerate(sums):
            token = total.halve(token)
            total.exchange()
            if at == 0 and sum_value.step == 2:
                token = sum_value.outer(token)
                sum_value.exchange()
    pieces = []
    for total in sums:
        pieces.extend([total.got, total.keep])
    grad_wqkv, grad_wout = call(
        total_kernel,
        "weight_total",
        [((3, span, inner), F32), ((span, inner), F32)],
        pieces,
        [],
        4,
        1 << 22,
    )

    attn_mine = width_sum(parts, width_part)
    gate_mine = lax.dynamic_slice_in_dim(
        mod, model_width + model_place * width_part, width_part, 1
    )
    mixed = (latents.astype(F32) + gate_mine.astype(F32) * attn_mine).astype(BF)

    full_dot = part_dot
    for t in range(1, lax.axis_size("mp")):
        full_dot = full_dot + swap(part_dot, "mp", t)
    grad_mine = width_sum(hidden_parts, width_part)
    scale_mine = lax.dynamic_slice_in_dim(mod, model_place * width_part, width_part, 1)
    normed_mine = latents.astype(F32) * inv_norm
    grad_normed = grad_mine * (1.0 + scale_mine.astype(F32))
    inner_mean = full_dot[0][:, None] / model_width
    grad_inputs = inv_norm * (grad_normed - normed_mine * inner_mean)
    grad_latents = (grad_out.astype(F32) + grad_inputs).astype(BF)

    return (
        mixed[None],
        grad_latents[None],
        jnp.transpose(grad_wqkv, (1, 0, 2)),
        jnp.transpose(grad_wout),
    )


def solution(mesh):
    in_specs = (
        P("dp", "seq", "mp"),
        P("dp", "seq", "mp"),
        P("dp", "seq", None),
        P(None, None, "mp"),
        P("mp", None),
        P("mp", None),
        P("mp", None),
        P("dp", "seq"),
        P("dp", None),
        P("dp"),
    )
    out_specs = (
        P("dp", "seq", "mp"),
        P("dp", "seq", "mp"),
        P(("seq", "dp"), None, "mp"),
        P("mp", ("seq", "dp")),
    )
    return jax.shard_map(
        on_device, mesh=mesh, in_specs=in_specs, out_specs=out_specs, check_vma=False
    )
```

time: 182 us -> 154 us (0.85)
  local copies, waits for them, and re-layouts: 43.5 us -> 8.49 us
  waiting for transfers between devices: 49.7 us -> 63.5 us
  Pallas kernels: 34.2 us -> 25.1 us
  other arithmetic: 4.05 us -> 6.33 us
    unnamed x117 -> x34, local copies, waits for them, and re-layouts: 26.6 us -> 7.28 us
    ppermute x3, waiting for transfers between devices: 0.01 us -> 9.24 us  [on_device(): lax.ppermute(lefts[u * clips + w], ('seq', 'dp'), pairs)]
    pallas_call x13 -> x19, Pallas kernels: 34.2 us -> 25.1 us  [call(): pl.pallas_call(body, out_shape=[jax.ShapeDtypeStruct(*o) for o in out], i...]
    reshape x2 -> x1, local copies, waits for them, and re-layouts: 8.47 us -> 0.09 us  [attention_groups(): query_group = lax.dynamic_index_in_dim(group_ids.reshape(heads, sharers,...]
    ppermute x45 -> x42, waiting for transfers between devices: 49.7 us -> 54.2 us  [swap(): return lax.ppermute(value, axis, [(i, i ^ distance) for i in range(count)])]
    squeeze x4 -> x0, local copies, waits for them, and re-layouts: 3.95 us -> none  [on_device(): left_grad = [left[1] for left in lefts]]
    slice x4 -> x0, local copies, waits for them, and re-layouts: 2.58 us -> none  [on_device(): own[t][1:]]
    ppermute x45 -> x42, starting transfers between devices: 41.1 us -> 41.9 us  [swap(): return lax.ppermute(value, axis, [(i, i ^ distance) for i in range(count)])]
  transfers between devices with their start and end apart: 49 -> 46, of which waited for: 17 -> 18; matrix products, arithmetic and copies ran while one was open for 15% -> 6% of each run, Pallas kernels for 13% -> 11%
where the time goes in v3:
time: 154 us; the launch traced here: 153 us
  waiting for transfers between devices  63.5 us (41%)
  starting transfers between devices  46.4 us (30%)
  Pallas kernels  25.1 us (16%)
  local copies, waits for them, and re-layouts  8.49 us (6%)
  other arithmetic  6.33 us (4%)
  matrix products  1.94 us (1%)
  between operations  1.54 us (1%)
    ppermute x42, waiting for transfers between devices, swap(): return lax.ppermute(value, axis, [(i, i ^ distance) for i in range(count)])  54.2 us
    ppermute x42, starting transfers between devices, swap(): return lax.ppermute(value, axis, [(i, i ^ distance) for i in range(count)])  41.9 us
    pallas_call x19, Pallas kernels, call(): pl.pallas_call(body, out_shape=[jax.ShapeDtypeStruct(*o) for o in out], i...  25.1 us
    ppermute x3, waiting for transfers between devices, on_device(): lax.ppermute(lefts[u * clips + w], ('seq', 'dp'), pairs)  9.24 us
    unnamed x34, local copies, waits for them, and re-layouts  7.28 us
  transfers between devices with their start and end apart: 46, of which 18 were waited for; matrix products, arithmetic and copies ran while one was open for 6% of the time, Pallas kernels for 11%

profile of v3, /device:TPU:0, one launch (start us, length us, event | category | flops | bytes accessed | tf_op | source)
XLA Modules:
  0.0 153.2 jit_solution(5717725593702483807)
XLA Ops:
  0.6 1.0 slice_bitcast_fusion
  1.7 2.4 %collective-permute-start = (bf16[32,3584]{1,0:T(8,128)(2,1)S(1)}, bf16[32,3584]{1,0:T(8,128)(2,1)S(1)}, u32[]{:S(2)}, u32[]{:S(2)}) collective-permute-start(bf16[32,3584]{1,0:T(8,128)(2,1)S(1)} %slice_bitcast_fusion), channel_id=1, source_target_pairs={{0,4},{4,8},{8,12},{12,16},{16,20},{20,24},{24,28},{1,5},{5,9},{9,... | collective-permute-start | bytes 688136 | tf_op jit(solution)/shard_map/ppermute | solution.py:512
  4.0 2.4 %collective-permute-start.9 = (bf16[192,896]{1,0:T(8,128)(2,1)}, bf16[192,896]{1,0:T(8,128)(2,1)S(1)}, u32[]{:S(2)}, u32[]{:S(2)}) collective-permute-start(bf16[192,896]{1,0:T(8,128)(2,1)} %bitcast.23), channel_id=1, source_target_pairs={{0,2},{2,0},{1,3},{3,1},{4,6},{6,4},{5,7},{7,5},{8,10},{10,8},{9,1... | collective-permute-start | bytes 1032200 | tf_op jit(solution)/shard_map/ppermute | solution.py:29
  7.2 0.7 fusion.14
  8.8 1.9 %convolution_convert_fusion.refs_4_.refs_3_.refs_1_ = bf16[192,3584]{1,0:T(8,128)(2,1)S(1)} fusion(bf16[150,3584]{1,0:T(8,128)(2,1)} %bitcast.25, bf16[32,3584]{1,0:T(8,128)(2,1)S(1)} %collective-permute-done, s32[192]{0:T(256)S(1)} %bitcast.27), kind=kOutput, calls=%fused_computation | convolution fusion | flops 253810816 | bytes 2681600 | tf_op jit(solution)/shard_map/dot_general | solution.py:520
  10.8 2.6 %copy-done = bf16[1792,3,512]{2,0,1:T(8,128)(2,1)S(1)} copy-done((bf16[1792,3,512]{2,0,1:T(8,128)(2,1)S(1)}, bf16[1792,3,512]{2,0,1:T(8,128)(2,1)}, u32[]{:S(2)}) %copy-start) | copy-done | bytes 5505048
  13.9 7.9 %collective-permute-done.1.refs_5_.refs_7_ = bf16[192,896]{1,0:T(8,128)(2,1)S(1)} collective-permute-done((bf16[192,896]{1,0:T(8,128)(2,1)}, bf16[192,896]{1,0:T(8,128)(2,1)S(1)}, u32[]{:S(2)}, u32[]{:S(2)}) %collective-permute-start.1) | collective-permute-done | bytes 344096 | tf_op jit(solution)/shard_map/ppermute | solution.py:29
  21.8 1.5 %project.1 = (bf16[3,192,128]{2,1,0:T(8,128)(2,1)S(1)}, bf16[3,192,128]{2,1,0:T(8,128)(2,1)S(1)}, bf16[3,192,128]{2,1,0:T(8,128)(2,1)S(1)}, bf16[3,192,128]{2,1,...) custom-call(f32[4,128]{1,0:T(4,128)S(1)} %copy-done.13, ...), custom_call_target="tpu_custom_call" | custom-call | flops 1056964608 | bytes 1048576 | tf_op jit(solution)/shard_map/project/pallas_call | solution.py:70
  23.3 2.9 %collective-permute-start.2 = (bf16[3,192,128]{2,1,0:T(8,128)(2,1)S(1)}, bf16[3,192,128]{2,1,0:T(8,128)(2,1)S(1)}, u32[]{:S(2)}, u32[]{:S(2)}) collective-permute-start(bf16[3,192,128]{2,1,0:T(8,128)(2,1)S(1)} %get-tuple-element.66), channel_id=1, source_target_pairs={{0,8},{4,12},{8,0},{12,4},{16,24},{20,28},{24,16},{28,20},{1,9},{5... | collective-permute-start | bytes 442376 | tf_op jit(solution)/shard_map/ppermute | solution.py:29
  26.2 1.5 collective-permute-start.3
  27.7 1.0 collective-permute-start.4
  28.7 0.8 upstream.1
  29.5 1.1 collective-permute-start.10
  30.6 3.1 %collective-permute-done.2.refs_3_ = bf16[3,192,128]{2,1,0:T(8,128)(2,1)S(1)} collective-permute-done((bf16[3,192,128]{2,1,0:T(8,128)(2,1)S(1)}, bf16[3,192,128]{2,1,0:T(8,128)(2,1)S(1)}, u32[]{:S(2)}, u32[]{:S(2)}) %collective-permute-start.2) | collective-permute-done | bytes 147488 | tf_op jit(solution)/shard_map/ppermute | solution.py:29
  33.6 6.5 %collective-permute-done.3.refs_4_ = bf16[3,192,128]{2,1,0:T(8,128)(2,1)S(1)} collective-permute-done((bf16[3,192,128]{2,1,0:T(8,128)(2,1)S(1)}, bf16[3,192,128]{2,1,0:T(8,128)(2,1)S(1)}, u32[]{:S(2)}, u32[]{:S(2)}) %collective-permute-start.3) | collective-permute-done | bytes 147488 | tf_op jit(solution)/shard_map/ppermute | solution.py:29
  40.6 3.5 %collective-permute-start.11 = (bf16[192,128]{1,0:T(8,128)(2,1)S(1)}, bf16[192,128]{1,0:T(8,128)(2,1)S(1)}, u32[]{:S(2)}, u32[]{:S(2)}) collective-permute-start(bf16[192,128]{1,0:T(8,128)(2,1)S(1)} %get-tuple-element.72), channel_id=1, source_target_pairs={{0,16},{4,20},{8,24},{12,28},{16,0},{20,4},{24,8},{28,12},{1,17},{... | collective-permute-start | bytes 147464 | tf_op jit(solution)/shard_map/ppermute | solution.py:29
  44.1 2.4 %collective-permute-done.11.refs_12_ = bf16[192,128]{1,0:T(8,128)(2,1)S(1)} collective-permute-done((bf16[192,128]{1,0:T(8,128)(2,1)S(1)}, bf16[192,128]{1,0:T(8,128)(2,1)S(1)}, u32[]{:S(2)}, u32[]{:S(2)}) %collective-permute-start.11) | collective-permute-done | bytes 49184 | tf_op jit(solution)/shard_map/ppermute | solution.py:29
  46.6 1.6 %collective-permute-start.12 = (bf16[192,128]{1,0:T(8,128)(2,1)S(1)}, bf16[192,128]{1,0:T(8,128)(2,1)S(1)}, u32[]{:S(2)}, u32[]{:S(2)}) collective-permute-start(bf16[192,128]{1,0:T(8,128)(2,1)S(1)} %get-tuple-element.73), channel_id=1, source_target_pairs={{0,24},{4,28},{8,16},{12,20},{16,8},{20,12},{24,0},{28,4},{1,25},{... | collective-permute-start | bytes 147464 | tf_op jit(solution)/shard_map/ppermute | solution.py:29
  48.8 3.7 %collective-permute-done.12.refs_13_ = bf16[192,128]{1,0:T(8,128)(2,1)S(1)} collective-permute-done((bf16[192,128]{1,0:T(8,128)(2,1)S(1)}, bf16[192,128]{1,0:T(8,128)(2,1)S(1)}, u32[]{:S(2)}, u32[]{:S(2)}) %collective-permute-start.12) | collective-permute-done | bytes 49184 | tf_op jit(solution)/shard_map/ppermute | solution.py:29
  52.5 7.2 %attention.1 = (bf16[2,192,128]{2,1,0:T(8,128)(2,1)S(1)}, bf16[2,192,128]{2,1,0:T(8,128)(2,1)S(1)}, bf16[2,192,128]{2,1,0:T(8,128)(2,1)S(1)}, bf16[2,192,128]{2,...) custom-call(s32[1,1536]{1,0:T(1,128)S(1)} %get-tuple-element.63.refs_0_, ...), custom_call_target="tpu_custom_call" | custom-call | flops 1811939328 | bytes 1048576 | tf_op jit(solution)/shard_map/attention/pallas_call | solution.py:70
  59.8 1.6 %collective-permute-start.21 = (bf16[2,4,112,192]{3,2,1,0:T(8,128)(2,1)S(1)}, bf16[2,4,112,192]{3,2,1,0:T(8,128)(2,1)S(1)}, u32[]{:S(2)}, u32[]{:S(2)}) collective-permute-start(bf16[2,4,112,192]{3,2,1,0:T(8,128)(2,1)S(1)} %get-tuple-element.94), channel_id=1, source_target_pairs={{0,1},{1,0},{4,5},{5,4},{8,9},{9,8},{12,13},{13,12},{16,17},{17,16... | collective-permute-start | bytes 1032200 | tf_op jit(solution)/shard_map/ppermute | solution.py:582
  61.5 2.0 %collective-permute-start.14 = (bf16[2,192,128]{2,1,0:T(8,128)(2,1)S(1)}, bf16[2,192,128]{2,1,0:T(8,128)(2,1)S(1)}, u32[]{:S(2)}, u32[]{:S(2)}) collective-permute-start(bf16[2,192,128]{2,1,0:T(8,128)(2,1)S(1)} %get-tuple-element.79), channel_id=1, source_target_pairs={{0,16},{4,20},{8,24},{12,28},{16,0},{20,4},{24,8},{28,12},{1,17},{... | collective-permute-start | bytes 294920 | tf_op jit(solution)/shard_map/ppermute | solution.py:29
  63.5 9.2 %collective-permute-done.21.refs_1_ = bf16[2,4,112,192]{3,2,1,0:T(8,128)(2,1)S(1)} collective-permute-done((bf16[2,4,112,192]{3,2,1,0:T(8,128)(2,1)S(1)}, bf16[2,4,112,192]{3,2,1,0:T(8,128)(2,1)S(1)}, u32[]{:S(2)}, u32[]{:S(2)}) %collective-permute-start.21) | collective-permute-done | bytes 344096 | tf_op jit(solution)/shard_map/ppermute | solution.py:582
  72.7 1.6 %collective-permute-start.15 = (bf16[2,192,128]{2,1,0:T(8,128)(2,1)S(1)}, bf16[2,192,128]{2,1,0:T(8,128)(2,1)S(1)}, u32[]{:S(2)}, u32[]{:S(2)}) collective-permute-start(bf16[2,192,128]{2,1,0:T(8,128)(2,1)S(1)} %get-tuple-element.80), channel_id=1, source_target_pairs={{0,24},{4,28},{8,16},{12,20},{16,8},{20,12},{24,0},{28,4},{1,25},{... | collective-permute-start | bytes 294920 | tf_op jit(solution)/shard_map/ppermute | solution.py:29
  75.1 2.6 %collective-permute-start.19 = (bf16[2,192,128]{2,1,0:T(8,128)(2,1)S(1)}, bf16[2,192,128]{2,1,0:T(8,128)(2,1)S(1)}, u32[]{:S(2)}, u32[]{:S(2)}) collective-permute-start(bf16[2,192,128]{2,1,0:T(8,128)(2,1)S(1)} %get-tuple-element.90), channel_id=1, source_target_pairs={{0,16},{4,20},{8,24},{12,28},{16,0},{20,4},{24,8},{28,12},{1,17},{... | collective-permute-start | bytes 294920 | tf_op jit(solution)/shard_map/ppermute | solution.py:29
  77.7 1.5 collective-permute-done.15.refs_5_
  79.2 1.6 %collective-permute-start.20 = (bf16[2,192,128]{2,1,0:T(8,128)(2,1)S(1)}, bf16[2,192,128]{2,1,0:T(8,128)(2,1)S(1)}, u32[]{:S(2)}, u32[]{:S(2)}) collective-permute-start(bf16[2,192,128]{2,1,0:T(8,128)(2,1)S(1)} %get-tuple-element.91), channel_id=1, source_target_pairs={{0,24},{4,28},{8,16},{12,20},{16,8},{20,12},{24,0},{28,4},{1,25},{... | collective-permute-start | bytes 294920 | tf_op jit(solution)/shard_map/ppermute | solution.py:29
  81.1 1.9 %collective-permute-done.18.refs_3_ = bf16[2,192,128]{2,1,0:T(8,128)(2,1)S(1)} collective-permute-done((bf16[2,192,128]{2,1,0:T(8,128)(2,1)S(1)}, bf16[2,192,128]{2,1,0:T(8,128)(2,1)S(1)}, u32[]{:S(2)}, u32[]{:S(2)}) %collective-permute-start.18) | collective-permute-done | bytes 98336 | tf_op jit(solution)/shard_map/ppermute | solution.py:29
  83.0 1.8 %collective-permute-start.24 = (bf16[192,512]{1,0:T(8,128)(2,1)S(1)}, bf16[192,512]{1,0:T(8,128)(2,1)S(1)}, u32[]{:S(2)}, u32[]{:S(2)}) collective-permute-start(bf16[192,512]{1,0:T(8,128)(2,1)S(1)} %get-tuple-element.84.refs_0_.refs_4_), channel_id=1, source_target_pairs={{0,1},{1,0},{2,3},{3,2},{4,5},{5,4},{6,7},{7,6},{8,9},{9,8},{10,11... | collective-permute-start | bytes 589832 | tf_op jit(solution)/shard_map/ppermute | solution.py:29
  84.9 0.9 collective-permute-done.19.refs_4_
  85.9 2.2 %collective-permute-start.33 = (bf16[192,512]{1,0:T(8,128)(2,1)S(1)}, bf16[192,512]{1,0:T(8,128)(2,1)S(1)}, u32[]{:S(2)}, u32[]{:S(2)}) collective-permute-start(bf16[192,512]{1,0:T(8,128)(2,1)S(1)} %get-tuple-element.88.refs_0_.refs_4_), channel_id=1, source_target_pairs={{0,1},{1,0},{2,3},{3,2},{4,5},{5,4},{6,7},{7,6},{8,9},{9,8},{10,11... | collective-permute-start | bytes 589832 | tf_op jit(solution)/shard_map/ppermute | solution.py:29
  88.1 1.4 mix.1
  89.9 1.5 collective-permute-done.24.refs_5_
  92.0 3.6 %collective-permute-done.33.refs_5_ = bf16[192,512]{1,0:T(8,128)(2,1)S(1)} collective-permute-done((bf16[192,512]{1,0:T(8,128)(2,1)S(1)}, bf16[192,512]{1,0:T(8,128)(2,1)S(1)}, u32[]{:S(2)}, u32[]{:S(2)}) %collective-permute-start.33) | collective-permute-done | bytes 196640 | tf_op jit(solution)/shard_map/ppermute | solution.py:29
  95.6 1.3 collective-permute-start.38
  96.9 2.9 %collective-permute-done.30.refs_5_ = bf16[192,512]{1,0:T(8,128)(2,1)S(1)} collective-permute-done((bf16[192,512]{1,0:T(8,128)(2,1)S(1)}, bf16[192,512]{1,0:T(8,128)(2,1)S(1)}, u32[]{:S(2)}, u32[]{:S(2)}) %collective-permute-start.30) | collective-permute-done | bytes 196640 | tf_op jit(solution)/shard_map/ppermute | solution.py:29
  101.0 0.8 collective-permute-start.29
  101.7 2.2 %collective-permute-done.38.refs_5_ = bf16[192,512]{1,0:T(8,128)(2,1)S(1)} collective-permute-done((bf16[192,512]{1,0:T(8,128)(2,1)S(1)}, bf16[192,512]{1,0:T(8,128)(2,1)S(1)}, u32[]{:S(2)}, u32[]{:S(2)}) %collective-permute-start.38) | collective-permute-done | bytes 196640 | tf_op jit(solution)/shard_map/ppermute | solution.py:29
  104.1 3.0 %hidden_back.1 = (f32[8,192]{1,0:T(8,128)S(1)}, f32[192,896]{1,0:T(8,128)S(1)}, bf16[192,896]{1,0:T(8,128)(2,1)}) custom-call(bf16[192,512]{1,0:T(8,128)(2,1)S(1)} %get-tuple-element.88.refs_0_.refs_4_, bf16[192,512]{1,0:T(8,128)(2,1)S(1)} %get-tuple-element.92.refs_8_.refs_1_.refs_4_, bf16[192,512]{1,0:T(8,128)(2,1)S(1)} %get-tuple-element.93.refs_2_.refs_4_, ...), custom_call_target="tpu_custom_call" | custom-call | flops 1056964608 | bytes 1048576 | tf_op jit(solution)/shard_map/hidden_back/pallas_call | solution.py:70
  107.0 0.8 copy-done.4
  107.9 1.5 collective-permute-start.17
  109.9 1.3 weight_sum.5
  111.2 0.8 copy-done.5
  112.0 1.3 weight_sum.6
  114.8 1.5 collective-permute-start.28
  116.3 1.9 %collective-permute-start.42 = (bf16[2,112,512]{2,1,0:T(8,128)(2,1)}, bf16[2,112,512]{2,1,0:T(8,128)(2,1)}, u32[]{:S(2)}, u32[]{:S(2)}) collective-permute-start(bf16[2,112,512]{2,1,0:T(8,128)(2,1)} %get-tuple-element.103.refs_2_), channel_id=1, source_target_pairs={{0,8},{4,12},{8,0},{12,4},{16,24},{20,28},{24,16},{28,20},{1,9},{5... | collective-permute-start | bytes 688136 | tf_op jit(solution)/shard_map/ppermute | solution.py:29
  118.3 1.3 weight_sum.7
  119.6 0.8 copy-done.7
  120.3 5.7 %collective-permute-done.28 = f32[8,192]{1,0:T(8,128)S(1)} collective-permute-done((f32[8,192]{1,0:T(8,128)S(1)}, f32[8,192]{1,0:T(8,128)S(1)}, u32[]{:S(2)}, u32[]{:S(2)}) %collective-permute-start.28) | collective-permute-done | bytes 6176 | tf_op jit(solution)/shard_map/ppermute | solution.py:29
  126.8 1.6 %reduce.1 = f32[192]{0:T(256)} reduce(f32[192,1]{1,0:T(8,128)} %copy-done.9, f32[]{:T(128)} %constant.55), dimensions={1}, to_apply=%get-tuple-element.87.reduce_sub_computation | reduce | bytes 1540 | tf_op jit(solution)/shard_map/project/pallas_call | solution.py:70
  128.4 0.7 fusion.12
  129.1 2.7 %collective-permute-start.36 = (bf16[1,112,512]{2,1,0:T(8,128)(2,1)}, bf16[1,112,512]{2,1,0:T(8,128)(2,1)S(1)}, u32[]{:S(2)}, u32[]{:S(2)}) collective-permute-start(bf16[1,112,512]{2,1,0:T(8,128)(2,1)} %get-tuple-element.104.refs_8_), channel_id=1, source_target_pairs={{0,16},{4,20},{8,24},{12,28},{16,0},{20,4},{24,8},{28,12},{1,17},{... | collective-permute-start | bytes 344072 | tf_op jit(solution)/shard_map/ppermute | solution.py:29
  131.8 1.0 copy-done.6
  132.8 1.1 weight_step.5
  134.3 1.0 weight_step.6
  135.3 1.1 collective-permute-done.44.refs_0_
  136.4 1.6 %collective-permute-start.43 = (bf16[1,112,512]{2,1,0:T(8,128)(2,1)S(1)}, bf16[1,112,512]{2,1,0:T(8,128)(2,1)S(1)}, u32[]{:S(2)}, u32[]{:S(2)}) collective-permute-start(bf16[1,112,512]{2,1,0:T(8,128)(2,1)S(1)} %get-tuple-element.111.refs_2_), channel_id=1, source_target_pairs={{0,16},{4,20},{8,24},{12,28},{16,0},{20,4},{24,8},{28,12},{1,17},{... | collective-permute-start | bytes 344072 | tf_op jit(solution)/shard_map/ppermute | solution.py:29
  138.0 1.0 weight_step.7
  139.0 1.4 collective-permute-start.45
  140.4 2.6 %fusion.9 = (bf16[1,192,896]{2,1,0:T(8,128)(2,1)}, bf16[1,192,896]{2,1,0:T(8,128)(2,1)}) fusion(f32[192,896]{1,0:T(8,128)} %copy-done.4, bf16[192,896]{1,0:T(8,128)(2,1)} %collective-permute-done.27, f32[192]{0:T(256)S(1)} %bitcast.26, bf16[192,3584]{1,0:T(8,128)(2,1)S(1)} %convolution_convert_fusion.refs_4_.refs_3_.refs_1_, s32[]{:T(128)S(6)} %select_n.26, ...), kind=kLoop, calls=%fused_computation.12 | loop fusion | flops 3268608 | bytes 4130312 | tf_op jit(solution)/shard_map/broadcast_in_dim | solution.py:688
  143.0 4.6 %collective-permute-done.41.refs_2_ = bf16[1,112,512]{2,1,0:T(8,128)(2,1)S(1)} collective-permute-done((bf16[1,112,512]{2,1,0:T(8,128)(2,1)S(1)}, bf16[1,112,512]{2,1,0:T(8,128)(2,1)S(1)}, u32[]{:S(2)}, u32[]{:S(2)}) %collective-permute-start.41) | collective-permute-done | bytes 114720 | tf_op jit(solution)/shard_map/ppermute | solution.py:29
  147.6 2.5 %collective-permute-done.43.refs_4_ = bf16[1,112,512]{2,1,0:T(8,128)(2,1)S(1)} collective-permute-done((bf16[1,112,512]{2,1,0:T(8,128)(2,1)S(1)}, bf16[1,112,512]{2,1,0:T(8,128)(2,1)S(1)}, u32[]{:S(2)}, u32[]{:S(2)}) %collective-permute-start.43) | collective-permute-done | bytes 114720 | tf_op jit(solution)/shard_map/ppermute | solution.py:29
  150.0 2.2 %collective-permute-done.45.refs_6_ = bf16[1,112,512]{2,1,0:T(8,128)(2,1)S(1)} collective-permute-done((bf16[1,112,512]{2,1,0:T(8,128)(2,1)S(1)}, bf16[1,112,512]{2,1,0:T(8,128)(2,1)S(1)}, u32[]{:S(2)}, u32[]{:S(2)}) %collective-permute-start.45) | collective-permute-done | bytes 114720 | tf_op jit(solution)/shard_map/ppermute | solution.py:29
  152.2 1.0 weight_total.1
  (91 shorter events, 9.4 us)
Async XLA Ops:
  1.7 7.1 %collective-permute-start = (bf16[32,3584]{1,0:T(8,128)(2,1)S(1)}, bf16[32,3584]{1,0:T(8,128)(2,1)S(1)}, u32[]{:S(2)}, u32[]{:S(2)}) collective-permute-start(bf16[32,3584]{1,0:T(8,128)(2,1)S(1)} %slice_bitcast_fusion), channel_id=1, source_target_pairs={{0,4},{4,8},{8,12},{12,16},{16,20},{20,24},{24,28},{1,5},{5,9},{9,... | collective-permute-start | bytes 688136 | tf_op jit(solution)/shard_map/ppermute | solution.py:512
  4.0 24.6 %collective-permute-start.9 = (bf16[192,896]{1,0:T(8,128)(2,1)}, bf16[192,896]{1,0:T(8,128)(2,1)S(1)}, u32[]{:S(2)}, u32[]{:S(2)}) collective-permute-start(bf16[192,896]{1,0:T(8,128)(2,1)} %bitcast.23), channel_id=1, source_target_pairs={{0,2},{2,0},{1,3},{3,1},{4,6},{6,4},{5,7},{7,5},{8,10},{10,8},{9,1... | collective-permute-start | bytes 1032200 | tf_op jit(solution)/shard_map/ppermute | solution.py:29
  6.4 15.3 %collective-permute-start.1 = (bf16[192,896]{1,0:T(8,128)(2,1)}, bf16[192,896]{1,0:T(8,128)(2,1)S(1)}, u32[]{:S(2)}, u32[]{:S(2)}) collective-permute-start(bf16[192,896]{1,0:T(8,128)(2,1)} %bitcast.20), channel_id=1, source_target_pairs={{0,2},{2,0},{1,3},{3,1},{4,6},{6,4},{5,7},{7,5},{8,10},{10,8},{9,1... | collective-permute-start | bytes 1032200 | tf_op jit(solution)/shard_map/ppermute | solution.py:29
  8.8 2.0 %copy-start.2 = (bf16[512,1792]{1,0:T(8,128)(2,1)S(1)}, bf16[512,1792]{1,0:T(8,128)(2,1)}, u32[]{:S(2)}) copy-start(bf16[512,1792]{1,0:T(8,128)(2,1)} %refs_1_.2) | copy-start | bytes 5505028
  10.8 2.6 %copy-start = (bf16[1792,3,512]{2,0,1:T(8,128)(2,1)S(1)}, bf16[1792,3,512]{2,0,1:T(8,128)(2,1)}, u32[]{:S(2)}) copy-start(bf16[1792,3,512]{2,0,1:T(8,128)(2,1)} %param.13) | copy-start | bytes 16515076
  13.3 8.4 %copy-start.1 = (bf16[1,192,896]{2,1,0:T(8,128)(2,1)S(1)}, bf16[1,192,896]{2,1,0:T(8,128)(2,1)}, u32[]{:S(2)}) copy-start(bf16[1,192,896]{2,1,0:T(8,128)(2,1)} %param.10) | copy-start | bytes 1032196
  13.3 8.4 %copy-start.13 = (f32[4,128]{1,0:T(4,128)S(1)}, f32[4,128]{1,0:T(4,128)}, u32[]{:S(2)}) copy-start(f32[4,128]{1,0:T(4,128)} %refs_0_.4) | copy-start | bytes 6148
  13.3 8.4 %copy-start.14 = (f32[4,128]{1,0:T(4,128)S(1)}, f32[4,128]{1,0:T(4,128)}, u32[]{:S(2)}) copy-start(f32[4,128]{1,0:T(4,128)} %refs_0_.5) | copy-start | bytes 6148
  21.7 6.9 %copy-start.3 = (bf16[1,192,896]{2,1,0:T(8,128)(2,1)S(1)}, bf16[1,192,896]{2,1,0:T(8,128)(2,1)}, u32[]{:S(2)}) copy-start(bf16[1,192,896]{2,1,0:T(8,128)(2,1)} %param.11) | copy-start | bytes 1032196
  23.3 80.7 %copy-start.9 = (f32[192,1]{1,0:T(8,128)}, f32[192,1]{1,0:T(8,128)S(1)}, u32[]{:S(2)}) copy-start(f32[192,1]{1,0:T(8,128)S(1)} %get-tuple-element.87.refs_5_) | copy-start | bytes 2308
  23.3 10.3 %collective-permute-start.2 = (bf16[3,192,128]{2,1,0:T(8,128)(2,1)S(1)}, bf16[3,192,128]{2,1,0:T(8,128)(2,1)S(1)}, u32[]{:S(2)}, u32[]{:S(2)}) collective-permute-start(bf16[3,192,128]{2,1,0:T(8,128)(2,1)S(1)} %get-tuple-element.66), channel_id=1, source_target_pairs={{0,8},{4,12},{8,0},{12,4},{16,24},{20,28},{24,16},{28,20},{1,9},{5... | collective-permute-start | bytes 442376 | tf_op jit(solution)/shard_map/ppermute | solution.py:29
  26.2 13.9 %collective-permute-start.3 = (bf16[3,192,128]{2,1,0:T(8,128)(2,1)S(1)}, bf16[3,192,128]{2,1,0:T(8,128)(2,1)S(1)}, u32[]{:S(2)}, u32[]{:S(2)}) collective-permute-start(bf16[3,192,128]{2,1,0:T(8,128)(2,1)S(1)} %get-tuple-element.67), channel_id=1, source_target_pairs={{0,16},{4,20},{8,24},{12,28},{16,0},{20,4},{24,8},{28,12},{1,17},{... | collective-permute-start | bytes 442376 | tf_op jit(solution)/shard_map/ppermute | solution.py:29
  27.7 12.5 %collective-permute-start.4 = (bf16[3,192,128]{2,1,0:T(8,128)(2,1)S(1)}, bf16[3,192,128]{2,1,0:T(8,128)(2,1)S(1)}, u32[]{:S(2)}, u32[]{:S(2)}) collective-permute-start(bf16[3,192,128]{2,1,0:T(8,128)(2,1)S(1)} %get-tuple-element.68), channel_id=1, source_target_pairs={{0,24},{4,28},{8,16},{12,20},{16,8},{20,12},{24,0},{28,4},{1,25},{... | collective-permute-start | bytes 442376 | tf_op jit(solution)/shard_map/ppermute | solution.py:29
  29.5 11.2 %collective-permute-start.10 = (bf16[192,128]{1,0:T(8,128)(2,1)S(1)}, bf16[192,128]{1,0:T(8,128)(2,1)S(1)}, u32[]{:S(2)}, u32[]{:S(2)}) collective-permute-start(bf16[192,128]{1,0:T(8,128)(2,1)S(1)} %get-tuple-element.71), channel_id=1, source_target_pairs={{0,8},{4,12},{8,0},{12,4},{16,24},{20,28},{24,16},{28,20},{1,9},{5... | collective-permute-start | bytes 147464 | tf_op jit(solution)/shard_map/ppermute | solution.py:29
  30.6 21.9 %collective-permute-start.5 = (bf16[3,192,128]{2,1,0:T(8,128)(2,1)S(1)}, bf16[3,192,128]{2,1,0:T(8,128)(2,1)S(1)}, u32[]{:S(2)}, u32[]{:S(2)}) collective-permute-start(bf16[3,192,128]{2,1,0:T(8,128)(2,1)S(1)} %get-tuple-element.65.refs_2_), channel_id=1, source_target_pairs={{0,4},{4,0},{8,12},{12,8},{16,20},{20,16},{24,28},{28,24},{1,5},{5... | collective-permute-start | bytes 442376 | tf_op jit(solution)/shard_map/ppermute | solution.py:29
  33.6 18.8 %collective-permute-start.6 = (bf16[3,192,128]{2,1,0:T(8,128)(2,1)S(1)}, bf16[3,192,128]{2,1,0:T(8,128)(2,1)S(1)}, u32[]{:S(2)}, u32[]{:S(2)}) collective-permute-start(bf16[3,192,128]{2,1,0:T(8,128)(2,1)S(1)} %collective-permute-done.2.refs_3_), channel_id=1, source_target_pairs={{0,4},{4,0},{8,12},{12,8},{16,20},{20,16},{24,28},{28,24},{1,5},{5... | collective-permute-start | bytes 442376 | tf_op jit(solution)/shard_map/ppermute | solution.py:29
  40.1 12.3 %collective-permute-start.7 = (bf16[3,192,128]{2,1,0:T(8,128)(2,1)S(1)}, bf16[3,192,128]{2,1,0:T(8,128)(2,1)S(1)}, u32[]{:S(2)}, u32[]{:S(2)}) collective-permute-start(bf16[3,192,128]{2,1,0:T(8,128)(2,1)S(1)} %collective-permute-done.3.refs_4_), channel_id=1, source_target_pairs={{0,4},{4,0},{8,12},{12,8},{16,20},{20,16},{24,28},{28,24},{1,5},{5... | collective-permute-start | bytes 442376 | tf_op jit(solution)/shard_map/ppermute | solution.py:29
  40.1 12.3 %collective-permute-start.8 = (bf16[3,192,128]{2,1,0:T(8,128)(2,1)S(1)}, bf16[3,192,128]{2,1,0:T(8,128)(2,1)S(1)}, u32[]{:S(2)}, u32[]{:S(2)}) collective-permute-start(bf16[3,192,128]{2,1,0:T(8,128)(2,1)S(1)} %collective-permute-done.4.refs_5_), channel_id=1, source_target_pairs={{0,4},{4,0},{8,12},{12,8},{16,20},{20,16},{24,28},{28,24},{1,5},{5... | collective-permute-start | bytes 442376 | tf_op jit(solution)/shard_map/ppermute | solution.py:29
  40.6 5.9 %collective-permute-start.11 = (bf16[192,128]{1,0:T(8,128)(2,1)S(1)}, bf16[192,128]{1,0:T(8,128)(2,1)S(1)}, u32[]{:S(2)}, u32[]{:S(2)}) collective-permute-start(bf16[192,128]{1,0:T(8,128)(2,1)S(1)} %get-tuple-element.72), channel_id=1, source_target_pairs={{0,16},{4,20},{8,24},{12,28},{16,0},{20,4},{24,8},{28,12},{1,17},{... | collective-permute-start | bytes 147464 | tf_op jit(solution)/shard_map/ppermute | solution.py:29
  46.6 5.9 %collective-permute-start.12 = (bf16[192,128]{1,0:T(8,128)(2,1)S(1)}, bf16[192,128]{1,0:T(8,128)(2,1)S(1)}, u32[]{:S(2)}, u32[]{:S(2)}) collective-permute-start(bf16[192,128]{1,0:T(8,128)(2,1)S(1)} %get-tuple-element.73), channel_id=1, source_target_pairs={{0,24},{4,28},{8,16},{12,20},{16,8},{20,12},{24,0},{28,4},{1,25},{... | collective-permute-start | bytes 147464 | tf_op jit(solution)/shard_map/ppermute | solution.py:29
  59.7 14.6 %collective-permute-start.16 = (bf16[4,2,192,128]{3,2,1,0:T(8,128)(2,1)S(1)}, bf16[4,2,192,128]{3,2,1,0:T(8,128)(2,1)S(1)}, u32[]{:S(2)}, u32[]{:S(2)}) collective-permute-start(bf16[4,2,192,128]{3,2,1,0:T(8,128)(2,1)S(1)} %get-tuple-element.82), channel_id=1, source_target_pairs={{0,4},{4,0},{8,12},{12,8},{16,20},{20,16},{24,28},{28,24},{1,5},{5... | collective-permute-start | bytes 1179656 | tf_op jit(solution)/shard_map/ppermute | solution.py:29
  59.8 12.9 %collective-permute-start.21 = (bf16[2,4,112,192]{3,2,1,0:T(8,128)(2,1)S(1)}, bf16[2,4,112,192]{3,2,1,0:T(8,128)(2,1)S(1)}, u32[]{:S(2)}, u32[]{:S(2)}) collective-permute-start(bf16[2,4,112,192]{3,2,1,0:T(8,128)(2,1)S(1)} %get-tuple-element.94), channel_id=1, source_target_pairs={{0,1},{1,0},{4,5},{5,4},{8,9},{9,8},{12,13},{13,12},{16,17},{17,16... | collective-permute-start | bytes 1032200 | tf_op jit(solution)/shard_map/ppermute | solution.py:582
  61.3 13.5 %collective-permute-start.13 = (bf16[2,192,128]{2,1,0:T(8,128)(2,1)S(1)}, bf16[2,192,128]{2,1,0:T(8,128)(2,1)S(1)}, u32[]{:S(2)}, u32[]{:S(2)}) collective-permute-start(bf16[2,192,128]{2,1,0:T(8,128)(2,1)S(1)} %get-tuple-element.78), channel_id=1, source_target_pairs={{0,8},{4,12},{8,0},{12,4},{16,24},{20,28},{24,16},{28,20},{1,9},{5... | collective-permute-start | bytes 294920 | tf_op jit(solution)/shard_map/ppermute | solution.py:29
  61.4 28.4 %collective-permute-start.22 = (bf16[2,4,112,192]{3,2,1,0:T(8,128)(2,1)S(1)}, bf16[2,4,112,192]{3,2,1,0:T(8,128)(2,1)S(1)}, u32[]{:S(2)}, u32[]{:S(2)}) collective-permute-start(bf16[2,4,112,192]{3,2,1,0:T(8,128)(2,1)S(1)} %get-tuple-element.95), channel_id=1, source_target_pairs={{0,4},{1,5},{4,0},{5,1},{8,12},{9,13},{12,8},{13,9},{16,20},{17,21... | collective-permute-start | bytes 1032200 | tf_op jit(solution)/shard_map/ppermute | solution.py:582
  61.5 13.6 %collective-permute-start.14 = (bf16[2,192,128]{2,1,0:T(8,128)(2,1)S(1)}, bf16[2,192,128]{2,1,0:T(8,128)(2,1)S(1)}, u32[]{:S(2)}, u32[]{:S(2)}) collective-permute-start(bf16[2,192,128]{2,1,0:T(8,128)(2,1)S(1)} %get-tuple-element.79), channel_id=1, source_target_pairs={{0,16},{4,20},{8,24},{12,28},{16,0},{20,4},{24,8},{28,12},{1,17},{... | collective-permute-start | bytes 294920 | tf_op jit(solution)/shard_map/ppermute | solution.py:29
  72.7 6.5 %collective-permute-start.15 = (bf16[2,192,128]{2,1,0:T(8,128)(2,1)S(1)}, bf16[2,192,128]{2,1,0:T(8,128)(2,1)S(1)}, u32[]{:S(2)}, u32[]{:S(2)}) collective-permute-start(bf16[2,192,128]{2,1,0:T(8,128)(2,1)S(1)} %get-tuple-element.80), channel_id=1, source_target_pairs={{0,24},{4,28},{8,16},{12,20},{16,8},{20,12},{24,0},{28,4},{1,25},{... | collective-permute-start | bytes 294920 | tf_op jit(solution)/shard_map/ppermute | solution.py:29
  74.3 17.1 %collective-permute-start.23 = (bf16[2,4,112,192]{3,2,1,0:T(8,128)(2,1)S(1)}, bf16[2,4,112,192]{3,2,1,0:T(8,128)(2,1)S(1)}, u32[]{:S(2)}, u32[]{:S(2)}) collective-permute-start(bf16[2,4,112,192]{3,2,1,0:T(8,128)(2,1)S(1)} %get-tuple-element.96), channel_id=1, source_target_pairs={{0,5},{1,4},{4,1},{5,0},{8,13},{9,12},{12,9},{13,8},{16,21},{17,20... | collective-permute-start | bytes 1032200 | tf_op jit(solution)/shard_map/ppermute | solution.py:582
  74.9 8.2 %collective-permute-start.18 = (bf16[2,192,128]{2,1,0:T(8,128)(2,1)S(1)}, bf16[2,192,128]{2,1,0:T(8,128)(2,1)S(1)}, u32[]{:S(2)}, u32[]{:S(2)}) collective-permute-start(bf16[2,192,128]{2,1,0:T(8,128)(2,1)S(1)} %get-tuple-element.89), channel_id=1, source_target_pairs={{0,8},{4,12},{8,0},{12,4},{16,24},{20,28},{24,16},{28,20},{1,9},{5... | collective-permute-start | bytes 294920 | tf_op jit(solution)/shard_map/ppermute | solution.py:29
  75.1 10.7 %collective-permute-start.19 = (bf16[2,192,128]{2,1,0:T(8,128)(2,1)S(1)}, bf16[2,192,128]{2,1,0:T(8,128)(2,1)S(1)}, u32[]{:S(2)}, u32[]{:S(2)}) collective-permute-start(bf16[2,192,128]{2,1,0:T(8,128)(2,1)S(1)} %get-tuple-element.90), channel_id=1, source_target_pairs={{0,16},{4,20},{8,24},{12,28},{16,0},{20,4},{24,8},{28,12},{1,17},{... | collective-permute-start | bytes 294920 | tf_op jit(solution)/shard_map/ppermute | solution.py:29
  79.2 6.7 %collective-permute-start.20 = (bf16[2,192,128]{2,1,0:T(8,128)(2,1)S(1)}, bf16[2,192,128]{2,1,0:T(8,128)(2,1)S(1)}, u32[]{:S(2)}, u32[]{:S(2)}) collective-permute-start(bf16[2,192,128]{2,1,0:T(8,128)(2,1)S(1)} %get-tuple-element.91), channel_id=1, source_target_pairs={{0,24},{4,28},{8,16},{12,20},{16,8},{20,12},{24,0},{28,4},{1,25},{... | collective-permute-start | bytes 294920 | tf_op jit(solution)/shard_map/ppermute | solution.py:29
  83.0 8.4 %collective-permute-start.24 = (bf16[192,512]{1,0:T(8,128)(2,1)S(1)}, bf16[192,512]{1,0:T(8,128)(2,1)S(1)}, u32[]{:S(2)}, u32[]{:S(2)}) collective-permute-start(bf16[192,512]{1,0:T(8,128)(2,1)S(1)} %get-tuple-element.84.refs_0_.refs_4_), channel_id=1, source_target_pairs={{0,1},{1,0},{2,3},{3,2},{4,5},{5,4},{6,7},{7,6},{8,9},{9,8},{10,11... | collective-permute-start | bytes 589832 | tf_op jit(solution)/shard_map/ppermute | solution.py:29
  85.8 6.1 %collective-permute-start.25 = (bf16[192,512]{1,0:T(8,128)(2,1)S(1)}, bf16[192,512]{1,0:T(8,128)(2,1)S(1)}, u32[]{:S(2)}, u32[]{:S(2)}) collective-permute-start(bf16[192,512]{1,0:T(8,128)(2,1)S(1)} %get-tuple-element.84.refs_0_.refs_4_), channel_id=1, source_target_pairs={{0,4},{4,0},{8,12},{12,8},{16,20},{20,16},{24,28},{28,24},{1,5},{5... | collective-permute-start | bytes 589832 | tf_op jit(solution)/shard_map/ppermute | solution.py:29
  85.9 9.7 %collective-permute-start.33 = (bf16[192,512]{1,0:T(8,128)(2,1)S(1)}, bf16[192,512]{1,0:T(8,128)(2,1)S(1)}, u32[]{:S(2)}, u32[]{:S(2)}) collective-permute-start(bf16[192,512]{1,0:T(8,128)(2,1)S(1)} %get-tuple-element.88.refs_0_.refs_4_), channel_id=1, source_target_pairs={{0,1},{1,0},{2,3},{3,2},{4,5},{5,4},{6,7},{7,6},{8,9},{9,8},{10,11... | collective-permute-start | bytes 589832 | tf_op jit(solution)/shard_map/ppermute | solution.py:29
  89.8 10.0 %collective-permute-start.30 = (bf16[192,512]{1,0:T(8,128)(2,1)S(1)}, bf16[192,512]{1,0:T(8,128)(2,1)S(1)}, u32[]{:S(2)}, u32[]{:S(2)}) collective-permute-start(bf16[192,512]{1,0:T(8,128)(2,1)S(1)} %get-tuple-element.92.refs_8_.refs_1_.refs_4_), channel_id=1, source_target_pairs={{0,1},{1,0},{2,3},{3,2},{4,5},{5,4},{6,7},{7,6},{8,9},{9,8},{10,11... | collective-permute-start | bytes 589832 | tf_op jit(solution)/shard_map/ppermute | solution.py:29
  91.4 8.5 %collective-permute-start.26 = (bf16[192,512]{1,0:T(8,128)(2,1)S(1)}, bf16[192,512]{1,0:T(8,128)(2,1)S(1)}, u32[]{:S(2)}, u32[]{:S(2)}) collective-permute-start(bf16[192,512]{1,0:T(8,128)(2,1)S(1)} %collective-permute-done.24.refs_5_), channel_id=1, source_target_pairs={{0,4},{4,0},{8,12},{12,8},{16,20},{20,16},{24,28},{28,24},{1,5},{5... | collective-permute-start | bytes 589832 | tf_op jit(solution)/shard_map/ppermute | solution.py:29
  91.4 9.5 %collective-permute-start.34 = (bf16[192,512]{1,0:T(8,128)(2,1)S(1)}, bf16[192,512]{1,0:T(8,128)(2,1)S(1)}, u32[]{:S(2)}, u32[]{:S(2)}) collective-permute-start(bf16[192,512]{1,0:T(8,128)(2,1)S(1)} %get-tuple-element.88.refs_0_.refs_4_), channel_id=1, source_target_pairs={{0,4},{4,0},{8,12},{12,8},{16,20},{20,16},{24,28},{28,24},{1,5},{5... | collective-permute-start | bytes 589832 | tf_op jit(solution)/shard_map/ppermute | solution.py:29
  91.9 9.8 %collective-permute-start.31 = (bf16[192,512]{1,0:T(8,128)(2,1)S(1)}, bf16[192,512]{1,0:T(8,128)(2,1)S(1)}, u32[]{:S(2)}, u32[]{:S(2)}) collective-permute-start(bf16[192,512]{1,0:T(8,128)(2,1)S(1)} %get-tuple-element.92.refs_8_.refs_1_.refs_4_), channel_id=1, source_target_pairs={{0,4},{4,0},{8,12},{12,8},{16,20},{20,16},{24,28},{28,24},{1,5},{5... | collective-permute-start | bytes 589832 | tf_op jit(solution)/shard_map/ppermute | solution.py:29
  95.6 8.4 %collective-permute-start.38 = (bf16[192,512]{1,0:T(8,128)(2,1)S(1)}, bf16[192,512]{1,0:T(8,128)(2,1)S(1)}, u32[]{:S(2)}, u32[]{:S(2)}) collective-permute-start(bf16[192,512]{1,0:T(8,128)(2,1)S(1)} %get-tuple-element.93.refs_2_.refs_4_), channel_id=1, source_target_pairs={{0,1},{1,0},{2,3},{3,2},{4,5},{5,4},{6,7},{7,6},{8,9},{9,8},{10,11... | collective-permute-start | bytes 589832 | tf_op jit(solution)/shard_map/ppermute | solution.py:29
  99.8 8.1 %collective-permute-start.35 = (bf16[192,512]{1,0:T(8,128)(2,1)S(1)}, bf16[192,512]{1,0:T(8,128)(2,1)S(1)}, u32[]{:S(2)}, u32[]{:S(2)}) collective-permute-start(bf16[192,512]{1,0:T(8,128)(2,1)S(1)} %collective-permute-done.33.refs_5_), channel_id=1, source_target_pairs={{0,4},{4,0},{8,12},{12,8},{16,20},{20,16},{24,28},{28,24},{1,5},{5... | collective-permute-start | bytes 589832 | tf_op jit(solution)/shard_map/ppermute | solution.py:29
  99.8 9.5 %collective-permute-start.32 = (bf16[192,512]{1,0:T(8,128)(2,1)S(1)}, bf16[192,512]{1,0:T(8,128)(2,1)S(1)}, u32[]{:S(2)}, u32[]{:S(2)}) collective-permute-start(bf16[192,512]{1,0:T(8,128)(2,1)S(1)} %collective-permute-done.30.refs_5_), channel_id=1, source_target_pairs={{0,4},{4,0},{8,12},{12,8},{16,20},{20,16},{24,28},{28,24},{1,5},{5... | collective-permute-start | bytes 589832 | tf_op jit(solution)/shard_map/ppermute | solution.py:29
  101.0 12.4 %collective-permute-start.29 = (bf16[2,112,512]{2,1,0:T(8,128)(2,1)S(1)}, bf16[2,112,512]{2,1,0:T(8,128)(2,1)S(1)}, u32[]{:S(2)}, u32[]{:S(2)}) collective-permute-start(bf16[2,112,512]{2,1,0:T(8,128)(2,1)S(1)} %get-tuple-element.97.refs_8_), channel_id=1, source_target_pairs={{0,8},{4,12},{8,0},{12,4},{16,24},{20,28},{24,16},{28,20},{1,9},{5... | collective-permute-start | bytes 688136 | tf_op jit(solution)/shard_map/ppermute | solution.py:29
  101.7 13.1 %collective-permute-start.39 = (bf16[192,512]{1,0:T(8,128)(2,1)S(1)}, bf16[192,512]{1,0:T(8,128)(2,1)S(1)}, u32[]{:S(2)}, u32[]{:S(2)}) collective-permute-start(bf16[192,512]{1,0:T(8,128)(2,1)S(1)} %get-tuple-element.93.refs_2_.refs_4_), channel_id=1, source_target_pairs={{0,4},{4,0},{8,12},{12,8},{16,20},{20,16},{24,28},{28,24},{1,5},{5... | collective-permute-start | bytes 589832 | tf_op jit(solution)/shard_map/ppermute | solution.py:29
  104.0 12.3 %collective-permute-start.40 = (bf16[192,512]{1,0:T(8,128)(2,1)S(1)}, bf16[192,512]{1,0:T(8,128)(2,1)S(1)}, u32[]{:S(2)}, u32[]{:S(2)}) collective-permute-start(bf16[192,512]{1,0:T(8,128)(2,1)S(1)} %collective-permute-done.38.refs_5_), channel_id=1, source_target_pairs={{0,4},{4,0},{8,12},{12,8},{16,20},{20,16},{24,28},{28,24},{1,5},{5... | collective-permute-start | bytes 589832 | tf_op jit(solution)/shard_map/ppermute | solution.py:29
  107.0 0.8 copy-start.4
  107.9 6.9 %copy-start.12 = (f32[8,192]{1,0:T(8,128)}, f32[8,192]{1,0:T(8,128)S(1)}, u32[]{:S(2)}) copy-start(f32[8,192]{1,0:T(8,128)S(1)} %get-tuple-element.100.refs_8_) | copy-start | bytes 18436
  107.9 31.1 %collective-permute-start.17 = (bf16[192,896]{1,0:T(8,128)(2,1)}, bf16[192,896]{1,0:T(8,128)(2,1)}, u32[]{:S(2)}, u32[]{:S(2)}) collective-permute-start(bf16[192,896]{1,0:T(8,128)(2,1)} %get-tuple-element.86), channel_id=1, source_target_pairs={{0,2},{2,0},{1,3},{3,1},{4,6},{6,4},{5,7},{7,5},{8,10},{10,8},{9,1... | collective-permute-start | bytes 1032200 | tf_op jit(solution)/shard_map/ppermute | solution.py:29
  109.4 31.0 %collective-permute-start.27 = (bf16[192,896]{1,0:T(8,128)(2,1)}, bf16[192,896]{1,0:T(8,128)(2,1)}, u32[]{:S(2)}, u32[]{:S(2)}) collective-permute-start(bf16[192,896]{1,0:T(8,128)(2,1)} %get-tuple-element.99), channel_id=1, source_target_pairs={{0,2},{2,0},{1,3},{3,1},{4,6},{6,4},{5,7},{7,5},{8,10},{10,8},{9,1... | collective-permute-start | bytes 1032200 | tf_op jit(solution)/shard_map/ppermute | solution.py:29
  111.2 0.8 copy-start.5
  113.3 15.8 %collective-permute-start.37 = (bf16[2,112,512]{2,1,0:T(8,128)(2,1)}, bf16[2,112,512]{2,1,0:T(8,128)(2,1)}, u32[]{:S(2)}, u32[]{:S(2)}) collective-permute-start(bf16[2,112,512]{2,1,0:T(8,128)(2,1)} %get-tuple-element.102.refs_8_), channel_id=1, source_target_pairs={{0,8},{4,12},{8,0},{12,4},{16,24},{20,28},{24,16},{28,20},{1,9},{5... | collective-permute-start | bytes 688136 | tf_op jit(solution)/shard_map/ppermute | solution.py:29
  114.1 0.7 copy-start.10
  114.8 11.3 %collective-permute-start.28 = (f32[8,192]{1,0:T(8,128)S(1)}, f32[8,192]{1,0:T(8,128)S(1)}, u32[]{:S(2)}, u32[]{:S(2)}) collective-permute-start(f32[8,192]{1,0:T(8,128)S(1)} %get-tuple-element.100.refs_8_), channel_id=1, source_target_pairs={{0,2},{2,0},{1,3},{3,1},{4,6},{6,4},{5,7},{7,5},{8,10},{10,8},{9,1... | collective-permute-start | bytes 18440 | tf_op jit(solution)/shard_map/ppermute | solution.py:29
  116.3 17.6 %collective-permute-start.42 = (bf16[2,112,512]{2,1,0:T(8,128)(2,1)}, bf16[2,112,512]{2,1,0:T(8,128)(2,1)}, u32[]{:S(2)}, u32[]{:S(2)}) collective-permute-start(bf16[2,112,512]{2,1,0:T(8,128)(2,1)} %get-tuple-element.103.refs_2_), channel_id=1, source_target_pairs={{0,8},{4,12},{8,0},{12,4},{16,24},{20,28},{24,16},{28,20},{1,9},{5... | collective-permute-start | bytes 688136 | tf_op jit(solution)/shard_map/ppermute | solution.py:29
  119.6 0.8 copy-start.7
  126.1 0.6 copy-start.16
  126.6 9.7 %collective-permute-start.44 = (bf16[2,112,512]{2,1,0:T(8,128)(2,1)}, bf16[2,112,512]{2,1,0:T(8,128)(2,1)}, u32[]{:S(2)}, u32[]{:S(2)}) collective-permute-start(bf16[2,112,512]{2,1,0:T(8,128)(2,1)} %get-tuple-element.107.refs_2_), channel_id=1, source_target_pairs={{0,8},{4,12},{8,0},{12,4},{16,24},{20,28},{24,16},{28,20},{1,9},{5... | collective-permute-start | bytes 688136 | tf_op jit(solution)/shard_map/ppermute | solution.py:29
  128.4 12.0 %copy-start.15 = (f32[192]{0:T(256)S(1)}, f32[192]{0:T(256)}, u32[]{:S(2)}) copy-start(f32[192]{0:T(256)} %reduce.1) | copy-start | bytes 2308
  129.1 18.4 %collective-permute-start.36 = (bf16[1,112,512]{2,1,0:T(8,128)(2,1)}, bf16[1,112,512]{2,1,0:T(8,128)(2,1)S(1)}, u32[]{:S(2)}, u32[]{:S(2)}) collective-permute-start(bf16[1,112,512]{2,1,0:T(8,128)(2,1)} %get-tuple-element.104.refs_8_), channel_id=1, source_target_pairs={{0,16},{4,20},{8,24},{12,28},{16,0},{20,4},{24,8},{28,12},{1,17},{... | collective-permute-start | bytes 344072 | tf_op jit(solution)/shard_map/ppermute | solution.py:29
  131.8 1.0 copy-start.6
  132.8 5.1 %copy-start.8 = (f32[2,112,512]{2,1,0:T(8,128)S(1)}, f32[2,112,512]{2,1,0:T(8,128)}, u32[]{:S(2)}) copy-start(f32[2,112,512]{2,1,0:T(8,128)} %copy-done.7) | copy-start | bytes 1376260
  133.9 13.6 %collective-permute-start.41 = (bf16[1,112,512]{2,1,0:T(8,128)(2,1)S(1)}, bf16[1,112,512]{2,1,0:T(8,128)(2,1)S(1)}, u32[]{:S(2)}, u32[]{:S(2)}) collective-permute-start(bf16[1,112,512]{2,1,0:T(8,128)(2,1)S(1)} %get-tuple-element.108.refs_2_), channel_id=1, source_target_pairs={{0,16},{4,20},{8,24},{12,28},{16,0},{20,4},{24,8},{28,12},{1,17},{... | collective-permute-start | bytes 344072 | tf_op jit(solution)/shard_map/ppermute | solution.py:29
  136.4 13.7 %collective-permute-start.43 = (bf16[1,112,512]{2,1,0:T(8,128)(2,1)S(1)}, bf16[1,112,512]{2,1,0:T(8,128)(2,1)S(1)}, u32[]{:S(2)}, u32[]{:S(2)}) collective-permute-start(bf16[1,112,512]{2,1,0:T(8,128)(2,1)S(1)} %get-tuple-element.111.refs_2_), channel_id=1, source_target_pairs={{0,16},{4,20},{8,24},{12,28},{16,0},{20,4},{24,8},{28,12},{1,17},{... | collective-permute-start | bytes 344072 | tf_op jit(solution)/shard_map/ppermute | solution.py:29
  139.0 13.2 %collective-permute-start.45 = (bf16[1,112,512]{2,1,0:T(8,128)(2,1)S(1)}, bf16[1,112,512]{2,1,0:T(8,128)(2,1)S(1)}, u32[]{:S(2)}, u32[]{:S(2)}) collective-permute-start(bf16[1,112,512]{2,1,0:T(8,128)(2,1)S(1)} %get-tuple-element.114), channel_id=1, source_target_pairs={{0,16},{4,20},{8,24},{12,28},{16,0},{20,4},{24,8},{28,12},{1,17},{... | collective-permute-start | bytes 344072 | tf_op jit(solution)/shard_map/ppermute | solution.py:29
  140.4 11.9 %copy-start.11 = (f32[1,112,512]{2,1,0:T(8,128)S(1)}, f32[1,112,512]{2,1,0:T(8,128)}, u32[]{:S(2)}) copy-start(f32[1,112,512]{2,1,0:T(8,128)} %copy-done.10) | copy-start | bytes 688132

commit v4 on v3

--- a/solution.py
+++ b/solution.py
@@ -13,7 +13,12 @@
 GROUP_MOST = 96
 FRAME_UP, FRAME_DOWN = 96, 125
 NO_GROUP = 1 << 30
-ATTENTION_MIB = 24
+ATTENTION_MIB = 16
+COST = {}
+ORDER = ("share", "query", "mix", "key", "a", "a", "hidden", "b", "b", "a", "b", "mixed", "latents")
+SPLIT = False
+LEFT_FIRST = True
+LIMITS = {"share": 1, "query_back": 1, "key_back": 1, "weight_total": 1}
 LANES = 128
 BF = jnp.bfloat16
 F32 = jnp.float32
@@ -58,6 +63,7 @@
 
 
 def call(kernel, name, out, args, scratch, mib, flops, after=(), specs=None, copies=0):
+    mib = LIMITS.get(name, mib)
     given, late = len(args), len(after)
 
     def body(*refs):
@@ -73,8 +79,10 @@
             in_specs=(specs or [VMEM] * given) + [ANY] * late,
             out_specs=[VMEM] * len(out),
             scratch_shapes=scratch,
-            compiler_params=pltpu.CompilerParams(vmem_limit_bytes=mib << 20),
-            cost_estimate=pl.CostEstimate(flops=flops, bytes_accessed=1 << 20, transcendentals=0),
+            compiler_params=pltpu.CompilerParams(vmem_limit_bytes=int(mib * (1 << 20))),
+            cost_estimate=pl.CostEstimate(
+                flops=0, bytes_accessed=COST.get(name, 1) << 10, transcendentals=0
+            ),
             name=name,
         )(*args, *after)
     )
@@ -122,11 +130,11 @@
     return pieces
 
 
-def width_outs(rows, width, width_part):
+def width_outs(rows, width, width_part, extra=0):
     if width_part % LANES:
         return [((rows, width), F32)]
     others = width // width_part - 1
-    return [((rows, width_part), F32)] + [((rows, width_part), BF)] * others
+    return [((rows, width_part), F32)] + [((rows, width_part + extra), BF)] * others
 
 
 def write_width(source, refs):
@@ -134,8 +142,9 @@
         refs[0][...] = source[...]
         return
     place = lax.axis_index("mp")
+    width = refs[0].shape[-1]
     for t, ref in enumerate(refs):
-        ref[...] = source[:, columns_of(place ^ t, ref.shape[-1])].astype(ref.dtype)
+        ref[:, :width] = source[:, columns_of(place ^ t, width)].astype(ref.dtype)
 
 
 def width_sum(parts, width_part):
@@ -147,10 +156,12 @@
             lax.dynamic_slice_in_dim(whole, (place ^ t) * width_part, width_part, 1)
             for t in range(count)
         ]
-    total = parts[0]
+    total, beside = parts[0], []
     for t in range(1, count):
-        total = total + swap(parts[t].astype(BF), "mp", t).astype(F32)
-    return total
+        got = swap(parts[t].astype(BF), "mp", t)
+        total = total + got[:, :width_part].astype(F32)
+        beside.append(got[:, width_part : width_part + 3])
+    return total, beside
 
 
 def project_kernel(heads, width_count, *refs):
@@ -200,22 +211,33 @@
         pieces[t][...] = heads_s[:, columns_of(head ^ t, dim)]
 
 
-def turn_kernel(blocks, clips, *refs):
-    sources = refs[:2]
-    pieces = refs[2 : 2 + 2 * clips]
-    turned_s = refs[-1]
-    span = turned_s.shape[-2]
-    core, clip = lax.axis_index("seq") % 2, lax.axis_index("dp")
-    for at, ref in enumerate(sources):
-        turned = jnp.transpose(ref[...].astype(F32))
-        for b in range(blocks * 2 * clips):
-            rows = turned[b * span : (b + 1) * span]
-            turned_s[at, b // (2 * clips), b % (2 * clips)] = rows.astype(BF)
-        for u in range(2):
-            for w in range(clips):
-                own = (core ^ u) * clips + (clip ^ w)
-                for b in range(blocks):
-                    pieces[u * clips + w][at, b] = turned_s[at, b, own]
+def turn_kernel(count, clips, source_ref, *refs):
+    pieces, turned_s = refs[:clips], refs[clips]
+    span, rows = turned_s.shape[-2], source_ref.shape[0]
+    clip = lax.axis_index("dp")
+    turned_s[...] = jnp.zeros_like(turned_s)
+    turned = jnp.transpose(source_ref[...].astype(F32))
+    for b in range(count * clips):
+        turned_s[b % clips, b // clips, :, :rows] = turned[b * span : (b + 1) * span].astype(BF)
+    for w in range(clips):
+        pieces[w][...] = turned_s[clip ^ w]
+
+
+def turned(source, after):
+    count, clips = lax.axis_size("seq"), lax.axis_size("dp")
+    rows, width = source.shape
+    shape = (count, width // (count * clips), round_up(rows, LANES))
+    pieces = call(
+        functools.partial(turn_kernel, count, clips),
+        "turn",
+        [(shape, BF)] * clips,
+        [source],
+        [((clips,) + shape, BF)],
+        6,
+        1 << 27,
+        after,
+    )
+    return [pieces[0]] + [swap(pieces[w], "dp", w) for w in range(1, clips)]
 
 
 def attention_kernel(heads, sharers, rows, block, factor, *refs):
@@ -353,24 +375,24 @@
 
 def query_kernel(heads, *refs):
     gain_ref, raw_ref = refs[:2]
-    pieces, (rows_ref, grad_ref) = refs[2 : 2 + heads], refs[2 + heads :]
+    pieces, pair_ref = refs[2 : 2 + heads], refs[2 + heads]
     inner = raw_ref.shape[-1]
     dim = inner // heads
     head, _ = head_place(heads)
     for t in range(heads):
         own = head ^ t
-        rows_ref[:, columns_of(own, dim)] = pieces[t][0]
+        pair_ref[:, columns_of(own, dim)] = pieces[t][0]
         grad = norm_back(
             raw_ref[0, :, columns_of(own, dim)],
             gain_ref[pl.ds(own, 1), :],
             pieces[t][1].astype(F32),
         )
-        grad_ref[:, columns_of(own, dim)] = grad.astype(BF)
+        pair_ref[:, columns_of(heads + own, dim)] = grad.astype(BF)
 
 
 def key_kernel(heads, *refs):
     gain_ref, raw_ref = refs[:2]
-    pieces, (key_ref, value_ref) = refs[2 : 2 + heads], refs[2 + heads :]
+    pieces, pair_ref = refs[2 : 2 + heads], refs[2 + heads]
     inner = raw_ref.shape[-1]
     dim = inner // heads
     head, _ = head_place(heads)
@@ -381,27 +403,34 @@
             gain_ref[pl.ds(own, 1), :],
             pieces[t][0].astype(F32),
         )
-        key_ref[:, columns_of(own, dim)] = grad.astype(BF)
-        value_ref[:, columns_of(own, dim)] = pieces[t][1]
+        pair_ref[:, columns_of(own, dim)] = grad.astype(BF)
+        pair_ref[:, columns_of(heads + own, dim)] = pieces[t][1]
 
 
 def mix_kernel(rows_ref, weight_ref, *refs):
     whole_s = refs[-1]
-    whole_s[...] = jnp.dot(rows_ref[...], weight_ref[...], preferred_element_type=F32)
+    inner = weight_ref.shape[0]
+    whole_s[...] = jnp.dot(rows_ref[:, :inner], weight_ref[...], preferred_element_type=F32)
     write_width(whole_s, refs[:-1])
 
 
 def hidden_kernel(width_count, *refs):
-    grads, (weight_ref, mod_ref, inv_ref) = refs[:3], refs[3:6]
-    inputs = refs[6 : 6 + width_count]
-    dot_ref = refs[6 + width_count]
-    outs = refs[7 + width_count : -2]
-    whole_s, inputs_s = refs[-2:]
+    first_ref, second_ref, weight_ref, mod_ref, inv_ref = refs[:5]
+    inputs = refs[5 : 5 + width_count]
+    dot_ref = refs[5 + width_count]
+    outs = refs[6 + width_count : -4]
+    whole_s, inputs_s, weight_s, sems = refs[-4:]
+    copies = Copies(sems)
+    for at in range(3):
+        copies.start(weight_ref.at[at], weight_s.at[at])
     spread(inputs, inputs_s)
+    inner = weight_ref.shape[2]
+    grads = (first_ref[:, inner:], second_ref[:, :inner], second_ref[:, inner:])
     total = 0.0
     for at, grad in enumerate(grads):
+        copies.made[at].wait()
         total = total + lax.dot_general(
-            grad[...], weight_ref[at], OVER_LAST, preferred_element_type=F32
+            grad, weight_s[at], OVER_LAST, preferred_element_type=F32
         )
     whole_s[...] = total
     write_width(whole_s, outs)
@@ -409,8 +438,14 @@
     scale = 1.0 + mod_ref[:, :model_width].astype(F32)
     normed = inputs_s[...].astype(F32) * inv_ref[...]
     dot = jnp.sum(whole_s[...] * scale * normed, axis=1, keepdims=True)
-    turned = jnp.transpose(jnp.broadcast_to(dot, (dot.shape[0], LANES)))
-    dot_ref[...] = turned[:8]
+    dot_ref[...] = dot
+    for ref in outs[1:]:
+        high = dot.astype(BF).astype(F32)
+        middle = (dot - high).astype(BF).astype(F32)
+        low = dot - high - middle
+        lane = lax.broadcasted_iota(jnp.int32, (dot.shape[0], LANES), 1)
+        beside = jnp.where(lane == 0, high, jnp.where(lane == 1, middle, low))
+        ref[:, outs[0].shape[1] :] = beside.astype(BF)
 
 
 def halve(total, step, send_ref, keep_ref):
@@ -421,16 +456,21 @@
         send_ref[b] = jnp.where(odd, first, second).astype(BF)
 
 
-def outer_kernel(which, *refs):
-    count = (len(refs) - 2) // 2
-    lefts, rights = refs[:count], refs[count : 2 * count]
-    _, blocks, span, rows = lefts[0].shape
-    total = 0.0
-    for left, right in zip(lefts, rights):
-        total = total + jnp.dot(
-            left[which].reshape(blocks * span, rows), right[...], preferred_element_type=F32
-        )
-    halve(total.reshape(blocks, span, total.shape[1]), 2, *refs[2 * count :])
+def outer_kernel(clips, *refs):
+    rights, (send_ref, keep_ref, total_s) = refs[:clips], refs[-3:]
+    lefts = refs[clips:-3]
+    blocks, span, lanes = lefts[0].shape
+    rows, width = rights[0].shape
+    groups = len(lefts) // clips
+    width = width // groups
+    for at in range(groups):
+        columns = slice(at * width, (at + 1) * width)
+        total = 0.0
+        for left, right in zip(lefts[at * clips : (at + 1) * clips], rights):
+            left = left[...].reshape(blocks * span, lanes)[:, :rows]
+            total = total + jnp.dot(left, right[:, columns], preferred_element_type=F32)
+        total_s[:, :, columns] = total.reshape(blocks, span, width)
+    halve(total_s, 1, send_ref, keep_ref)
 
 
 def step_kernel(step, got_ref, kept_ref, send_ref, keep_ref):
@@ -442,22 +482,23 @@
 
 
 class WeightSum:
-    def __init__(self, lefts, which, right):
-        rights = [right] + [swap(right, "dp", w) for w in range(1, lax.axis_size("dp"))]
-        self.rights = rights + [swap(far, "seq", 1) for far in rights]
-        self.lefts, self.which, self.step = lefts, which, 2
+    def __init__(self, name, lefts, right):
+        self.name = name
+        far = [swap(right, "dp", w) for w in range(1, lax.axis_size("dp"))]
+        self.rights = [right] + far
+        self.lefts, self.step = lefts, 1
 
     def outer(self, after):
-        _, blocks, span, rows = self.lefts[0].shape
-        width = self.rights[0].shape[1]
+        blocks, span, _ = self.lefts[0].shape
+        rows, width = self.rights[0].shape
         self.send, self.keep = call(
-            functools.partial(outer_kernel, self.which),
-            "weight_sum",
+            functools.partial(outer_kernel, len(self.rights)),
+            "weight_sum_" + self.name,
             halves(blocks, span, width),
-            [*self.lefts, *self.rights],
-            [],
-            8,
-            2 * blocks * span * rows * width * len(self.lefts),
+            [*self.rights, *self.lefts],
+            [((blocks, span, width), F32)],
+            12,
+            2 * blocks * span * rows * width * len(self.rights),
             after,
         )
         return [self.send]
@@ -469,7 +510,7 @@
     def halve(self, after):
         self.send, self.keep = call(
             functools.partial(step_kernel, self.step),
-            "weight_step",
+            "weight_step_" + self.name,
             halves(*self.keep.shape),
             [self.got, self.keep],
             [],
@@ -481,10 +522,86 @@
 
 
 def total_kernel(*refs):
-    out_ref, in_ref = refs[-1], refs[-2]
-    targets = (out_ref, in_ref.at[0], in_ref.at[1], in_ref.at[2])
-    for at, target in enumerate(targets):
-        target[...] = refs[2 * at][0].astype(F32) + refs[2 * at + 1][0]
+    in_ref, out_ref = refs[-2:]
+    inner = out_ref.shape[1]
+    targets = [out_ref, in_ref.at[0], in_ref.at[1], in_ref.at[2]]
+    for got, kept in zip(refs[0:-2:2], refs[1:-2:2]):
+        for at in range(got.shape[2] // inner):
+            columns = slice(at * inner, (at + 1) * inner)
+            targets.pop(0)[...] = got[0, :, columns].astype(F32) + kept[0, :, columns]
+
+
+def finish_mix_kernel(latents_ref, mod_ref, own_ref, *refs):
+    gots, out_ref = refs[:-1], refs[-1]
+    width = own_ref.shape[1]
+    place = lax.axis_index("mp") + mod_ref.shape[1] // 2 // width
+    gate = mod_ref[:, columns_of(place, width)].astype(F32)
+    total = own_ref[...]
+    for got in gots:
+        total = total + got[...].astype(F32)
+    out_ref[...] = (latents_ref[...].astype(F32) + gate * total).astype(BF)
+
+
+def finish_latents_kernel(latents_ref, upstream_ref, mod_ref, inv_ref, dot_ref, own_ref, *refs):
+    gots, out_ref = refs[:-1], refs[-1]
+    width = own_ref.shape[1]
+    scale = 1.0 + mod_ref[:, columns_of(lax.axis_index("mp"), width)].astype(F32)
+    total, dot = own_ref[...], dot_ref[...]
+    for got in gots:
+        total = total + got[:, :width].astype(F32)
+        lane = lax.broadcasted_iota(jnp.int32, (got.shape[0], LANES), 1)
+        beside = jnp.where(lane < 3, got[:, width:].astype(F32), 0.0)
+        dot = dot + jnp.sum(beside, axis=1, keepdims=True)
+    inv_norm = inv_ref[...]
+    normed = latents_ref[...].astype(F32) * inv_norm
+    mean = dot * (1.0 / (mod_ref.shape[1] // 2))
+    grad = inv_norm * (total * scale - normed * mean)
+    out_ref[...] = (upstream_ref[...].astype(F32) + grad).astype(BF)
+
+
+def finish_mix(latents, mod, parts, after):
+    width = latents.shape[1]
+    if width % LANES:
+        place = lax.axis_index("mp") * width + mod.shape[1] // 2
+        gate = lax.dynamic_slice_in_dim(mod, place, width, 1).astype(F32)
+        total, _ = width_sum(parts, width)
+        return (latents.astype(F32) + gate * total).astype(BF), after
+    gots = [swap(parts[t], "mp", t) for t in range(1, len(parts))]
+    (mixed,) = call(
+        finish_mix_kernel,
+        "finish_mix",
+        [(latents.shape, BF)],
+        [latents, mod, parts[0], *gots],
+        [],
+        4,
+        1 << 22,
+        after,
+    )
+    return mixed, [mixed]
+
+
+def finish_latents(latents, grad_out, mod, inv_norm, dot, parts, after):
+    width = latents.shape[1]
+    if width % LANES:
+        total, _ = width_sum(parts, width)
+        dot = sum([swap(dot, "mp", t) for t in range(1, lax.axis_size("mp"))], dot)
+        place = lax.axis_index("mp") * width
+        scale = 1.0 + lax.dynamic_slice_in_dim(mod, place, width, 1).astype(F32)
+        normed = latents.astype(F32) * inv_norm
+        grad = inv_norm * (total * scale - normed * (dot / (mod.shape[1] // 2)))
+        return (grad_out.astype(F32) + grad).astype(BF), after
+    gots = [swap(parts[t], "mp", t) for t in range(1, len(parts))]
+    (grad,) = call(
+        finish_latents_kernel,
+        "finish_latents",
+        [(latents.shape, BF)],
+        [latents, grad_out, mod, inv_norm, dot, parts[0], *gots],
+        [],
+        4,
+        1 << 22,
+        after,
+    )
+    return grad, [grad]
 
 
 def on_device(
@@ -501,10 +618,8 @@
     sharers = count // heads
     seq = lax.axis_index("seq")
     _, part = head_place(heads)
-    model_place = lax.axis_index("mp")
 
     inputs = width_pieces(latents)
-    upstream = width_pieces(grad_out)
     width_count = len(inputs)
 
     back = max(frame_count * j - (FRAME_UP * rows * j) // FRAME_DOWN for j in range(count))
@@ -521,8 +636,9 @@
 
     key_group, query_group = attention_groups(part, group_id, clip_len, heads, sharers)
     weight = jnp.transpose(w_qkv, (1, 0, 2))
-    staged = [weight, w_out, key_group, query_group]
-    weight, w_out, key_group, query_group = call(
+    weight_far = weight
+    staged = [weight, w_out, key_group, query_group, grad_out]
+    weight, w_out, key_group, query_group, grad_out = call(
         functools.partial(stage_kernel, len(staged)),
         "stage",
         [(array.shape, array.dtype) for array in staged],
@@ -531,9 +647,10 @@
         2,
         1 << 22,
         [mod],
-        [HBM, HBM, VMEM, VMEM],
+        [HBM, HBM, VMEM, VMEM, HBM],
         len(staged),
     )
+    upstream = width_pieces(grad_out)
     got = call(
         functools.partial(project_kernel, heads, width_count),
         "project",
@@ -548,6 +665,7 @@
     own = [own[0]] + [swap(own[t], "seq", t * sharers) for t in range(1, heads)]
     shared = [swap(own[t], "seq", u) for t in range(heads) for u in range(1, sharers)]
 
+    left_hidden = turned(hidden, [])
     got = call(
         functools.partial(upstream_kernel, heads, width_count),
         "upstream",
@@ -556,105 +674,130 @@
         [((rows, model_width), BF), ((rows, inner), BF)],
         8,
         2 * rows * model_width * inner,
+        left_hidden[:1],
     )
     ups, grad_attn = got[:heads], got[heads]
+    left_grad = turned(grad_attn, [])
     ups = [ups[0]] + [swap(ups[t], "seq", t * sharers) for t in range(1, heads)]
 
-    blocks = count // 2
-    span = model_width // (count * clips)
-    lefts = call(
-        functools.partial(turn_kernel, blocks, clips),
-        "turn",
-        [((2, blocks, span, rows), BF)] * (2 * clips),
-        [hidden, grad_attn],
-        [((2, blocks, 2 * clips, span, rows), BF)],
-        8,
-        1 << 28,
-    )
-    for u in range(2):
-        for w in range(clips):
-            if u or w:
-                pairs = [
-                    (s * clips + x, (s ^ u) * clips + (x ^ w))
-                    for s in range(count)
-                    for x in range(clips)
-                ]
-                lefts[u * clips + w] = lax.ppermute(lefts[u * clips + w], ("seq", "dp"), pairs)
-
-    outs, key_grads = attention(key_group, query_group, own, shared, ups, lefts[:1])
-    back_out = [outs[0]] + [swap(outs[t], "seq", t * sharers) for t in range(1, heads)]
+    outs, key_grads = attention(key_group, query_group, own, shared, ups, [*left_hidden[1:], left_grad[0]])
     terms = key_grads[:1] + [swap(key_grads[u], "seq", u) for u in range(1, sharers)]
     pair = (2, rows, head_dim)
-    sums = call(
-        functools.partial(share_kernel, sharers),
-        "share",
-        [(pair, BF)] * heads,
-        terms,
-        [],
-        4,
-        1 << 24,
-    )
-    back_key = [sums[0]] + [swap(sums[t], "seq", t * sharers) for t in range(1, heads)]
-    out_rows, grad_query = call(
-        functools.partial(query_kernel, heads),
-        "query_back",
-        [((rows, inner), BF)] * 2,
-        [q_gain, raw, *back_out],
-        [],
-        4,
-        1 << 24,
-        sums[:1],
-    )
-    sum_out = WeightSum(lefts, 1, out_rows)
-    sum_query = WeightSum(lefts, 0, grad_query)
-    parts = call(
-        mix_kernel,
-        "mix",
-        width_outs(rows, model_width, width_part),
-        [out_rows, w_out],
-        [((rows, model_width), F32)],
-        8,
-        2 * rows * model_width * inner,
-    )
-    grad_key, grad_value = call(
-        functools.partial(key_kernel, heads),
-        "key_back",
-        [((rows, inner), BF)] * 2,
-        [k_gain, raw, *back_key],
-        [],
-        4,
-        1 << 24,
-        parts[:1],
-    )
-    sum_key = WeightSum(lefts, 0, grad_key)
-    sum_value = WeightSum(lefts, 0, grad_value)
-    token = sum_out.outer([grad_key])
-    got = call(
-        functools.partial(hidden_kernel, width_count),
-        "hidden_back",
-        [((8, rows), F32)] + width_outs(rows, model_width, width_part),
-        [grad_query, grad_key, grad_value, weight, mod, inv_norm, *inputs],
-        [((rows, model_width), F32), ((rows, model_width), BF)],
-        8,
-        6 * rows * model_width * inner,
-        token,
-    )
-    part_dot, hidden_parts = got[0], got[1:]
-    sum_out.exchange()
-    token = sum_query.outer([part_dot])
-    sum_query.exchange()
-    token = sum_key.outer(token)
-    sum_key.exchange()
-    sums = [sum_out, sum_query, sum_key, sum_value]
-    while sum_out.keep.shape[0] > 1:
-        for at, total in enumerate(sums):
+    back_out = [outs[0]] + [swap(outs[t], "seq", t * sharers) for t in range(1, heads)]
+    state = {}
+
+    def share(after):
+        sums = call(
+            functools.partial(share_kernel, sharers),
+            "share",
+            [(pair, BF)] * heads,
+            terms,
+            [],
+            4,
+            1 << 24,
+            left_grad[1:] if LEFT_FIRST else (),
+        )
+        state["back_key"] = sums[:1] + [
+            swap(sums[t], "seq", t * sharers) for t in range(1, heads)
+        ]
+        return sums[:1]
+
+    def query(after):
+        state["first"] = call(
+            functools.partial(query_kernel, heads),
+            "query_back",
+            [((rows, 2 * inner), BF)],
+            [q_gain, raw, *back_out],
+            [],
+            4,
+            1 << 24,
+            after,
+        )[0]
+        state["a"] = WeightSum("a", left_grad + left_hidden, state["first"])
+        return [state["first"]]
+
+    def mix(after):
+        state["parts"] = call(
+            mix_kernel,
+            "mix",
+            width_outs(rows, model_width, width_part),
+            [state["first"], w_out],
+            [((rows, model_width), F32)],
+            8,
+            2 * rows * model_width * inner,
+            after,
+        )
+        return state["parts"][:1]
+
+    def key(after):
+        state["second"] = call(
+            functools.partial(key_kernel, heads),
+            "key_back",
+            [((rows, 2 * inner), BF)],
+            [k_gain, raw, *state["back_key"]],
+            [],
+            4,
+            1 << 24,
+            after,
+        )[0]
+        if SPLIT:
+            state["b"] = WeightSum("b", left_hidden, state["second"][:, :inner])
+            state["c"] = WeightSum("c", left_hidden, state["second"][:, inner:])
+        else:
+            state["b"] = WeightSum("b", left_hidden, state["second"])
+        return [state["second"]]
+
+    def advance(name, after):
+        total = state[name]
+        token = total.halve(after) if hasattr(total, "keep") else total.outer(after)
+        total.exchange()
+        return token
+
+    def hidden_back(after):
+        got = call(
+            functools.partial(hidden_kernel, width_count),
+            "hidden_back",
+            [((rows, 1), F32)] + width_outs(rows, model_width, width_part, LANES),
+            [state["first"], state["second"], weight_far, mod, inv_norm, *inputs],
+            [
+                ((rows, model_width), F32),
+                ((rows, model_width), BF),
+                (weight_far.shape, BF),
+            ],
+            10,
+            6 * rows * model_width * inner,
+            after,
+            [VMEM] * 2 + [HBM] + [VMEM] * (2 + width_count),
+            3,
+        )
+        state["dot"], state["hidden"] = got[0], got[1:]
+        return [state["dot"]]
+
+    def finish(name, after):
+        if name == "mixed":
+            state["mixed"], token = finish_mix(latents, mod, state["parts"], after)
+        else:
+            state["latents"], token = finish_latents(
+                latents, grad_out, mod, inv_norm, state["dot"], state["hidden"], after
+            )
+        return token
+
+    steps = dict(share=share, query=query, mix=mix, key=key, hidden=hidden_back)
+    for name in ("a", "b", "c"):
+        steps[name] = functools.partial(advance, name)
+    for name in ("mixed", "latents"):
+        steps[name] = functools.partial(finish, name)
+    token = ()
+    for name in ORDER:
+        token = steps[name](token)
+    totals = [state[name] for name in (("a", "b", "c") if SPLIT else ("a", "b"))]
+    while totals[-1].keep.shape[0] > 1:
+        for total in totals:
             token = total.halve(token)
             total.exchange()
-            if at == 0 and sum_value.step == 2:
-                token = sum_value.outer(token)
-                sum_value.exchange()
+    span = totals[0].keep.shape[1]
     pieces = []
-    for total in sums:
+    for total in totals:
         pieces.extend([total.got, total.keep])
     grad_wqkv, grad_wout = call(
         total_kernel,
@@ -665,24 +808,7 @@
         4,
         1 << 22,
     )
-
-    attn_mine = width_sum(parts, width_part)
-    gate_mine = lax.dynamic_slice_in_dim(
-        mod, model_width + model_place * width_part, width_part, 1
-    )
-    mixed = (latents.astype(F32) + gate_mine.astype(F32) * attn_mine).astype(BF)
-
-    full_dot = part_dot
-    for t in range(1, lax.axis_size("mp")):
-        full_dot = full_dot + swap(part_dot, "mp", t)
-    grad_mine = width_sum(hidden_parts, width_part)
-    scale_mine = lax.dynamic_slice_in_dim(mod, model_place * width_part, width_part, 1)
-    normed_mine = latents.astype(F32) * inv_norm
-    grad_normed = grad_mine * (1.0 + scale_mine.astype(F32))
-    inner_mean = full_dot[0][:, None] / model_width
-    grad_inputs = inv_norm * (grad_normed - normed_mine * inner_mean)
-    grad_latents = (grad_out.astype(F32) + grad_inputs).astype(BF)
-
+    mixed, grad_latents = state["mixed"], state["latents"]
     return (
         mixed[None],
         grad_latents[None],

time: 154 us -> 135 us (0.88)
  starting transfers between devices: 46.4 us -> 37.9 us
  other arithmetic: 6.33 us -> 1.4 us
  local copies, waits for them, and re-layouts: 8.49 us -> 4.93 us
  Pallas kernels: 25.1 us -> 21.9 us
  waiting for transfers between devices: 63.5 us -> 65.4 us
    ppermute x42 -> x31, waiting for transfers between devices: 54.2 us -> 65.4 us  [swap(): return lax.ppermute(value, axis, [(i, i ^ distance) for i in range(count)])]
    ppermute x3 -> x0, waiting for transfers between devices: 9.24 us -> none  [on_device(): lax.ppermute(lefts[u * clips + w], ('seq', 'dp'), pairs)]
    ppermute x42 -> x31, starting transfers between devices: 41.9 us -> 35.5 us  [swap(): return lax.ppermute(value, axis, [(i, i ^ distance) for i in range(count)])]
    unnamed x34 -> x18, local copies, waits for them, and re-layouts: 7.28 us -> 3.56 us
    pallas_call x19 -> x20, Pallas kernels: 25.1 us -> 21.9 us  [call(): pl.pallas_call(body, out_shape=[jax.ShapeDtypeStruct(*o) for o in out], i...]
    broadcast_in_dim x1 -> x0, other arithmetic: 2.61 us -> none  [on_device(): grad_latents[None]]
    ppermute x3 -> x0, starting transfers between devices: 2.15 us -> none  [on_device(): lax.ppermute(lefts[u * clips + w], ('seq', 'dp'), pairs)]
    pallas_call x1 -> x0, other arithmetic: 1.6 us -> none  [call(): pl.pallas_call(body, out_shape=[jax.ShapeDtypeStruct(*o) for o in out], i...]
  transfers between devices with their start and end apart: 46 -> 32, of which waited for: 18 -> 15; matrix products, arithmetic and copies ran while one was open for 6% -> 3% of each run, Pallas kernels for 11% -> 14%
where the time goes in v4:
time: 135 us
  waiting for transfers between devices  65.4 us (48%)
  starting transfers between devices  37.9 us (28%)
  Pallas kernels  21.9 us (16%)
  local copies, waits for them, and re-layouts  4.93 us (4%)
  matrix products  1.81 us (1%)
  between operations  1.6 us (1%)
  other arithmetic  1.4 us (1%)
    ppermute x31, waiting for transfers between devices, swap(): return lax.ppermute(value, axis, [(i, i ^ distance) for i in range(count)])  65.4 us
    ppermute x31, starting transfers between devices, swap(): return lax.ppermute(value, axis, [(i, i ^ distance) for i in range(count)])  35.5 us
    pallas_call x20, Pallas kernels, call(): pl.pallas_call(body, out_shape=[jax.ShapeDtypeStruct(*o) for o in out], i...  21.9 us
    unnamed x18, local copies, waits for them, and re-layouts  3.56 us
  transfers between devices with their start and end apart: 32, of which 15 were waited for; matrix products, arithmetic and copies ran while one was open for 3% of the time, Pallas kernels for 14%

profile of v4, /device:TPU:0, one launch (start us, length us, event | category | flops | bytes accessed | tf_op | source)
XLA Modules:
  0.0 135.0 jit_solution(10891221959954360205)
XLA Ops:
  0.7 1.2 slice_bitcast_fusion
  1.8 2.4 %collective-permute-start = (bf16[32,3584]{1,0:T(8,128)(2,1)S(1)}, bf16[32,3584]{1,0:T(8,128)(2,1)S(1)}, u32[]{:S(2)}, u32[]{:S(2)}) collective-permute-start(bf16[32,3584]{1,0:T(8,128)(2,1)S(1)} %slice_bitcast_fusion), channel_id=1, source_target_pairs={{0,4},{4,8},{8,12},{12,16},{16,20},{20,24},{24,28},{1,5},{5,9},{9,... | collective-permute-start | bytes 688136 | tf_op jit(solution)/shard_map/ppermute | solution.py:627
  4.2 2.4 %collective-permute-start.1 = (bf16[192,896]{1,0:T(8,128)(2,1)}, bf16[192,896]{1,0:T(8,128)(2,1)S(1)}, u32[]{:S(2)}, u32[]{:S(2)}) collective-permute-start(bf16[192,896]{1,0:T(8,128)(2,1)} %bitcast.17), channel_id=1, source_target_pairs={{0,2},{2,0},{1,3},{3,1},{4,6},{6,4},{5,7},{7,5},{8,10},{10,8},{9,1... | collective-permute-start | bytes 1032200 | tf_op jit(solution)/shard_map/ppermute | solution.py:34
  7.3 0.7 fusion.5
  8.1 0.1 reshape.27.refs_3_
  8.2 0.7 broadcast_subtract_fusion
  8.9 1.8 %convolution_convert_fusion.refs_5_.refs_3_.refs_1_.refs_2_ = bf16[192,3584]{1,0:T(8,128)(2,1)S(1)} fusion(bf16[150,3584]{1,0:T(8,128)(2,1)} %bitcast.25, bf16[32,3584]{1,0:T(8,128)(2,1)S(1)} %collective-permute-done, s32[192]{0:T(256)S(1)} %bitcast.26), kind=kOutput, calls=%fused_computation | convolution fusion | flops 253810816 | bytes 2681600 | tf_op jit(solution)/shard_map/dot_general | solution.py:635
  10.7 2.6 %copy-done = bf16[1792,3,512]{2,0,1:T(8,128)(2,1)S(1)} copy-done((bf16[1792,3,512]{2,0,1:T(8,128)(2,1)S(1)}, bf16[1792,3,512]{2,0,1:T(8,128)(2,1)}, u32[]{:S(2)}) %copy-start) | copy-done | bytes 5505048
  13.3 0.7 stage.1
  14.0 0.5 collective-permute-done.1.refs_5_.refs_6_
  14.5 1.6 %project.1 = (bf16[3,192,128]{2,1,0:T(8,128)(2,1)S(1)}, bf16[3,192,128]{2,1,0:T(8,128)(2,1)S(1)}, bf16[3,192,128]{2,1,0:T(8,128)(2,1)S(1)}, bf16[3,192,128]{2,1,...) custom-call(f32[4,128]{1,0:T(4,128)S(1)} %copy-done.5, ...), custom_call_target="tpu_custom_call" | custom-call | bytes 1024 | tf_op jit(solution)/shard_map/project/pallas_call | solution.py:76
  16.1 0.5 turn.2
  16.6 2.4 %collective-permute-start.13 = (bf16[8,112,256]{2,1,0:T(8,128)(2,1)S(1)}, bf16[8,112,256]{2,1,0:T(8,128)(2,1)S(1)}, u32[]{:S(2)}, u32[]{:S(2)}) collective-permute-start(bf16[8,112,256]{2,1,0:T(8,128)(2,1)S(1)} %get-tuple-element.70), channel_id=1, source_target_pairs={{0,1},{1,0},{2,3},{3,2},{4,5},{5,4},{6,7},{7,6},{8,9},{9,8},{10,11... | collective-permute-start | bytes 1376264 | tf_op jit(solution)/shard_map/ppermute | solution.py:34
  19.0 3.5 %collective-permute-start.2 = (bf16[3,192,128]{2,1,0:T(8,128)(2,1)S(1)}, bf16[3,192,128]{2,1,0:T(8,128)(2,1)S(1)}, u32[]{:S(2)}, u32[]{:S(2)}) collective-permute-start(bf16[3,192,128]{2,1,0:T(8,128)(2,1)S(1)} %get-tuple-element.59), channel_id=1, source_target_pairs={{0,8},{4,12},{8,0},{12,4},{16,24},{20,28},{24,16},{28,20},{1,9},{5... | collective-permute-start | bytes 442376 | tf_op jit(solution)/shard_map/ppermute | solution.py:34
  22.5 2.6 %collective-permute-start.3 = (bf16[3,192,128]{2,1,0:T(8,128)(2,1)S(1)}, bf16[3,192,128]{2,1,0:T(8,128)(2,1)S(1)}, u32[]{:S(2)}, u32[]{:S(2)}) collective-permute-start(bf16[3,192,128]{2,1,0:T(8,128)(2,1)S(1)} %get-tuple-element.60), channel_id=1, source_target_pairs={{0,16},{4,20},{8,24},{12,28},{16,0},{20,4},{24,8},{28,12},{1,17},{... | collective-permute-start | bytes 442376 | tf_op jit(solution)/shard_map/ppermute | solution.py:34
  25.1 0.8 upstream.1
  25.9 1.3 collective-permute-done.2.refs_3_
  27.2 2.1 %collective-permute-start.10 = (bf16[192,128]{1,0:T(8,128)(2,1)S(1)}, bf16[192,128]{1,0:T(8,128)(2,1)S(1)}, u32[]{:S(2)}, u32[]{:S(2)}) collective-permute-start(bf16[192,128]{1,0:T(8,128)(2,1)S(1)} %get-tuple-element.67), channel_id=1, source_target_pairs={{0,8},{4,12},{8,0},{12,4},{16,24},{20,28},{24,16},{28,20},{1,9},{5... | collective-permute-start | bytes 147464 | tf_op jit(solution)/shard_map/ppermute | solution.py:34
  29.3 6.8 %collective-permute-done.3.refs_4_ = bf16[3,192,128]{2,1,0:T(8,128)(2,1)S(1)} collective-permute-done((bf16[3,192,128]{2,1,0:T(8,128)(2,1)S(1)}, bf16[3,192,128]{2,1,0:T(8,128)(2,1)S(1)}, u32[]{:S(2)}, u32[]{:S(2)}) %collective-permute-start.3) | collective-permute-done | bytes 147488 | tf_op jit(solution)/shard_map/ppermute | solution.py:34
  36.1 0.5 collective-permute-start.7
  36.7 4.4 %collective-permute-done.11.refs_12_ = bf16[192,128]{1,0:T(8,128)(2,1)S(1)} collective-permute-done((bf16[192,128]{1,0:T(8,128)(2,1)S(1)}, bf16[192,128]{1,0:T(8,128)(2,1)S(1)}, u32[]{:S(2)}, u32[]{:S(2)}) %collective-permute-start.11) | collective-permute-done | bytes 49184 | tf_op jit(solution)/shard_map/ppermute | solution.py:34
  41.1 2.0 %collective-permute-start.12 = (bf16[192,128]{1,0:T(8,128)(2,1)S(1)}, bf16[192,128]{1,0:T(8,128)(2,1)S(1)}, u32[]{:S(2)}, u32[]{:S(2)}) collective-permute-start(bf16[192,128]{1,0:T(8,128)(2,1)S(1)} %get-tuple-element.69), channel_id=1, source_target_pairs={{0,24},{4,28},{8,16},{12,20},{16,8},{20,12},{24,0},{28,4},{1,25},{... | collective-permute-start | bytes 147464 | tf_op jit(solution)/shard_map/ppermute | solution.py:34
  43.0 0.5 turn.3
  43.5 3.4 %collective-permute-done.12.refs_13_ = bf16[192,128]{1,0:T(8,128)(2,1)S(1)} collective-permute-done((bf16[192,128]{1,0:T(8,128)(2,1)S(1)}, bf16[192,128]{1,0:T(8,128)(2,1)S(1)}, u32[]{:S(2)}, u32[]{:S(2)}) %collective-permute-start.12) | collective-permute-done | bytes 49184 | tf_op jit(solution)/shard_map/ppermute | solution.py:34
  46.9 0.5 collective-permute-start.18
  47.5 7.3 %attention.1 = (bf16[2,192,128]{2,1,0:T(8,128)(2,1)S(1)}, bf16[2,192,128]{2,1,0:T(8,128)(2,1)S(1)}, bf16[2,192,128]{2,1,0:T(8,128)(2,1)S(1)}, bf16[2,192,128]{2,...) custom-call(s32[1,1536]{1,0:T(1,128)S(1)} %get-tuple-element.56.refs_0_, ...), custom_call_target="tpu_custom_call" | custom-call | bytes 1024 | tf_op jit(solution)/shard_map/attention/pallas_call | solution.py:76
  54.9 2.5 %collective-permute-start.15 = (bf16[2,192,128]{2,1,0:T(8,128)(2,1)S(1)}, bf16[2,192,128]{2,1,0:T(8,128)(2,1)S(1)}, u32[]{:S(2)}, u32[]{:S(2)}) collective-permute-start(bf16[2,192,128]{2,1,0:T(8,128)(2,1)S(1)} %get-tuple-element.75), channel_id=1, source_target_pairs={{0,16},{4,20},{8,24},{12,28},{16,0},{20,4},{24,8},{28,12},{1,17},{... | collective-permute-start | bytes 294920 | tf_op jit(solution)/shard_map/ppermute | solution.py:34
  57.4 1.9 %collective-permute-start.16 = (bf16[2,192,128]{2,1,0:T(8,128)(2,1)S(1)}, bf16[2,192,128]{2,1,0:T(8,128)(2,1)S(1)}, u32[]{:S(2)}, u32[]{:S(2)}) collective-permute-start(bf16[2,192,128]{2,1,0:T(8,128)(2,1)S(1)} %get-tuple-element.76), channel_id=1, source_target_pairs={{0,24},{4,28},{8,16},{12,20},{16,8},{20,12},{24,0},{28,4},{1,25},{... | collective-permute-start | bytes 294920 | tf_op jit(solution)/shard_map/ppermute | solution.py:34
  59.3 0.1 share.1
  59.4 2.1 %collective-permute-done.14.refs_3_ = bf16[2,192,128]{2,1,0:T(8,128)(2,1)S(1)} collective-permute-done((bf16[2,192,128]{2,1,0:T(8,128)(2,1)S(1)}, bf16[2,192,128]{2,1,0:T(8,128)(2,1)S(1)}, u32[]{:S(2)}, u32[]{:S(2)}) %collective-permute-start.14) | collective-permute-done | bytes 98336 | tf_op jit(solution)/shard_map/ppermute | solution.py:34
  61.5 4.2 %collective-permute-done.15.refs_4_ = bf16[2,192,128]{2,1,0:T(8,128)(2,1)S(1)} collective-permute-done((bf16[2,192,128]{2,1,0:T(8,128)(2,1)S(1)}, bf16[2,192,128]{2,1,0:T(8,128)(2,1)S(1)}, u32[]{:S(2)}, u32[]{:S(2)}) %collective-permute-start.15) | collective-permute-done | bytes 98336 | tf_op jit(solution)/shard_map/ppermute | solution.py:34
  65.8 0.3 query_back.1.refs_0_.refs_2_
  66.1 1.6 %collective-permute-start.24 = (bf16[192,1024]{1,0:T(8,128)(2,1)S(1)}, bf16[192,1024]{1,0:T(8,128)(2,1)S(1)}, u32[]{:S(2)}, u32[]{:S(2)}) collective-permute-start(bf16[192,1024]{1,0:T(8,128)(2,1)S(1)} %query_back.1.refs_0_.refs_2_), channel_id=1, source_target_pairs={{0,1},{1,0},{2,3},{3,2},{4,5},{5,4},{6,7},{7,6},{8,9},{9,8},{10,11... | collective-permute-start | bytes 1179656 | tf_op jit(solution)/shard_map/ppermute | solution.py:34
  67.6 2.1 %collective-permute-start.20 = (bf16[2,192,128]{2,1,0:T(8,128)(2,1)S(1)}, bf16[2,192,128]{2,1,0:T(8,128)(2,1)S(1)}, u32[]{:S(2)}, u32[]{:S(2)}) collective-permute-start(bf16[2,192,128]{2,1,0:T(8,128)(2,1)S(1)} %get-tuple-element.83), channel_id=1, source_target_pairs={{0,8},{4,12},{8,0},{12,4},{16,24},{20,28},{24,16},{28,20},{1,9},{5... | collective-permute-start | bytes 294920 | tf_op jit(solution)/shard_map/ppermute | solution.py:34
  69.8 0.5 collective-permute-start.21
  70.2 1.9 %collective-permute-start.22 = (bf16[2,192,128]{2,1,0:T(8,128)(2,1)S(1)}, bf16[2,192,128]{2,1,0:T(8,128)(2,1)S(1)}, u32[]{:S(2)}, u32[]{:S(2)}) collective-permute-start(bf16[2,192,128]{2,1,0:T(8,128)(2,1)S(1)} %get-tuple-element.85), channel_id=1, source_target_pairs={{0,24},{4,28},{8,16},{12,20},{16,8},{20,12},{24,0},{28,4},{1,25},{... | collective-permute-start | bytes 294920 | tf_op jit(solution)/shard_map/ppermute | solution.py:34
  72.1 0.6 mix.1
  72.7 0.3 collective-permute-done.20.refs_3_
  73.0 6.4 %collective-permute-done.21.refs_4_ = bf16[2,192,128]{2,1,0:T(8,128)(2,1)S(1)} collective-permute-done((bf16[2,192,128]{2,1,0:T(8,128)(2,1)S(1)}, bf16[2,192,128]{2,1,0:T(8,128)(2,1)S(1)}, u32[]{:S(2)}, u32[]{:S(2)}) %collective-permute-start.21) | collective-permute-done | bytes 98336 | tf_op jit(solution)/shard_map/ppermute | solution.py:34
  79.4 0.3 key_back.1.refs_6_.refs_1_.refs_0_
  79.8 1.1 weight_sum_a.1
  81.0 0.6 collective-permute-start.23
  81.6 1.9 %collective-permute-done.25.refs_0_ = bf16[4,112,1024]{2,1,0:T(8,128)(2,1)S(1)} collective-permute-done((bf16[4,112,1024]{2,1,0:T(8,128)(2,1)S(1)}, bf16[4,112,1024]{2,1,0:T(8,128)(2,1)S(1)}, u32[]{:S(2)}, u32[]{:S(2)}) %collective-permute-start.25) | collective-permute-done | bytes 917536 | tf_op jit(solution)/shard_map/ppermute | solution.py:34
  83.4 0.2 weight_step_a.2
  83.7 3.3 %hidden_back.1 = (f32[192,1]{1,0:T(8,128)S(1)}, f32[192,896]{1,0:T(8,128)S(1)}, bf16[192,1024]{1,0:T(8,128)(2,1)S(1)}) custom-call(bf16[192,1024]{1,0:T(8,128)(2,1)S(1)} %query_back.1.refs_0_.refs_2_, bf16[192,1024]{1,0:T(8,128)(2,1)S(1)} %key_back.1.refs_6_.refs_1_.refs_0_, bf16[3,1792,512]{2,1,0:T(8,128)(2,1)S(1)} %bitcast.16, ...), custom_call_target="tpu_custom_call" | custom-call | bytes 1024 | tf_op jit(solution)/shard_map/hidden_back/pallas_call | solution.py:76
  87.0 5.5 %collective-permute-done.23.refs_1_ = bf16[192,1024]{1,0:T(8,128)(2,1)S(1)} collective-permute-done((bf16[192,1024]{1,0:T(8,128)(2,1)S(1)}, bf16[192,1024]{1,0:T(8,128)(2,1)S(1)}, u32[]{:S(2)}, u32[]{:S(2)}) %collective-permute-start.23) | collective-permute-done | bytes 393248 | tf_op jit(solution)/shard_map/ppermute | solution.py:34
  92.5 1.1 weight_sum_b.1
  93.7 1.9 %collective-permute-start.28 = (bf16[2,112,1024]{2,1,0:T(8,128)(2,1)S(1)}, bf16[2,112,1024]{2,1,0:T(8,128)(2,1)S(1)}, u32[]{:S(2)}, u32[]{:S(2)}) collective-permute-start(bf16[2,112,1024]{2,1,0:T(8,128)(2,1)S(1)} %get-tuple-element.89.refs_7_), channel_id=1, source_target_pairs={{0,8},{4,12},{8,0},{12,4},{16,24},{20,28},{24,16},{28,20},{1,9},{5... | collective-permute-start | bytes 1376264 | tf_op jit(solution)/shard_map/ppermute | solution.py:34
  95.6 0.6 collective-permute-done.26.refs_0_
  96.2 0.2 weight_step_b.2
  96.4 1.9 %collective-permute-start.27 = (bf16[2,112,1024]{2,1,0:T(8,128)(2,1)S(1)}, bf16[2,112,1024]{2,1,0:T(8,128)(2,1)S(1)}, u32[]{:S(2)}, u32[]{:S(2)}) collective-permute-start(bf16[2,112,1024]{2,1,0:T(8,128)(2,1)S(1)} %get-tuple-element.93.refs_2_), channel_id=1, source_target_pairs={{0,8},{4,12},{8,0},{12,4},{16,24},{20,28},{24,16},{28,20},{1,9},{5... | collective-permute-start | bytes 1376264 | tf_op jit(solution)/shard_map/ppermute | solution.py:34
  98.3 1.5 %collective-permute-start.29 = (bf16[192,1024]{1,0:T(8,128)(2,1)S(1)}, bf16[192,1024]{1,0:T(8,128)(2,1)S(1)}, u32[]{:S(2)}, u32[]{:S(2)}) collective-permute-start(bf16[192,1024]{1,0:T(8,128)(2,1)S(1)} %get-tuple-element.99), channel_id=1, source_target_pairs={{0,2},{2,0},{1,3},{3,1},{4,6},{6,4},{5,7},{7,5},{8,10},{10,8},{9,1... | collective-permute-start | bytes 1179656 | tf_op jit(solution)/shard_map/ppermute | solution.py:34
  99.8 0.5 collective-permute-start.19
  100.3 6.8 %collective-permute-done.28.refs_0_ = bf16[2,112,1024]{2,1,0:T(8,128)(2,1)S(1)} collective-permute-done((bf16[2,112,1024]{2,1,0:T(8,128)(2,1)S(1)}, bf16[2,112,1024]{2,1,0:T(8,128)(2,1)S(1)}, u32[]{:S(2)}, u32[]{:S(2)}) %collective-permute-start.28) | collective-permute-done | bytes 458784 | tf_op jit(solution)/shard_map/ppermute | solution.py:34
  107.1 0.1 weight_step_a.3
  107.2 2.4 %collective-permute-start.30 = (bf16[1,112,1024]{2,1,0:T(8,128)(2,1)S(1)}, bf16[1,112,1024]{2,1,0:T(8,128)(2,1)S(1)}, u32[]{:S(2)}, u32[]{:S(2)}) collective-permute-start(bf16[1,112,1024]{2,1,0:T(8,128)(2,1)S(1)} %get-tuple-element.96.refs_2_), channel_id=1, source_target_pairs={{0,16},{4,20},{8,24},{12,28},{16,0},{20,4},{24,8},{28,12},{1,17},{... | collective-permute-start | bytes 688136 | tf_op jit(solution)/shard_map/ppermute | solution.py:34
  109.6 11.9 %collective-permute-done.27.refs_0_ = bf16[2,112,1024]{2,1,0:T(8,128)(2,1)S(1)} collective-permute-done((bf16[2,112,1024]{2,1,0:T(8,128)(2,1)S(1)}, bf16[2,112,1024]{2,1,0:T(8,128)(2,1)S(1)}, u32[]{:S(2)}, u32[]{:S(2)}) %collective-permute-start.27) | collective-permute-done | bytes 458784 | tf_op jit(solution)/shard_map/ppermute | solution.py:34
  121.4 0.1 weight_step_b.3
  121.6 0.1 collective-permute-start.31
  121.7 0.9 finish_mix.1.refs_7_
  122.6 1.0 copy-done.3
  123.6 1.1 finish_latents.1
  124.7 9.3 %collective-permute-done.31.refs_2_ = bf16[1,112,1024]{2,1,0:T(8,128)(2,1)S(1)} collective-permute-done((bf16[1,112,1024]{2,1,0:T(8,128)(2,1)S(1)}, bf16[1,112,1024]{2,1,0:T(8,128)(2,1)S(1)}, u32[]{:S(2)}, u32[]{:S(2)}) %collective-permute-start.31) | collective-permute-done | bytes 229408 | tf_op jit(solution)/shard_map/ppermute | solution.py:34
  134.0 1.0 weight_total.1
  (46 shorter events, 0.6 us)
Async XLA Ops:
  0.6 10.1 %copy-start.2 = (bf16[512,1792]{1,0:T(8,128)(2,1)S(1)}, bf16[512,1792]{1,0:T(8,128)(2,1)}, u32[]{:S(2)}) copy-start(bf16[512,1792]{1,0:T(8,128)(2,1)} %refs_1_.2) | copy-start | bytes 5505028
  0.6 10.1 %copy-start.4 = (bf16[1,192,896]{2,1,0:T(8,128)(2,1)S(1)}, bf16[1,192,896]{2,1,0:T(8,128)(2,1)}, u32[]{:S(2)}) copy-start(bf16[1,192,896]{2,1,0:T(8,128)(2,1)} %param.11) | copy-start | bytes 1032196
  1.8 7.1 %collective-permute-start = (bf16[32,3584]{1,0:T(8,128)(2,1)S(1)}, bf16[32,3584]{1,0:T(8,128)(2,1)S(1)}, u32[]{:S(2)}, u32[]{:S(2)}) collective-permute-start(bf16[32,3584]{1,0:T(8,128)(2,1)S(1)} %slice_bitcast_fusion), channel_id=1, source_target_pairs={{0,4},{4,8},{8,12},{12,16},{16,20},{20,24},{24,28},{1,5},{5,9},{9,... | collective-permute-start | bytes 688136 | tf_op jit(solution)/shard_map/ppermute | solution.py:627
  4.2 10.3 %collective-permute-start.1 = (bf16[192,896]{1,0:T(8,128)(2,1)}, bf16[192,896]{1,0:T(8,128)(2,1)S(1)}, u32[]{:S(2)}, u32[]{:S(2)}) collective-permute-start(bf16[192,896]{1,0:T(8,128)(2,1)} %bitcast.17), channel_id=1, source_target_pairs={{0,2},{2,0},{1,3},{3,1},{4,6},{6,4},{5,7},{7,5},{8,10},{10,8},{9,1... | collective-permute-start | bytes 1032200 | tf_op jit(solution)/shard_map/ppermute | solution.py:34
  10.7 2.6 %copy-start = (bf16[1792,3,512]{2,0,1:T(8,128)(2,1)S(1)}, bf16[1792,3,512]{2,0,1:T(8,128)(2,1)}, u32[]{:S(2)}) copy-start(bf16[1792,3,512]{2,0,1:T(8,128)(2,1)} %param.13) | copy-start | bytes 16515076
  13.3 1.2 copy-start.1
  13.3 1.2 copy-start.5
  13.3 1.3 copy-start.6
  14.0 11.1 %collective-permute-start.9 = (bf16[192,896]{1,0:T(8,128)(2,1)S(1)}, bf16[192,896]{1,0:T(8,128)(2,1)S(1)}, u32[]{:S(2)}, u32[]{:S(2)}) collective-permute-start(bf16[192,896]{1,0:T(8,128)(2,1)S(1)} %get-tuple-element.63.refs_2_.refs_1_), channel_id=1, source_target_pairs={{0,2},{2,0},{1,3},{3,1},{4,6},{6,4},{5,7},{7,5},{8,10},{10,8},{9,1... | collective-permute-start | bytes 1032200 | tf_op jit(solution)/shard_map/ppermute | solution.py:34
  16.6 30.9 %collective-permute-start.13 = (bf16[8,112,256]{2,1,0:T(8,128)(2,1)S(1)}, bf16[8,112,256]{2,1,0:T(8,128)(2,1)S(1)}, u32[]{:S(2)}, u32[]{:S(2)}) collective-permute-start(bf16[8,112,256]{2,1,0:T(8,128)(2,1)S(1)} %get-tuple-element.70), channel_id=1, source_target_pairs={{0,1},{1,0},{2,3},{3,2},{4,5},{5,4},{6,7},{7,6},{8,9},{9,8},{10,11... | collective-permute-start | bytes 1376264 | tf_op jit(solution)/shard_map/ppermute | solution.py:34
  19.0 8.2 %collective-permute-start.2 = (bf16[3,192,128]{2,1,0:T(8,128)(2,1)S(1)}, bf16[3,192,128]{2,1,0:T(8,128)(2,1)S(1)}, u32[]{:S(2)}, u32[]{:S(2)}) collective-permute-start(bf16[3,192,128]{2,1,0:T(8,128)(2,1)S(1)} %get-tuple-element.59), channel_id=1, source_target_pairs={{0,8},{4,12},{8,0},{12,4},{16,24},{20,28},{24,16},{28,20},{1,9},{5... | collective-permute-start | bytes 442376 | tf_op jit(solution)/shard_map/ppermute | solution.py:34
  22.5 13.6 %collective-permute-start.3 = (bf16[3,192,128]{2,1,0:T(8,128)(2,1)S(1)}, bf16[3,192,128]{2,1,0:T(8,128)(2,1)S(1)}, u32[]{:S(2)}, u32[]{:S(2)}) collective-permute-start(bf16[3,192,128]{2,1,0:T(8,128)(2,1)S(1)} %get-tuple-element.60), channel_id=1, source_target_pairs={{0,16},{4,20},{8,24},{12,28},{16,0},{20,4},{24,8},{28,12},{1,17},{... | collective-permute-start | bytes 442376 | tf_op jit(solution)/shard_map/ppermute | solution.py:34
  25.1 11.0 %collective-permute-start.4 = (bf16[3,192,128]{2,1,0:T(8,128)(2,1)S(1)}, bf16[3,192,128]{2,1,0:T(8,128)(2,1)S(1)}, u32[]{:S(2)}, u32[]{:S(2)}) collective-permute-start(bf16[3,192,128]{2,1,0:T(8,128)(2,1)S(1)} %get-tuple-element.61), channel_id=1, source_target_pairs={{0,24},{4,28},{8,16},{12,20},{16,8},{20,12},{24,0},{28,4},{1,25},{... | collective-permute-start | bytes 442376 | tf_op jit(solution)/shard_map/ppermute | solution.py:34
  25.1 11.0 %collective-permute-start.5 = (bf16[3,192,128]{2,1,0:T(8,128)(2,1)S(1)}, bf16[3,192,128]{2,1,0:T(8,128)(2,1)S(1)}, u32[]{:S(2)}, u32[]{:S(2)}) collective-permute-start(bf16[3,192,128]{2,1,0:T(8,128)(2,1)S(1)} %get-tuple-element.58.refs_2_), channel_id=1, source_target_pairs={{0,4},{4,0},{8,12},{12,8},{16,20},{20,16},{24,28},{28,24},{1,5},{5... | collective-permute-start | bytes 442376 | tf_op jit(solution)/shard_map/ppermute | solution.py:34
  27.2 9.4 %collective-permute-start.10 = (bf16[192,128]{1,0:T(8,128)(2,1)S(1)}, bf16[192,128]{1,0:T(8,128)(2,1)S(1)}, u32[]{:S(2)}, u32[]{:S(2)}) collective-permute-start(bf16[192,128]{1,0:T(8,128)(2,1)S(1)} %get-tuple-element.67), channel_id=1, source_target_pairs={{0,8},{4,12},{8,0},{12,4},{16,24},{20,28},{24,16},{28,20},{1,9},{5... | collective-permute-start | bytes 147464 | tf_op jit(solution)/shard_map/ppermute | solution.py:34
  36.1 5.0 %collective-permute-start.11 = (bf16[192,128]{1,0:T(8,128)(2,1)S(1)}, bf16[192,128]{1,0:T(8,128)(2,1)S(1)}, u32[]{:S(2)}, u32[]{:S(2)}) collective-permute-start(bf16[192,128]{1,0:T(8,128)(2,1)S(1)} %get-tuple-element.68), channel_id=1, source_target_pairs={{0,16},{4,20},{8,24},{12,28},{16,0},{20,4},{24,8},{28,12},{1,17},{... | collective-permute-start | bytes 147464 | tf_op jit(solution)/shard_map/ppermute | solution.py:34
  36.1 11.4 %collective-permute-start.6 = (bf16[3,192,128]{2,1,0:T(8,128)(2,1)S(1)}, bf16[3,192,128]{2,1,0:T(8,128)(2,1)S(1)}, u32[]{:S(2)}, u32[]{:S(2)}) collective-permute-start(bf16[3,192,128]{2,1,0:T(8,128)(2,1)S(1)} %collective-permute-done.2.refs_3_), channel_id=1, source_target_pairs={{0,4},{4,0},{8,12},{12,8},{16,20},{20,16},{24,28},{28,24},{1,5},{5... | collective-permute-start | bytes 442376 | tf_op jit(solution)/shard_map/ppermute | solution.py:34
  36.1 11.4 %collective-permute-start.7 = (bf16[3,192,128]{2,1,0:T(8,128)(2,1)S(1)}, bf16[3,192,128]{2,1,0:T(8,128)(2,1)S(1)}, u32[]{:S(2)}, u32[]{:S(2)}) collective-permute-start(bf16[3,192,128]{2,1,0:T(8,128)(2,1)S(1)} %collective-permute-done.3.refs_4_), channel_id=1, source_target_pairs={{0,4},{4,0},{8,12},{12,8},{16,20},{20,16},{24,28},{28,24},{1,5},{5... | collective-permute-start | bytes 442376 | tf_op jit(solution)/shard_map/ppermute | solution.py:34
  36.6 10.9 %collective-permute-start.8 = (bf16[3,192,128]{2,1,0:T(8,128)(2,1)S(1)}, bf16[3,192,128]{2,1,0:T(8,128)(2,1)S(1)}, u32[]{:S(2)}, u32[]{:S(2)}) collective-permute-start(bf16[3,192,128]{2,1,0:T(8,128)(2,1)S(1)} %collective-permute-done.4.refs_5_), channel_id=1, source_target_pairs={{0,4},{4,0},{8,12},{12,8},{16,20},{20,16},{24,28},{28,24},{1,5},{5... | collective-permute-start | bytes 442376 | tf_op jit(solution)/shard_map/ppermute | solution.py:34
  41.1 5.9 %collective-permute-start.12 = (bf16[192,128]{1,0:T(8,128)(2,1)S(1)}, bf16[192,128]{1,0:T(8,128)(2,1)S(1)}, u32[]{:S(2)}, u32[]{:S(2)}) collective-permute-start(bf16[192,128]{1,0:T(8,128)(2,1)S(1)} %get-tuple-element.69), channel_id=1, source_target_pairs={{0,24},{4,28},{8,16},{12,20},{16,8},{20,12},{24,0},{28,4},{1,25},{... | collective-permute-start | bytes 147464 | tf_op jit(solution)/shard_map/ppermute | solution.py:34
  46.9 12.4 %collective-permute-start.18 = (bf16[8,112,256]{2,1,0:T(8,128)(2,1)S(1)}, bf16[8,112,256]{2,1,0:T(8,128)(2,1)S(1)}, u32[]{:S(2)}, u32[]{:S(2)}) collective-permute-start(bf16[8,112,256]{2,1,0:T(8,128)(2,1)S(1)} %get-tuple-element.79), channel_id=1, source_target_pairs={{0,1},{1,0},{2,3},{3,2},{4,5},{5,4},{6,7},{7,6},{8,9},{9,8},{10,11... | collective-permute-start | bytes 1376264 | tf_op jit(solution)/shard_map/ppermute | solution.py:34
  54.8 4.5 %collective-permute-start.17 = (bf16[4,2,192,128]{3,2,1,0:T(8,128)(2,1)S(1)}, bf16[4,2,192,128]{3,2,1,0:T(8,128)(2,1)S(1)}, u32[]{:S(2)}, u32[]{:S(2)}) collective-permute-start(bf16[4,2,192,128]{3,2,1,0:T(8,128)(2,1)S(1)} %get-tuple-element.78), channel_id=1, source_target_pairs={{0,4},{4,0},{8,12},{12,8},{16,20},{20,16},{24,28},{28,24},{1,5},{5... | collective-permute-start | bytes 1179656 | tf_op jit(solution)/shard_map/ppermute | solution.py:34
  54.8 6.7 %collective-permute-start.14 = (bf16[2,192,128]{2,1,0:T(8,128)(2,1)S(1)}, bf16[2,192,128]{2,1,0:T(8,128)(2,1)S(1)}, u32[]{:S(2)}, u32[]{:S(2)}) collective-permute-start(bf16[2,192,128]{2,1,0:T(8,128)(2,1)S(1)} %get-tuple-element.74), channel_id=1, source_target_pairs={{0,8},{4,12},{8,0},{12,4},{16,24},{20,28},{24,16},{28,20},{1,9},{5... | collective-permute-start | bytes 294920 | tf_op jit(solution)/shard_map/ppermute | solution.py:34
  54.9 10.8 %collective-permute-start.15 = (bf16[2,192,128]{2,1,0:T(8,128)(2,1)S(1)}, bf16[2,192,128]{2,1,0:T(8,128)(2,1)S(1)}, u32[]{:S(2)}, u32[]{:S(2)}) collective-permute-start(bf16[2,192,128]{2,1,0:T(8,128)(2,1)S(1)} %get-tuple-element.75), channel_id=1, source_target_pairs={{0,16},{4,20},{8,24},{12,28},{16,0},{20,4},{24,8},{28,12},{1,17},{... | collective-permute-start | bytes 294920 | tf_op jit(solution)/shard_map/ppermute | solution.py:34
  57.4 8.3 %collective-permute-start.16 = (bf16[2,192,128]{2,1,0:T(8,128)(2,1)S(1)}, bf16[2,192,128]{2,1,0:T(8,128)(2,1)S(1)}, u32[]{:S(2)}, u32[]{:S(2)}) collective-permute-start(bf16[2,192,128]{2,1,0:T(8,128)(2,1)S(1)} %get-tuple-element.76), channel_id=1, source_target_pairs={{0,24},{4,28},{8,16},{12,20},{16,8},{20,12},{24,0},{28,4},{1,25},{... | collective-permute-start | bytes 294920 | tf_op jit(solution)/shard_map/ppermute | solution.py:34
  59.3 24.4 %slice-start = ((s8[5505024]{0:T(1024)(128)(4,1)}), s8[4194304]{0:T(1024)(128)(4,1)S(1)}, s32[]{:S(2)}) async-start(s8[5505024]{0:T(1024)(128)(4,1)} %bitcast.14), calls=%async_computation | async-start | bytes 8388608
  66.1 13.7 %collective-permute-start.24 = (bf16[192,1024]{1,0:T(8,128)(2,1)S(1)}, bf16[192,1024]{1,0:T(8,128)(2,1)S(1)}, u32[]{:S(2)}, u32[]{:S(2)}) collective-permute-start(bf16[192,1024]{1,0:T(8,128)(2,1)S(1)} %query_back.1.refs_0_.refs_2_), channel_id=1, source_target_pairs={{0,1},{1,0},{2,3},{3,2},{4,5},{5,4},{6,7},{7,6},{8,9},{9,8},{10,11... | collective-permute-start | bytes 1179656 | tf_op jit(solution)/shard_map/ppermute | solution.py:34
  67.6 5.4 %collective-permute-start.20 = (bf16[2,192,128]{2,1,0:T(8,128)(2,1)S(1)}, bf16[2,192,128]{2,1,0:T(8,128)(2,1)S(1)}, u32[]{:S(2)}, u32[]{:S(2)}) collective-permute-start(bf16[2,192,128]{2,1,0:T(8,128)(2,1)S(1)} %get-tuple-element.83), channel_id=1, source_target_pairs={{0,8},{4,12},{8,0},{12,4},{16,24},{20,28},{24,16},{28,20},{1,9},{5... | collective-permute-start | bytes 294920 | tf_op jit(solution)/shard_map/ppermute | solution.py:34
  69.8 9.7 %collective-permute-start.21 = (bf16[2,192,128]{2,1,0:T(8,128)(2,1)S(1)}, bf16[2,192,128]{2,1,0:T(8,128)(2,1)S(1)}, u32[]{:S(2)}, u32[]{:S(2)}) collective-permute-start(bf16[2,192,128]{2,1,0:T(8,128)(2,1)S(1)} %get-tuple-element.84), channel_id=1, source_target_pairs={{0,16},{4,20},{8,24},{12,28},{16,0},{20,4},{24,8},{28,12},{1,17},{... | collective-permute-start | bytes 294920 | tf_op jit(solution)/shard_map/ppermute | solution.py:34
  70.2 9.2 %collective-permute-start.22 = (bf16[2,192,128]{2,1,0:T(8,128)(2,1)S(1)}, bf16[2,192,128]{2,1,0:T(8,128)(2,1)S(1)}, u32[]{:S(2)}, u32[]{:S(2)}) collective-permute-start(bf16[2,192,128]{2,1,0:T(8,128)(2,1)S(1)} %get-tuple-element.85), channel_id=1, source_target_pairs={{0,24},{4,28},{8,16},{12,20},{16,8},{20,12},{24,0},{28,4},{1,25},{... | collective-permute-start | bytes 294920 | tf_op jit(solution)/shard_map/ppermute | solution.py:34
  79.4 4.3 %slice-start.1 = ((s8[5505024]{0:T(1024)(128)(4,1)}), s8[1310720]{0:T(1024)(128)(4,1)S(1)}, s32[]{:S(2)}) async-start(s8[5505024]{0:T(1024)(128)(4,1)} %bitcast.14), calls=%async_computation.1 | async-start | bytes 2621440
  80.9 2.5 %collective-permute-start.25 = (bf16[4,112,1024]{2,1,0:T(8,128)(2,1)S(1)}, bf16[4,112,1024]{2,1,0:T(8,128)(2,1)S(1)}, u32[]{:S(2)}, u32[]{:S(2)}) collective-permute-start(bf16[4,112,1024]{2,1,0:T(8,128)(2,1)S(1)} %get-tuple-element.87.refs_2_), channel_id=1, source_target_pairs={{0,4},{4,0},{8,12},{12,8},{16,20},{20,16},{24,28},{28,24},{1,5},{5... | collective-permute-start | bytes 2752520 | tf_op jit(solution)/shard_map/ppermute | solution.py:34
  81.0 11.5 %collective-permute-start.23 = (bf16[192,1024]{1,0:T(8,128)(2,1)S(1)}, bf16[192,1024]{1,0:T(8,128)(2,1)S(1)}, u32[]{:S(2)}, u32[]{:S(2)}) collective-permute-start(bf16[192,1024]{1,0:T(8,128)(2,1)S(1)} %key_back.1.refs_6_.refs_1_.refs_0_), channel_id=1, source_target_pairs={{0,1},{1,0},{2,3},{3,2},{4,5},{5,4},{6,7},{7,6},{8,9},{9,8},{10,11... | collective-permute-start | bytes 1179656 | tf_op jit(solution)/shard_map/ppermute | solution.py:34
  93.6 2.5 %collective-permute-start.26 = (bf16[4,112,1024]{2,1,0:T(8,128)(2,1)S(1)}, bf16[4,112,1024]{2,1,0:T(8,128)(2,1)S(1)}, u32[]{:S(2)}, u32[]{:S(2)}) collective-permute-start(bf16[4,112,1024]{2,1,0:T(8,128)(2,1)S(1)} %get-tuple-element.91.refs_2_), channel_id=1, source_target_pairs={{0,4},{4,0},{8,12},{12,8},{16,20},{20,16},{24,28},{28,24},{1,5},{5... | collective-permute-start | bytes 2752520 | tf_op jit(solution)/shard_map/ppermute | solution.py:34
  93.7 13.4 %collective-permute-start.28 = (bf16[2,112,1024]{2,1,0:T(8,128)(2,1)S(1)}, bf16[2,112,1024]{2,1,0:T(8,128)(2,1)S(1)}, u32[]{:S(2)}, u32[]{:S(2)}) collective-permute-start(bf16[2,112,1024]{2,1,0:T(8,128)(2,1)S(1)} %get-tuple-element.89.refs_7_), channel_id=1, source_target_pairs={{0,8},{4,12},{8,0},{12,4},{16,24},{20,28},{24,16},{28,20},{1,9},{5... | collective-permute-start | bytes 1376264 | tf_op jit(solution)/shard_map/ppermute | solution.py:34
  96.4 25.0 %collective-permute-start.27 = (bf16[2,112,1024]{2,1,0:T(8,128)(2,1)S(1)}, bf16[2,112,1024]{2,1,0:T(8,128)(2,1)S(1)}, u32[]{:S(2)}, u32[]{:S(2)}) collective-permute-start(bf16[2,112,1024]{2,1,0:T(8,128)(2,1)S(1)} %get-tuple-element.93.refs_2_), channel_id=1, source_target_pairs={{0,8},{4,12},{8,0},{12,4},{16,24},{20,28},{24,16},{28,20},{1,9},{5... | collective-permute-start | bytes 1376264 | tf_op jit(solution)/shard_map/ppermute | solution.py:34
  98.3 24.3 %collective-permute-start.29 = (bf16[192,1024]{1,0:T(8,128)(2,1)S(1)}, bf16[192,1024]{1,0:T(8,128)(2,1)S(1)}, u32[]{:S(2)}, u32[]{:S(2)}) collective-permute-start(bf16[192,1024]{1,0:T(8,128)(2,1)S(1)} %get-tuple-element.99), channel_id=1, source_target_pairs={{0,2},{2,0},{1,3},{3,1},{4,6},{6,4},{5,7},{7,5},{8,10},{10,8},{9,1... | collective-permute-start | bytes 1179656 | tf_op jit(solution)/shard_map/ppermute | solution.py:34
  99.8 21.9 %collective-permute-start.19 = (bf16[192,896]{1,0:T(8,128)(2,1)S(1)}, bf16[192,896]{1,0:T(8,128)(2,1)S(1)}, u32[]{:S(2)}, u32[]{:S(2)}) collective-permute-start(bf16[192,896]{1,0:T(8,128)(2,1)S(1)} %get-tuple-element.82), channel_id=1, source_target_pairs={{0,2},{2,0},{1,3},{3,1},{4,6},{6,4},{5,7},{7,5},{8,10},{10,8},{9,1... | collective-permute-start | bytes 1032200 | tf_op jit(solution)/shard_map/ppermute | solution.py:34
  107.2 17.5 %collective-permute-start.30 = (bf16[1,112,1024]{2,1,0:T(8,128)(2,1)S(1)}, bf16[1,112,1024]{2,1,0:T(8,128)(2,1)S(1)}, u32[]{:S(2)}, u32[]{:S(2)}) collective-permute-start(bf16[1,112,1024]{2,1,0:T(8,128)(2,1)S(1)} %get-tuple-element.96.refs_2_), channel_id=1, source_target_pairs={{0,16},{4,20},{8,24},{12,28},{16,0},{20,4},{24,8},{28,12},{1,17},{... | collective-permute-start | bytes 688136 | tf_op jit(solution)/shard_map/ppermute | solution.py:34
  121.6 12.4 %collective-permute-start.31 = (bf16[1,112,1024]{2,1,0:T(8,128)(2,1)S(1)}, bf16[1,112,1024]{2,1,0:T(8,128)(2,1)S(1)}, u32[]{:S(2)}, u32[]{:S(2)}) collective-permute-start(bf16[1,112,1024]{2,1,0:T(8,128)(2,1)S(1)} %get-tuple-element.97.refs_4_), channel_id=1, source_target_pairs={{0,16},{4,20},{8,24},{12,28},{16,0},{20,4},{24,8},{28,12},{1,17},{... | collective-permute-start | bytes 688136 | tf_op jit(solution)/shard_map/ppermute | solution.py:34
  122.6 1.0 copy-start.3

commit v5 on v4

--- a/solution.py
+++ b/solution.py
@@ -15,9 +15,10 @@
 NO_GROUP = 1 << 30
 ATTENTION_MIB = 16
 COST = {}
-ORDER = ("share", "query", "mix", "key", "a", "a", "hidden", "b", "b", "a", "b", "mixed", "latents")
-SPLIT = False
+ORDER = ('share', 'query', 'mix', 'key', 'a', 'b', 'a', 'b', 'hidden', 'c', 'd', 'a', 'b', 'c', 'd', 'mixed', 'c', 'd', 'latents')
 LEFT_FIRST = True
+CORE_PIECES = 2
+CLIP_PIECES = {"a": 1, "b": 1, "c": 1, "d": 1}
 LIMITS = {"share": 1, "query_back": 1, "key_back": 1, "weight_total": 1}
 LANES = 128
 BF = jnp.bfloat16
@@ -240,13 +241,19 @@
     return [pieces[0]] + [swap(pieces[w], "dp", w) for w in range(1, clips)]
 
 
+def gather_kernel(heads, *refs):
+    out_ref = refs[heads]
+    for t in range(heads):
+        out_ref[t] = refs[t][1:]
+
+
 def attention_kernel(heads, sharers, rows, block, factor, *refs):
     key_group_ref, query_group_ref = refs[:2]
     at = 2
     own = refs[at : at + heads]
     at += heads
-    shared = refs[at : at + heads * (sharers - 1)]
-    at += heads * (sharers - 1)
+    shared = refs[at : at + sharers - 1]
+    at += sharers - 1
     ups = refs[at : at + heads]
     at += heads
     outs = refs[at : at + heads]
@@ -262,9 +269,9 @@
     for t in range(heads):
         m = head ^ t
         for u in range(1, sharers):
-            piece = shared[t * (sharers - 1) + u - 1]
-            copies.start(piece.at[1], key_s.at[m * sharers + (part ^ u)])
-            copies.start(piece.at[2], value_s.at[m * sharers + (part ^ u)])
+            piece = shared[u - 1].at[t]
+            copies.start(piece.at[0], key_s.at[m * sharers + (part ^ u)])
+            copies.start(piece.at[1], value_s.at[m * sharers + (part ^ u)])
         if t:
             copies.start(own[t].at[0], query_s.at[m])
             copies.start(own[t].at[1], key_s.at[m * sharers + part])
@@ -332,7 +339,7 @@
 
 def attention(key_group, query_group, own, shared, ups, after):
     heads = len(own)
-    sharers = len(shared) // heads + 1
+    sharers = len(shared) + 1
     rows, width = ups[0].shape
     span = heads * sharers * rows
     total = heads * rows
@@ -356,7 +363,7 @@
         12 * total * span * width,
         after,
         [VMEM] * 3
-        + [HBM] * (heads - 1 + heads * (sharers - 1))
+        + [HBM] * (heads - 1 + sharers - 1)
         + [VMEM]
         + [HBM] * (heads - 1),
         2 * heads * (sharers - 1) + 4 * (heads - 1),
@@ -373,26 +380,28 @@
         ref[...] = total.astype(BF)
 
 
-def query_kernel(heads, *refs):
+def query_kernel(heads, parts, *refs):
     gain_ref, raw_ref = refs[:2]
-    pieces, pair_ref = refs[2 : 2 + heads], refs[2 + heads]
+    pieces, outs = refs[2 : 2 + heads], refs[2 + heads :]
+    row_refs, grad_refs = outs[:parts], outs[parts:]
     inner = raw_ref.shape[-1]
     dim = inner // heads
     head, _ = head_place(heads)
     for t in range(heads):
         own = head ^ t
-        pair_ref[:, columns_of(own, dim)] = pieces[t][0]
+        write_pieces(row_refs, own, pieces[t][0])
         grad = norm_back(
             raw_ref[0, :, columns_of(own, dim)],
             gain_ref[pl.ds(own, 1), :],
             pieces[t][1].astype(F32),
         )
-        pair_ref[:, columns_of(heads + own, dim)] = grad.astype(BF)
-
-
-def key_kernel(heads, *refs):
+        write_pieces(grad_refs, own, grad.astype(BF))
+
+
+def key_kernel(heads, parts, *refs):
     gain_ref, raw_ref = refs[:2]
-    pieces, pair_ref = refs[2 : 2 + heads], refs[2 + heads]
+    pieces, outs = refs[2 : 2 + heads], refs[2 + heads :]
+    key_refs, value_refs = outs[:parts], outs[parts:]
     inner = raw_ref.shape[-1]
     dim = inner // heads
     head, _ = head_place(heads)
@@ -403,29 +412,35 @@
             gain_ref[pl.ds(own, 1), :],
             pieces[t][0].astype(F32),
         )
-        pair_ref[:, columns_of(own, dim)] = grad.astype(BF)
-        pair_ref[:, columns_of(heads + own, dim)] = pieces[t][1]
-
-
-def mix_kernel(rows_ref, weight_ref, *refs):
-    whole_s = refs[-1]
-    inner = weight_ref.shape[0]
-    whole_s[...] = jnp.dot(rows_ref[:, :inner], weight_ref[...], preferred_element_type=F32)
-    write_width(whole_s, refs[:-1])
-
-
-def hidden_kernel(width_count, *refs):
-    first_ref, second_ref, weight_ref, mod_ref, inv_ref = refs[:5]
-    inputs = refs[5 : 5 + width_count]
-    dot_ref = refs[5 + width_count]
-    outs = refs[6 + width_count : -4]
+        write_pieces(key_refs, own, grad.astype(BF))
+        write_pieces(value_refs, own, pieces[t][1])
+
+
+def join_columns(refs):
+    return jnp.concatenate([ref[...] for ref in refs], axis=1)
+
+
+def mix_kernel(parts, *refs):
+    rows, weight_ref, whole_s = refs[:parts], refs[parts], refs[-1]
+    whole_s[...] = jnp.dot(join_columns(rows), weight_ref[...], preferred_element_type=F32)
+    write_width(whole_s, refs[parts + 1 : -1])
+
+
+def hidden_kernel(width_count, parts, *refs):
+    grads = []
+    for part in parts:
+        grads.append(join_columns(refs[:part]))
+        refs = refs[part:]
+    refs = (None,) * 3 + refs
+    weight_ref, mod_ref, inv_ref = refs[3:6]
+    inputs = refs[6 : 6 + width_count]
+    dot_ref = refs[6 + width_count]
+    outs = refs[7 + width_count : -4]
     whole_s, inputs_s, weight_s, sems = refs[-4:]
     copies = Copies(sems)
     for at in range(3):
         copies.start(weight_ref.at[at], weight_s.at[at])
     spread(inputs, inputs_s)
-    inner = weight_ref.shape[2]
-    grads = (first_ref[:, inner:], second_ref[:, :inner], second_ref[:, inner:])
     total = 0.0
     for at, grad in enumerate(grads):
         copies.made[at].wait()
@@ -448,77 +463,99 @@
         ref[:, outs[0].shape[1] :] = beside.astype(BF)
 
 
-def halve(total, step, send_ref, keep_ref):
+def halve(total, step, sends, keep_ref):
     odd = (lax.axis_index("seq") // step) % 2 == 1
+    each = sends[0].shape[0]
     for b in range(total.shape[0] // 2):
         first, second = total[2 * b], total[2 * b + 1]
         keep_ref[b] = jnp.where(odd, second, first)
-        send_ref[b] = jnp.where(odd, first, second).astype(BF)
-
-
-def outer_kernel(clips, *refs):
-    rights, (send_ref, keep_ref, total_s) = refs[:clips], refs[-3:]
-    lefts = refs[clips:-3]
+        sends[b // each][b % each] = jnp.where(odd, first, second).astype(BF)
+
+
+def outer_kernel(clips, pieces, parts, *refs):
+    rights, lefts = refs[: clips * pieces], refs[clips * pieces : clips * pieces + clips]
+    sends, (keep_ref, total_s) = refs[-2 - parts : -2], refs[-2:]
     blocks, span, lanes = lefts[0].shape
     rows, width = rights[0].shape
-    groups = len(lefts) // clips
-    width = width // groups
-    for at in range(groups):
-        columns = slice(at * width, (at + 1) * width)
+    for at in range(pieces):
         total = 0.0
-        for left, right in zip(lefts[at * clips : (at + 1) * clips], rights):
+        for w, left in enumerate(lefts):
             left = left[...].reshape(blocks * span, lanes)[:, :rows]
-            total = total + jnp.dot(left, right[:, columns], preferred_element_type=F32)
-        total_s[:, :, columns] = total.reshape(blocks, span, width)
-    halve(total_s, 1, send_ref, keep_ref)
-
-
-def step_kernel(step, got_ref, kept_ref, send_ref, keep_ref):
-    halve(kept_ref[...] + got_ref[...].astype(F32), step, send_ref, keep_ref)
-
-
-def halves(blocks, span, width):
-    return [((blocks // 2, span, width), BF), ((blocks // 2, span, width), F32)]
+            right = rights[w * pieces + at][...]
+            total = total + jnp.dot(left, right, preferred_element_type=F32)
+        total_s[:, :, at * width : (at + 1) * width] = total.reshape(blocks, span, width)
+    halve(total_s, 1, sends, keep_ref)
+
+
+def step_kernel(step, parts, *refs):
+    gots, (kept_ref, send_ref, keep_ref) = refs[:parts], refs[parts:]
+    got = jnp.concatenate([ref[...].astype(F32) for ref in gots], axis=0)
+    halve(kept_ref[...] + got, step, [send_ref], keep_ref)
+
+
+def halves(blocks, span, width, parts=1):
+    send = (blocks // 2 // parts, span, width)
+    return [(send, BF)] * parts + [((blocks // 2, span, width), F32)]
+
+
+def clip_pieces(name, width):
+    return CLIP_PIECES[name] if width % (CLIP_PIECES[name] * LANES) == 0 else 1
+
+
+def write_pieces(pieces, place, value):
+    width, dim = pieces[0].shape[1], value.shape[1]
+    each = width // dim
+    for at, piece in enumerate(pieces):
+        if len(pieces) == 1:
+            piece[:, columns_of(place, dim)] = value
+        else:
+
+            @pl.when(place // each == at)
+            def _(piece=piece):
+                piece[:, columns_of(place % each, dim)] = value
 
 
 class WeightSum:
-    def __init__(self, name, lefts, right):
-        self.name = name
-        far = [swap(right, "dp", w) for w in range(1, lax.axis_size("dp"))]
-        self.rights = [right] + far
+    def __init__(self, name, lefts, rights):
+        self.name, self.pieces = name, len(rights)
+        self.rights = list(rights)
+        for w in range(1, lax.axis_size("dp")):
+            self.rights.extend(swap(right, "dp", w) for right in rights)
         self.lefts, self.step = lefts, 1
 
     def outer(self, after):
         blocks, span, _ = self.lefts[0].shape
         rows, width = self.rights[0].shape
-        self.send, self.keep = call(
-            functools.partial(outer_kernel, len(self.rights)),
+        width = width * self.pieces
+        parts = min(CORE_PIECES, blocks // 2)
+        *self.sends, self.keep = call(
+            functools.partial(outer_kernel, len(self.lefts), self.pieces, parts),
             "weight_sum_" + self.name,
-            halves(blocks, span, width),
+            halves(blocks, span, width, parts),
             [*self.rights, *self.lefts],
             [((blocks, span, width), F32)],
             12,
             2 * blocks * span * rows * width * len(self.rights),
             after,
         )
-        return [self.send]
+        return [self.sends[0]]
 
     def exchange(self):
-        self.got = swap(self.send, "seq", self.step)
+        self.gots = [swap(send, "seq", self.step) for send in self.sends]
         self.step *= 2
 
     def halve(self, after):
-        self.send, self.keep = call(
-            functools.partial(step_kernel, self.step),
-            "weight_step_" + self.name,
+        *self.sends, self.keep = call(
+            functools.partial(step_kernel, self.step, len(self.gots)),
+            "weight_step_%s%d" % (self.name, self.step),
             halves(*self.keep.shape),
-            [self.got, self.keep],
+            [*self.gots, self.keep],
             [],
             4,
             1 << 22,
             after,
         )
-        return [self.send]
+        return [self.sends[0]]
 
 
 def total_kernel(*refs):
@@ -663,7 +700,16 @@
     )
     own, (hidden, raw, inv_norm) = got[:heads], got[heads:]
     own = [own[0]] + [swap(own[t], "seq", t * sharers) for t in range(1, heads)]
-    shared = [swap(own[t], "seq", u) for t in range(heads) for u in range(1, sharers)]
+    (keys_values,) = call(
+        functools.partial(gather_kernel, heads),
+        "gather",
+        [((heads, 2, rows, head_dim), BF)],
+        own,
+        [],
+        2,
+        0,
+    )
+    shared = [swap(keys_values, "seq", u) for u in range(1, sharers)]
 
     left_hidden = turned(hidden, [])
     got = call(
@@ -685,6 +731,18 @@
     pair = (2, rows, head_dim)
     back_out = [outs[0]] + [swap(outs[t], "seq", t * sharers) for t in range(1, heads)]
     state = {}
+
+    def cut(names, made):
+        first = clip_pieces(names[0], inner)
+        return made[:first], made[first:]
+
+    def pair_outs(names):
+        outs = []
+        for name in names:
+            pieces = clip_pieces(name, inner)
+            outs.extend([((rows, inner // pieces), BF)] * pieces)
+        return outs
+
 
     def share(after):
         sums = call(
@@ -703,25 +761,27 @@
         return sums[:1]
 
     def query(after):
-        state["first"] = call(
-            functools.partial(query_kernel, heads),
+        made = call(
+            functools.partial(query_kernel, heads, clip_pieces("a", inner)),
             "query_back",
-            [((rows, 2 * inner), BF)],
+            pair_outs("ab"),
             [q_gain, raw, *back_out],
             [],
             4,
             1 << 24,
             after,
-        )[0]
-        state["a"] = WeightSum("a", left_grad + left_hidden, state["first"])
-        return [state["first"]]
+        )
+        state["rows"], state["query"] = cut("ab", made)
+        state["a"] = WeightSum("a", left_grad, state["rows"])
+        state["b"] = WeightSum("b", left_hidden, state["query"])
+        return made[:1]
 
     def mix(after):
         state["parts"] = call(
-            mix_kernel,
+            functools.partial(mix_kernel, len(state["rows"])),
             "mix",
             width_outs(rows, model_width, width_part),
-            [state["first"], w_out],
+            [*state["rows"], w_out],
             [((rows, model_width), F32)],
             8,
             2 * rows * model_width * inner,
@@ -730,22 +790,20 @@
         return state["parts"][:1]
 
     def key(after):
-        state["second"] = call(
-            functools.partial(key_kernel, heads),
+        made = call(
+            functools.partial(key_kernel, heads, clip_pieces("c", inner)),
             "key_back",
-            [((rows, 2 * inner), BF)],
+            pair_outs("cd"),
             [k_gain, raw, *state["back_key"]],
             [],
             4,
             1 << 24,
             after,
-        )[0]
-        if SPLIT:
-            state["b"] = WeightSum("b", left_hidden, state["second"][:, :inner])
-            state["c"] = WeightSum("c", left_hidden, state["second"][:, inner:])
-        else:
-            state["b"] = WeightSum("b", left_hidden, state["second"])
-        return [state["second"]]
+        )
+        state["key"], state["value"] = cut("cd", made)
+        state["c"] = WeightSum("c", left_hidden, state["key"])
+        state["d"] = WeightSum("d", left_hidden, state["value"])
+        return made[:1]
 
     def advance(name, after):
         total = state[name]
@@ -754,11 +812,12 @@
         return token
 
     def hidden_back(after):
+        grads = [state[name] for name in ("query", "key", "value")]
         got = call(
-            functools.partial(hidden_kernel, width_count),
+            functools.partial(hidden_kernel, width_count, [len(g) for g in grads]),
             "hidden_back",
             [((rows, 1), F32)] + width_outs(rows, model_width, width_part, LANES),
-            [state["first"], state["second"], weight_far, mod, inv_norm, *inputs],
+            [*sum(grads, []), weight_far, mod, inv_norm, *inputs],
             [
                 ((rows, model_width), F32),
                 ((rows, model_width), BF),
@@ -767,7 +826,7 @@
             10,
             6 * rows * model_width * inner,
             after,
-            [VMEM] * 2 + [HBM] + [VMEM] * (2 + width_count),
+            [VMEM] * sum(len(g) for g in grads) + [HBM] + [VMEM] * (2 + width_count),
             3,
         )
         state["dot"], state["hidden"] = got[0], got[1:]
@@ -783,22 +842,23 @@
         return token
 
     steps = dict(share=share, query=query, mix=mix, key=key, hidden=hidden_back)
-    for name in ("a", "b", "c"):
+    for name in "abcd":
         steps[name] = functools.partial(advance, name)
     for name in ("mixed", "latents"):
         steps[name] = functools.partial(finish, name)
     token = ()
     for name in ORDER:
         token = steps[name](token)
-    totals = [state[name] for name in (("a", "b", "c") if SPLIT else ("a", "b"))]
-    while totals[-1].keep.shape[0] > 1:
+    totals = [state[name] for name in "abcd"]
+    while max(total.keep.shape[0] for total in totals) > 1:
         for total in totals:
-            token = total.halve(token)
-            total.exchange()
+            if total.keep.shape[0] == max(other.keep.shape[0] for other in totals):
+                token = total.halve(token)
+                total.exchange()
     span = totals[0].keep.shape[1]
     pieces = []
     for total in totals:
-        pieces.extend([total.got, total.keep])
+        pieces.extend([total.gots[0], total.keep])
     grad_wqkv, grad_wout = call(
         total_kernel,
         "weight_total",

time: 135 us -> 125 us (0.926)
  waiting for transfers between devices: 65.4 us -> 42.8 us
  starting transfers between devices: 37.9 us -> 50.2 us
    ppermute x31 -> x40, waiting for transfers between devices: 65.4 us -> 42.8 us  [swap(): return lax.ppermute(value, axis, [(i, i ^ distance) for i in range(count)])]
    ppermute x31 -> x40, starting transfers between devices: 35.5 us -> 47.8 us  [swap(): return lax.ppermute(value, axis, [(i, i ^ distance) for i in range(count)])]
    pallas_call x20 -> x27, Pallas kernels: 21.9 us -> 22.2 us  [call(): pl.pallas_call(body, out_shape=[jax.ShapeDtypeStruct(*o) for o in out], i...]
  transfers between devices with their start and end apart: 32 -> 41, of which waited for: 15 -> 16; matrix products, arithmetic and copies ran while one was open for 3% -> 3% of each run, Pallas kernels for 14% -> 15%
where the time goes in v5:
time: 125 us
  starting transfers between devices  50.2 us (40%)
  waiting for transfers between devices  42.8 us (34%)
  Pallas kernels  22.2 us (18%)
  local copies, waits for them, and re-layouts  4.77 us (4%)
  matrix products  1.96 us (2%)
  between operations  1.62 us (1%)
  other arithmetic  1.4 us (1%)
    ppermute x40, starting transfers between devices, swap(): return lax.ppermute(value, axis, [(i, i ^ distance) for i in range(count)])  47.8 us
    ppermute x40, waiting for transfers between devices, swap(): return lax.ppermute(value, axis, [(i, i ^ distance) for i in range(count)])  42.8 us
    pallas_call x27, Pallas kernels, call(): pl.pallas_call(body, out_shape=[jax.ShapeDtypeStruct(*o) for o in out], i...  22.2 us
    unnamed x18, local copies, waits for them, and re-layouts  3.56 us
  transfers between devices with their start and end apart: 41, of which 16 were waited for; matrix products, arithmetic and copies ran while one was open for 3% of the time, Pallas kernels for 15%

profile of v5, /device:TPU:0, one launch (start us, length us, event | category | flops | bytes accessed | tf_op | source)
XLA Modules:
  0.0 125.0 jit_solution(17524729842290635975)
XLA Ops:
  0.6 1.0 slice_bitcast_fusion
  1.7 2.4 %collective-permute-start = (bf16[32,3584]{1,0:T(8,128)(2,1)S(1)}, bf16[32,3584]{1,0:T(8,128)(2,1)S(1)}, u32[]{:S(2)}, u32[]{:S(2)}) collective-permute-start(bf16[32,3584]{1,0:T(8,128)(2,1)S(1)} %slice_bitcast_fusion), channel_id=1, source_target_pairs={{0,4},{4,8},{8,12},{12,16},{16,20},{20,24},{24,28},{1,5},{5,9},{9,... | collective-permute-start | bytes 688136 | tf_op jit(solution)/shard_map/ppermute | solution.py:664
  4.0 2.4 %collective-permute-start.1 = (bf16[192,896]{1,0:T(8,128)(2,1)}, bf16[192,896]{1,0:T(8,128)(2,1)S(1)}, u32[]{:S(2)}, u32[]{:S(2)}) collective-permute-start(bf16[192,896]{1,0:T(8,128)(2,1)} %bitcast.17), channel_id=1, source_target_pairs={{0,2},{2,0},{1,3},{3,1},{4,6},{6,4},{5,7},{7,5},{8,10},{10,8},{9,1... | collective-permute-start | bytes 1032200 | tf_op jit(solution)/shard_map/ppermute | solution.py:35
  7.1 0.7 fusion.5
  7.8 0.7 broadcast_subtract_fusion
  8.7 2.0 %convolution_convert_fusion.refs_5_.refs_3_.refs_1_.refs_4_.refs_2_ = bf16[192,3584]{1,0:T(8,128)(2,1)S(1)} fusion(bf16[150,3584]{1,0:T(8,128)(2,1)} %bitcast.25, bf16[32,3584]{1,0:T(8,128)(2,1)S(1)} %collective-permute-done, s32[192]{0:T(256)S(1)} %bitcast.26), kind=kOutput, calls=%fused_computation | convolution fusion | flops 253810816 | bytes 2681600 | tf_op jit(solution)/shard_map/dot_general | solution.py:672
  10.7 2.6 %copy-done = bf16[1792,3,512]{2,0,1:T(8,128)(2,1)S(1)} copy-done((bf16[1792,3,512]{2,0,1:T(8,128)(2,1)S(1)}, bf16[1792,3,512]{2,0,1:T(8,128)(2,1)}, u32[]{:S(2)}) %copy-start) | copy-done | bytes 5505048
  13.3 0.7 stage.1
  14.4 1.7 %project.1 = (bf16[3,192,128]{2,1,0:T(8,128)(2,1)S(1)}, bf16[3,192,128]{2,1,0:T(8,128)(2,1)S(1)}, bf16[3,192,128]{2,1,0:T(8,128)(2,1)S(1)}, bf16[3,192,128]{2,1,...) custom-call(f32[4,128]{1,0:T(4,128)S(1)} %copy-done.5, ...), custom_call_target="tpu_custom_call" | custom-call | bytes 1024 | tf_op jit(solution)/shard_map/project/pallas_call | solution.py:77
  16.0 3.3 %collective-permute-start.2 = (bf16[3,192,128]{2,1,0:T(8,128)(2,1)S(1)}, bf16[3,192,128]{2,1,0:T(8,128)(2,1)S(1)}, u32[]{:S(2)}, u32[]{:S(2)}) collective-permute-start(bf16[3,192,128]{2,1,0:T(8,128)(2,1)S(1)} %get-tuple-element.79), channel_id=1, source_target_pairs={{0,8},{4,12},{8,0},{12,4},{16,24},{20,28},{24,16},{28,20},{1,9},{5... | collective-permute-start | bytes 442376 | tf_op jit(solution)/shard_map/ppermute | solution.py:35
  19.3 2.6 %collective-permute-start.3 = (bf16[3,192,128]{2,1,0:T(8,128)(2,1)S(1)}, bf16[3,192,128]{2,1,0:T(8,128)(2,1)S(1)}, u32[]{:S(2)}, u32[]{:S(2)}) collective-permute-start(bf16[3,192,128]{2,1,0:T(8,128)(2,1)S(1)} %get-tuple-element.80), channel_id=1, source_target_pairs={{0,16},{4,20},{8,24},{12,28},{16,0},{20,4},{24,8},{28,12},{1,17},{... | collective-permute-start | bytes 442376 | tf_op jit(solution)/shard_map/ppermute | solution.py:35
  21.9 0.5 turn.2
  22.4 1.5 %collective-permute-start.10 = (bf16[8,112,256]{2,1,0:T(8,128)(2,1)S(1)}, bf16[8,112,256]{2,1,0:T(8,128)(2,1)S(1)}, u32[]{:S(2)}, u32[]{:S(2)}) collective-permute-start(bf16[8,112,256]{2,1,0:T(8,128)(2,1)S(1)} %get-tuple-element.90), channel_id=1, source_target_pairs={{0,1},{1,0},{2,3},{3,2},{4,5},{5,4},{6,7},{7,6},{8,9},{9,8},{10,11... | collective-permute-start | bytes 1376264 | tf_op jit(solution)/shard_map/ppermute | solution.py:35
  23.9 1.5 %collective-permute-start.6 = (bf16[192,896]{1,0:T(8,128)(2,1)S(1)}, bf16[192,896]{1,0:T(8,128)(2,1)S(1)}, u32[]{:S(2)}, u32[]{:S(2)}) collective-permute-start(bf16[192,896]{1,0:T(8,128)(2,1)S(1)} %get-tuple-element.83.refs_2_.refs_1_), channel_id=1, source_target_pairs={{0,2},{2,0},{1,3},{3,1},{4,6},{6,4},{5,7},{7,5},{8,10},{10,8},{9,1... | collective-permute-start | bytes 1032200 | tf_op jit(solution)/shard_map/ppermute | solution.py:35
  25.7 7.6 %collective-permute-done.3.refs_2_.refs_4_ = bf16[3,192,128]{2,1,0:T(8,128)(2,1)S(1)} collective-permute-done((bf16[3,192,128]{2,1,0:T(8,128)(2,1)S(1)}, bf16[3,192,128]{2,1,0:T(8,128)(2,1)S(1)}, u32[]{:S(2)}, u32[]{:S(2)}) %collective-permute-start.3) | collective-permute-done | bytes 147488 | tf_op jit(solution)/shard_map/ppermute | solution.py:35
  33.4 0.8 upstream.1
  34.2 2.6 %collective-permute-start.7 = (bf16[192,128]{1,0:T(8,128)(2,1)S(1)}, bf16[192,128]{1,0:T(8,128)(2,1)S(1)}, u32[]{:S(2)}, u32[]{:S(2)}) collective-permute-start(bf16[192,128]{1,0:T(8,128)(2,1)S(1)} %get-tuple-element.87), channel_id=1, source_target_pairs={{0,8},{4,12},{8,0},{12,4},{16,24},{20,28},{24,16},{28,20},{1,9},{5... | collective-permute-start | bytes 147464 | tf_op jit(solution)/shard_map/ppermute | solution.py:35
  36.8 0.5 turn.3
  37.3 1.6 %collective-permute-start.15 = (bf16[8,112,256]{2,1,0:T(8,128)(2,1)S(1)}, bf16[8,112,256]{2,1,0:T(8,128)(2,1)S(1)}, u32[]{:S(2)}, u32[]{:S(2)}) collective-permute-start(bf16[8,112,256]{2,1,0:T(8,128)(2,1)S(1)} %get-tuple-element.99), channel_id=1, source_target_pairs={{0,1},{1,0},{2,3},{3,2},{4,5},{5,4},{6,7},{7,6},{8,9},{9,8},{10,11... | collective-permute-start | bytes 1376264 | tf_op jit(solution)/shard_map/ppermute | solution.py:35
  38.9 1.0 collective-permute-start.8
  39.9 1.8 %collective-permute-start.9 = (bf16[192,128]{1,0:T(8,128)(2,1)S(1)}, bf16[192,128]{1,0:T(8,128)(2,1)S(1)}, u32[]{:S(2)}, u32[]{:S(2)}) collective-permute-start(bf16[192,128]{1,0:T(8,128)(2,1)S(1)} %get-tuple-element.89), channel_id=1, source_target_pairs={{0,24},{4,28},{8,16},{12,20},{16,8},{20,12},{24,0},{28,4},{1,25},{... | collective-permute-start | bytes 147464 | tf_op jit(solution)/shard_map/ppermute | solution.py:35
  41.7 3.3 %collective-permute-done.8.refs_9_ = bf16[192,128]{1,0:T(8,128)(2,1)S(1)} collective-permute-done((bf16[192,128]{1,0:T(8,128)(2,1)S(1)}, bf16[192,128]{1,0:T(8,128)(2,1)S(1)}, u32[]{:S(2)}, u32[]{:S(2)}) %collective-permute-start.8) | collective-permute-done | bytes 49184 | tf_op jit(solution)/shard_map/ppermute | solution.py:35
  45.0 0.9 collective-permute-done.9.refs_10_
  45.9 7.1 %attention.1 = (bf16[2,192,128]{2,1,0:T(8,128)(2,1)S(1)}, bf16[2,192,128]{2,1,0:T(8,128)(2,1)S(1)}, bf16[2,192,128]{2,1,0:T(8,128)(2,1)S(1)}, bf16[2,192,128]{2,...) custom-call(s32[1,1536]{1,0:T(1,128)S(1)} %get-tuple-element.76.refs_0_, ...), custom_call_target="tpu_custom_call" | custom-call | bytes 1024 | tf_op jit(solution)/shard_map/attention/pallas_call | solution.py:77
  53.1 1.1 collective-permute-start.11
  54.2 1.6 %collective-permute-start.12 = (bf16[2,192,128]{2,1,0:T(8,128)(2,1)S(1)}, bf16[2,192,128]{2,1,0:T(8,128)(2,1)S(1)}, u32[]{:S(2)}, u32[]{:S(2)}) collective-permute-start(bf16[2,192,128]{2,1,0:T(8,128)(2,1)S(1)} %get-tuple-element.95), channel_id=1, source_target_pairs={{0,16},{4,20},{8,24},{12,28},{16,0},{20,4},{24,8},{28,12},{1,17},{... | collective-permute-start | bytes 294920 | tf_op jit(solution)/shard_map/ppermute | solution.py:35
  55.8 1.7 %collective-permute-start.13 = (bf16[2,192,128]{2,1,0:T(8,128)(2,1)S(1)}, bf16[2,192,128]{2,1,0:T(8,128)(2,1)S(1)}, u32[]{:S(2)}, u32[]{:S(2)}) collective-permute-start(bf16[2,192,128]{2,1,0:T(8,128)(2,1)S(1)} %get-tuple-element.96), channel_id=1, source_target_pairs={{0,24},{4,28},{8,16},{12,20},{16,8},{20,12},{24,0},{28,4},{1,25},{... | collective-permute-start | bytes 294920 | tf_op jit(solution)/shard_map/ppermute | solution.py:35
  57.6 2.1 %collective-permute-done.11.refs_3_ = bf16[2,192,128]{2,1,0:T(8,128)(2,1)S(1)} collective-permute-done((bf16[2,192,128]{2,1,0:T(8,128)(2,1)S(1)}, bf16[2,192,128]{2,1,0:T(8,128)(2,1)S(1)}, u32[]{:S(2)}, u32[]{:S(2)}) %collective-permute-start.11) | collective-permute-done | bytes 98336 | tf_op jit(solution)/shard_map/ppermute | solution.py:35
  59.7 5.2 %collective-permute-done.12.refs_4_ = bf16[2,192,128]{2,1,0:T(8,128)(2,1)S(1)} collective-permute-done((bf16[2,192,128]{2,1,0:T(8,128)(2,1)S(1)}, bf16[2,192,128]{2,1,0:T(8,128)(2,1)S(1)}, u32[]{:S(2)}, u32[]{:S(2)}) %collective-permute-start.12) | collective-permute-done | bytes 98336 | tf_op jit(solution)/shard_map/ppermute | solution.py:35
  65.3 0.7 collective-permute-start.23
  66.0 1.9 %collective-permute-start.17 = (bf16[2,192,128]{2,1,0:T(8,128)(2,1)S(1)}, bf16[2,192,128]{2,1,0:T(8,128)(2,1)S(1)}, u32[]{:S(2)}, u32[]{:S(2)}) collective-permute-start(bf16[2,192,128]{2,1,0:T(8,128)(2,1)S(1)} %get-tuple-element.104), channel_id=1, source_target_pairs={{0,8},{4,12},{8,0},{12,4},{16,24},{20,28},{24,16},{28,20},{1,9},{5... | collective-permute-start | bytes 294920 | tf_op jit(solution)/shard_map/ppermute | solution.py:35
  67.9 0.9 collective-permute-start.18
  68.8 1.6 %collective-permute-start.19 = (bf16[2,192,128]{2,1,0:T(8,128)(2,1)S(1)}, bf16[2,192,128]{2,1,0:T(8,128)(2,1)S(1)}, u32[]{:S(2)}, u32[]{:S(2)}) collective-permute-start(bf16[2,192,128]{2,1,0:T(8,128)(2,1)S(1)} %get-tuple-element.106), channel_id=1, source_target_pairs={{0,24},{4,28},{8,16},{12,20},{16,8},{20,12},{24,0},{28,4},{1,25},{... | collective-permute-start | bytes 294920 | tf_op jit(solution)/shard_map/ppermute | solution.py:35
  70.4 1.4 %collective-permute-start.22 = (bf16[192,512]{1,0:T(8,128)(2,1)S(1)}, bf16[192,512]{1,0:T(8,128)(2,1)S(1)}, u32[]{:S(2)}, u32[]{:S(2)}) collective-permute-start(bf16[192,512]{1,0:T(8,128)(2,1)S(1)} %get-tuple-element.109.refs_0_), channel_id=1, source_target_pairs={{0,1},{1,0},{2,3},{3,2},{4,5},{5,4},{6,7},{7,6},{8,9},{9,8},{10,11... | collective-permute-start | bytes 589832 | tf_op jit(solution)/shard_map/ppermute | solution.py:35
  71.8 0.6 mix.1
  72.4 5.1 %collective-permute-done.18.refs_4_ = bf16[2,192,128]{2,1,0:T(8,128)(2,1)S(1)} collective-permute-done((bf16[2,192,128]{2,1,0:T(8,128)(2,1)S(1)}, bf16[2,192,128]{2,1,0:T(8,128)(2,1)S(1)}, u32[]{:S(2)}, u32[]{:S(2)}) %collective-permute-start.18) | collective-permute-done | bytes 98336 | tf_op jit(solution)/shard_map/ppermute | solution.py:35
  77.8 0.6 weight_sum_a.1
  78.5 0.5 collective-permute-start.26
  79.0 0.6 weight_sum_b.1
  80.3 1.4 %collective-permute-start.21 = (bf16[192,512]{1,0:T(8,128)(2,1)S(1)}, bf16[192,512]{1,0:T(8,128)(2,1)S(1)}, u32[]{:S(2)}, u32[]{:S(2)}) collective-permute-start(bf16[192,512]{1,0:T(8,128)(2,1)S(1)} %get-tuple-element.108.refs_4_.refs_1_.refs_0_), channel_id=1, source_target_pairs={{0,1},{1,0},{2,3},{3,2},{4,5},{5,4},{6,7},{7,6},{8,9},{9,8},{10,11... | collective-permute-start | bytes 589832 | tf_op jit(solution)/shard_map/ppermute | solution.py:35
  81.8 1.7 %collective-permute-start.33 = (bf16[2,112,512]{2,1,0:T(8,128)(2,1)S(1)}, bf16[2,112,512]{2,1,0:T(8,128)(2,1)S(1)}, u32[]{:S(2)}, u32[]{:S(2)}) collective-permute-start(bf16[2,112,512]{2,1,0:T(8,128)(2,1)S(1)} %get-tuple-element.117.refs_3_), channel_id=1, source_target_pairs={{0,8},{4,12},{8,0},{12,4},{16,24},{20,28},{24,16},{28,20},{1,9},{5... | collective-permute-start | bytes 688136 | tf_op jit(solution)/shard_map/ppermute | solution.py:35
  83.5 0.6 collective-permute-start.20
  84.7 3.3 %hidden_back.1 = (f32[192,1]{1,0:T(8,128)S(1)}, f32[192,896]{1,0:T(8,128)S(1)}, bf16[192,1024]{1,0:T(8,128)(2,1)S(1)}) custom-call(bf16[192,512]{1,0:T(8,128)(2,1)S(1)} %get-tuple-element.109.refs_0_, bf16[192,512]{1,0:T(8,128)(2,1)S(1)} %get-tuple-element.108.refs_4_.refs_1_.refs_0_, bf16[192,512]{1,0:T(8,128)(2,1)S(1)} %get-tuple-element.107.refs_2_.refs_0_, ...), custom_call_target="tpu_custom_call" | custom-call | bytes 1024 | tf_op jit(solution)/shard_map/hidden_back/pallas_call | solution.py:77
  88.0 0.6 weight_sum_c.1
  88.8 0.5 collective-permute-start.30
  89.3 2.1 %collective-permute-done.20.refs_1_ = bf16[192,512]{1,0:T(8,128)(2,1)S(1)} collective-permute-done((bf16[192,512]{1,0:T(8,128)(2,1)S(1)}, bf16[192,512]{1,0:T(8,128)(2,1)S(1)}, u32[]{:S(2)}, u32[]{:S(2)}) %collective-permute-start.20) | collective-permute-done | bytes 196640 | tf_op jit(solution)/shard_map/ppermute | solution.py:35
  91.4 0.6 weight_sum_d.1
  92.1 0.5 collective-permute-start.28
  92.6 1.6 %collective-permute-done.32.refs_0_ = bf16[2,112,512]{2,1,0:T(8,128)(2,1)S(1)} collective-permute-done((bf16[2,112,512]{2,1,0:T(8,128)(2,1)S(1)}, bf16[2,112,512]{2,1,0:T(8,128)(2,1)S(1)}, u32[]{:S(2)}, u32[]{:S(2)}) %collective-permute-start.32) | collective-permute-done | bytes 229408 | tf_op jit(solution)/shard_map/ppermute | solution.py:35
  94.1 1.5 %collective-permute-start.16 = (bf16[192,896]{1,0:T(8,128)(2,1)S(1)}, bf16[192,896]{1,0:T(8,128)(2,1)S(1)}, u32[]{:S(2)}, u32[]{:S(2)}) collective-permute-start(bf16[192,896]{1,0:T(8,128)(2,1)S(1)} %get-tuple-element.103), channel_id=1, source_target_pairs={{0,2},{2,0},{1,3},{3,1},{4,6},{6,4},{5,7},{7,5},{8,10},{10,8},{9,1... | collective-permute-start | bytes 1032200 | tf_op jit(solution)/shard_map/ppermute | solution.py:35
  95.6 0.5 collective-permute-start.34
  96.4 1.7 %collective-permute-start.36 = (bf16[2,112,512]{2,1,0:T(8,128)(2,1)S(1)}, bf16[2,112,512]{2,1,0:T(8,128)(2,1)S(1)}, u32[]{:S(2)}, u32[]{:S(2)}) collective-permute-start(bf16[2,112,512]{2,1,0:T(8,128)(2,1)S(1)} %get-tuple-element.130.refs_3_), channel_id=1, source_target_pairs={{0,8},{4,12},{8,0},{12,4},{16,24},{20,28},{24,16},{28,20},{1,9},{5... | collective-permute-start | bytes 688136 | tf_op jit(solution)/shard_map/ppermute | solution.py:35
  98.7 2.4 %collective-permute-start.38 = (bf16[1,112,512]{2,1,0:T(8,128)(2,1)S(1)}, bf16[1,112,512]{2,1,0:T(8,128)(2,1)S(1)}, u32[]{:S(2)}, u32[]{:S(2)}) collective-permute-start(bf16[1,112,512]{2,1,0:T(8,128)(2,1)S(1)} %get-tuple-element.129.refs_3_), channel_id=1, source_target_pairs={{0,16},{4,20},{8,24},{12,28},{16,0},{20,4},{24,8},{28,12},{1,17},{... | collective-permute-start | bytes 344072 | tf_op jit(solution)/shard_map/ppermute | solution.py:35
  101.1 4.0 %collective-permute-done.16.refs_3_ = bf16[192,896]{1,0:T(8,128)(2,1)S(1)} collective-permute-done((bf16[192,896]{1,0:T(8,128)(2,1)S(1)}, bf16[192,896]{1,0:T(8,128)(2,1)S(1)}, u32[]{:S(2)}, u32[]{:S(2)}) %collective-permute-start.16) | collective-permute-done | bytes 344096 | tf_op jit(solution)/shard_map/ppermute | solution.py:35
  105.1 2.4 %collective-permute-start.37 = (bf16[1,112,512]{2,1,0:T(8,128)(2,1)S(1)}, bf16[1,112,512]{2,1,0:T(8,128)(2,1)S(1)}, u32[]{:S(2)}, u32[]{:S(2)}) collective-permute-start(bf16[1,112,512]{2,1,0:T(8,128)(2,1)S(1)} %get-tuple-element.128.refs_2_), channel_id=1, source_target_pairs={{0,16},{4,20},{8,24},{12,28},{16,0},{20,4},{24,8},{28,12},{1,17},{... | collective-permute-start | bytes 344072 | tf_op jit(solution)/shard_map/ppermute | solution.py:35
  107.5 0.9 finish_mix.1.refs_2_
  108.5 1.0 copy-done.3
  109.6 2.6 %collective-permute-done.35.refs_0_ = bf16[2,112,512]{2,1,0:T(8,128)(2,1)S(1)} collective-permute-done((bf16[2,112,512]{2,1,0:T(8,128)(2,1)S(1)}, bf16[2,112,512]{2,1,0:T(8,128)(2,1)S(1)}, u32[]{:S(2)}, u32[]{:S(2)}) %collective-permute-start.35) | collective-permute-done | bytes 229408 | tf_op jit(solution)/shard_map/ppermute | solution.py:35
  112.5 2.8 %collective-permute-start.39 = (bf16[1,112,512]{2,1,0:T(8,128)(2,1)S(1)}, bf16[1,112,512]{2,1,0:T(8,128)(2,1)S(1)}, u32[]{:S(2)}, u32[]{:S(2)}) collective-permute-start(bf16[1,112,512]{2,1,0:T(8,128)(2,1)S(1)} %get-tuple-element.136.refs_2_), channel_id=1, source_target_pairs={{0,16},{4,20},{8,24},{12,28},{16,0},{20,4},{24,8},{28,12},{1,17},{... | collective-permute-start | bytes 344072 | tf_op jit(solution)/shard_map/ppermute | solution.py:35
  115.2 1.1 finish_latents.1
  116.4 1.5 %collective-permute-done.37.refs_0_ = bf16[1,112,512]{2,1,0:T(8,128)(2,1)S(1)} collective-permute-done((bf16[1,112,512]{2,1,0:T(8,128)(2,1)S(1)}, bf16[1,112,512]{2,1,0:T(8,128)(2,1)S(1)}, u32[]{:S(2)}, u32[]{:S(2)}) %collective-permute-start.37) | collective-permute-done | bytes 114720 | tf_op jit(solution)/shard_map/ppermute | solution.py:35
  117.8 3.6 %collective-permute-done.40.refs_6_ = bf16[1,112,512]{2,1,0:T(8,128)(2,1)S(1)} collective-permute-done((bf16[1,112,512]{2,1,0:T(8,128)(2,1)S(1)}, bf16[1,112,512]{2,1,0:T(8,128)(2,1)S(1)}, u32[]{:S(2)}, u32[]{:S(2)}) %collective-permute-start.40) | collective-permute-done | bytes 114720 | tf_op jit(solution)/shard_map/ppermute | solution.py:35
  121.5 2.5 %collective-permute-done.39.refs_4_ = bf16[1,112,512]{2,1,0:T(8,128)(2,1)S(1)} collective-permute-done((bf16[1,112,512]{2,1,0:T(8,128)(2,1)S(1)}, bf16[1,112,512]{2,1,0:T(8,128)(2,1)S(1)}, u32[]{:S(2)}, u32[]{:S(2)}) %collective-permute-start.39) | collective-permute-done | bytes 114720 | tf_op jit(solution)/shard_map/ppermute | solution.py:35
  123.9 1.0 weight_total.1
  (71 shorter events, 4.6 us)
Async XLA Ops:
  1.7 7.1 %collective-permute-start = (bf16[32,3584]{1,0:T(8,128)(2,1)S(1)}, bf16[32,3584]{1,0:T(8,128)(2,1)S(1)}, u32[]{:S(2)}, u32[]{:S(2)}) collective-permute-start(bf16[32,3584]{1,0:T(8,128)(2,1)S(1)} %slice_bitcast_fusion), channel_id=1, source_target_pairs={{0,4},{4,8},{8,12},{12,16},{16,20},{20,24},{24,28},{1,5},{5,9},{9,... | collective-permute-start | bytes 688136 | tf_op jit(solution)/shard_map/ppermute | solution.py:664
  4.0 10.3 %collective-permute-start.1 = (bf16[192,896]{1,0:T(8,128)(2,1)}, bf16[192,896]{1,0:T(8,128)(2,1)S(1)}, u32[]{:S(2)}, u32[]{:S(2)}) collective-permute-start(bf16[192,896]{1,0:T(8,128)(2,1)} %bitcast.17), channel_id=1, source_target_pairs={{0,2},{2,0},{1,3},{3,1},{4,6},{6,4},{5,7},{7,5},{8,10},{10,8},{9,1... | collective-permute-start | bytes 1032200 | tf_op jit(solution)/shard_map/ppermute | solution.py:35
  8.7 2.0 %copy-start.2 = (bf16[512,1792]{1,0:T(8,128)(2,1)S(1)}, bf16[512,1792]{1,0:T(8,128)(2,1)}, u32[]{:S(2)}) copy-start(bf16[512,1792]{1,0:T(8,128)(2,1)} %refs_1_.2) | copy-start | bytes 5505028
  8.7 2.0 %copy-start.4 = (bf16[1,192,896]{2,1,0:T(8,128)(2,1)S(1)}, bf16[1,192,896]{2,1,0:T(8,128)(2,1)}, u32[]{:S(2)}) copy-start(bf16[1,192,896]{2,1,0:T(8,128)(2,1)} %param.11) | copy-start | bytes 1032196
  10.7 2.6 %copy-start = (bf16[1792,3,512]{2,0,1:T(8,128)(2,1)S(1)}, bf16[1792,3,512]{2,0,1:T(8,128)(2,1)}, u32[]{:S(2)}) copy-start(bf16[1792,3,512]{2,0,1:T(8,128)(2,1)} %param.13) | copy-start | bytes 16515076
  13.3 1.1 copy-start.1
  13.3 1.1 copy-start.5
  13.3 1.1 copy-start.6
  16.0 9.7 %collective-permute-start.2 = (bf16[3,192,128]{2,1,0:T(8,128)(2,1)S(1)}, bf16[3,192,128]{2,1,0:T(8,128)(2,1)S(1)}, u32[]{:S(2)}, u32[]{:S(2)}) collective-permute-start(bf16[3,192,128]{2,1,0:T(8,128)(2,1)S(1)} %get-tuple-element.79), channel_id=1, source_target_pairs={{0,8},{4,12},{8,0},{12,4},{16,24},{20,28},{24,16},{28,20},{1,9},{5... | collective-permute-start | bytes 442376 | tf_op jit(solution)/shard_map/ppermute | solution.py:35
  19.3 14.0 %collective-permute-start.3 = (bf16[3,192,128]{2,1,0:T(8,128)(2,1)S(1)}, bf16[3,192,128]{2,1,0:T(8,128)(2,1)S(1)}, u32[]{:S(2)}, u32[]{:S(2)}) collective-permute-start(bf16[3,192,128]{2,1,0:T(8,128)(2,1)S(1)} %get-tuple-element.80), channel_id=1, source_target_pairs={{0,16},{4,20},{8,24},{12,28},{16,0},{20,4},{24,8},{28,12},{1,17},{... | collective-permute-start | bytes 442376 | tf_op jit(solution)/shard_map/ppermute | solution.py:35
  21.9 11.4 %collective-permute-start.4 = (bf16[3,192,128]{2,1,0:T(8,128)(2,1)S(1)}, bf16[3,192,128]{2,1,0:T(8,128)(2,1)S(1)}, u32[]{:S(2)}, u32[]{:S(2)}) collective-permute-start(bf16[3,192,128]{2,1,0:T(8,128)(2,1)S(1)} %get-tuple-element.81), channel_id=1, source_target_pairs={{0,24},{4,28},{8,16},{12,20},{16,8},{20,12},{24,0},{28,4},{1,25},{... | collective-permute-start | bytes 442376 | tf_op jit(solution)/shard_map/ppermute | solution.py:35
  22.4 23.5 %collective-permute-start.10 = (bf16[8,112,256]{2,1,0:T(8,128)(2,1)S(1)}, bf16[8,112,256]{2,1,0:T(8,128)(2,1)S(1)}, u32[]{:S(2)}, u32[]{:S(2)}) collective-permute-start(bf16[8,112,256]{2,1,0:T(8,128)(2,1)S(1)} %get-tuple-element.90), channel_id=1, source_target_pairs={{0,1},{1,0},{2,3},{3,2},{4,5},{5,4},{6,7},{7,6},{8,9},{9,8},{10,11... | collective-permute-start | bytes 1376264 | tf_op jit(solution)/shard_map/ppermute | solution.py:35
  23.9 9.4 %collective-permute-start.6 = (bf16[192,896]{1,0:T(8,128)(2,1)S(1)}, bf16[192,896]{1,0:T(8,128)(2,1)S(1)}, u32[]{:S(2)}, u32[]{:S(2)}) collective-permute-start(bf16[192,896]{1,0:T(8,128)(2,1)S(1)} %get-tuple-element.83.refs_2_.refs_1_), channel_id=1, source_target_pairs={{0,2},{2,0},{1,3},{3,1},{4,6},{6,4},{5,7},{7,5},{8,10},{10,8},{9,1... | collective-permute-start | bytes 1032200 | tf_op jit(solution)/shard_map/ppermute | solution.py:35
  33.3 12.6 %collective-permute-start.5 = (bf16[4,2,192,128]{3,2,1,0:T(8,128)(2,1)S(1)}, bf16[4,2,192,128]{3,2,1,0:T(8,128)(2,1)S(1)}, u32[]{:S(2)}, u32[]{:S(2)}) collective-permute-start(bf16[4,2,192,128]{3,2,1,0:T(8,128)(2,1)S(1)} %gather.1), channel_id=1, source_target_pairs={{0,4},{4,0},{8,12},{12,8},{16,20},{20,16},{24,28},{28,24},{1,5},{5... | collective-permute-start | bytes 1179656 | tf_op jit(solution)/shard_map/ppermute | solution.py:35
  34.2 5.7 %collective-permute-start.7 = (bf16[192,128]{1,0:T(8,128)(2,1)S(1)}, bf16[192,128]{1,0:T(8,128)(2,1)S(1)}, u32[]{:S(2)}, u32[]{:S(2)}) collective-permute-start(bf16[192,128]{1,0:T(8,128)(2,1)S(1)} %get-tuple-element.87), channel_id=1, source_target_pairs={{0,8},{4,12},{8,0},{12,4},{16,24},{20,28},{24,16},{28,20},{1,9},{5... | collective-permute-start | bytes 147464 | tf_op jit(solution)/shard_map/ppermute | solution.py:35
  37.3 20.2 %collective-permute-start.15 = (bf16[8,112,256]{2,1,0:T(8,128)(2,1)S(1)}, bf16[8,112,256]{2,1,0:T(8,128)(2,1)S(1)}, u32[]{:S(2)}, u32[]{:S(2)}) collective-permute-start(bf16[8,112,256]{2,1,0:T(8,128)(2,1)S(1)} %get-tuple-element.99), channel_id=1, source_target_pairs={{0,1},{1,0},{2,3},{3,2},{4,5},{5,4},{6,7},{7,6},{8,9},{9,8},{10,11... | collective-permute-start | bytes 1376264 | tf_op jit(solution)/shard_map/ppermute | solution.py:35
  38.9 6.1 %collective-permute-start.8 = (bf16[192,128]{1,0:T(8,128)(2,1)S(1)}, bf16[192,128]{1,0:T(8,128)(2,1)S(1)}, u32[]{:S(2)}, u32[]{:S(2)}) collective-permute-start(bf16[192,128]{1,0:T(8,128)(2,1)S(1)} %get-tuple-element.88), channel_id=1, source_target_pairs={{0,16},{4,20},{8,24},{12,28},{16,0},{20,4},{24,8},{28,12},{1,17},{... | collective-permute-start | bytes 147464 | tf_op jit(solution)/shard_map/ppermute | solution.py:35
  39.9 5.9 %collective-permute-start.9 = (bf16[192,128]{1,0:T(8,128)(2,1)S(1)}, bf16[192,128]{1,0:T(8,128)(2,1)S(1)}, u32[]{:S(2)}, u32[]{:S(2)}) collective-permute-start(bf16[192,128]{1,0:T(8,128)(2,1)S(1)} %get-tuple-element.89), channel_id=1, source_target_pairs={{0,24},{4,28},{8,16},{12,20},{16,8},{20,12},{24,0},{28,4},{1,25},{... | collective-permute-start | bytes 147464 | tf_op jit(solution)/shard_map/ppermute | solution.py:35
  53.0 4.5 %collective-permute-start.14 = (bf16[4,2,192,128]{3,2,1,0:T(8,128)(2,1)S(1)}, bf16[4,2,192,128]{3,2,1,0:T(8,128)(2,1)S(1)}, u32[]{:S(2)}, u32[]{:S(2)}) collective-permute-start(bf16[4,2,192,128]{3,2,1,0:T(8,128)(2,1)S(1)} %get-tuple-element.98), channel_id=1, source_target_pairs={{0,4},{4,0},{8,12},{12,8},{16,20},{20,16},{24,28},{28,24},{1,5},{5... | collective-permute-start | bytes 1179656 | tf_op jit(solution)/shard_map/ppermute | solution.py:35
  53.1 6.7 %collective-permute-start.11 = (bf16[2,192,128]{2,1,0:T(8,128)(2,1)S(1)}, bf16[2,192,128]{2,1,0:T(8,128)(2,1)S(1)}, u32[]{:S(2)}, u32[]{:S(2)}) collective-permute-start(bf16[2,192,128]{2,1,0:T(8,128)(2,1)S(1)} %get-tuple-element.94), channel_id=1, source_target_pairs={{0,8},{4,12},{8,0},{12,4},{16,24},{20,28},{24,16},{28,20},{1,9},{5... | collective-permute-start | bytes 294920 | tf_op jit(solution)/shard_map/ppermute | solution.py:35
  54.2 10.8 %collective-permute-start.12 = (bf16[2,192,128]{2,1,0:T(8,128)(2,1)S(1)}, bf16[2,192,128]{2,1,0:T(8,128)(2,1)S(1)}, u32[]{:S(2)}, u32[]{:S(2)}) collective-permute-start(bf16[2,192,128]{2,1,0:T(8,128)(2,1)S(1)} %get-tuple-element.95), channel_id=1, source_target_pairs={{0,16},{4,20},{8,24},{12,28},{16,0},{20,4},{24,8},{28,12},{1,17},{... | collective-permute-start | bytes 294920 | tf_op jit(solution)/shard_map/ppermute | solution.py:35
  55.8 9.2 %collective-permute-start.13 = (bf16[2,192,128]{2,1,0:T(8,128)(2,1)S(1)}, bf16[2,192,128]{2,1,0:T(8,128)(2,1)S(1)}, u32[]{:S(2)}, u32[]{:S(2)}) collective-permute-start(bf16[2,192,128]{2,1,0:T(8,128)(2,1)S(1)} %get-tuple-element.96), channel_id=1, source_target_pairs={{0,24},{4,28},{8,16},{12,20},{16,8},{20,12},{24,0},{28,4},{1,25},{... | collective-permute-start | bytes 294920 | tf_op jit(solution)/shard_map/ppermute | solution.py:35
  57.5 27.2 %slice-start = ((s8[5505024]{0:T(1024)(128)(4,1)}), s8[4194304]{0:T(1024)(128)(4,1)S(1)}, s32[]{:S(2)}) async-start(s8[5505024]{0:T(1024)(128)(4,1)} %bitcast.14), calls=%async_computation | async-start | bytes 8388608
  65.3 12.5 %collective-permute-start.23 = (bf16[192,512]{1,0:T(8,128)(2,1)S(1)}, bf16[192,512]{1,0:T(8,128)(2,1)S(1)}, u32[]{:S(2)}, u32[]{:S(2)}) collective-permute-start(bf16[192,512]{1,0:T(8,128)(2,1)S(1)} %get-tuple-element.101.refs_0_.refs_2_), channel_id=1, source_target_pairs={{0,1},{1,0},{2,3},{3,2},{4,5},{5,4},{6,7},{7,6},{8,9},{9,8},{10,11... | collective-permute-start | bytes 589832 | tf_op jit(solution)/shard_map/ppermute | solution.py:35
  66.0 6.4 %collective-permute-start.17 = (bf16[2,192,128]{2,1,0:T(8,128)(2,1)S(1)}, bf16[2,192,128]{2,1,0:T(8,128)(2,1)S(1)}, u32[]{:S(2)}, u32[]{:S(2)}) collective-permute-start(bf16[2,192,128]{2,1,0:T(8,128)(2,1)S(1)} %get-tuple-element.104), channel_id=1, source_target_pairs={{0,8},{4,12},{8,0},{12,4},{16,24},{20,28},{24,16},{28,20},{1,9},{5... | collective-permute-start | bytes 294920 | tf_op jit(solution)/shard_map/ppermute | solution.py:35
  67.9 9.6 %collective-permute-start.18 = (bf16[2,192,128]{2,1,0:T(8,128)(2,1)S(1)}, bf16[2,192,128]{2,1,0:T(8,128)(2,1)S(1)}, u32[]{:S(2)}, u32[]{:S(2)}) collective-permute-start(bf16[2,192,128]{2,1,0:T(8,128)(2,1)S(1)} %get-tuple-element.105), channel_id=1, source_target_pairs={{0,16},{4,20},{8,24},{12,28},{16,0},{20,4},{24,8},{28,12},{1,17},{... | collective-permute-start | bytes 294920 | tf_op jit(solution)/shard_map/ppermute | solution.py:35
  68.8 8.7 %collective-permute-start.19 = (bf16[2,192,128]{2,1,0:T(8,128)(2,1)S(1)}, bf16[2,192,128]{2,1,0:T(8,128)(2,1)S(1)}, u32[]{:S(2)}, u32[]{:S(2)}) collective-permute-start(bf16[2,192,128]{2,1,0:T(8,128)(2,1)S(1)} %get-tuple-element.106), channel_id=1, source_target_pairs={{0,24},{4,28},{8,16},{12,20},{16,8},{20,12},{24,0},{28,4},{1,25},{... | collective-permute-start | bytes 294920 | tf_op jit(solution)/shard_map/ppermute | solution.py:35
  70.4 8.7 %collective-permute-start.22 = (bf16[192,512]{1,0:T(8,128)(2,1)S(1)}, bf16[192,512]{1,0:T(8,128)(2,1)S(1)}, u32[]{:S(2)}, u32[]{:S(2)}) collective-permute-start(bf16[192,512]{1,0:T(8,128)(2,1)S(1)} %get-tuple-element.109.refs_0_), channel_id=1, source_target_pairs={{0,1},{1,0},{2,3},{3,2},{4,5},{5,4},{6,7},{7,6},{8,9},{9,8},{10,11... | collective-permute-start | bytes 589832 | tf_op jit(solution)/shard_map/ppermute | solution.py:35
  77.5 7.2 %slice-start.1 = ((s8[5505024]{0:T(1024)(128)(4,1)}), s8[1310720]{0:T(1024)(128)(4,1)S(1)}, s32[]{:S(2)}) async-start(s8[5505024]{0:T(1024)(128)(4,1)} %bitcast.14), calls=%async_computation.1 | async-start | bytes 2621440
  78.5 3.2 %collective-permute-start.27 = (bf16[2,112,512]{2,1,0:T(8,128)(2,1)S(1)}, bf16[2,112,512]{2,1,0:T(8,128)(2,1)S(1)}, u32[]{:S(2)}, u32[]{:S(2)}) collective-permute-start(bf16[2,112,512]{2,1,0:T(8,128)(2,1)S(1)} %get-tuple-element.115), channel_id=1, source_target_pairs={{0,4},{4,0},{8,12},{12,8},{16,20},{20,16},{24,28},{28,24},{1,5},{5... | collective-permute-start | bytes 688136 | tf_op jit(solution)/shard_map/ppermute | solution.py:35
  78.5 3.1 %collective-permute-start.26 = (bf16[2,112,512]{2,1,0:T(8,128)(2,1)S(1)}, bf16[2,112,512]{2,1,0:T(8,128)(2,1)S(1)}, u32[]{:S(2)}, u32[]{:S(2)}) collective-permute-start(bf16[2,112,512]{2,1,0:T(8,128)(2,1)S(1)} %get-tuple-element.111.refs_4_), channel_id=1, source_target_pairs={{0,4},{4,0},{8,12},{12,8},{16,20},{20,16},{24,28},{28,24},{1,5},{5... | collective-permute-start | bytes 688136 | tf_op jit(solution)/shard_map/ppermute | solution.py:35
  79.7 4.5 %collective-permute-start.25 = (bf16[2,112,512]{2,1,0:T(8,128)(2,1)S(1)}, bf16[2,112,512]{2,1,0:T(8,128)(2,1)S(1)}, u32[]{:S(2)}, u32[]{:S(2)}) collective-permute-start(bf16[2,112,512]{2,1,0:T(8,128)(2,1)S(1)} %get-tuple-element.113), channel_id=1, source_target_pairs={{0,4},{4,0},{8,12},{12,8},{16,20},{20,16},{24,28},{28,24},{1,5},{5... | collective-permute-start | bytes 688136 | tf_op jit(solution)/shard_map/ppermute | solution.py:35
  79.8 4.3 %collective-permute-start.24 = (bf16[2,112,512]{2,1,0:T(8,128)(2,1)S(1)}, bf16[2,112,512]{2,1,0:T(8,128)(2,1)S(1)}, u32[]{:S(2)}, u32[]{:S(2)}) collective-permute-start(bf16[2,112,512]{2,1,0:T(8,128)(2,1)S(1)} %get-tuple-element.112.refs_3_), channel_id=1, source_target_pairs={{0,4},{4,0},{8,12},{12,8},{16,20},{20,16},{24,28},{28,24},{1,5},{5... | collective-permute-start | bytes 688136 | tf_op jit(solution)/shard_map/ppermute | solution.py:35
  80.3 7.8 %collective-permute-start.21 = (bf16[192,512]{1,0:T(8,128)(2,1)S(1)}, bf16[192,512]{1,0:T(8,128)(2,1)S(1)}, u32[]{:S(2)}, u32[]{:S(2)}) collective-permute-start(bf16[192,512]{1,0:T(8,128)(2,1)S(1)} %get-tuple-element.108.refs_4_.refs_1_.refs_0_), channel_id=1, source_target_pairs={{0,1},{1,0},{2,3},{3,2},{4,5},{5,4},{6,7},{7,6},{8,9},{9,8},{10,11... | collective-permute-start | bytes 589832 | tf_op jit(solution)/shard_map/ppermute | solution.py:35
  81.8 10.2 %collective-permute-start.33 = (bf16[2,112,512]{2,1,0:T(8,128)(2,1)S(1)}, bf16[2,112,512]{2,1,0:T(8,128)(2,1)S(1)}, u32[]{:S(2)}, u32[]{:S(2)}) collective-permute-start(bf16[2,112,512]{2,1,0:T(8,128)(2,1)S(1)} %get-tuple-element.117.refs_3_), channel_id=1, source_target_pairs={{0,8},{4,12},{8,0},{12,4},{16,24},{20,28},{24,16},{28,20},{1,9},{5... | collective-permute-start | bytes 688136 | tf_op jit(solution)/shard_map/ppermute | solution.py:35
  83.5 7.8 %collective-permute-start.20 = (bf16[192,512]{1,0:T(8,128)(2,1)S(1)}, bf16[192,512]{1,0:T(8,128)(2,1)S(1)}, u32[]{:S(2)}, u32[]{:S(2)}) collective-permute-start(bf16[192,512]{1,0:T(8,128)(2,1)S(1)} %get-tuple-element.107.refs_2_.refs_0_), channel_id=1, source_target_pairs={{0,1},{1,0},{2,3},{3,2},{4,5},{5,4},{6,7},{7,6},{8,9},{9,8},{10,11... | collective-permute-start | bytes 589832 | tf_op jit(solution)/shard_map/ppermute | solution.py:35
  84.3 9.8 %collective-permute-start.32 = (bf16[2,112,512]{2,1,0:T(8,128)(2,1)S(1)}, bf16[2,112,512]{2,1,0:T(8,128)(2,1)S(1)}, u32[]{:S(2)}, u32[]{:S(2)}) collective-permute-start(bf16[2,112,512]{2,1,0:T(8,128)(2,1)S(1)} %get-tuple-element.118.refs_8_), channel_id=1, source_target_pairs={{0,8},{4,12},{8,0},{12,4},{16,24},{20,28},{24,16},{28,20},{1,9},{5... | collective-permute-start | bytes 688136 | tf_op jit(solution)/shard_map/ppermute | solution.py:35
  88.7 7.0 %collective-permute-start.31 = (bf16[2,112,512]{2,1,0:T(8,128)(2,1)S(1)}, bf16[2,112,512]{2,1,0:T(8,128)(2,1)S(1)}, u32[]{:S(2)}, u32[]{:S(2)}) collective-permute-start(bf16[2,112,512]{2,1,0:T(8,128)(2,1)S(1)} %get-tuple-element.124), channel_id=1, source_target_pairs={{0,4},{4,0},{8,12},{12,8},{16,20},{20,16},{24,28},{28,24},{1,5},{5... | collective-permute-start | bytes 688136 | tf_op jit(solution)/shard_map/ppermute | solution.py:35
  88.8 7.6 %collective-permute-start.30 = (bf16[2,112,512]{2,1,0:T(8,128)(2,1)S(1)}, bf16[2,112,512]{2,1,0:T(8,128)(2,1)S(1)}, u32[]{:S(2)}, u32[]{:S(2)}) collective-permute-start(bf16[2,112,512]{2,1,0:T(8,128)(2,1)S(1)} %get-tuple-element.120.refs_4_), channel_id=1, source_target_pairs={{0,4},{4,0},{8,12},{12,8},{16,20},{20,16},{24,28},{28,24},{1,5},{5... | collective-permute-start | bytes 688136 | tf_op jit(solution)/shard_map/ppermute | solution.py:35
  92.0 6.1 %collective-permute-start.29 = (bf16[2,112,512]{2,1,0:T(8,128)(2,1)S(1)}, bf16[2,112,512]{2,1,0:T(8,128)(2,1)S(1)}, u32[]{:S(2)}, u32[]{:S(2)}) collective-permute-start(bf16[2,112,512]{2,1,0:T(8,128)(2,1)S(1)} %get-tuple-element.122), channel_id=1, source_target_pairs={{0,4},{4,0},{8,12},{12,8},{16,20},{20,16},{24,28},{28,24},{1,5},{5... | collective-permute-start | bytes 688136 | tf_op jit(solution)/shard_map/ppermute | solution.py:35
  92.1 6.1 %collective-permute-start.28 = (bf16[2,112,512]{2,1,0:T(8,128)(2,1)S(1)}, bf16[2,112,512]{2,1,0:T(8,128)(2,1)S(1)}, u32[]{:S(2)}, u32[]{:S(2)}) collective-permute-start(bf16[2,112,512]{2,1,0:T(8,128)(2,1)S(1)} %get-tuple-element.121.refs_2_), channel_id=1, source_target_pairs={{0,4},{4,0},{8,12},{12,8},{16,20},{20,16},{24,28},{28,24},{1,5},{5... | collective-permute-start | bytes 688136 | tf_op jit(solution)/shard_map/ppermute | solution.py:35
  94.1 11.0 %collective-permute-start.16 = (bf16[192,896]{1,0:T(8,128)(2,1)S(1)}, bf16[192,896]{1,0:T(8,128)(2,1)S(1)}, u32[]{:S(2)}, u32[]{:S(2)}) collective-permute-start(bf16[192,896]{1,0:T(8,128)(2,1)S(1)} %get-tuple-element.103), channel_id=1, source_target_pairs={{0,2},{2,0},{1,3},{3,1},{4,6},{6,4},{5,7},{7,5},{8,10},{10,8},{9,1... | collective-permute-start | bytes 1032200 | tf_op jit(solution)/shard_map/ppermute | solution.py:35
  95.6 19.6 %collective-permute-start.34 = (bf16[192,1024]{1,0:T(8,128)(2,1)S(1)}, bf16[192,1024]{1,0:T(8,128)(2,1)S(1)}, u32[]{:S(2)}, u32[]{:S(2)}) collective-permute-start(bf16[192,1024]{1,0:T(8,128)(2,1)S(1)} %get-tuple-element.133), channel_id=1, source_target_pairs={{0,2},{2,0},{1,3},{3,1},{4,6},{6,4},{5,7},{7,5},{8,10},{10,8},{9,1... | collective-permute-start | bytes 1179656 | tf_op jit(solution)/shard_map/ppermute | solution.py:35
  96.4 12.1 %collective-permute-start.36 = (bf16[2,112,512]{2,1,0:T(8,128)(2,1)S(1)}, bf16[2,112,512]{2,1,0:T(8,128)(2,1)S(1)}, u32[]{:S(2)}, u32[]{:S(2)}) collective-permute-start(bf16[2,112,512]{2,1,0:T(8,128)(2,1)S(1)} %get-tuple-element.130.refs_3_), channel_id=1, source_target_pairs={{0,8},{4,12},{8,0},{12,4},{16,24},{20,28},{24,16},{28,20},{1,9},{5... | collective-permute-start | bytes 688136 | tf_op jit(solution)/shard_map/ppermute | solution.py:35
  98.3 13.9 %collective-permute-start.35 = (bf16[2,112,512]{2,1,0:T(8,128)(2,1)S(1)}, bf16[2,112,512]{2,1,0:T(8,128)(2,1)S(1)}, u32[]{:S(2)}, u32[]{:S(2)}) collective-permute-start(bf16[2,112,512]{2,1,0:T(8,128)(2,1)S(1)} %get-tuple-element.131.refs_4_), channel_id=1, source_target_pairs={{0,8},{4,12},{8,0},{12,4},{16,24},{20,28},{24,16},{28,20},{1,9},{5... | collective-permute-start | bytes 688136 | tf_op jit(solution)/shard_map/ppermute | solution.py:35
  98.7 17.6 %collective-permute-start.38 = (bf16[1,112,512]{2,1,0:T(8,128)(2,1)S(1)}, bf16[1,112,512]{2,1,0:T(8,128)(2,1)S(1)}, u32[]{:S(2)}, u32[]{:S(2)}) collective-permute-start(bf16[1,112,512]{2,1,0:T(8,128)(2,1)S(1)} %get-tuple-element.129.refs_3_), channel_id=1, source_target_pairs={{0,16},{4,20},{8,24},{12,28},{16,0},{20,4},{24,8},{28,12},{1,17},{... | collective-permute-start | bytes 344072 | tf_op jit(solution)/shard_map/ppermute | solution.py:35
  105.1 12.7 %collective-permute-start.37 = (bf16[1,112,512]{2,1,0:T(8,128)(2,1)S(1)}, bf16[1,112,512]{2,1,0:T(8,128)(2,1)S(1)}, u32[]{:S(2)}, u32[]{:S(2)}) collective-permute-start(bf16[1,112,512]{2,1,0:T(8,128)(2,1)S(1)} %get-tuple-element.128.refs_2_), channel_id=1, source_target_pairs={{0,16},{4,20},{8,24},{12,28},{16,0},{20,4},{24,8},{28,12},{1,17},{... | collective-permute-start | bytes 344072 | tf_op jit(solution)/shard_map/ppermute | solution.py:35
  108.5 1.0 copy-start.3
  112.3 9.2 %collective-permute-start.40 = (bf16[1,112,512]{2,1,0:T(8,128)(2,1)S(1)}, bf16[1,112,512]{2,1,0:T(8,128)(2,1)S(1)}, u32[]{:S(2)}, u32[]{:S(2)}) collective-permute-start(bf16[1,112,512]{2,1,0:T(8,128)(2,1)S(1)} %get-tuple-element.137.refs_7_), channel_id=1, source_target_pairs={{0,16},{4,20},{8,24},{12,28},{16,0},{20,4},{24,8},{28,12},{1,17},{... | collective-permute-start | bytes 344072 | tf_op jit(solution)/shard_map/ppermute | solution.py:35
  112.5 11.5 %collective-permute-start.39 = (bf16[1,112,512]{2,1,0:T(8,128)(2,1)S(1)}, bf16[1,112,512]{2,1,0:T(8,128)(2,1)S(1)}, u32[]{:S(2)}, u32[]{:S(2)}) collective-permute-start(bf16[1,112,512]{2,1,0:T(8,128)(2,1)S(1)} %get-tuple-element.136.refs_2_), channel_id=1, source_target_pairs={{0,16},{4,20},{8,24},{12,28},{16,0},{20,4},{24,8},{28,12},{1,17},{... | collective-permute-start | bytes 344072 | tf_op jit(solution)/shard_map/ppermute | solution.py:35

commit v6 on v5

--- a/solution.py
+++ b/solution.py
@@ -700,17 +700,6 @@
     )
     own, (hidden, raw, inv_norm) = got[:heads], got[heads:]
     own = [own[0]] + [swap(own[t], "seq", t * sharers) for t in range(1, heads)]
-    (keys_values,) = call(
-        functools.partial(gather_kernel, heads),
-        "gather",
-        [((heads, 2, rows, head_dim), BF)],
-        own,
-        [],
-        2,
-        0,
-    )
-    shared = [swap(keys_values, "seq", u) for u in range(1, sharers)]
-
     left_hidden = turned(hidden, [])
     got = call(
         functools.partial(upstream_kernel, heads, width_count),
@@ -725,6 +714,18 @@
     ups, grad_attn = got[:heads], got[heads]
     left_grad = turned(grad_attn, [])
     ups = [ups[0]] + [swap(ups[t], "seq", t * sharers) for t in range(1, heads)]
+    (keys_values,) = call(
+        functools.partial(gather_kernel, heads),
+        "gather",
+        [((heads, 2, rows, head_dim), BF)],
+        own,
+        [],
+        2,
+        0,
+        ups[1:],
+    )
+    shared = [swap(keys_values, "seq", u) for u in range(1, sharers)]
+
 
     outs, key_grads = attention(key_group, query_group, own, shared, ups, [*left_hidden[1:], left_grad[0]])
     terms = key_grads[:1] + [swap(key_grads[u], "seq", u) for u in range(1, sharers)]
@@ -807,6 +808,8 @@
 
     def advance(name, after):
         total = state[name]
+        if hasattr(total, "keep") and total.keep.shape[0] == 1:
+            return after
         token = total.halve(after) if hasattr(total, "keep") else total.outer(after)
         total.exchange()
         return token

time: 125 us -> 122 us (0.976)
  waiting for transfers between devices: 42.8 us -> 39.2 us
    ppermute x40, waiting for transfers between devices: 42.8 us -> 39.2 us  [swap(): return lax.ppermute(value, axis, [(i, i ^ distance) for i in range(count)])]
  transfers between devices with their start and end apart: 41 -> 41, of which waited for: 16 -> 15; matrix products, arithmetic and copies ran while one was open for 3% -> 3% of each run, Pallas kernels for 15% -> 17%
where the time goes in v6:
time: 122 us
  starting transfers between devices  50.8 us (42%)
  waiting for transfers between devices  39.2 us (32%)
  Pallas kernels  22.2 us (18%)
  local copies, waits for them, and re-layouts  4.77 us (4%)
  matrix products  1.96 us (2%)
  between operations  1.62 us (1%)
  other arithmetic  1.4 us (1%)
    ppermute x40, starting transfers between devices, swap(): return lax.ppermute(value, axis, [(i, i ^ distance) for i in range(count)])  48.5 us
    ppermute x40, waiting for transfers between devices, swap(): return lax.ppermute(value, axis, [(i, i ^ distance) for i in range(count)])  39.2 us
    pallas_call x27, Pallas kernels, call(): pl.pallas_call(body, out_shape=[jax.ShapeDtypeStruct(*o) for o in out], i...  22.2 us
    unnamed x18, local copies, waits for them, and re-layouts  3.56 us
  transfers between devices with their start and end apart: 41, of which 15 were waited for; matrix products, arithmetic and copies ran while one was open for 3% of the time, Pallas kernels for 17%

profile of v6, /device:TPU:0, one launch (start us, length us, event | category | flops | bytes accessed | tf_op | source)
XLA Modules:
  0.0 122.0 jit_solution(8702245171938409675)
XLA Ops:
  0.6 1.0 slice_bitcast_fusion
  1.7 2.4 %collective-permute-start = (bf16[32,3584]{1,0:T(8,128)(2,1)S(1)}, bf16[32,3584]{1,0:T(8,128)(2,1)S(1)}, u32[]{:S(2)}, u32[]{:S(2)}) collective-permute-start(bf16[32,3584]{1,0:T(8,128)(2,1)S(1)} %slice_bitcast_fusion), channel_id=1, source_target_pairs={{0,4},{4,8},{8,12},{12,16},{16,20},{20,24},{24,28},{1,5},{5,9},{9,... | collective-permute-start | bytes 688136 | tf_op jit(solution)/shard_map/ppermute | solution.py:664
  4.0 2.4 %collective-permute-start.1 = (bf16[192,896]{1,0:T(8,128)(2,1)}, bf16[192,896]{1,0:T(8,128)(2,1)S(1)}, u32[]{:S(2)}, u32[]{:S(2)}) collective-permute-start(bf16[192,896]{1,0:T(8,128)(2,1)} %bitcast.17), channel_id=1, source_target_pairs={{0,2},{2,0},{1,3},{3,1},{4,6},{6,4},{5,7},{7,5},{8,10},{10,8},{9,1... | collective-permute-start | bytes 1032200 | tf_op jit(solution)/shard_map/ppermute | solution.py:35
  7.1 0.7 fusion.5
  8.0 0.7 broadcast_subtract_fusion
  8.7 2.0 %convolution_convert_fusion.refs_5_.refs_3_.refs_1_.refs_4_.refs_2_ = bf16[192,3584]{1,0:T(8,128)(2,1)S(1)} fusion(bf16[150,3584]{1,0:T(8,128)(2,1)} %bitcast.25, bf16[32,3584]{1,0:T(8,128)(2,1)S(1)} %collective-permute-done, s32[192]{0:T(256)S(1)} %bitcast.26), kind=kOutput, calls=%fused_computation | convolution fusion | flops 253810816 | bytes 2681600 | tf_op jit(solution)/shard_map/dot_general | solution.py:672
  10.7 2.6 %copy-done = bf16[1792,3,512]{2,0,1:T(8,128)(2,1)S(1)} copy-done((bf16[1792,3,512]{2,0,1:T(8,128)(2,1)S(1)}, bf16[1792,3,512]{2,0,1:T(8,128)(2,1)}, u32[]{:S(2)}) %copy-start) | copy-done | bytes 5505048
  13.3 0.7 stage.1
  14.4 1.7 %project.1 = (bf16[3,192,128]{2,1,0:T(8,128)(2,1)S(1)}, bf16[3,192,128]{2,1,0:T(8,128)(2,1)S(1)}, bf16[3,192,128]{2,1,0:T(8,128)(2,1)S(1)}, bf16[3,192,128]{2,1,...) custom-call(f32[4,128]{1,0:T(4,128)S(1)} %copy-done.5, ...), custom_call_target="tpu_custom_call" | custom-call | bytes 1024 | tf_op jit(solution)/shard_map/project/pallas_call | solution.py:77
  16.0 4.6 %collective-permute-start.2 = (bf16[3,192,128]{2,1,0:T(8,128)(2,1)S(1)}, bf16[3,192,128]{2,1,0:T(8,128)(2,1)S(1)}, u32[]{:S(2)}, u32[]{:S(2)}) collective-permute-start(bf16[3,192,128]{2,1,0:T(8,128)(2,1)S(1)} %get-tuple-element.79), channel_id=1, source_target_pairs={{0,8},{4,12},{8,0},{12,4},{16,24},{20,28},{24,16},{28,20},{1,9},{5... | collective-permute-start | bytes 442376 | tf_op jit(solution)/shard_map/ppermute | solution.py:35
  20.6 2.6 %collective-permute-start.3 = (bf16[3,192,128]{2,1,0:T(8,128)(2,1)S(1)}, bf16[3,192,128]{2,1,0:T(8,128)(2,1)S(1)}, u32[]{:S(2)}, u32[]{:S(2)}) collective-permute-start(bf16[3,192,128]{2,1,0:T(8,128)(2,1)S(1)} %get-tuple-element.80), channel_id=1, source_target_pairs={{0,16},{4,20},{8,24},{12,28},{16,0},{20,4},{24,8},{28,12},{1,17},{... | collective-permute-start | bytes 442376 | tf_op jit(solution)/shard_map/ppermute | solution.py:35
  23.2 0.5 turn.2
  23.7 1.5 %collective-permute-start.10 = (bf16[8,112,256]{2,1,0:T(8,128)(2,1)S(1)}, bf16[8,112,256]{2,1,0:T(8,128)(2,1)S(1)}, u32[]{:S(2)}, u32[]{:S(2)}) collective-permute-start(bf16[8,112,256]{2,1,0:T(8,128)(2,1)S(1)} %get-tuple-element.90), channel_id=1, source_target_pairs={{0,1},{1,0},{2,3},{3,2},{4,5},{5,4},{6,7},{7,6},{8,9},{9,8},{10,11... | collective-permute-start | bytes 1376264 | tf_op jit(solution)/shard_map/ppermute | solution.py:35
  25.2 0.8 upstream.1
  26.1 1.9 %collective-permute-start.6 = (bf16[192,128]{1,0:T(8,128)(2,1)S(1)}, bf16[192,128]{1,0:T(8,128)(2,1)S(1)}, u32[]{:S(2)}, u32[]{:S(2)}) collective-permute-start(bf16[192,128]{1,0:T(8,128)(2,1)S(1)} %get-tuple-element.86), channel_id=1, source_target_pairs={{0,8},{4,12},{8,0},{12,4},{16,24},{20,28},{24,16},{28,20},{1,9},{5... | collective-permute-start | bytes 147464 | tf_op jit(solution)/shard_map/ppermute | solution.py:35
  28.0 2.5 %collective-permute-start.7 = (bf16[192,128]{1,0:T(8,128)(2,1)S(1)}, bf16[192,128]{1,0:T(8,128)(2,1)S(1)}, u32[]{:S(2)}, u32[]{:S(2)}) collective-permute-start(bf16[192,128]{1,0:T(8,128)(2,1)S(1)} %get-tuple-element.87), channel_id=1, source_target_pairs={{0,16},{4,20},{8,24},{12,28},{16,0},{20,4},{24,8},{28,12},{1,17},{... | collective-permute-start | bytes 147464 | tf_op jit(solution)/shard_map/ppermute | solution.py:35
  30.5 4.9 %collective-permute-done.3.refs_2_.refs_4_ = bf16[3,192,128]{2,1,0:T(8,128)(2,1)S(1)} collective-permute-done((bf16[3,192,128]{2,1,0:T(8,128)(2,1)S(1)}, bf16[3,192,128]{2,1,0:T(8,128)(2,1)S(1)}, u32[]{:S(2)}, u32[]{:S(2)}) %collective-permute-start.3) | collective-permute-done | bytes 147488 | tf_op jit(solution)/shard_map/ppermute | solution.py:35
  35.5 2.0 %collective-permute-start.8 = (bf16[192,128]{1,0:T(8,128)(2,1)S(1)}, bf16[192,128]{1,0:T(8,128)(2,1)S(1)}, u32[]{:S(2)}, u32[]{:S(2)}) collective-permute-start(bf16[192,128]{1,0:T(8,128)(2,1)S(1)} %get-tuple-element.88), channel_id=1, source_target_pairs={{0,24},{4,28},{8,16},{12,20},{16,8},{20,12},{24,0},{28,4},{1,25},{... | collective-permute-start | bytes 147464 | tf_op jit(solution)/shard_map/ppermute | solution.py:35
  37.4 1.2 collective-permute-done.7.refs_5_.refs_9_
  38.6 2.8 %collective-permute-done.8.refs_6_.refs_10_ = bf16[192,128]{1,0:T(8,128)(2,1)S(1)} collective-permute-done((bf16[192,128]{1,0:T(8,128)(2,1)S(1)}, bf16[192,128]{1,0:T(8,128)(2,1)S(1)}, u32[]{:S(2)}, u32[]{:S(2)}) %collective-permute-start.8) | collective-permute-done | bytes 49184 | tf_op jit(solution)/shard_map/ppermute | solution.py:35
  41.5 0.5 turn.3
  42.0 1.5 %collective-permute-start.15 = (bf16[8,112,256]{2,1,0:T(8,128)(2,1)S(1)}, bf16[8,112,256]{2,1,0:T(8,128)(2,1)S(1)}, u32[]{:S(2)}, u32[]{:S(2)}) collective-permute-start(bf16[8,112,256]{2,1,0:T(8,128)(2,1)S(1)} %get-tuple-element.99), channel_id=1, source_target_pairs={{0,1},{1,0},{2,3},{3,2},{4,5},{5,4},{6,7},{7,6},{8,9},{9,8},{10,11... | collective-permute-start | bytes 1376264 | tf_op jit(solution)/shard_map/ppermute | solution.py:35
  43.5 7.1 %attention.1 = (bf16[2,192,128]{2,1,0:T(8,128)(2,1)S(1)}, bf16[2,192,128]{2,1,0:T(8,128)(2,1)S(1)}, bf16[2,192,128]{2,1,0:T(8,128)(2,1)S(1)}, bf16[2,192,128]{2,...) custom-call(s32[1,1536]{1,0:T(1,128)S(1)} %get-tuple-element.76.refs_0_, ...), custom_call_target="tpu_custom_call" | custom-call | bytes 1024 | tf_op jit(solution)/shard_map/attention/pallas_call | solution.py:77
  50.9 2.5 %collective-permute-start.12 = (bf16[2,192,128]{2,1,0:T(8,128)(2,1)S(1)}, bf16[2,192,128]{2,1,0:T(8,128)(2,1)S(1)}, u32[]{:S(2)}, u32[]{:S(2)}) collective-permute-start(bf16[2,192,128]{2,1,0:T(8,128)(2,1)S(1)} %get-tuple-element.95), channel_id=1, source_target_pairs={{0,16},{4,20},{8,24},{12,28},{16,0},{20,4},{24,8},{28,12},{1,17},{... | collective-permute-start | bytes 294920 | tf_op jit(solution)/shard_map/ppermute | solution.py:35
  53.4 1.9 %collective-permute-start.13 = (bf16[2,192,128]{2,1,0:T(8,128)(2,1)S(1)}, bf16[2,192,128]{2,1,0:T(8,128)(2,1)S(1)}, u32[]{:S(2)}, u32[]{:S(2)}) collective-permute-start(bf16[2,192,128]{2,1,0:T(8,128)(2,1)S(1)} %get-tuple-element.96), channel_id=1, source_target_pairs={{0,24},{4,28},{8,16},{12,20},{16,8},{20,12},{24,0},{28,4},{1,25},{... | collective-permute-start | bytes 294920 | tf_op jit(solution)/shard_map/ppermute | solution.py:35
  55.4 2.0 %collective-permute-done.11.refs_3_ = bf16[2,192,128]{2,1,0:T(8,128)(2,1)S(1)} collective-permute-done((bf16[2,192,128]{2,1,0:T(8,128)(2,1)S(1)}, bf16[2,192,128]{2,1,0:T(8,128)(2,1)S(1)}, u32[]{:S(2)}, u32[]{:S(2)}) %collective-permute-start.11) | collective-permute-done | bytes 98336 | tf_op jit(solution)/shard_map/ppermute | solution.py:35
  57.4 4.3 %collective-permute-done.12.refs_4_ = bf16[2,192,128]{2,1,0:T(8,128)(2,1)S(1)} collective-permute-done((bf16[2,192,128]{2,1,0:T(8,128)(2,1)S(1)}, bf16[2,192,128]{2,1,0:T(8,128)(2,1)S(1)}, u32[]{:S(2)}, u32[]{:S(2)}) %collective-permute-start.12) | collective-permute-done | bytes 98336 | tf_op jit(solution)/shard_map/ppermute | solution.py:35
  62.0 1.1 collective-permute-start.23
  63.1 2.1 %collective-permute-start.17 = (bf16[2,192,128]{2,1,0:T(8,128)(2,1)S(1)}, bf16[2,192,128]{2,1,0:T(8,128)(2,1)S(1)}, u32[]{:S(2)}, u32[]{:S(2)}) collective-permute-start(bf16[2,192,128]{2,1,0:T(8,128)(2,1)S(1)} %get-tuple-element.104), channel_id=1, source_target_pairs={{0,8},{4,12},{8,0},{12,4},{16,24},{20,28},{24,16},{28,20},{1,9},{5... | collective-permute-start | bytes 294920 | tf_op jit(solution)/shard_map/ppermute | solution.py:35
  65.2 0.5 collective-permute-start.18
  65.7 1.9 %collective-permute-start.19 = (bf16[2,192,128]{2,1,0:T(8,128)(2,1)S(1)}, bf16[2,192,128]{2,1,0:T(8,128)(2,1)S(1)}, u32[]{:S(2)}, u32[]{:S(2)}) collective-permute-start(bf16[2,192,128]{2,1,0:T(8,128)(2,1)S(1)} %get-tuple-element.106), channel_id=1, source_target_pairs={{0,24},{4,28},{8,16},{12,20},{16,8},{20,12},{24,0},{28,4},{1,25},{... | collective-permute-start | bytes 294920 | tf_op jit(solution)/shard_map/ppermute | solution.py:35
  67.6 0.9 collective-permute-start.22
  68.5 0.6 mix.1
  69.1 5.8 %collective-permute-done.18.refs_4_ = bf16[2,192,128]{2,1,0:T(8,128)(2,1)S(1)} collective-permute-done((bf16[2,192,128]{2,1,0:T(8,128)(2,1)S(1)}, bf16[2,192,128]{2,1,0:T(8,128)(2,1)S(1)}, u32[]{:S(2)}, u32[]{:S(2)}) %collective-permute-start.18) | collective-permute-done | bytes 98336 | tf_op jit(solution)/shard_map/ppermute | solution.py:35
  75.2 0.6 weight_sum_a.1
  76.0 0.5 collective-permute-start.26
  76.5 0.6 weight_sum_b.1
  77.2 0.4 collective-permute-start.24
  77.7 0.8 collective-permute-start.21
  78.7 1.9 %collective-permute-start.33 = (bf16[2,112,512]{2,1,0:T(8,128)(2,1)S(1)}, bf16[2,112,512]{2,1,0:T(8,128)(2,1)S(1)}, u32[]{:S(2)}, u32[]{:S(2)}) collective-permute-start(bf16[2,112,512]{2,1,0:T(8,128)(2,1)S(1)} %get-tuple-element.117.refs_3_), channel_id=1, source_target_pairs={{0,8},{4,12},{8,0},{12,4},{16,24},{20,28},{24,16},{28,20},{1,9},{5... | collective-permute-start | bytes 688136 | tf_op jit(solution)/shard_map/ppermute | solution.py:35
  80.5 1.2 collective-permute-start.20
  82.1 3.3 %hidden_back.1 = (f32[192,1]{1,0:T(8,128)S(1)}, f32[192,896]{1,0:T(8,128)S(1)}, bf16[192,1024]{1,0:T(8,128)(2,1)S(1)}) custom-call(bf16[192,512]{1,0:T(8,128)(2,1)S(1)} %get-tuple-element.109.refs_0_, bf16[192,512]{1,0:T(8,128)(2,1)S(1)} %get-tuple-element.108.refs_4_.refs_1_.refs_0_, bf16[192,512]{1,0:T(8,128)(2,1)S(1)} %get-tuple-element.107.refs_2_.refs_0_, ...), custom_call_target="tpu_custom_call" | custom-call | bytes 1024 | tf_op jit(solution)/shard_map/hidden_back/pallas_call | solution.py:77
  85.5 0.6 weight_sum_c.1
  86.2 0.5 collective-permute-start.30
  86.7 2.1 %collective-permute-done.20.refs_1_ = bf16[192,512]{1,0:T(8,128)(2,1)S(1)} collective-permute-done((bf16[192,512]{1,0:T(8,128)(2,1)S(1)}, bf16[192,512]{1,0:T(8,128)(2,1)S(1)}, u32[]{:S(2)}, u32[]{:S(2)}) %collective-permute-start.20) | collective-permute-done | bytes 196640 | tf_op jit(solution)/shard_map/ppermute | solution.py:35
  88.8 0.6 weight_sum_d.1
  89.5 0.5 collective-permute-start.28
  90.0 1.0 collective-permute-done.32.refs_0_
  91.0 1.2 collective-permute-start.16
  92.2 0.8 collective-permute-start.34
  93.3 1.8 %collective-permute-start.36 = (bf16[2,112,512]{2,1,0:T(8,128)(2,1)S(1)}, bf16[2,112,512]{2,1,0:T(8,128)(2,1)S(1)}, u32[]{:S(2)}, u32[]{:S(2)}) collective-permute-start(bf16[2,112,512]{2,1,0:T(8,128)(2,1)S(1)} %get-tuple-element.130.refs_3_), channel_id=1, source_target_pairs={{0,8},{4,12},{8,0},{12,4},{16,24},{20,28},{24,16},{28,20},{1,9},{5... | collective-permute-start | bytes 688136 | tf_op jit(solution)/shard_map/ppermute | solution.py:35
  95.6 2.2 %collective-permute-start.38 = (bf16[1,112,512]{2,1,0:T(8,128)(2,1)S(1)}, bf16[1,112,512]{2,1,0:T(8,128)(2,1)S(1)}, u32[]{:S(2)}, u32[]{:S(2)}) collective-permute-start(bf16[1,112,512]{2,1,0:T(8,128)(2,1)S(1)} %get-tuple-element.129.refs_3_), channel_id=1, source_target_pairs={{0,16},{4,20},{8,24},{12,28},{16,0},{20,4},{24,8},{28,12},{1,17},{... | collective-permute-start | bytes 344072 | tf_op jit(solution)/shard_map/ppermute | solution.py:35
  97.8 4.1 %collective-permute-done.16.refs_3_ = bf16[192,896]{1,0:T(8,128)(2,1)S(1)} collective-permute-done((bf16[192,896]{1,0:T(8,128)(2,1)S(1)}, bf16[192,896]{1,0:T(8,128)(2,1)S(1)}, u32[]{:S(2)}, u32[]{:S(2)}) %collective-permute-start.16) | collective-permute-done | bytes 344096 | tf_op jit(solution)/shard_map/ppermute | solution.py:35
  102.0 2.2 %collective-permute-start.37 = (bf16[1,112,512]{2,1,0:T(8,128)(2,1)S(1)}, bf16[1,112,512]{2,1,0:T(8,128)(2,1)S(1)}, u32[]{:S(2)}, u32[]{:S(2)}) collective-permute-start(bf16[1,112,512]{2,1,0:T(8,128)(2,1)S(1)} %get-tuple-element.128.refs_2_), channel_id=1, source_target_pairs={{0,16},{4,20},{8,24},{12,28},{16,0},{20,4},{24,8},{28,12},{1,17},{... | collective-permute-start | bytes 344072 | tf_op jit(solution)/shard_map/ppermute | solution.py:35
  104.2 0.9 finish_mix.1.refs_2_
  105.1 0.4 collective-permute-done.36.refs_0_
  105.6 1.0 copy-done.3
  106.7 2.5 %collective-permute-done.35.refs_0_ = bf16[2,112,512]{2,1,0:T(8,128)(2,1)S(1)} collective-permute-done((bf16[2,112,512]{2,1,0:T(8,128)(2,1)S(1)}, bf16[2,112,512]{2,1,0:T(8,128)(2,1)S(1)}, u32[]{:S(2)}, u32[]{:S(2)}) %collective-permute-start.35) | collective-permute-done | bytes 229408 | tf_op jit(solution)/shard_map/ppermute | solution.py:35
  109.3 2.9 %collective-permute-start.39 = (bf16[1,112,512]{2,1,0:T(8,128)(2,1)S(1)}, bf16[1,112,512]{2,1,0:T(8,128)(2,1)S(1)}, u32[]{:S(2)}, u32[]{:S(2)}) collective-permute-start(bf16[1,112,512]{2,1,0:T(8,128)(2,1)S(1)} %get-tuple-element.136.refs_2_), channel_id=1, source_target_pairs={{0,16},{4,20},{8,24},{12,28},{16,0},{20,4},{24,8},{28,12},{1,17},{... | collective-permute-start | bytes 344072 | tf_op jit(solution)/shard_map/ppermute | solution.py:35
  112.2 1.1 finish_latents.1
  113.4 1.5 %collective-permute-done.37.refs_0_ = bf16[1,112,512]{2,1,0:T(8,128)(2,1)S(1)} collective-permute-done((bf16[1,112,512]{2,1,0:T(8,128)(2,1)S(1)}, bf16[1,112,512]{2,1,0:T(8,128)(2,1)S(1)}, u32[]{:S(2)}, u32[]{:S(2)}) %collective-permute-start.37) | collective-permute-done | bytes 114720 | tf_op jit(solution)/shard_map/ppermute | solution.py:35
  114.9 3.7 %collective-permute-done.40.refs_6_ = bf16[1,112,512]{2,1,0:T(8,128)(2,1)S(1)} collective-permute-done((bf16[1,112,512]{2,1,0:T(8,128)(2,1)S(1)}, bf16[1,112,512]{2,1,0:T(8,128)(2,1)S(1)}, u32[]{:S(2)}, u32[]{:S(2)}) %collective-permute-start.40) | collective-permute-done | bytes 114720 | tf_op jit(solution)/shard_map/ppermute | solution.py:35
  118.6 2.4 %collective-permute-done.39.refs_4_ = bf16[1,112,512]{2,1,0:T(8,128)(2,1)S(1)} collective-permute-done((bf16[1,112,512]{2,1,0:T(8,128)(2,1)S(1)}, bf16[1,112,512]{2,1,0:T(8,128)(2,1)S(1)}, u32[]{:S(2)}, u32[]{:S(2)}) %collective-permute-start.39) | collective-permute-done | bytes 114720 | tf_op jit(solution)/shard_map/ppermute | solution.py:35
  121.0 1.0 weight_total.1
  (71 shorter events, 3.7 us)
Async XLA Ops:
  1.7 7.1 %collective-permute-start = (bf16[32,3584]{1,0:T(8,128)(2,1)S(1)}, bf16[32,3584]{1,0:T(8,128)(2,1)S(1)}, u32[]{:S(2)}, u32[]{:S(2)}) collective-permute-start(bf16[32,3584]{1,0:T(8,128)(2,1)S(1)} %slice_bitcast_fusion), channel_id=1, source_target_pairs={{0,4},{4,8},{8,12},{12,16},{16,20},{20,24},{24,28},{1,5},{5,9},{9,... | collective-permute-start | bytes 688136 | tf_op jit(solution)/shard_map/ppermute | solution.py:664
  4.0 10.3 %collective-permute-start.1 = (bf16[192,896]{1,0:T(8,128)(2,1)}, bf16[192,896]{1,0:T(8,128)(2,1)S(1)}, u32[]{:S(2)}, u32[]{:S(2)}) collective-permute-start(bf16[192,896]{1,0:T(8,128)(2,1)} %bitcast.17), channel_id=1, source_target_pairs={{0,2},{2,0},{1,3},{3,1},{4,6},{6,4},{5,7},{7,5},{8,10},{10,8},{9,1... | collective-permute-start | bytes 1032200 | tf_op jit(solution)/shard_map/ppermute | solution.py:35
  8.7 2.0 %copy-start.2 = (bf16[512,1792]{1,0:T(8,128)(2,1)S(1)}, bf16[512,1792]{1,0:T(8,128)(2,1)}, u32[]{:S(2)}) copy-start(bf16[512,1792]{1,0:T(8,128)(2,1)} %refs_1_.2) | copy-start | bytes 5505028
  8.7 2.0 %copy-start.4 = (bf16[1,192,896]{2,1,0:T(8,128)(2,1)S(1)}, bf16[1,192,896]{2,1,0:T(8,128)(2,1)}, u32[]{:S(2)}) copy-start(bf16[1,192,896]{2,1,0:T(8,128)(2,1)} %param.11) | copy-start | bytes 1032196
  10.7 2.6 %copy-start = (bf16[1792,3,512]{2,0,1:T(8,128)(2,1)S(1)}, bf16[1792,3,512]{2,0,1:T(8,128)(2,1)}, u32[]{:S(2)}) copy-start(bf16[1792,3,512]{2,0,1:T(8,128)(2,1)} %param.13) | copy-start | bytes 16515076
  13.3 1.1 copy-start.1
  13.3 1.1 copy-start.5
  13.3 1.1 copy-start.6
  14.0 11.3 %collective-permute-start.5 = (bf16[192,896]{1,0:T(8,128)(2,1)S(1)}, bf16[192,896]{1,0:T(8,128)(2,1)S(1)}, u32[]{:S(2)}, u32[]{:S(2)}) collective-permute-start(bf16[192,896]{1,0:T(8,128)(2,1)S(1)} %get-tuple-element.83.refs_2_.refs_1_), channel_id=1, source_target_pairs={{0,2},{2,0},{1,3},{3,1},{4,6},{6,4},{5,7},{7,5},{8,10},{10,8},{9,1... | collective-permute-start | bytes 1032200 | tf_op jit(solution)/shard_map/ppermute | solution.py:35
  16.0 12.0 %collective-permute-start.2 = (bf16[3,192,128]{2,1,0:T(8,128)(2,1)S(1)}, bf16[3,192,128]{2,1,0:T(8,128)(2,1)S(1)}, u32[]{:S(2)}, u32[]{:S(2)}) collective-permute-start(bf16[3,192,128]{2,1,0:T(8,128)(2,1)S(1)} %get-tuple-element.79), channel_id=1, source_target_pairs={{0,8},{4,12},{8,0},{12,4},{16,24},{20,28},{24,16},{28,20},{1,9},{5... | collective-permute-start | bytes 442376 | tf_op jit(solution)/shard_map/ppermute | solution.py:35
  20.6 14.9 %collective-permute-start.3 = (bf16[3,192,128]{2,1,0:T(8,128)(2,1)S(1)}, bf16[3,192,128]{2,1,0:T(8,128)(2,1)S(1)}, u32[]{:S(2)}, u32[]{:S(2)}) collective-permute-start(bf16[3,192,128]{2,1,0:T(8,128)(2,1)S(1)} %get-tuple-element.80), channel_id=1, source_target_pairs={{0,16},{4,20},{8,24},{12,28},{16,0},{20,4},{24,8},{28,12},{1,17},{... | collective-permute-start | bytes 442376 | tf_op jit(solution)/shard_map/ppermute | solution.py:35
  23.2 14.2 %collective-permute-start.4 = (bf16[3,192,128]{2,1,0:T(8,128)(2,1)S(1)}, bf16[3,192,128]{2,1,0:T(8,128)(2,1)S(1)}, u32[]{:S(2)}, u32[]{:S(2)}) collective-permute-start(bf16[3,192,128]{2,1,0:T(8,128)(2,1)S(1)} %get-tuple-element.81), channel_id=1, source_target_pairs={{0,24},{4,28},{8,16},{12,20},{16,8},{20,12},{24,0},{28,4},{1,25},{... | collective-permute-start | bytes 442376 | tf_op jit(solution)/shard_map/ppermute | solution.py:35
  23.7 19.8 %collective-permute-start.10 = (bf16[8,112,256]{2,1,0:T(8,128)(2,1)S(1)}, bf16[8,112,256]{2,1,0:T(8,128)(2,1)S(1)}, u32[]{:S(2)}, u32[]{:S(2)}) collective-permute-start(bf16[8,112,256]{2,1,0:T(8,128)(2,1)S(1)} %get-tuple-element.90), channel_id=1, source_target_pairs={{0,1},{1,0},{2,3},{3,2},{4,5},{5,4},{6,7},{7,6},{8,9},{9,8},{10,11... | collective-permute-start | bytes 1376264 | tf_op jit(solution)/shard_map/ppermute | solution.py:35
  26.1 11.4 %collective-permute-start.6 = (bf16[192,128]{1,0:T(8,128)(2,1)S(1)}, bf16[192,128]{1,0:T(8,128)(2,1)S(1)}, u32[]{:S(2)}, u32[]{:S(2)}) collective-permute-start(bf16[192,128]{1,0:T(8,128)(2,1)S(1)} %get-tuple-element.86), channel_id=1, source_target_pairs={{0,8},{4,12},{8,0},{12,4},{16,24},{20,28},{24,16},{28,20},{1,9},{5... | collective-permute-start | bytes 147464 | tf_op jit(solution)/shard_map/ppermute | solution.py:35
  28.0 10.6 %collective-permute-start.7 = (bf16[192,128]{1,0:T(8,128)(2,1)S(1)}, bf16[192,128]{1,0:T(8,128)(2,1)S(1)}, u32[]{:S(2)}, u32[]{:S(2)}) collective-permute-start(bf16[192,128]{1,0:T(8,128)(2,1)S(1)} %get-tuple-element.87), channel_id=1, source_target_pairs={{0,16},{4,20},{8,24},{12,28},{16,0},{20,4},{24,8},{28,12},{1,17},{... | collective-permute-start | bytes 147464 | tf_op jit(solution)/shard_map/ppermute | solution.py:35
  35.5 5.9 %collective-permute-start.8 = (bf16[192,128]{1,0:T(8,128)(2,1)S(1)}, bf16[192,128]{1,0:T(8,128)(2,1)S(1)}, u32[]{:S(2)}, u32[]{:S(2)}) collective-permute-start(bf16[192,128]{1,0:T(8,128)(2,1)S(1)} %get-tuple-element.88), channel_id=1, source_target_pairs={{0,24},{4,28},{8,16},{12,20},{16,8},{20,12},{24,0},{28,4},{1,25},{... | collective-permute-start | bytes 147464 | tf_op jit(solution)/shard_map/ppermute | solution.py:35
  41.4 2.1 %collective-permute-start.9 = (bf16[4,2,192,128]{3,2,1,0:T(8,128)(2,1)S(1)}, bf16[4,2,192,128]{3,2,1,0:T(8,128)(2,1)S(1)}, u32[]{:S(2)}, u32[]{:S(2)}) collective-permute-start(bf16[4,2,192,128]{3,2,1,0:T(8,128)(2,1)S(1)} %gather.1), channel_id=1, source_target_pairs={{0,4},{4,0},{8,12},{12,8},{16,20},{20,16},{24,28},{28,24},{1,5},{5... | collective-permute-start | bytes 1179656 | tf_op jit(solution)/shard_map/ppermute | solution.py:35
  42.0 13.3 %collective-permute-start.15 = (bf16[8,112,256]{2,1,0:T(8,128)(2,1)S(1)}, bf16[8,112,256]{2,1,0:T(8,128)(2,1)S(1)}, u32[]{:S(2)}, u32[]{:S(2)}) collective-permute-start(bf16[8,112,256]{2,1,0:T(8,128)(2,1)S(1)} %get-tuple-element.99), channel_id=1, source_target_pairs={{0,1},{1,0},{2,3},{3,2},{4,5},{5,4},{6,7},{7,6},{8,9},{9,8},{10,11... | collective-permute-start | bytes 1376264 | tf_op jit(solution)/shard_map/ppermute | solution.py:35
  50.6 4.7 %collective-permute-start.14 = (bf16[4,2,192,128]{3,2,1,0:T(8,128)(2,1)S(1)}, bf16[4,2,192,128]{3,2,1,0:T(8,128)(2,1)S(1)}, u32[]{:S(2)}, u32[]{:S(2)}) collective-permute-start(bf16[4,2,192,128]{3,2,1,0:T(8,128)(2,1)S(1)} %get-tuple-element.98), channel_id=1, source_target_pairs={{0,4},{4,0},{8,12},{12,8},{16,20},{20,16},{24,28},{28,24},{1,5},{5... | collective-permute-start | bytes 1179656 | tf_op jit(solution)/shard_map/ppermute | solution.py:35
  50.9 6.5 %collective-permute-start.11 = (bf16[2,192,128]{2,1,0:T(8,128)(2,1)S(1)}, bf16[2,192,128]{2,1,0:T(8,128)(2,1)S(1)}, u32[]{:S(2)}, u32[]{:S(2)}) collective-permute-start(bf16[2,192,128]{2,1,0:T(8,128)(2,1)S(1)} %get-tuple-element.94), channel_id=1, source_target_pairs={{0,8},{4,12},{8,0},{12,4},{16,24},{20,28},{24,16},{28,20},{1,9},{5... | collective-permute-start | bytes 294920 | tf_op jit(solution)/shard_map/ppermute | solution.py:35
  50.9 10.8 %collective-permute-start.12 = (bf16[2,192,128]{2,1,0:T(8,128)(2,1)S(1)}, bf16[2,192,128]{2,1,0:T(8,128)(2,1)S(1)}, u32[]{:S(2)}, u32[]{:S(2)}) collective-permute-start(bf16[2,192,128]{2,1,0:T(8,128)(2,1)S(1)} %get-tuple-element.95), channel_id=1, source_target_pairs={{0,16},{4,20},{8,24},{12,28},{16,0},{20,4},{24,8},{28,12},{1,17},{... | collective-permute-start | bytes 294920 | tf_op jit(solution)/shard_map/ppermute | solution.py:35
  53.4 8.3 %collective-permute-start.13 = (bf16[2,192,128]{2,1,0:T(8,128)(2,1)S(1)}, bf16[2,192,128]{2,1,0:T(8,128)(2,1)S(1)}, u32[]{:S(2)}, u32[]{:S(2)}) collective-permute-start(bf16[2,192,128]{2,1,0:T(8,128)(2,1)S(1)} %get-tuple-element.96), channel_id=1, source_target_pairs={{0,24},{4,28},{8,16},{12,20},{16,8},{20,12},{24,0},{28,4},{1,25},{... | collective-permute-start | bytes 294920 | tf_op jit(solution)/shard_map/ppermute | solution.py:35
  55.3 26.9 %slice-start = ((s8[5505024]{0:T(1024)(128)(4,1)}), s8[4194304]{0:T(1024)(128)(4,1)S(1)}, s32[]{:S(2)}) async-start(s8[5505024]{0:T(1024)(128)(4,1)} %bitcast.14), calls=%async_computation | async-start | bytes 8388608
  62.0 13.2 %collective-permute-start.23 = (bf16[192,512]{1,0:T(8,128)(2,1)S(1)}, bf16[192,512]{1,0:T(8,128)(2,1)S(1)}, u32[]{:S(2)}, u32[]{:S(2)}) collective-permute-start(bf16[192,512]{1,0:T(8,128)(2,1)S(1)} %get-tuple-element.101.refs_0_.refs_2_), channel_id=1, source_target_pairs={{0,1},{1,0},{2,3},{3,2},{4,5},{5,4},{6,7},{7,6},{8,9},{9,8},{10,11... | collective-permute-start | bytes 589832 | tf_op jit(solution)/shard_map/ppermute | solution.py:35
  63.1 6.0 %collective-permute-start.17 = (bf16[2,192,128]{2,1,0:T(8,128)(2,1)S(1)}, bf16[2,192,128]{2,1,0:T(8,128)(2,1)S(1)}, u32[]{:S(2)}, u32[]{:S(2)}) collective-permute-start(bf16[2,192,128]{2,1,0:T(8,128)(2,1)S(1)} %get-tuple-element.104), channel_id=1, source_target_pairs={{0,8},{4,12},{8,0},{12,4},{16,24},{20,28},{24,16},{28,20},{1,9},{5... | collective-permute-start | bytes 294920 | tf_op jit(solution)/shard_map/ppermute | solution.py:35
  65.2 9.7 %collective-permute-start.18 = (bf16[2,192,128]{2,1,0:T(8,128)(2,1)S(1)}, bf16[2,192,128]{2,1,0:T(8,128)(2,1)S(1)}, u32[]{:S(2)}, u32[]{:S(2)}) collective-permute-start(bf16[2,192,128]{2,1,0:T(8,128)(2,1)S(1)} %get-tuple-element.105), channel_id=1, source_target_pairs={{0,16},{4,20},{8,24},{12,28},{16,0},{20,4},{24,8},{28,12},{1,17},{... | collective-permute-start | bytes 294920 | tf_op jit(solution)/shard_map/ppermute | solution.py:35
  65.7 9.2 %collective-permute-start.19 = (bf16[2,192,128]{2,1,0:T(8,128)(2,1)S(1)}, bf16[2,192,128]{2,1,0:T(8,128)(2,1)S(1)}, u32[]{:S(2)}, u32[]{:S(2)}) collective-permute-start(bf16[2,192,128]{2,1,0:T(8,128)(2,1)S(1)} %get-tuple-element.106), channel_id=1, source_target_pairs={{0,24},{4,28},{8,16},{12,20},{16,8},{20,12},{24,0},{28,4},{1,25},{... | collective-permute-start | bytes 294920 | tf_op jit(solution)/shard_map/ppermute | solution.py:35
  67.6 8.9 %collective-permute-start.22 = (bf16[192,512]{1,0:T(8,128)(2,1)S(1)}, bf16[192,512]{1,0:T(8,128)(2,1)S(1)}, u32[]{:S(2)}, u32[]{:S(2)}) collective-permute-start(bf16[192,512]{1,0:T(8,128)(2,1)S(1)} %get-tuple-element.109.refs_0_), channel_id=1, source_target_pairs={{0,1},{1,0},{2,3},{3,2},{4,5},{5,4},{6,7},{7,6},{8,9},{9,8},{10,11... | collective-permute-start | bytes 589832 | tf_op jit(solution)/shard_map/ppermute | solution.py:35
  74.9 7.2 %slice-start.1 = ((s8[5505024]{0:T(1024)(128)(4,1)}), s8[1310720]{0:T(1024)(128)(4,1)S(1)}, s32[]{:S(2)}) async-start(s8[5505024]{0:T(1024)(128)(4,1)} %bitcast.14), calls=%async_computation.1 | async-start | bytes 2621440
  75.9 2.6 %collective-permute-start.27 = (bf16[2,112,512]{2,1,0:T(8,128)(2,1)S(1)}, bf16[2,112,512]{2,1,0:T(8,128)(2,1)S(1)}, u32[]{:S(2)}, u32[]{:S(2)}) collective-permute-start(bf16[2,112,512]{2,1,0:T(8,128)(2,1)S(1)} %get-tuple-element.115), channel_id=1, source_target_pairs={{0,4},{4,0},{8,12},{12,8},{16,20},{20,16},{24,28},{28,24},{1,5},{5... | collective-permute-start | bytes 688136 | tf_op jit(solution)/shard_map/ppermute | solution.py:35
  76.0 2.6 %collective-permute-start.26 = (bf16[2,112,512]{2,1,0:T(8,128)(2,1)S(1)}, bf16[2,112,512]{2,1,0:T(8,128)(2,1)S(1)}, u32[]{:S(2)}, u32[]{:S(2)}) collective-permute-start(bf16[2,112,512]{2,1,0:T(8,128)(2,1)S(1)} %get-tuple-element.111.refs_4_), channel_id=1, source_target_pairs={{0,4},{4,0},{8,12},{12,8},{16,20},{20,16},{24,28},{28,24},{1,5},{5... | collective-permute-start | bytes 688136 | tf_op jit(solution)/shard_map/ppermute | solution.py:35
  77.1 4.6 %collective-permute-start.25 = (bf16[2,112,512]{2,1,0:T(8,128)(2,1)S(1)}, bf16[2,112,512]{2,1,0:T(8,128)(2,1)S(1)}, u32[]{:S(2)}, u32[]{:S(2)}) collective-permute-start(bf16[2,112,512]{2,1,0:T(8,128)(2,1)S(1)} %get-tuple-element.113), channel_id=1, source_target_pairs={{0,4},{4,0},{8,12},{12,8},{16,20},{20,16},{24,28},{28,24},{1,5},{5... | collective-permute-start | bytes 688136 | tf_op jit(solution)/shard_map/ppermute | solution.py:35
  77.2 4.5 %collective-permute-start.24 = (bf16[2,112,512]{2,1,0:T(8,128)(2,1)S(1)}, bf16[2,112,512]{2,1,0:T(8,128)(2,1)S(1)}, u32[]{:S(2)}, u32[]{:S(2)}) collective-permute-start(bf16[2,112,512]{2,1,0:T(8,128)(2,1)S(1)} %get-tuple-element.112.refs_3_), channel_id=1, source_target_pairs={{0,4},{4,0},{8,12},{12,8},{16,20},{20,16},{24,28},{28,24},{1,5},{5... | collective-permute-start | bytes 688136 | tf_op jit(solution)/shard_map/ppermute | solution.py:35
  77.7 7.8 %collective-permute-start.21 = (bf16[192,512]{1,0:T(8,128)(2,1)S(1)}, bf16[192,512]{1,0:T(8,128)(2,1)S(1)}, u32[]{:S(2)}, u32[]{:S(2)}) collective-permute-start(bf16[192,512]{1,0:T(8,128)(2,1)S(1)} %get-tuple-element.108.refs_4_.refs_1_.refs_0_), channel_id=1, source_target_pairs={{0,1},{1,0},{2,3},{3,2},{4,5},{5,4},{6,7},{7,6},{8,9},{9,8},{10,11... | collective-permute-start | bytes 589832 | tf_op jit(solution)/shard_map/ppermute | solution.py:35
  78.7 10.8 %collective-permute-start.33 = (bf16[2,112,512]{2,1,0:T(8,128)(2,1)S(1)}, bf16[2,112,512]{2,1,0:T(8,128)(2,1)S(1)}, u32[]{:S(2)}, u32[]{:S(2)}) collective-permute-start(bf16[2,112,512]{2,1,0:T(8,128)(2,1)S(1)} %get-tuple-element.117.refs_3_), channel_id=1, source_target_pairs={{0,8},{4,12},{8,0},{12,4},{16,24},{20,28},{24,16},{28,20},{1,9},{5... | collective-permute-start | bytes 688136 | tf_op jit(solution)/shard_map/ppermute | solution.py:35
  80.5 8.3 %collective-permute-start.20 = (bf16[192,512]{1,0:T(8,128)(2,1)S(1)}, bf16[192,512]{1,0:T(8,128)(2,1)S(1)}, u32[]{:S(2)}, u32[]{:S(2)}) collective-permute-start(bf16[192,512]{1,0:T(8,128)(2,1)S(1)} %get-tuple-element.107.refs_2_.refs_0_), channel_id=1, source_target_pairs={{0,1},{1,0},{2,3},{3,2},{4,5},{5,4},{6,7},{7,6},{8,9},{9,8},{10,11... | collective-permute-start | bytes 589832 | tf_op jit(solution)/shard_map/ppermute | solution.py:35
  81.8 9.2 %collective-permute-start.32 = (bf16[2,112,512]{2,1,0:T(8,128)(2,1)S(1)}, bf16[2,112,512]{2,1,0:T(8,128)(2,1)S(1)}, u32[]{:S(2)}, u32[]{:S(2)}) collective-permute-start(bf16[2,112,512]{2,1,0:T(8,128)(2,1)S(1)} %get-tuple-element.118.refs_8_), channel_id=1, source_target_pairs={{0,8},{4,12},{8,0},{12,4},{16,24},{20,28},{24,16},{28,20},{1,9},{5... | collective-permute-start | bytes 688136 | tf_op jit(solution)/shard_map/ppermute | solution.py:35
  86.1 6.1 %collective-permute-start.31 = (bf16[2,112,512]{2,1,0:T(8,128)(2,1)S(1)}, bf16[2,112,512]{2,1,0:T(8,128)(2,1)S(1)}, u32[]{:S(2)}, u32[]{:S(2)}) collective-permute-start(bf16[2,112,512]{2,1,0:T(8,128)(2,1)S(1)} %get-tuple-element.124), channel_id=1, source_target_pairs={{0,4},{4,0},{8,12},{12,8},{16,20},{20,16},{24,28},{28,24},{1,5},{5... | collective-permute-start | bytes 688136 | tf_op jit(solution)/shard_map/ppermute | solution.py:35
  86.2 7.0 %collective-permute-start.30 = (bf16[2,112,512]{2,1,0:T(8,128)(2,1)S(1)}, bf16[2,112,512]{2,1,0:T(8,128)(2,1)S(1)}, u32[]{:S(2)}, u32[]{:S(2)}) collective-permute-start(bf16[2,112,512]{2,1,0:T(8,128)(2,1)S(1)} %get-tuple-element.120.refs_4_), channel_id=1, source_target_pairs={{0,4},{4,0},{8,12},{12,8},{16,20},{20,16},{24,28},{28,24},{1,5},{5... | collective-permute-start | bytes 688136 | tf_op jit(solution)/shard_map/ppermute | solution.py:35
  89.4 5.7 %collective-permute-start.29 = (bf16[2,112,512]{2,1,0:T(8,128)(2,1)S(1)}, bf16[2,112,512]{2,1,0:T(8,128)(2,1)S(1)}, u32[]{:S(2)}, u32[]{:S(2)}) collective-permute-start(bf16[2,112,512]{2,1,0:T(8,128)(2,1)S(1)} %get-tuple-element.122), channel_id=1, source_target_pairs={{0,4},{4,0},{8,12},{12,8},{16,20},{20,16},{24,28},{28,24},{1,5},{5... | collective-permute-start | bytes 688136 | tf_op jit(solution)/shard_map/ppermute | solution.py:35
  89.5 5.6 %collective-permute-start.28 = (bf16[2,112,512]{2,1,0:T(8,128)(2,1)S(1)}, bf16[2,112,512]{2,1,0:T(8,128)(2,1)S(1)}, u32[]{:S(2)}, u32[]{:S(2)}) collective-permute-start(bf16[2,112,512]{2,1,0:T(8,128)(2,1)S(1)} %get-tuple-element.121.refs_2_), channel_id=1, source_target_pairs={{0,4},{4,0},{8,12},{12,8},{16,20},{20,16},{24,28},{28,24},{1,5},{5... | collective-permute-start | bytes 688136 | tf_op jit(solution)/shard_map/ppermute | solution.py:35
  91.0 11.0 %collective-permute-start.16 = (bf16[192,896]{1,0:T(8,128)(2,1)S(1)}, bf16[192,896]{1,0:T(8,128)(2,1)S(1)}, u32[]{:S(2)}, u32[]{:S(2)}) collective-permute-start(bf16[192,896]{1,0:T(8,128)(2,1)S(1)} %get-tuple-element.103), channel_id=1, source_target_pairs={{0,2},{2,0},{1,3},{3,1},{4,6},{6,4},{5,7},{7,5},{8,10},{10,8},{9,1... | collective-permute-start | bytes 1032200 | tf_op jit(solution)/shard_map/ppermute | solution.py:35
  92.2 20.0 %collective-permute-start.34 = (bf16[192,1024]{1,0:T(8,128)(2,1)S(1)}, bf16[192,1024]{1,0:T(8,128)(2,1)S(1)}, u32[]{:S(2)}, u32[]{:S(2)}) collective-permute-start(bf16[192,1024]{1,0:T(8,128)(2,1)S(1)} %get-tuple-element.133), channel_id=1, source_target_pairs={{0,2},{2,0},{1,3},{3,1},{4,6},{6,4},{5,7},{7,5},{8,10},{10,8},{9,1... | collective-permute-start | bytes 1179656 | tf_op jit(solution)/shard_map/ppermute | solution.py:35
  93.3 12.3 %collective-permute-start.36 = (bf16[2,112,512]{2,1,0:T(8,128)(2,1)S(1)}, bf16[2,112,512]{2,1,0:T(8,128)(2,1)S(1)}, u32[]{:S(2)}, u32[]{:S(2)}) collective-permute-start(bf16[2,112,512]{2,1,0:T(8,128)(2,1)S(1)} %get-tuple-element.130.refs_3_), channel_id=1, source_target_pairs={{0,8},{4,12},{8,0},{12,4},{16,24},{20,28},{24,16},{28,20},{1,9},{5... | collective-permute-start | bytes 688136 | tf_op jit(solution)/shard_map/ppermute | solution.py:35
  95.3 13.9 %collective-permute-start.35 = (bf16[2,112,512]{2,1,0:T(8,128)(2,1)S(1)}, bf16[2,112,512]{2,1,0:T(8,128)(2,1)S(1)}, u32[]{:S(2)}, u32[]{:S(2)}) collective-permute-start(bf16[2,112,512]{2,1,0:T(8,128)(2,1)S(1)} %get-tuple-element.131.refs_4_), channel_id=1, source_target_pairs={{0,8},{4,12},{8,0},{12,4},{16,24},{20,28},{24,16},{28,20},{1,9},{5... | collective-permute-start | bytes 688136 | tf_op jit(solution)/shard_map/ppermute | solution.py:35
  95.6 17.8 %collective-permute-start.38 = (bf16[1,112,512]{2,1,0:T(8,128)(2,1)S(1)}, bf16[1,112,512]{2,1,0:T(8,128)(2,1)S(1)}, u32[]{:S(2)}, u32[]{:S(2)}) collective-permute-start(bf16[1,112,512]{2,1,0:T(8,128)(2,1)S(1)} %get-tuple-element.129.refs_3_), channel_id=1, source_target_pairs={{0,16},{4,20},{8,24},{12,28},{16,0},{20,4},{24,8},{28,12},{1,17},{... | collective-permute-start | bytes 344072 | tf_op jit(solution)/shard_map/ppermute | solution.py:35
  102.0 12.9 %collective-permute-start.37 = (bf16[1,112,512]{2,1,0:T(8,128)(2,1)S(1)}, bf16[1,112,512]{2,1,0:T(8,128)(2,1)S(1)}, u32[]{:S(2)}, u32[]{:S(2)}) collective-permute-start(bf16[1,112,512]{2,1,0:T(8,128)(2,1)S(1)} %get-tuple-element.128.refs_2_), channel_id=1, source_target_pairs={{0,16},{4,20},{8,24},{12,28},{16,0},{20,4},{24,8},{28,12},{1,17},{... | collective-permute-start | bytes 344072 | tf_op jit(solution)/shard_map/ppermute | solution.py:35
  105.6 1.0 copy-start.3
  109.2 9.3 %collective-permute-start.40 = (bf16[1,112,512]{2,1,0:T(8,128)(2,1)S(1)}, bf16[1,112,512]{2,1,0:T(8,128)(2,1)S(1)}, u32[]{:S(2)}, u32[]{:S(2)}) collective-permute-start(bf16[1,112,512]{2,1,0:T(8,128)(2,1)S(1)} %get-tuple-element.137.refs_7_), channel_id=1, source_target_pairs={{0,16},{4,20},{8,24},{12,28},{16,0},{20,4},{24,8},{28,12},{1,17},{... | collective-permute-start | bytes 344072 | tf_op jit(solution)/shard_map/ppermute | solution.py:35
  109.3 11.6 %collective-permute-start.39 = (bf16[1,112,512]{2,1,0:T(8,128)(2,1)S(1)}, bf16[1,112,512]{2,1,0:T(8,128)(2,1)S(1)}, u32[]{:S(2)}, u32[]{:S(2)}) collective-permute-start(bf16[1,112,512]{2,1,0:T(8,128)(2,1)S(1)} %get-tuple-element.136.refs_2_), channel_id=1, source_target_pairs={{0,16},{4,20},{8,24},{12,28},{16,0},{20,4},{24,8},{28,12},{1,17},{... | collective-permute-start | bytes 344072 | tf_op jit(solution)/shard_map/ppermute | solution.py:35
